TPU v7x, 32 devices: a whole 2x2x4 slice. The times are simulated.
32 devices in a mesh: lat: 4 (over y, x), lev: 8 (over z, core).
Axes of the slice: x: 2, y: 2, z: 4, core: 2. Of those that a mesh axis runs over, the one named last changes fastest.
Arguments:
- adjoint_grid: bfloat16 [128, 768, 1536], P('lev', 'lat'), may hold values from -6 to 6
- wind: bfloat16 [128, 768, 1536], P('lev', 'lat'), may hold values from -6 to 6
- legendre: bfloat16 [1024, 768, 520], P(('lat', 'lev')), may hold values from -0.21875 to 0.21875
- vertical: bfloat16 [16, 128, 128], replicated, may hold values from -0.5 to 0.5
- pair_table: int32 [256], replicated, may hold values from 0 to 255, each once
- degree_matrix: int32 [512], replicated, may hold values from 0 to 15
Outputs:
- adjoint_out: bfloat16 [128, 768, 1536], P('lev', 'lat')
Inputs may be any that keep to these rules, and one draw needn't show every extreme that they name: `pair_table`: the values are distinct: every pair (m, 511 - m) with m < 256 stands in exactly one slot.
All inputs are finite; a program needn't handle non-finite values.
Results may differ from a plain program's by a relative error of at most 0.008.
Values may be sent and summed in bfloat16 or wider, within the bound.
No kernel may reach another device: no remote copies, remote signals or barrier semaphores. Data moves between devices by JAX's collectives and lax.ppermute only.
A program may use at most 128 MiB of HBM per device.

v0:
```python
import math

import jax
import jax.numpy as jnp
from jax import lax
from jax.sharding import PartitionSpec as P

N = 512


def fourier_basis(wavenumbers, points):
    longitude = jnp.arange(points, dtype=jnp.int32)
    phases = wavenumbers[:, :, None] * longitude[None, None, :] % points
    angles = phases.astype(jnp.float32) * (2.0 * jnp.pi / points)
    basis = jnp.stack([jnp.cos(angles), -jnp.sin(angles)], axis=2)
    return basis.reshape(-1, points)


def member_layout(lower_wave, row_total):
    packed_buffer = jnp.arange(row_total, dtype=jnp.int32)
    first_member = packed_buffer[None, :] < (N - lower_wave)[:, None]
    second_member = jnp.logical_not(first_member) & (packed_buffer[None, :] <= N)
    degree = jnp.where(
        first_member, lower_wave[:, None] + packed_buffer[None, :], packed_buffer[None, :] - 1
    )
    degree = jnp.clip(degree, 0, N - 1)
    return (first_member, second_member, degree)


def solve_columns(spectral_state, matrix_index, vertical):

    def add_matrix(operator_index, running):
        product = jnp.einsum(
            "xjm,mg->xjg",
            spectral_state,
            vertical[operator_index],
            preferred_element_type=jnp.float32,
        )
        return running + jnp.where((matrix_index == operator_index)[:, :, None], product, 0.0)

    zero_sums = jnp.zeros(spectral_state.shape, jnp.float32)
    return lax.fori_loop(0, vertical.shape[0], add_matrix, zero_sums).astype(jnp.bfloat16)


def body(adjoint_grid, wind, legendre, vertical, pair_table, degree_matrix):
    vertical_level_rows, lat_rows, points = adjoint_grid.shape
    lat_devices = lax.axis_size("lat")
    lev_devices = lax.axis_size("lev")
    slots = legendre.shape[0]
    all_lats = legendre.shape[1]
    packed_rows = legendre.shape[2]
    levels = vertical.shape[1]
    wavenumbers = jnp.stack([pair_table, N - 1 - pair_table], axis=1)
    basis = fourier_basis(wavenumbers, points)
    analysis_table = (basis * (1.0 / math.sqrt(points))).astype(jnp.bfloat16)
    synthesis_table = (basis * (1.0 / math.sqrt(N))).astype(jnp.bfloat16)
    fourier = jnp.einsum(
        "cx,vlx->cvl", analysis_table, adjoint_grid, preferred_element_type=jnp.float32
    )
    fourier = fourier.astype(jnp.bfloat16).reshape(
        lat_devices, lev_devices, slots, vertical_level_rows, lat_rows
    )
    moved = lax.all_to_all(
        lax.all_to_all(fourier, "lev", split_axis=1, concat_axis=3, tiled=True),
        "lat",
        split_axis=0,
        concat_axis=4,
        tiled=True,
    )
    field_stack = moved.reshape(slots, levels, all_lats)
    first_slot = (lax.axis_index("lat") * lev_devices + lax.axis_index("lev")) * slots
    column = first_slot + jnp.arange(slots, dtype=jnp.int32)
    lower_cols = jnp.take(pair_table, column // 4)
    member = column // 2 % 2
    first_member, second_member, degree = member_layout(lower_cols, packed_rows)
    own_rows = jnp.where((member == 0)[:, None], first_member, second_member).astype(jnp.float32)
    spectral_state = jnp.einsum(
        "peq,pae->pqa", legendre, field_stack, preferred_element_type=jnp.float32
    )
    spectral_state = (spectral_state * own_rows[:, :, None]).astype(jnp.bfloat16)
    matrix_index = jnp.take(degree_matrix, degree)
    solved_columns = solve_columns(spectral_state, matrix_index, vertical)
    gridpoint_coefficients = jnp.einsum(
        "ncb,nba->nac", legendre, solved_columns, preferred_element_type=jnp.float32
    )
    gridpoint_coefficients = gridpoint_coefficients.astype(jnp.bfloat16).reshape(
        1, 1, slots, levels, all_lats
    )
    returned = lax.all_to_all(
        lax.all_to_all(gridpoint_coefficients, "lat", split_axis=4, concat_axis=0, tiled=True),
        "lev",
        split_axis=3,
        concat_axis=1,
        tiled=True,
    )
    columns = returned.reshape(lat_devices * lev_devices * slots, vertical_level_rows, lat_rows)
    regridded = jnp.einsum(
        "cvl,cx->vlx", columns, synthesis_table, preferred_element_type=jnp.float32
    )
    return (regridded * wind.astype(jnp.float32)).astype(jnp.bfloat16)


def solution(mesh):
    placed = (
        P("lev", "lat", None),
        P("lev", "lat", None),
        P(("lat", "lev"), None, None),
        P(),
        P(),
        P(),
    )
    return jax.shard_map(
        body, mesh=mesh, in_specs=placed, out_specs=P("lev", "lat", None), check_vma=False
    )
```

profile of v0, /device:TPU:0, one launch (start us, length us, event | category | flops | bytes accessed | tf_op | source)
XLA Modules:
  0.0 918.2 jit_solution(6341435232611330366)
XLA Ops:
  0.0 0.0 copy-start
  0.0 0.7 broadcast_subtract_fusion
  0.7 0.7 pad_add_fusion
  1.4 13.3 %fusion.13 = (f32[256,2,1,1536]{3,0,2,1:T(8,128)S(1)}, f32[256,2,1,1536]{3,0,2,1:T(8,128)S(1)}) fusion(s32[256,2]{0,1:T(2,128)S(1)} %pad_add_fusion), kind=kLoop, calls=%fused_computation.25 | loop fusion | flops 7864320 | bytes 6293504 | tf_op jit(solution)/shard_map/cos | solution.py:15
  14.7 2.3 multiply_convert_fusion.3
  17.1 3.2 copy.49
  20.3 2.7 reshape.385
  23.0 15.2 %convolution_convert_fusion = bf16[1024,16,192]{0,2,1:T(8,128)(2,1)} fusion(bf16[1024,1536,1]{1,0,2:T(8,128)(2,1)} %reshape.385, bf16[16,192,1536]{2,1,0:T(8,128)(2,1)} %param.8), kind=kOutput, calls=%fused_computation.18 | convolution fusion | flops 9666822144 | bytes 18874368 | tf_op jit(solution)/shard_map/cx,vlx->cvl/dot_general | solution.py:57
  38.2 12.5 %copy.50 = bf16[1024,16,192]{2,1,0:T(8,128)(2,1)} copy(bf16[1024,16,192]{0,2,1:T(8,128)(2,1)} %convolution_convert_fusion) | data formatting | bytes 12582912 | tf_op jit(solution)/shard_map/convert_element_type | solution.py:60
  50.7 7.5 copy.51
  58.2 190.4 %all_to_all.66 = bf16[4,8,32,16,192]{4,3,2,0,1:T(8,128)(2,1)} all-to-all(bf16[4,8,32,16,192]{4,3,2,0,1:T(8,128)(2,1)} %copy.51), channel_id=1, replica_groups=mesh['lat'=4,'lev'=8] {'lev'}, dimensions={1} | all-to-all | bytes 12582912 | tf_op jit(solution)/shard_map/all_to_all | solution.py:64
  248.6 8.1 copy.52
  256.7 10.7 %copy.53 = bf16[4,1,32,128,192]{3,4,2,1,0:T(8,128)(2,1)} copy(bf16[4,1,32,128,192]{4,3,2,0,1:T(8,128)(2,1)} %bitcast.50) | data formatting | bytes 12582912 | tf_op jit(solution)/shard_map/all_to_all | solution.py:64
  267.4 0.0 copy-start.2
  267.4 5.5 all-to-all-start.1
  273.0 0.0 copy-done.2
  273.0 0.7 gather_fusion
  273.7 0.1 compare_select_fusion
  273.8 0.1 reshape.377
  274.0 0.0 copy-done
  274.0 97.2 %gather_fusion.1 = s32[16640]{0:T(1024)S(1)} fusion(s32[512]{0:T(512)S(1)} %copy-done, s32[17408]{0:T(1024)S(1)} %pad_clamp_fusion), kind=kCustom, calls=%fused_computation.1 | custom fusion | bytes 199680 | tf_op jit(solution)/shard_map/jit(_take)/gather | solution.py:81
  371.2 0.1 reshape.376
  371.4 0.1 fusion.22
  371.5 0.1 fusion.20
  371.6 0.0 all-to-all-done.1
  371.6 6.1 copy.54
  377.7 15.6 %fusion.4 = bf16[32,520,128]{2,1,0:T(8,128)(2,1)} fusion(f32[32,520]{1,0:T(8,128)S(1)} %fusion.22, bf16[32,128,768]{1,2,0:T(8,128)(2,1)} %bitcast.53, bf16[32,768,520]{1,2,0:T(8,128)(2,1)} %param.10), kind=kOutput, calls=%fused_computation.15 | convolution fusion | flops 3275816960 | bytes 36176896 | tf_op jit(solution)/shard_map/peq,pae->pqa/dot_general | solution.py:77
  393.2 169.4 %while.14 = (s32[]{:T(128)}, f32[32,520,128]{2,1,0:T(8,128)}, s32[32,520]{1,0:T(8,128)S(1)}, bf16[16,128,128]{2,1,0:T(8,128)(2,1)}, bf16[32,520,128]{2,1,0:T(8,128)(2,1)}, /*index=5*/s32[]{:T(128)}, s32[]{:T(128)}) while((s32[]{:T(128)}, f32[32,520,128]{2,1,0:T(8,128)}, s32[32,520]{1,0:T(8,128)S(1)}, ...), condition=%wide.region_1.2_spmd.clone, body=%wide.region_0.1_spmd.clone.sunk | while | flops 551665920 | bytes 21432408 | solution.py:42
  393.3 7.9 bitcast_add_fusion.2
  401.2 10.7 %bitcast_add_fusion.2 = f32[32,520,128]{2,1,0:T(8,128)} fusion(f32[32,520,128]{2,1,0:T(8,128)} %get-tuple-element.173, pred[]{:T(512)S(6)} %compare.35, pred[32,520]{1,0:T(8,128)(4,1)S(1)} %broadcast_compare_fusion.2, bf16[32,520,128]{2,1,0:T(8,128)(2,1)} %get-tuple-element.183, bf16[16,128,128]{2,1,0:T(8,128)(2,1)} %get-tuple-element.182, ...), kind=kOutput, calls=%fused_computation.2.clone.1 | convolution fusion | flops 551649280 | bytes 21349120 | tf_op jit(solution)/shard_map/while/body/eval_jaxpr/xjm,mg->xjg/dot_general | solution.py:33
  411.9 10.7 %bitcast_add_fusion.2 = f32[32,520,128]{2,1,0:T(8,128)} fusion(f32[32,520,128]{2,1,0:T(8,128)} %get-tuple-element.173, pred[]{:T(512)S(6)} %compare.35, pred[32,520]{1,0:T(8,128)(4,1)S(1)} %broadcast_compare_fusion.2, bf16[32,520,128]{2,1,0:T(8,128)(2,1)} %get-tuple-element.183, bf16[16,128,128]{2,1,0:T(8,128)(2,1)} %get-tuple-element.182, ...), kind=kOutput, calls=%fused_computation.2.clone.1 | convolution fusion | flops 551649280 | bytes 21349120 | tf_op jit(solution)/shard_map/while/body/eval_jaxpr/xjm,mg->xjg/dot_general | solution.py:33
  422.7 10.7 %bitcast_add_fusion.2 = f32[32,520,128]{2,1,0:T(8,128)} fusion(f32[32,520,128]{2,1,0:T(8,128)} %get-tuple-element.173, pred[]{:T(512)S(6)} %compare.35, pred[32,520]{1,0:T(8,128)(4,1)S(1)} %broadcast_compare_fusion.2, bf16[32,520,128]{2,1,0:T(8,128)(2,1)} %get-tuple-element.183, bf16[16,128,128]{2,1,0:T(8,128)(2,1)} %get-tuple-element.182, ...), kind=kOutput, calls=%fused_computation.2.clone.1 | convolution fusion | flops 551649280 | bytes 21349120 | tf_op jit(solution)/shard_map/while/body/eval_jaxpr/xjm,mg->xjg/dot_general | solution.py:33
  433.5 10.7 %bitcast_add_fusion.2 = f32[32,520,128]{2,1,0:T(8,128)} fusion(f32[32,520,128]{2,1,0:T(8,128)} %get-tuple-element.173, pred[]{:T(512)S(6)} %compare.35, pred[32,520]{1,0:T(8,128)(4,1)S(1)} %broadcast_compare_fusion.2, bf16[32,520,128]{2,1,0:T(8,128)(2,1)} %get-tuple-element.183, bf16[16,128,128]{2,1,0:T(8,128)(2,1)} %get-tuple-element.182, ...), kind=kOutput, calls=%fused_computation.2.clone.1 | convolution fusion | flops 551649280 | bytes 21349120 | tf_op jit(solution)/shard_map/while/body/eval_jaxpr/xjm,mg->xjg/dot_general | solution.py:33
  444.2 10.7 %bitcast_add_fusion.2 = f32[32,520,128]{2,1,0:T(8,128)} fusion(f32[32,520,128]{2,1,0:T(8,128)} %get-tuple-element.173, pred[]{:T(512)S(6)} %compare.35, pred[32,520]{1,0:T(8,128)(4,1)S(1)} %broadcast_compare_fusion.2, bf16[32,520,128]{2,1,0:T(8,128)(2,1)} %get-tuple-element.183, bf16[16,128,128]{2,1,0:T(8,128)(2,1)} %get-tuple-element.182, ...), kind=kOutput, calls=%fused_computation.2.clone.1 | convolution fusion | flops 551649280 | bytes 21349120 | tf_op jit(solution)/shard_map/while/body/eval_jaxpr/xjm,mg->xjg/dot_general | solution.py:33
  455.0 10.7 %bitcast_add_fusion.2 = f32[32,520,128]{2,1,0:T(8,128)} fusion(f32[32,520,128]{2,1,0:T(8,128)} %get-tuple-element.173, pred[]{:T(512)S(6)} %compare.35, pred[32,520]{1,0:T(8,128)(4,1)S(1)} %broadcast_compare_fusion.2, bf16[32,520,128]{2,1,0:T(8,128)(2,1)} %get-tuple-element.183, bf16[16,128,128]{2,1,0:T(8,128)(2,1)} %get-tuple-element.182, ...), kind=kOutput, calls=%fused_computation.2.clone.1 | convolution fusion | flops 551649280 | bytes 21349120 | tf_op jit(solution)/shard_map/while/body/eval_jaxpr/xjm,mg->xjg/dot_general | solution.py:33
  465.8 10.7 %bitcast_add_fusion.2 = f32[32,520,128]{2,1,0:T(8,128)} fusion(f32[32,520,128]{2,1,0:T(8,128)} %get-tuple-element.173, pred[]{:T(512)S(6)} %compare.35, pred[32,520]{1,0:T(8,128)(4,1)S(1)} %broadcast_compare_fusion.2, bf16[32,520,128]{2,1,0:T(8,128)(2,1)} %get-tuple-element.183, bf16[16,128,128]{2,1,0:T(8,128)(2,1)} %get-tuple-element.182, ...), kind=kOutput, calls=%fused_computation.2.clone.1 | convolution fusion | flops 551649280 | bytes 21349120 | tf_op jit(solution)/shard_map/while/body/eval_jaxpr/xjm,mg->xjg/dot_general | solution.py:33
  476.6 10.7 %bitcast_add_fusion.2 = f32[32,520,128]{2,1,0:T(8,128)} fusion(f32[32,520,128]{2,1,0:T(8,128)} %get-tuple-element.173, pred[]{:T(512)S(6)} %compare.35, pred[32,520]{1,0:T(8,128)(4,1)S(1)} %broadcast_compare_fusion.2, bf16[32,520,128]{2,1,0:T(8,128)(2,1)} %get-tuple-element.183, bf16[16,128,128]{2,1,0:T(8,128)(2,1)} %get-tuple-element.182, ...), kind=kOutput, calls=%fused_computation.2.clone.1 | convolution fusion | flops 551649280 | bytes 21349120 | tf_op jit(solution)/shard_map/while/body/eval_jaxpr/xjm,mg->xjg/dot_general | solution.py:33
  487.3 10.7 %bitcast_add_fusion.2 = f32[32,520,128]{2,1,0:T(8,128)} fusion(f32[32,520,128]{2,1,0:T(8,128)} %get-tuple-element.173, pred[]{:T(512)S(6)} %compare.35, pred[32,520]{1,0:T(8,128)(4,1)S(1)} %broadcast_compare_fusion.2, bf16[32,520,128]{2,1,0:T(8,128)(2,1)} %get-tuple-element.183, bf16[16,128,128]{2,1,0:T(8,128)(2,1)} %get-tuple-element.182, ...), kind=kOutput, calls=%fused_computation.2.clone.1 | convolution fusion | flops 551649280 | bytes 21349120 | tf_op jit(solution)/shard_map/while/body/eval_jaxpr/xjm,mg->xjg/dot_general | solution.py:33
  498.1 10.7 %bitcast_add_fusion.2 = f32[32,520,128]{2,1,0:T(8,128)} fusion(f32[32,520,128]{2,1,0:T(8,128)} %get-tuple-element.173, pred[]{:T(512)S(6)} %compare.35, pred[32,520]{1,0:T(8,128)(4,1)S(1)} %broadcast_compare_fusion.2, bf16[32,520,128]{2,1,0:T(8,128)(2,1)} %get-tuple-element.183, bf16[16,128,128]{2,1,0:T(8,128)(2,1)} %get-tuple-element.182, ...), kind=kOutput, calls=%fused_computation.2.clone.1 | convolution fusion | flops 551649280 | bytes 21349120 | tf_op jit(solution)/shard_map/while/body/eval_jaxpr/xjm,mg->xjg/dot_general | solution.py:33
  508.9 10.7 %bitcast_add_fusion.2 = f32[32,520,128]{2,1,0:T(8,128)} fusion(f32[32,520,128]{2,1,0:T(8,128)} %get-tuple-element.173, pred[]{:T(512)S(6)} %compare.35, pred[32,520]{1,0:T(8,128)(4,1)S(1)} %broadcast_compare_fusion.2, bf16[32,520,128]{2,1,0:T(8,128)(2,1)} %get-tuple-element.183, bf16[16,128,128]{2,1,0:T(8,128)(2,1)} %get-tuple-element.182, ...), kind=kOutput, calls=%fused_computation.2.clone.1 | convolution fusion | flops 551649280 | bytes 21349120 | tf_op jit(solution)/shard_map/while/body/eval_jaxpr/xjm,mg->xjg/dot_general | solution.py:33
  519.6 10.7 %bitcast_add_fusion.2 = f32[32,520,128]{2,1,0:T(8,128)} fusion(f32[32,520,128]{2,1,0:T(8,128)} %get-tuple-element.173, pred[]{:T(512)S(6)} %compare.35, pred[32,520]{1,0:T(8,128)(4,1)S(1)} %broadcast_compare_fusion.2, bf16[32,520,128]{2,1,0:T(8,128)(2,1)} %get-tuple-element.183, bf16[16,128,128]{2,1,0:T(8,128)(2,1)} %get-tuple-element.182, ...), kind=kOutput, calls=%fused_computation.2.clone.1 | convolution fusion | flops 551649280 | bytes 21349120 | tf_op jit(solution)/shard_map/while/body/eval_jaxpr/xjm,mg->xjg/dot_general | solution.py:33
  530.4 10.7 %bitcast_add_fusion.2 = f32[32,520,128]{2,1,0:T(8,128)} fusion(f32[32,520,128]{2,1,0:T(8,128)} %get-tuple-element.173, pred[]{:T(512)S(6)} %compare.35, pred[32,520]{1,0:T(8,128)(4,1)S(1)} %broadcast_compare_fusion.2, bf16[32,520,128]{2,1,0:T(8,128)(2,1)} %get-tuple-element.183, bf16[16,128,128]{2,1,0:T(8,128)(2,1)} %get-tuple-element.182, ...), kind=kOutput, calls=%fused_computation.2.clone.1 | convolution fusion | flops 551649280 | bytes 21349120 | tf_op jit(solution)/shard_map/while/body/eval_jaxpr/xjm,mg->xjg/dot_general | solution.py:33
  541.2 10.7 %bitcast_add_fusion.2 = f32[32,520,128]{2,1,0:T(8,128)} fusion(f32[32,520,128]{2,1,0:T(8,128)} %get-tuple-element.173, pred[]{:T(512)S(6)} %compare.35, pred[32,520]{1,0:T(8,128)(4,1)S(1)} %broadcast_compare_fusion.2, bf16[32,520,128]{2,1,0:T(8,128)(2,1)} %get-tuple-element.183, bf16[16,128,128]{2,1,0:T(8,128)(2,1)} %get-tuple-element.182, ...), kind=kOutput, calls=%fused_computation.2.clone.1 | convolution fusion | flops 551649280 | bytes 21349120 | tf_op jit(solution)/shard_map/while/body/eval_jaxpr/xjm,mg->xjg/dot_general | solution.py:33
  551.9 10.7 %bitcast_add_fusion.2 = f32[32,520,128]{2,1,0:T(8,128)} fusion(f32[32,520,128]{2,1,0:T(8,128)} %get-tuple-element.173, pred[]{:T(512)S(6)} %compare.35, pred[32,520]{1,0:T(8,128)(4,1)S(1)} %broadcast_compare_fusion.2, bf16[32,520,128]{2,1,0:T(8,128)(2,1)} %get-tuple-element.183, bf16[16,128,128]{2,1,0:T(8,128)(2,1)} %get-tuple-element.182, ...), kind=kOutput, calls=%fused_computation.2.clone.1 | convolution fusion | flops 551649280 | bytes 21349120 | tf_op jit(solution)/shard_map/while/body/eval_jaxpr/xjm,mg->xjg/dot_general | solution.py:33
  562.7 16.3 %convert_bitcast_fusion = bf16[1,1,32,128,768]{4,3,2,1,0:T(8,128)(2,1)} fusion(bf16[32,768,520]{1,2,0:T(8,128)(2,1)} %param.10, f32[32,520,128]{2,1,0:T(8,128)} %get-tuple-element.99), kind=kOutput, calls=%fused_computation.12 | convolution fusion | flops 3276832768 | bytes 40370176 | tf_op jit(solution)/shard_map/ncb,nba->nac/dot_general | solution.py:83
  579.0 8.9 copy.56
  587.9 74.9 %all_to_all.67 = bf16[1,1,32,128,768]{3,2,1,0,4:T(8,128)(2,1)S(1)} all-to-all(bf16[1,1,32,128,768]{3,2,1,0,4:T(8,128)(2,1)} %copy.56), channel_id=1, replica_groups=mesh['lat'=4,'lev'=8] {'lat'}, dimensions={4} | all-to-all | bytes 12582912 | tf_op jit(solution)/shard_map/all_to_all | solution.py:90
  662.8 5.1 copy.57
  667.9 14.1 %copy.58 = bf16[4,1,32,128,192]{4,0,2,1,3:T(4,128)(2,1)} copy(bf16[4,1,32,128,192]{3,4,0,2,1:T(8,128)(2,1)} %bitcast.54) | data formatting | bytes 12582912 | tf_op jit(solution)/shard_map/all_to_all | solution.py:90
  681.9 5.2 all-to-all-start.3
  687.1 5.1 copy.61
  692.2 2.8 reshape.386
  695.0 176.0 %all-to-all-done.3 = bf16[4,1,32,128,192]{4,0,2,1,3:T(4,128)(2,1)} async-done(((bf16[4,1,32,128,192]{4,0,2,1,3:T(4,128)(2,1)}), bf16[4,1,32,128,192]{4,0,2,1,3:T(4,128)(2,1)}, u32[]{:S(2)}, u32[]{:S(2)}) %all-to-all-start.3) | async-done | bytes 6291488 | tf_op jit(solution)/shard_map/all_to_all | solution.py:89
  871.0 11.5 %copy.59 = bf16[4,1,32,128,192]{4,3,2,0,1:T(8,128)(2,1)} copy(bf16[4,1,32,128,192]{4,0,2,1,3:T(4,128)(2,1)} %all-to-all-done.3) | data formatting | bytes 12582912 | tf_op jit(solution)/shard_map/all_to_all | solution.py:89
  882.5 0.0 copy-start.3
  882.5 7.9 copy.60
  890.4 0.0 copy-done.3
  890.4 0.0 copy-start.1
  890.4 27.3 %multiply_convert_fusion = bf16[16,192,1536]{2,1,0:T(8,128)(2,1)} fusion(bf16[16,192,1536]{2,1,0:T(8,128)(2,1)} %param.9, bf16[1024,1536,1]{1,0,2:T(8,128)(2,1)S(1)} %copy-done.3, bf16[1024,16,192]{2,1,0:T(8,128)(2,1)} %bitcast.55), kind=kOutput, calls=%fused_computation.7 | convolution fusion | flops 9677832192 | bytes 28311552 | tf_op jit(solution)/shard_map/cvl,cx->vlx/dot_general | solution.py:97
  917.8 0.0 copy-done.1
  (24 shorter events, 0.3 us)
Async XLA Ops:
  0.0 274.0 %copy-start = (s32[512]{0:T(512)S(1)}, s32[512]{0:T(512)}, u32[]{:S(2)}) copy-start(s32[512]{0:T(512)} %param.13) | copy-start | bytes 6148
  267.4 5.6 copy-start.2
  267.4 104.2 %all-to-all-start.1 = ((bf16[4,1,32,128,192]{3,4,2,1,0:T(8,128)(2,1)}), bf16[4,1,32,128,192]{3,4,2,1,0:T(8,128)(2,1)}, u32[]{:S(2)}, u32[]{:S(2)}) async-start(bf16[4,1,32,128,192]{3,4,2,1,0:T(8,128)(2,1)} %copy.53), calls=%async_computation.1 | async-start | bytes 12582912 | tf_op jit(solution)/shard_map/all_to_all | solution.py:63
  681.9 189.0 %all-to-all-start.3 = ((bf16[4,1,32,128,192]{4,0,2,1,3:T(4,128)(2,1)}), bf16[4,1,32,128,192]{4,0,2,1,3:T(4,128)(2,1)}, u32[]{:S(2)}, u32[]{:S(2)}) async-start(bf16[4,1,32,128,192]{4,0,2,1,3:T(4,128)(2,1)} %copy.58), calls=%async_computation.3 | async-start | bytes 16777216 | tf_op jit(solution)/shard_map/all_to_all | solution.py:89
  882.5 7.9 copy-start.3
  890.4 27.3 %copy-start.1 = (s32[512]{0:T(512)S(1)}, s32[512]{0:T(512)}, u32[]{:S(2)}) copy-start(s32[512]{0:T(512)} %param.13) | copy-start | bytes 6148
where the time goes:
time: 929 us; the launch traced here: 918 us
  blocking collectives  265 us (29%)
  matrix products  244 us (26%)
  local copies, waits for them, and re-layouts  204 us (22%)
  waiting for transfers between devices  176 us (19%)
  other arithmetic  17.7 us (2%)
  starting transfers between devices  10.7 us (1%)
    all_to_all x1, blocking collectives, body(): lax.all_to_all(fourier, 'lev', split_axis=1, concat_axis=3, tiled=True)  190 us
    all_to_all x1, waiting for transfers between devices, body(): lax.all_to_all(lax.all_to_all(gridpoint_coefficients, 'lat', split_axis=4...  176 us
    dot_general x16, matrix products, add_matrix(): jnp.einsum('xjm,mg->xjg', spectral_state, vertical[operator_index], prefe...  169 us
    gather x2, local copies, waits for them, and re-layouts, body(): matrix_index = jnp.take(degree_matrix, degree)  97.3 us
    all_to_all x1, blocking collectives, body(): lax.all_to_all(gridpoint_coefficients, 'lat', split_axis=4, concat_axis=0...  74.9 us
    dot_general x1, matrix products, body(): jnp.einsum('cvl,cx->vlx', columns, synthesis_table, preferred_element_typ...  27.3 us
    all_to_all x2, local copies, waits for them, and re-layouts, body(): lax.all_to_all(lax.all_to_all(gridpoint_coefficients, 'lat', split_axis=4...  19.5 us
    all_to_all x2, local copies, waits for them, and re-layouts, body(): lax.all_to_all(gridpoint_coefficients, 'lat', split_axis=4, concat_axis=0...  19.1 us
  transfers between devices with their start and end apart: 2, of which 1 were waited for; matrix products, arithmetic and copies ran while one was open for 12% of the time, Pallas kernels for 0%

commit v1 on v0

--- a/solution.py
+++ b/solution.py
@@ -1,11 +1,18 @@
+import functools
 import math
 
 import jax
 import jax.numpy as jnp
 from jax import lax
+from jax.experimental import pallas as pl
+from jax.experimental.pallas import tpu as pltpu
 from jax.sharding import PartitionSpec as P
 
 N = 512
+CORES = 2
+ROWS = 8
+LANES = 128
+VMEM = 48 * 2**20
 
 
 def fourier_basis(wavenumbers, points):
@@ -42,7 +49,7 @@
     return lax.fori_loop(0, vertical.shape[0], add_matrix, zero_sums).astype(jnp.bfloat16)
 
 
-def body(adjoint_grid, wind, legendre, vertical, pair_table, degree_matrix):
+def general_body(adjoint_grid, wind, legendre, vertical, pair_table, degree_matrix):
     vertical_level_rows, lat_rows, points = adjoint_grid.shape
     lat_devices = lax.axis_size("lat")
     lev_devices = lax.axis_size("lev")
@@ -100,6 +107,404 @@
     return (regridded * wind.astype(jnp.float32)).astype(jnp.bfloat16)
 
 
+def dot(a, b, dims):
+    return lax.dot_general(a, b, (dims, ((), ())), preferred_element_type=jnp.float32)
+
+
+def make_table(wave, points, scale):
+    rows = wave.shape[0]
+    unit = 2.0 * math.pi / points
+    lane = lax.broadcasted_iota(jnp.int32, (rows, LANES), 1).astype(jnp.float32)
+    waves = jnp.broadcast_to(wave, (rows, LANES)).astype(jnp.float32)
+
+    def turn(steps):
+        return (steps - points * jnp.floor(steps * (1.0 / points))) * unit
+
+    fine = turn(waves * lane)
+    coarse = turn(waves * (lane * LANES))
+    cos_fine, sin_fine = jnp.cos(fine), jnp.sin(fine)
+    cos_coarse, sin_coarse = jnp.cos(coarse) * scale, jnp.sin(coarse) * scale
+    part = lax.broadcasted_iota(jnp.int32, (rows, LANES), 0) % 2
+    by_cos = jnp.where(part == 0, cos_coarse, -sin_coarse)
+    by_sin = jnp.where(part == 0, -sin_coarse, -cos_coarse)
+    pieces = [
+        by_cos[:, a : a + 1] * cos_fine + by_sin[:, a : a + 1] * sin_fine
+        for a in range(points // LANES)
+    ]
+    return jnp.concatenate(pieces, axis=1).astype(jnp.bfloat16)
+
+
+def fourier_kernel(parity_ref, wave_ref, grid_ref, out_ref, table_ref):
+    step = pl.program_id(0)
+    points = grid_ref.shape[-1]
+
+    @pl.when(step == 0)
+    def _():
+        table_ref[...] = make_table(wave_ref[...], points, 1.0 / math.sqrt(points))
+
+    half = LANES // 2
+    whole = pl.ds(pl.multiple_of(half * parity_ref[0], half), LANES)
+    rest = pl.ds(pl.multiple_of(LANES * (1 - parity_ref[0]), half), half)
+    rows = []
+    for j in range(2):
+        rows += [grid_ref[t, 0, j, whole, :] for t in range(2)]
+        rows += [grid_ref[t, 0, j, rest, :] for t in range(2)]
+    sums = dot(table_ref[...], jnp.concatenate(rows, axis=0), ((1,), (1,)))
+    sums = sums.reshape(-1, ROWS, sums.shape[1])
+    tiles = [sums[:, :, t * LANES : (t + 1) * LANES] for t in range(6)]
+    at = pl.ds(pl.multiple_of(step * 6 * ROWS, 6 * ROWS), 6 * ROWS)
+    out_ref[:, at, :] = jnp.concatenate(tiles, axis=1).astype(jnp.bfloat16)
+
+
+def fourier_chunk(grid, wave, parity):
+    _, steps, _, lat_rows, points = grid.shape
+    columns = wave.shape[0]
+    rows = steps * 6 * ROWS
+    slots = columns // ROWS
+    return pl.pallas_call(
+        fourier_kernel,
+        out_shape=jax.ShapeDtypeStruct((slots, rows, LANES), jnp.bfloat16),
+        grid_spec=pltpu.PrefetchScalarGridSpec(
+            num_scalar_prefetch=1,
+            grid=(steps,),
+            in_specs=[
+                pl.BlockSpec((columns, 1), lambda s, _: (0, 0)),
+                pl.BlockSpec((2, 1, 2, lat_rows, points), lambda s, _: (0, s, 0, 0, 0)),
+            ],
+            out_specs=pl.BlockSpec((slots, rows, LANES), lambda s, _: (0, 0, 0)),
+            scratch_shapes=[pltpu.VMEM((columns, points), jnp.bfloat16)],
+        ),
+        compiler_params=pltpu.CompilerParams(vmem_limit_bytes=VMEM),
+        cost_estimate=pl.CostEstimate(
+            flops=2 * columns * grid.size, bytes_accessed=2 * grid.size, transcendentals=0
+        ),
+        name="fourier_chunk",
+    )(parity, wave, grid)
+
+
+def table_kernel(wave_ref, out_ref):
+    out_ref[...] = make_table(wave_ref[...], out_ref.shape[1], 1.0 / math.sqrt(N))
+
+
+def synthesis_rows(wave, points, block):
+    columns = wave.shape[0]
+    return pl.pallas_call(
+        table_kernel,
+        out_shape=jax.ShapeDtypeStruct((columns, points), jnp.bfloat16),
+        grid=(columns // block,),
+        in_specs=[pl.BlockSpec((block, 1), lambda s: (s, 0))],
+        out_specs=pl.BlockSpec((block, points), lambda s: (s, 0)),
+        compiler_params=pltpu.CompilerParams(vmem_limit_bytes=VMEM),
+        name="synthesis_rows",
+    )(wave)
+
+
+def spectral_kernel(
+    lower_ref, field_ref, table_ref, vertical_ref, first_ref, second_ref, out_ref, field_all, out_all
+):
+    pair = pl.program_id(0)
+    lats, levs, wire_rows, _ = field_ref.shape
+    stride = 3 * ROWS
+    count = levs * wire_rows // stride
+    block = levs * wire_rows
+    half = LANES // 2
+    packed = table_ref.shape[1]
+    matrices = vertical_ref.shape[0] // LANES
+
+    @pl.when(pair == 0)
+    def _():
+        field_all[...] = field_ref[...].reshape(field_all.shape).astype(jnp.float32)
+
+    left = lax.broadcasted_iota(jnp.int32, (count, LANES), 1) < half
+    lower = lower_ref[pair]
+    row = lax.broadcasted_iota(jnp.int32, (packed, LANES), 0)
+    own = row < N - lower
+    valid = row <= N
+    operator = jnp.where(own, first_ref[pl.ds(lower, packed), :], second_ref[...])
+
+    def at(lat, t, column):
+        return pl.ds(lat * block + t * ROWS + column, count, stride=stride)
+
+    def swap(x):
+        return pltpu.roll(x, half, 1)
+
+    def read_field(column):
+        tiles = []
+        for lat in range(0, lats, 2):
+            low = field_all[at(lat, 2, column), :]
+            high = field_all[at(lat + 1, 2, column), :]
+            middle = [jnp.where(left, low, swap(high)), jnp.where(left, swap(low), high)]
+            tiles.append([field_all[at(lat, t, column), :] for t in range(2)])
+            tiles.append(middle)
+            tiles.append([field_all[at(lat + 1, t, column), :] for t in range(2)])
+        levels = [jnp.concatenate([tile[t] for tile in tiles], axis=1) for t in range(2)]
+        return jnp.concatenate(levels, axis=0).astype(jnp.bfloat16)
+
+    def write_field(column, value):
+        for lat in range(0, lats, 2):
+            first = lat // 2 * 3 * LANES
+            tile = [value[:, first + i * LANES : first + (i + 1) * LANES] for i in range(3)]
+            parts = [[x[:count], x[count:]] for x in tile]
+            for t in range(2):
+                out_all[at(lat, t, column), :] = parts[0][t]
+                out_all[at(lat + 1, t, column), :] = parts[2][t]
+            out_all[at(lat, 2, column), :] = jnp.where(left, parts[1][0], swap(parts[1][1]))
+            out_all[at(lat + 1, 2, column), :] = jnp.where(left, swap(parts[1][0]), parts[1][1])
+
+    for r in range(2):
+        state = []
+        for e in range(2):
+            field = read_field(4 * pair + 2 * e + r)
+            state.append(dot(table_ref[2 * e + r], field, ((1,), (1,))))
+        spectral = jnp.where(own, state[0], jnp.where(valid, state[1], 0.0))
+        spectral = spectral.astype(jnp.bfloat16).astype(jnp.float32)
+        spread = [
+            jnp.where(operator == g, spectral, 0.0).astype(jnp.bfloat16) for g in range(matrices)
+        ]
+        solved = dot(jnp.concatenate(spread, axis=1), vertical_ref[...], ((1,), (0,)))
+        for e in range(2):
+            mine = jnp.where(own, solved, 0.0) if e == 0 else jnp.where(own, 0.0, solved)
+            value = dot(mine.astype(jnp.bfloat16), table_ref[2 * e + r], ((0,), (0,)))
+            write_field(4 * pair + 2 * e + r, value)
+
+    @pl.when(pair == pl.num_programs(0) - 1)
+    def _():
+        out_ref[...] = out_all[...].astype(jnp.bfloat16).reshape(out_ref.shape)
+
+
+def spectral_chunk(field, table, vertical, first, second, lower, chunk):
+    lats, levs, wire_rows, _ = field.shape
+    columns, packed, all_lats = table.shape
+    pairs = ROWS // 4
+    rows = lats * levs * wire_rows
+    return pl.pallas_call(
+        spectral_kernel,
+        out_shape=jax.ShapeDtypeStruct(field.shape, jnp.bfloat16),
+        grid_spec=pltpu.PrefetchScalarGridSpec(
+            num_scalar_prefetch=1,
+            grid=(pairs,),
+            in_specs=[
+                pl.BlockSpec(field.shape, lambda p, _: (0, 0, 0, 0)),
+                pl.BlockSpec((4, packed, all_lats), lambda p, _: (chunk * pairs + p, 0, 0)),
+                pl.BlockSpec(vertical.shape, lambda p, _: (0, 0)),
+                pl.BlockSpec(first.shape, lambda p, _: (0, 0)),
+                pl.BlockSpec(second.shape, lambda p, _: (0, 0)),
+            ],
+            out_specs=pl.BlockSpec(field.shape, lambda p, _: (0, 0, 0, 0)),
+            scratch_shapes=[
+                pltpu.VMEM((rows, LANES), jnp.float32),
+                pltpu.VMEM((rows, LANES), jnp.float32),
+            ],
+        ),
+        compiler_params=pltpu.CompilerParams(vmem_limit_bytes=VMEM),
+        cost_estimate=pl.CostEstimate(
+            flops=4 * ROWS * packed * all_lats * LANES + pairs * 4 * packed * vertical.size,
+            bytes_accessed=2 * ROWS * packed * all_lats,
+            transcendentals=0,
+        ),
+        name="spectral_chunk",
+    )(lower, field, table, vertical, first, second)
+
+
+def synthesis_kernel(pieces, parity_ref, *refs):
+    field_refs, (table_ref, wind_ref) = refs[:pieces], refs[pieces : pieces + 2]
+    out_ref = refs[-1]
+    half = LANES // 2
+    whole = pl.ds(pl.multiple_of(half * parity_ref[0], half), LANES)
+    rest = pl.ds(pl.multiple_of(LANES * (1 - parity_ref[0]), half), half)
+    fields = [ref[...].astype(jnp.float32) for ref in field_refs]
+    fields = jnp.concatenate([f.reshape(-1, f.shape[-2], LANES) for f in fields], axis=0)
+    tiles = [
+        fields[:, t * ROWS : (t + 1) * ROWS, :].reshape(-1, LANES).astype(jnp.bfloat16)
+        for t in range(6)
+    ]
+    sums = dot(jnp.concatenate(tiles, axis=1), table_ref[...], ((0,), (0,)))
+
+    def put(t, j, rows, value):
+        gain = wind_ref[t, 0, j, rows, :].astype(jnp.float32)
+        out_ref[t, 0, j, rows, :] = (value * gain).astype(jnp.bfloat16)
+
+    for j in range(2):
+        first = j * 3 * LANES
+        for t in range(2):
+            put(t, j, whole, sums[first + t * LANES : first + (t + 1) * LANES])
+            start = first + 2 * LANES + t * half
+            put(t, j, rest, sums[start : start + half])
+
+
+def synthesis_part(fields, table, wind, parity, first_step, steps, before):
+    _, _, _, lat_rows, points = wind.shape
+    columns = table.shape[0]
+    rows = 6 * ROWS
+
+    def field_spec(array, offset):
+        lead = array.ndim - 2
+        return pl.BlockSpec(
+            array.shape[:-2] + (rows, LANES),
+            lambda s, _: (0,) * lead + (s + first_step - offset, 0),
+        )
+
+    grid_spec = pl.BlockSpec(
+        (2, 1, 2, lat_rows, points), lambda s, _: (0, s + first_step, 0, 0, 0)
+    )
+    in_specs = [field_spec(*f) for f in fields]
+    in_specs += [pl.BlockSpec(table.shape, lambda s, _: (0, 0)), grid_spec]
+    operands = [f for f, _ in fields] + [table, wind]
+    aliases = {}
+    if before is not None:
+        in_specs.append(pl.BlockSpec(memory_space=pl.ANY))
+        aliases = {1 + len(operands): 0}
+        operands.append(before)
+    part = 4 * steps * lat_rows * points
+    return pl.pallas_call(
+        functools.partial(synthesis_kernel, len(fields)),
+        out_shape=jax.ShapeDtypeStruct(wind.shape, jnp.bfloat16),
+        grid_spec=pltpu.PrefetchScalarGridSpec(
+            num_scalar_prefetch=1,
+            grid=(steps,),
+            in_specs=in_specs,
+            out_specs=grid_spec,
+        ),
+        input_output_aliases=aliases,
+        compiler_params=pltpu.CompilerParams(vmem_limit_bytes=VMEM),
+        cost_estimate=pl.CostEstimate(
+            flops=2 * columns * part, bytes_accessed=4 * part, transcendentals=0
+        ),
+        name="synthesis_part",
+    )(parity, *operands)
+
+
+def swap_along_z(slots):
+    lev_devices = lax.axis_size("lev")
+    moved = [slots[0]]
+    for kz in range(1, len(slots)):
+        pairs = [(b, b ^ (CORES * kz)) for b in range(lev_devices)]
+        moved.append(lax.ppermute(slots[kz], "lev", pairs))
+    return moved
+
+
+def exchange_in_plane(x, groups):
+    return lax.all_to_all(
+        x, ("lat", "lev"), split_axis=0, concat_axis=0, tiled=True, axis_index_groups=groups
+    )
+
+
+def xor_order(x, axis, index):
+    size = x.shape[axis]
+    bit = 1
+    while bit < size:
+        split = x.shape[:axis] + (size // (2 * bit), 2, bit) + x.shape[axis + 1 :]
+        halves = x.reshape(split)
+        halves = jnp.where(index & bit != 0, jnp.flip(halves, axis + 1), halves)
+        x = halves.reshape(x.shape)
+        bit *= 2
+    return x
+
+
+def pipelined_body(adjoint_grid, wind, legendre, vertical, pair_table, degree_matrix):
+    level_rows, lat_rows, points = adjoint_grid.shape
+    lats = lax.axis_size("lat")
+    levs = lax.axis_size("lev")
+    layers = levs // CORES
+    plane = lats * CORES
+    slots, all_lats, packed = legendre.shape
+    matrices, levels, _ = vertical.shape
+    chunks = slots // ROWS
+    pairs = ROWS // 4
+    steps = level_rows // 4
+    wire_rows = steps * 6 * ROWS
+
+    lat, lev = lax.axis_index("lat"), lax.axis_index("lev")
+    layer = lev // CORES
+    parity = (lat % 2).astype(jnp.int32).reshape(1)
+    groups = [
+        [a * levs + z * CORES + c for a in range(lats) for c in range(CORES)] for z in range(layers)
+    ]
+
+    table_pairs = xor_order(pair_table.reshape(lats, layers, CORES, chunks, pairs), 1, layer)
+    table_pairs = table_pairs.transpose(3, 1, 0, 2, 4)
+    waves = jnp.stack([table_pairs, N - 1 - table_pairs], axis=-1)
+    waves = jnp.broadcast_to(waves[..., None], waves.shape + (2,)).reshape(chunks, -1, 1)
+
+    grid = adjoint_grid.reshape(2, steps, 2, lat_rows, points)
+    wind = wind.reshape(2, steps, 2, lat_rows, points)
+    table = legendre.transpose(0, 2, 1)
+
+    slot_level = jnp.arange(levels, dtype=jnp.int32).reshape(layers, CORES, 2, level_rows // 2)
+    slot_level = xor_order(slot_level, 0, layer).transpose(2, 1, 0, 3).reshape(levels)
+    order = (slot_level[:, None] == jnp.arange(levels)[None, :]).astype(jnp.bfloat16)
+    operators = jnp.einsum("av,gvo->gao", order, vertical, preferred_element_type=jnp.float32)
+    operators = jnp.einsum(
+        "gao,bo->gab", operators.astype(jnp.bfloat16), order, preferred_element_type=jnp.float32
+    )
+    operators = operators.astype(jnp.bfloat16).reshape(matrices * levels, levels)
+
+    by_degree = jnp.concatenate([degree_matrix, jnp.broadcast_to(degree_matrix[-1:], (packed,))])
+    second = jnp.concatenate([degree_matrix[:1], by_degree[: packed - 1]])
+    first = jnp.broadcast_to(by_degree[:, None], (by_degree.shape[0], LANES))
+    second = jnp.broadcast_to(second[:, None], (packed, LANES))
+    first_pair = (lat * levs + lev) * (slots // 4)
+    lower = lax.dynamic_slice(pair_table, (first_pair,), (slots // 4,)).reshape(chunks, pairs)
+
+    returned = []
+    for q in range(chunks):
+        sent = fourier_chunk(grid, waves[q], parity)
+        sent = sent.reshape(layers, plane, wire_rows, LANES)
+        moved = swap_along_z([sent[k] for k in range(layers)])
+        moved = jnp.stack(moved, axis=1).reshape(plane, layers * wire_rows, LANES)
+        field = exchange_in_plane(moved, groups).reshape(lats, levs, wire_rows, LANES)
+        field = spectral_chunk(field, table, operators, first, second, lower[q], q)
+        moved = exchange_in_plane(field.reshape(plane, layers * wire_rows, LANES), groups)
+        returned.append(moved.reshape(plane, layers, wire_rows, LANES))
+
+    synthesis = synthesis_rows(waves.reshape(-1, 1), points, ROWS * layers * plane)
+    early = chunks // 2
+    fields = []
+    for q in range(early):
+        fields += swap_along_z([returned[q][:, k] for k in range(layers)])
+    out = None
+    rows = 6 * ROWS
+    parts = steps // 2 if steps % 2 == 0 else 1
+    parts = steps if parts == 0 else steps // parts
+    for first_step in range(0, steps, parts):
+        cut = slice(first_step * rows, (first_step + parts) * rows)
+        sent = [jnp.stack([x[:, k, cut] for x in returned[early:]]) for k in range(layers)]
+        moved = swap_along_z(sent)
+        late = [moved[k][i] for i in range(chunks - early) for k in range(layers)]
+        out = synthesis_part(
+            [(f, 0) for f in fields] + [(f, first_step) for f in late],
+            synthesis,
+            wind,
+            parity,
+            first_step,
+            parts,
+            out,
+        )
+    return out.reshape(level_rows, lat_rows, points)
+
+
+def body(adjoint_grid, wind, legendre, vertical, pair_table, degree_matrix):
+    level_rows, lat_rows, points = adjoint_grid.shape
+    lats, levs = lax.axis_size("lat"), lax.axis_size("lev")
+    layers = levs // CORES
+    fits = (
+        levs % CORES == 0
+        and layers & (layers - 1) == 0
+        and lats % 2 == 0
+        and lat_rows == LANES + LANES // 2
+        and level_rows % 16 == 0
+        and vertical.shape[1] == LANES
+        and points % LANES == 0
+        and points // LANES <= LANES
+        and legendre.shape[0] % (2 * ROWS) == 0
+        and legendre.shape[2] % 8 == 0
+        and legendre.shape[2] > N
+        and pair_table.shape[0] * 4 == legendre.shape[0] * lats * levs
+    )
+    plan = pipelined_body if fits else general_body
+    return plan(adjoint_grid, wind, legendre, vertical, pair_table, degree_matrix)
+
+
 def solution(mesh):
     placed = (
         P("lev", "lat", None),

time: 929 us -> 486 us (0.52)
  blocking collectives: 265 us -> 0 us
  matrix products: 244 us -> 0.55 us
  local copies, waits for them, and re-layouts: 204 us -> 24.7 us
  Pallas kernels: 0 us -> 118 us
  starting transfers between devices: 10.7 us -> 115 us
  waiting for transfers between devices: 176 us -> 216 us
  other arithmetic: 17.7 us -> 2.99 us
    all_to_all x2 -> x0, blocking collectives: 265 us -> none  [the longest x1 190 us: body(): lax.all_to_all(fourier, 'lev', split_axis=1, concat_axis=3, tiled=True)]
    dot_general x20 -> x1, matrix products: 244 us -> 0.55 us  [pipelined_body(): jnp.einsum('gao,bo->gab', operators.astype(jnp.bfloat16), order, preferre...]
    ppermute x0 -> x24, waiting for transfers between devices: none -> 190 us  [swap_along_z(): moved.append(lax.ppermute(slots[kz], 'lev', pairs))]
    all_to_all x2 -> x8, waiting for transfers between devices: 176 us -> 26.2 us  [exchange_in_plane(): lax.all_to_all(x, ('lat', 'lev'), split_axis=0, concat_axis=0, tiled=True...]
    pallas_call x0 -> x11, Pallas kernels: none -> 118 us  [the longest x4 58.9 us: spectral_chunk(): pl.pallas_call(spectral_kernel, out_shape=jax.ShapeDtypeStruct(field.shap...]
    gather x3 -> x0, local copies, waits for them, and re-layouts: 98 us -> none  [the longest x2 97.3 us: body(): matrix_index = jnp.take(degree_matrix, degree)]
    ppermute x0 -> x24, starting transfers between devices: none -> 82.2 us  [swap_along_z(): moved.append(lax.ppermute(slots[kz], 'lev', pairs))]
    all_to_all x7 -> x0, local copies, waits for them, and re-layouts: 63.5 us -> none  [the longest x2 19.5 us: body(): lax.all_to_all(lax.all_to_all(gridpoint_coefficients, 'lat', split_axis=4...]
  transfers between devices with their start and end apart: 2 -> 32, of which waited for: 1 -> 18; matrix products, arithmetic and copies ran while one was open for 12% -> 4% of each run, Pallas kernels for 0% -> 19%
where the time goes in v1:
time: 486 us; the launch traced here: 478 us
  waiting for transfers between devices  216 us (44%)
  Pallas kernels  118 us (24%)
  starting transfers between devices  115 us (24%)
  local copies, waits for them, and re-layouts  24.7 us (5%)
    ppermute x24, waiting for transfers between devices, swap_along_z(): moved.append(lax.ppermute(slots[kz], 'lev', pairs))  190 us
    ppermute x24, starting transfers between devices, swap_along_z(): moved.append(lax.ppermute(slots[kz], 'lev', pairs))  82.2 us
    pallas_call x4, Pallas kernels, spectral_chunk(): pl.pallas_call(spectral_kernel, out_shape=jax.ShapeDtypeStruct(field.shap...  58.9 us
    all_to_all x8, starting transfers between devices, exchange_in_plane(): lax.all_to_all(x, ('lat', 'lev'), split_axis=0, concat_axis=0, tiled=True...  33 us
    pallas_call x4, Pallas kernels, fourier_chunk(): pl.pallas_call(fourier_kernel, out_shape=jax.ShapeDtypeStruct((slots, row...  31.6 us
    all_to_all x8, waiting for transfers between devices, exchange_in_plane(): lax.all_to_all(x, ('lat', 'lev'), split_axis=0, concat_axis=0, tiled=True...  26.2 us
    pallas_call x2, Pallas kernels, synthesis_part(): pl.pallas_call(functools.partial(synthesis_kernel, len(fields)), out_shap...  19.3 us
  transfers between devices with their start and end apart: 32, of which 18 were waited for; matrix products, arithmetic and copies ran while one was open for 4% of the time, Pallas kernels for 19%

profile of v1, /device:TPU:0, one launch (start us, length us, event | category | flops | bytes accessed | tf_op | source)
XLA Modules:
  0.0 477.7 jit_solution(8584847948099982983)
XLA Ops:
  1.8 7.9 %fourier_chunk.7 = bf16[32,192,128]{2,1,0:T(8,128)(2,1)S(1)} custom-call(s32[1]{0:T(128)} %bitcast.parity_ref, s32[256,1]{1,0:T(8,128)S(1)} %broadcast_in_dim.55.wave_ref, bf16[2,4,2,192,1536]{4,3,2,1,0:T(8,128)(2,1)} %bitcast.208), custom_call_target="tpu_custom_call" | custom-call | flops 2415919104 | bytes 9437184 | tf_op jit(solution)/shard_map/fourier_chunk/pallas_call | solution.py:164
  9.8 5.1 %collective-permute-start.17 = (bf16[8,192,128]{2,1,0:T(8,128)(2,1)S(1)}, bf16[8,192,128]{2,1,0:T(8,128)(2,1)S(1)}, u32[]{:S(2)}, u32[]{:S(2)}) collective-permute-start(bf16[8,192,128]{2,1,0:T(8,128)(2,1)S(1)} %get-tuple-element.22), channel_id=1, source_target_pairs={{0,6},{1,7},{2,4},{3,5},{4,2},{5,3},{6,0},{7,1},{8,14},{9,15},{10,... | collective-permute-start | bytes 1179656 | tf_op jit(solution)/shard_map/ppermute | solution.py:382
  15.6 9.4 %collective-permute-done.17 = bf16[8,192,128]{2,1,0:T(8,128)(2,1)S(1)} collective-permute-done((bf16[8,192,128]{2,1,0:T(8,128)(2,1)S(1)}, bf16[8,192,128]{2,1,0:T(8,128)(2,1)S(1)}, u32[]{:S(2)}, u32[]{:S(2)}) %collective-permute-start.17) | collective-permute-done | bytes 393248 | tf_op jit(solution)/shard_map/ppermute | solution.py:382
  25.0 23.4 %collective-permute-done.16 = bf16[8,192,128]{2,1,0:T(8,128)(2,1)S(1)} collective-permute-done((bf16[8,192,128]{2,1,0:T(8,128)(2,1)S(1)}, bf16[8,192,128]{2,1,0:T(8,128)(2,1)S(1)}, u32[]{:S(2)}, u32[]{:S(2)}) %collective-permute-start.16) | collective-permute-done | bytes 393248 | tf_op jit(solution)/shard_map/ppermute | solution.py:382
  48.7 1.3 copy.39
  50.0 3.7 all-to-all-start.6
  54.2 7.9 %fourier_chunk.4 = bf16[32,192,128]{2,1,0:T(8,128)(2,1)S(1)} custom-call(s32[1]{0:T(128)} %bitcast.parity_ref, s32[256,1]{1,0:T(8,128)S(1)} %broadcast_in_dim.52.wave_ref, bf16[2,4,2,192,1536]{4,3,2,1,0:T(8,128)(2,1)} %bitcast.209), custom_call_target="tpu_custom_call" | custom-call | flops 2415919104 | bytes 9437184 | tf_op jit(solution)/shard_map/fourier_chunk/pallas_call | solution.py:164
  62.2 2.5 collective-permute-start.2
  64.8 1.9 collective-permute-start
  66.7 9.5 %collective-permute-done.2 = bf16[8,192,128]{2,1,0:T(8,128)(2,1)S(1)} collective-permute-done((bf16[8,192,128]{2,1,0:T(8,128)(2,1)S(1)}, bf16[8,192,128]{2,1,0:T(8,128)(2,1)S(1)}, u32[]{:S(2)}, u32[]{:S(2)}) %collective-permute-start.2) | collective-permute-done | bytes 393248 | tf_op jit(solution)/shard_map/ppermute | solution.py:382
  76.1 22.1 %collective-permute-done.1 = bf16[8,192,128]{2,1,0:T(8,128)(2,1)S(1)} collective-permute-done((bf16[8,192,128]{2,1,0:T(8,128)(2,1)S(1)}, bf16[8,192,128]{2,1,0:T(8,128)(2,1)S(1)}, u32[]{:S(2)}, u32[]{:S(2)}) %collective-permute-start.1) | collective-permute-done | bytes 393248 | tf_op jit(solution)/shard_map/ppermute | solution.py:382
  98.4 1.3 copy.19
  99.7 4.3 all-to-all-start
  104.5 7.9 %fourier_chunk.5 = bf16[32,192,128]{2,1,0:T(8,128)(2,1)S(1)} custom-call(s32[1]{0:T(128)} %bitcast.parity_ref, s32[256,1]{1,0:T(8,128)S(1)} %broadcast_in_dim.53.wave_ref, bf16[2,4,2,192,1536]{4,3,2,1,0:T(8,128)(2,1)} %bitcast.210), custom_call_target="tpu_custom_call" | custom-call | flops 2415919104 | bytes 9437184 | tf_op jit(solution)/shard_map/fourier_chunk/pallas_call | solution.py:164
  112.5 1.4 collective-permute-start.8
  113.9 3.0 collective-permute-start.6
  117.0 9.5 %collective-permute-done.8 = bf16[8,192,128]{2,1,0:T(8,128)(2,1)S(1)} collective-permute-done((bf16[8,192,128]{2,1,0:T(8,128)(2,1)S(1)}, bf16[8,192,128]{2,1,0:T(8,128)(2,1)S(1)}, u32[]{:S(2)}, u32[]{:S(2)}) %collective-permute-start.8) | collective-permute-done | bytes 393248 | tf_op jit(solution)/shard_map/ppermute | solution.py:382
  126.5 20.7 %collective-permute-done.7 = bf16[8,192,128]{2,1,0:T(8,128)(2,1)S(1)} collective-permute-done((bf16[8,192,128]{2,1,0:T(8,128)(2,1)S(1)}, bf16[8,192,128]{2,1,0:T(8,128)(2,1)S(1)}, u32[]{:S(2)}, u32[]{:S(2)}) %collective-permute-start.7) | collective-permute-done | bytes 393248 | tf_op jit(solution)/shard_map/ppermute | solution.py:382
  147.4 1.3 copy.27
  148.7 4.5 all-to-all-start.2
  153.7 7.9 %fourier_chunk.6 = bf16[32,192,128]{2,1,0:T(8,128)(2,1)S(1)} custom-call(s32[1]{0:T(128)} %bitcast.parity_ref, s32[256,1]{1,0:T(8,128)S(1)} %broadcast_in_dim.54.wave_ref, bf16[2,4,2,192,1536]{4,3,2,1,0:T(8,128)(2,1)} %bitcast.211), custom_call_target="tpu_custom_call" | custom-call | flops 2415919104 | bytes 9437184 | tf_op jit(solution)/shard_map/fourier_chunk/pallas_call | solution.py:164
  161.6 1.0 slice_bitcast_fusion.1
  162.6 2.5 collective-permute-start.14
  165.1 1.9 collective-permute-start.12
  168.5 8.3 %collective-permute-done.14 = bf16[8,192,128]{2,1,0:T(8,128)(2,1)} collective-permute-done((bf16[8,192,128]{2,1,0:T(8,128)(2,1)}, bf16[8,192,128]{2,1,0:T(8,128)(2,1)}, u32[]{:S(2)}, u32[]{:S(2)}) %collective-permute-start.14) | collective-permute-done | bytes 393248 | tf_op jit(solution)/shard_map/ppermute | solution.py:382
  176.8 22.0 %collective-permute-done.13 = bf16[8,192,128]{2,1,0:T(8,128)(2,1)} collective-permute-done((bf16[8,192,128]{2,1,0:T(8,128)(2,1)}, bf16[8,192,128]{2,1,0:T(8,128)(2,1)}, u32[]{:S(2)}, u32[]{:S(2)}) %collective-permute-start.13) | collective-permute-done | bytes 393248 | tf_op jit(solution)/shard_map/ppermute | solution.py:382
  198.8 1.4 pad_maximum_fusion.2
  200.2 1.3 copy.34
  201.5 4.3 all-to-all-start.4
  208.2 13.5 %spectral_chunk.7 = bf16[4,8,192,128]{3,2,1,0:T(8,128)(2,1)S(1)} custom-call(s32[2]{0:T(128)S(1)} %get-tuple-element.63.lower_ref, bf16[4,8,192,128]{3,2,1,0:T(8,128)(2,1)S(1)} %bitcast.202, bf16[32,520,768]{2,1,0:T(8,128)(2,1)} %bitcast.204, bf16[2048,128]{1,0:T(8,128)(2,1)S(1)} %bitcast.198, s32[1032,128]{1,0:T(8,128)S(1)} %broadcast_in_dim.43.first_ref, ...), custom_call_target="tpu_custom_call" | custom-call | flops 2726297600 | bytes 6389760 | tf_op jit(solution)/shard_map/spectral_chunk/pallas_call | solution.py:280
  221.8 1.2 copy-done.3
  222.9 3.9 all-to-all-done.4
  226.8 3.8 all-to-all-start.7
  230.6 15.1 %spectral_chunk.4 = bf16[4,8,192,128]{3,2,1,0:T(8,128)(2,1)} custom-call(s32[2]{0:T(128)S(1)} %get-tuple-element.66.lower_ref, bf16[4,8,192,128]{3,2,1,0:T(8,128)(2,1)} %bitcast.14.field_ref, bf16[32,520,768]{2,1,0:T(8,128)(2,1)} %bitcast.205, bf16[2048,128]{1,0:T(8,128)(2,1)S(1)} %bitcast.199, s32[1032,128]{1,0:T(8,128)S(1)} %broadcast_in_dim.43.first_ref, ...), custom_call_target="tpu_custom_call" | custom-call | flops 2726297600 | bytes 6389760 | tf_op jit(solution)/shard_map/spectral_chunk/pallas_call | solution.py:280
  245.8 5.8 %all-to-all-done.7 = bf16[8,768,128]{2,1,0:T(8,128)(2,1)S(1)} async-done(((bf16[8,768,128]{2,1,0:T(8,128)(2,1)}), bf16[8,768,128]{2,1,0:T(8,128)(2,1)S(1)}, u32[]{:S(2)}, u32[]{:S(2)}) %all-to-all-start.7) | async-done | bytes 1572896 | tf_op jit(solution)/shard_map/all_to_all | solution.py:387
  251.6 1.2 copy-done.4
  252.8 4.3 all-to-all-start.1
  257.1 15.1 %spectral_chunk.5 = bf16[4,8,192,128]{3,2,1,0:T(8,128)(2,1)} custom-call(s32[2]{0:T(128)S(1)} %get-tuple-element.65.lower_ref, bf16[4,8,192,128]{3,2,1,0:T(8,128)(2,1)} %bitcast.35.field_ref, bf16[32,520,768]{2,1,0:T(8,128)(2,1)} %bitcast.206, bf16[2048,128]{1,0:T(8,128)(2,1)S(1)} %bitcast.200, s32[1032,128]{1,0:T(8,128)S(1)} %broadcast_in_dim.43.first_ref, ...), custom_call_target="tpu_custom_call" | custom-call | flops 2726297600 | bytes 6389760 | tf_op jit(solution)/shard_map/spectral_chunk/pallas_call | solution.py:280
  272.2 5.9 %all-to-all-done.1 = bf16[8,768,128]{2,1,0:T(8,128)(2,1)} async-done(((bf16[8,768,128]{2,1,0:T(8,128)(2,1)}), bf16[8,768,128]{2,1,0:T(8,128)(2,1)}, u32[]{:S(2)}, u32[]{:S(2)}) %all-to-all-start.1) | async-done | bytes 1572896 | tf_op jit(solution)/shard_map/all_to_all | solution.py:387
  278.1 3.6 all-to-all-start.3
  281.7 15.1 %spectral_chunk.6 = bf16[4,8,192,128]{3,2,1,0:T(8,128)(2,1)} custom-call(s32[2]{0:T(128)S(1)} %get-tuple-element.64.lower_ref, bf16[4,8,192,128]{3,2,1,0:T(8,128)(2,1)} %bitcast.48.field_ref, bf16[32,520,768]{2,1,0:T(8,128)(2,1)} %bitcast.207, bf16[2048,128]{1,0:T(8,128)(2,1)S(1)} %bitcast.201, s32[1032,128]{1,0:T(8,128)S(1)} %broadcast_in_dim.43.first_ref, ...), custom_call_target="tpu_custom_call" | custom-call | flops 2726297600 | bytes 6389760 | tf_op jit(solution)/shard_map/spectral_chunk/pallas_call | solution.py:280
  296.8 5.8 %all-to-all-done.3 = bf16[8,768,128]{2,1,0:T(8,128)(2,1)S(1)} async-done(((bf16[8,768,128]{2,1,0:T(8,128)(2,1)}), bf16[8,768,128]{2,1,0:T(8,128)(2,1)S(1)}, u32[]{:S(2)}, u32[]{:S(2)}) %all-to-all-start.3) | async-done | bytes 1572896 | tf_op jit(solution)/shard_map/all_to_all | solution.py:387
  302.7 1.1 copy-done.6
  303.8 4.6 all-to-all-start.5
  309.6 7.7 %synthesis_rows.1.refs_16_ = bf16[1024,1536]{1,0:T(8,128)(2,1)S(1)} custom-call(s32[1024,1]{1,0:T(8,128)S(1)} %reshape_reshape.69.wave_ref), custom_call_target="tpu_custom_call" | custom-call | tf_op jit(solution)/shard_map/synthesis_rows/pallas_call | solution.py:191
  317.3 3.6 slice_bitcast_fusion.7
  320.9 1.4 collective-permute-start.5
  322.4 1.3 copy-done.7
  323.7 1.1 slice_bitcast_fusion.2
  324.7 4.7 all-to-all-done.5
  329.4 1.6 slice_bitcast_fusion.18
  331.2 2.0 collective-permute-start.19
  333.2 2.5 collective-permute-start.20
  335.9 13.0 %collective-permute-done.18 = bf16[2,8,96,128]{3,2,1,0:T(8,128)(2,1)S(1)} collective-permute-done((bf16[2,8,96,128]{3,2,1,0:T(8,128)(2,1)S(1)}, bf16[2,8,96,128]{3,2,1,0:T(8,128)(2,1)S(1)}, u32[]{:S(2)}, u32[]{:S(2)}) %collective-permute-start.18) | collective-permute-done | bytes 393248 | tf_op jit(solution)/shard_map/ppermute | solution.py:382
  348.8 2.5 collective-permute-start.21
  351.4 30.3 %collective-permute-done.19 = bf16[2,8,96,128]{3,2,1,0:T(8,128)(2,1)S(1)} collective-permute-done((bf16[2,8,96,128]{3,2,1,0:T(8,128)(2,1)S(1)}, bf16[2,8,96,128]{3,2,1,0:T(8,128)(2,1)S(1)}, u32[]{:S(2)}, u32[]{:S(2)}) %collective-permute-start.19) | collective-permute-done | bytes 393248 | tf_op jit(solution)/shard_map/ppermute | solution.py:382
  381.7 2.5 collective-permute-start.23
  384.2 24.9 %collective-permute-start.3 = (bf16[8,192,128]{2,1,0:T(8,128)(2,1)S(1)}, bf16[8,192,128]{2,1,0:T(8,128)(2,1)S(1)}, u32[]{:S(2)}, u32[]{:S(2)}) collective-permute-start(bf16[8,192,128]{2,1,0:T(8,128)(2,1)S(1)} %copy-done.8), channel_id=1, source_target_pairs={{0,2},{1,3},{2,0},{3,1},{4,6},{5,7},{6,4},{7,5},{8,10},{9,11},{10,... | collective-permute-start | bytes 1179656 | tf_op jit(solution)/shard_map/ppermute | solution.py:382
  409.2 1.4 collective-permute-start.11
  410.6 4.8 collective-permute-done.22
  415.4 25.8 %collective-permute-start.9 = (bf16[8,192,128]{2,1,0:T(8,128)(2,1)S(1)}, bf16[8,192,128]{2,1,0:T(8,128)(2,1)S(1)}, u32[]{:S(2)}, u32[]{:S(2)}) collective-permute-start(bf16[8,192,128]{2,1,0:T(8,128)(2,1)S(1)} %copy-done.9), channel_id=1, source_target_pairs={{0,2},{1,3},{2,0},{3,1},{4,6},{5,7},{6,4},{7,5},{8,10},{9,11},{10,... | collective-permute-start | bytes 1179656 | tf_op jit(solution)/shard_map/ppermute | solution.py:382
  441.3 15.7 %collective-permute-done.10.refs_6_ = bf16[8,192,128]{2,1,0:T(8,128)(2,1)S(1)} collective-permute-done((bf16[8,192,128]{2,1,0:T(8,128)(2,1)S(1)}, bf16[8,192,128]{2,1,0:T(8,128)(2,1)S(1)}, u32[]{:S(2)}, u32[]{:S(2)}) %collective-permute-start.10) | collective-permute-done | bytes 393248 | tf_op jit(solution)/shard_map/ppermute | solution.py:382
  457.9 9.7 %synthesis_part.2.refs_18_ = bf16[2,4,2,192,1536]{4,3,2,1,0:T(8,128)(2,1)} custom-call(s32[1]{0:T(128)} %bitcast.parity_ref, bf16[8,192,128]{2,1,0:T(8,128)(2,1)S(1)} %get-tuple-element.40.refs_0_, bf16[8,192,128]{2,1,0:T(8,128)(2,1)S(1)} %collective-permute-done.3.refs_1_, bf16[8,192,128]{2,1,0:T(8,128)(2,1)S(1)} %collective-permute-done.4.refs_2_, ...), custom_call_target="tpu_custom_call" | custom-call | flops 4831838208 | bytes 9437184 | tf_op jit(solution)/shard_map/synthesis_part/pallas_call | solution.py:359
  467.6 9.7 %synthesis_part.3 = bf16[2,4,2,192,1536]{4,3,2,1,0:T(8,128)(2,1)} custom-call(s32[1]{0:T(128)} %bitcast.parity_ref, bf16[8,192,128]{2,1,0:T(8,128)(2,1)S(1)} %get-tuple-element.40.refs_0_, bf16[8,192,128]{2,1,0:T(8,128)(2,1)S(1)} %collective-permute-done.3.refs_1_, ...), custom_call_target="tpu_custom_call", output_to_operand_aliasing={{}: (19, {})} | custom-call | flops 4831838208 | bytes 9437184 | tf_op jit(solution)/shard_map/synthesis_part/pallas_call | solution.py:359
  (103 shorter events, 11.3 us)
Async XLA Ops:
  0.0 207.3 %copy-start = (bf16[16,128,128]{2,1,0:T(8,128)(2,1)S(1)}, bf16[16,128,128]{2,1,0:T(8,128)(2,1)}, u32[]{:S(2)}) copy-start(bf16[16,128,128]{2,1,0:T(8,128)(2,1)} %param.9) | copy-start | bytes 1572868
  9.8 15.2 %collective-permute-start.17 = (bf16[8,192,128]{2,1,0:T(8,128)(2,1)S(1)}, bf16[8,192,128]{2,1,0:T(8,128)(2,1)S(1)}, u32[]{:S(2)}, u32[]{:S(2)}) collective-permute-start(bf16[8,192,128]{2,1,0:T(8,128)(2,1)S(1)} %get-tuple-element.22), channel_id=1, source_target_pairs={{0,6},{1,7},{2,4},{3,5},{4,2},{5,3},{6,0},{7,1},{8,14},{9,15},{10,... | collective-permute-start | bytes 1179656 | tf_op jit(solution)/shard_map/ppermute | solution.py:382
  14.9 33.5 %collective-permute-start.16 = (bf16[8,192,128]{2,1,0:T(8,128)(2,1)S(1)}, bf16[8,192,128]{2,1,0:T(8,128)(2,1)S(1)}, u32[]{:S(2)}, u32[]{:S(2)}) collective-permute-start(bf16[8,192,128]{2,1,0:T(8,128)(2,1)S(1)} %get-tuple-element.23), channel_id=1, source_target_pairs={{0,4},{1,5},{2,6},{3,7},{4,0},{5,1},{6,2},{7,3},{8,12},{9,13},{10,... | collective-permute-start | bytes 1179656 | tf_op jit(solution)/shard_map/ppermute | solution.py:382
  14.9 33.5 %collective-permute-start.15 = (bf16[8,192,128]{2,1,0:T(8,128)(2,1)S(1)}, bf16[8,192,128]{2,1,0:T(8,128)(2,1)S(1)}, u32[]{:S(2)}, u32[]{:S(2)}) collective-permute-start(bf16[8,192,128]{2,1,0:T(8,128)(2,1)S(1)} %get-tuple-element.24), channel_id=1, source_target_pairs={{0,2},{1,3},{2,0},{3,1},{4,6},{5,7},{6,4},{7,5},{8,10},{9,11},{10,... | collective-permute-start | bytes 1179656 | tf_op jit(solution)/shard_map/ppermute | solution.py:382
  50.0 49.7 %all-to-all-start.6 = ((bf16[8,768,128]{2,1,0:T(8,128)(2,1)}), bf16[8,768,128]{2,1,0:T(8,128)(2,1)S(1)}, u32[]{:S(2)}, u32[]{:S(2)}) async-start(bf16[8,768,128]{2,1,0:T(8,128)(2,1)} %bitcast.218), calls=%async_computation.6 | async-start | bytes 3145728 | tf_op jit(solution)/shard_map/all_to_all | solution.py:387
  62.2 13.9 %collective-permute-start.2 = (bf16[8,192,128]{2,1,0:T(8,128)(2,1)S(1)}, bf16[8,192,128]{2,1,0:T(8,128)(2,1)S(1)}, u32[]{:S(2)}, u32[]{:S(2)}) collective-permute-start(bf16[8,192,128]{2,1,0:T(8,128)(2,1)S(1)} %get-tuple-element.42), channel_id=1, source_target_pairs={{0,6},{1,7},{2,4},{3,5},{4,2},{5,3},{6,0},{7,1},{8,14},{9,15},{10,... | collective-permute-start | bytes 1179656 | tf_op jit(solution)/shard_map/ppermute | solution.py:382
  64.8 33.4 %collective-permute-start.1 = (bf16[8,192,128]{2,1,0:T(8,128)(2,1)S(1)}, bf16[8,192,128]{2,1,0:T(8,128)(2,1)S(1)}, u32[]{:S(2)}, u32[]{:S(2)}) collective-permute-start(bf16[8,192,128]{2,1,0:T(8,128)(2,1)S(1)} %get-tuple-element.43), channel_id=1, source_target_pairs={{0,4},{1,5},{2,6},{3,7},{4,0},{5,1},{6,2},{7,3},{8,12},{9,13},{10,... | collective-permute-start | bytes 1179656 | tf_op jit(solution)/shard_map/ppermute | solution.py:382
  64.8 33.4 %collective-permute-start = (bf16[8,192,128]{2,1,0:T(8,128)(2,1)S(1)}, bf16[8,192,128]{2,1,0:T(8,128)(2,1)S(1)}, u32[]{:S(2)}, u32[]{:S(2)}) collective-permute-start(bf16[8,192,128]{2,1,0:T(8,128)(2,1)S(1)} %get-tuple-element.44), channel_id=1, source_target_pairs={{0,2},{1,3},{2,0},{3,1},{4,6},{5,7},{6,4},{7,5},{8,10},{9,11},{10,... | collective-permute-start | bytes 1179656 | tf_op jit(solution)/shard_map/ppermute | solution.py:382
  99.7 49.0 %all-to-all-start = ((bf16[8,768,128]{2,1,0:T(8,128)(2,1)}), bf16[8,768,128]{2,1,0:T(8,128)(2,1)}, u32[]{:S(2)}, u32[]{:S(2)}) async-start(bf16[8,768,128]{2,1,0:T(8,128)(2,1)} %bitcast.217), calls=%async_computation | async-start | bytes 3145728 | tf_op jit(solution)/shard_map/all_to_all | solution.py:387
  112.5 14.0 %collective-permute-start.8 = (bf16[8,192,128]{2,1,0:T(8,128)(2,1)S(1)}, bf16[8,192,128]{2,1,0:T(8,128)(2,1)S(1)}, u32[]{:S(2)}, u32[]{:S(2)}) collective-permute-start(bf16[8,192,128]{2,1,0:T(8,128)(2,1)S(1)} %get-tuple-element.34), channel_id=1, source_target_pairs={{0,6},{1,7},{2,4},{3,5},{4,2},{5,3},{6,0},{7,1},{8,14},{9,15},{10,... | collective-permute-start | bytes 1179656 | tf_op jit(solution)/shard_map/ppermute | solution.py:382
  113.9 33.3 %collective-permute-start.7 = (bf16[8,192,128]{2,1,0:T(8,128)(2,1)S(1)}, bf16[8,192,128]{2,1,0:T(8,128)(2,1)S(1)}, u32[]{:S(2)}, u32[]{:S(2)}) collective-permute-start(bf16[8,192,128]{2,1,0:T(8,128)(2,1)S(1)} %get-tuple-element.35), channel_id=1, source_target_pairs={{0,4},{1,5},{2,6},{3,7},{4,0},{5,1},{6,2},{7,3},{8,12},{9,13},{10,... | collective-permute-start | bytes 1179656 | tf_op jit(solution)/shard_map/ppermute | solution.py:382
  113.9 33.3 %collective-permute-start.6 = (bf16[8,192,128]{2,1,0:T(8,128)(2,1)S(1)}, bf16[8,192,128]{2,1,0:T(8,128)(2,1)S(1)}, u32[]{:S(2)}, u32[]{:S(2)}) collective-permute-start(bf16[8,192,128]{2,1,0:T(8,128)(2,1)S(1)} %get-tuple-element.36), channel_id=1, source_target_pairs={{0,2},{1,3},{2,0},{3,1},{4,6},{5,7},{6,4},{7,5},{8,10},{9,11},{10,... | collective-permute-start | bytes 1179656 | tf_op jit(solution)/shard_map/ppermute | solution.py:382
  148.7 52.8 %all-to-all-start.2 = ((bf16[8,768,128]{2,1,0:T(8,128)(2,1)}), bf16[8,768,128]{2,1,0:T(8,128)(2,1)}, u32[]{:S(2)}, u32[]{:S(2)}) async-start(bf16[8,768,128]{2,1,0:T(8,128)(2,1)} %bitcast.214), calls=%async_computation.2 | async-start | bytes 3145728 | tf_op jit(solution)/shard_map/all_to_all | solution.py:387
  161.6 5.4 %copy-start.13 = (s32[256]{0:T(256)S(1)}, s32[256]{0:T(256)}, u32[]{:S(2)}) copy-start(s32[256]{0:T(256)} %param.10) | copy-start | bytes 3076
  161.6 5.5 %copy-start.12 = (s32[512]{0:T(512)S(1)}, s32[512]{0:T(512)}, u32[]{:S(2)}) copy-start(s32[512]{0:T(512)} %param.11) | copy-start | bytes 6148
  162.6 14.2 %collective-permute-start.14 = (bf16[8,192,128]{2,1,0:T(8,128)(2,1)}, bf16[8,192,128]{2,1,0:T(8,128)(2,1)}, u32[]{:S(2)}, u32[]{:S(2)}) collective-permute-start(bf16[8,192,128]{2,1,0:T(8,128)(2,1)} %get-tuple-element.26), channel_id=1, source_target_pairs={{0,6},{1,7},{2,4},{3,5},{4,2},{5,3},{6,0},{7,1},{8,14},{9,15},{10,... | collective-permute-start | bytes 1179656 | tf_op jit(solution)/shard_map/ppermute | solution.py:382
  165.1 33.7 %collective-permute-start.13 = (bf16[8,192,128]{2,1,0:T(8,128)(2,1)}, bf16[8,192,128]{2,1,0:T(8,128)(2,1)}, u32[]{:S(2)}, u32[]{:S(2)}) collective-permute-start(bf16[8,192,128]{2,1,0:T(8,128)(2,1)} %get-tuple-element.27), channel_id=1, source_target_pairs={{0,4},{1,5},{2,6},{3,7},{4,0},{5,1},{6,2},{7,3},{8,12},{9,13},{10,... | collective-permute-start | bytes 1179656 | tf_op jit(solution)/shard_map/ppermute | solution.py:382
  165.1 33.7 %collective-permute-start.12 = (bf16[8,192,128]{2,1,0:T(8,128)(2,1)S(1)}, bf16[8,192,128]{2,1,0:T(8,128)(2,1)}, u32[]{:S(2)}, u32[]{:S(2)}) collective-permute-start(bf16[8,192,128]{2,1,0:T(8,128)(2,1)S(1)} %get-tuple-element.28), channel_id=1, source_target_pairs={{0,2},{1,3},{2,0},{3,1},{4,6},{5,7},{6,4},{7,5},{8,10},{9,11},{10,... | collective-permute-start | bytes 1179656 | tf_op jit(solution)/shard_map/ppermute | solution.py:382
  201.5 25.4 %all-to-all-start.4 = ((bf16[8,768,128]{2,1,0:T(8,128)(2,1)}), bf16[8,768,128]{2,1,0:T(8,128)(2,1)}, u32[]{:S(2)}, u32[]{:S(2)}) async-start(bf16[8,768,128]{2,1,0:T(8,128)(2,1)} %bitcast.219), calls=%async_computation.4 | async-start | bytes 3145728 | tf_op jit(solution)/shard_map/all_to_all | solution.py:387
  221.8 1.2 copy-start.3
  226.8 24.8 %all-to-all-start.7 = ((bf16[8,768,128]{2,1,0:T(8,128)(2,1)}), bf16[8,768,128]{2,1,0:T(8,128)(2,1)S(1)}, u32[]{:S(2)}, u32[]{:S(2)}) async-start(bf16[8,768,128]{2,1,0:T(8,128)(2,1)} %bitcast.203), calls=%async_computation.7 | async-start | bytes 3145728 | tf_op jit(solution)/shard_map/all_to_all | solution.py:387
  251.6 1.2 copy-start.4
  252.8 25.3 %all-to-all-start.1 = ((bf16[8,768,128]{2,1,0:T(8,128)(2,1)}), bf16[8,768,128]{2,1,0:T(8,128)(2,1)}, u32[]{:S(2)}, u32[]{:S(2)}) async-start(bf16[8,768,128]{2,1,0:T(8,128)(2,1)} %bitcast.23), calls=%async_computation.1 | async-start | bytes 3145728 | tf_op jit(solution)/shard_map/all_to_all | solution.py:387
  278.1 24.5 %all-to-all-start.3 = ((bf16[8,768,128]{2,1,0:T(8,128)(2,1)}), bf16[8,768,128]{2,1,0:T(8,128)(2,1)S(1)}, u32[]{:S(2)}, u32[]{:S(2)}) async-start(bf16[8,768,128]{2,1,0:T(8,128)(2,1)} %bitcast.36), calls=%async_computation.3 | async-start | bytes 3145728 | tf_op jit(solution)/shard_map/all_to_all | solution.py:387
  302.7 1.1 copy-start.6
  303.8 25.6 %all-to-all-start.5 = ((bf16[8,768,128]{2,1,0:T(8,128)(2,1)}), bf16[8,768,128]{2,1,0:T(8,128)(2,1)}, u32[]{:S(2)}, u32[]{:S(2)}) async-start(bf16[8,768,128]{2,1,0:T(8,128)(2,1)} %bitcast.49), calls=%async_computation.5 | async-start | bytes 3145728 | tf_op jit(solution)/shard_map/all_to_all | solution.py:387
  317.3 3.6 copy-start.2
  317.3 5.0 %copy-start.5 = (bf16[8,768,128]{2,1,0:T(8,128)(2,1)S(1)}, bf16[8,768,128]{2,1,0:T(8,128)(2,1)}, u32[]{:S(2)}) copy-start(bf16[8,768,128]{2,1,0:T(8,128)(2,1)} %copy-done.4) | copy-start | bytes 4718596
  320.9 88.3 %collective-permute-start.5 = (bf16[8,192,128]{2,1,0:T(8,128)(2,1)}, bf16[8,192,128]{2,1,0:T(8,128)(2,1)S(1)}, u32[]{:S(2)}, u32[]{:S(2)}) collective-permute-start(bf16[8,192,128]{2,1,0:T(8,128)(2,1)} %get-tuple-element.37), channel_id=1, source_target_pairs={{0,6},{1,7},{2,4},{3,5},{4,2},{5,3},{6,0},{7,1},{8,14},{9,15},{10,... | collective-permute-start | bytes 1179656 | tf_op jit(solution)/shard_map/ppermute | solution.py:382
  322.2 119.0 %collective-permute-start.4 = (bf16[8,192,128]{2,1,0:T(8,128)(2,1)}, bf16[8,192,128]{2,1,0:T(8,128)(2,1)S(1)}, u32[]{:S(2)}, u32[]{:S(2)}) collective-permute-start(bf16[8,192,128]{2,1,0:T(8,128)(2,1)} %get-tuple-element.38), channel_id=1, source_target_pairs={{0,4},{1,5},{2,6},{3,7},{4,0},{5,1},{6,2},{7,3},{8,12},{9,13},{10,... | collective-permute-start | bytes 1179656 | tf_op jit(solution)/shard_map/ppermute | solution.py:382
  322.2 1.4 copy-start.7
  331.0 17.8 %collective-permute-start.18 = (bf16[2,8,96,128]{3,2,1,0:T(8,128)(2,1)S(1)}, bf16[2,8,96,128]{3,2,1,0:T(8,128)(2,1)S(1)}, u32[]{:S(2)}, u32[]{:S(2)}) collective-permute-start(bf16[2,8,96,128]{3,2,1,0:T(8,128)(2,1)S(1)} %pad_maximum_fusion.4), channel_id=1, source_target_pairs={{0,2},{1,3},{2,0},{3,1},{4,6},{5,7},{6,4},{7,5},{8,10},{9,11},{10,... | collective-permute-start | bytes 1179656 | tf_op jit(solution)/shard_map/ppermute | solution.py:382
  331.2 50.4 %collective-permute-start.19 = (bf16[2,8,96,128]{3,2,1,0:T(8,128)(2,1)S(1)}, bf16[2,8,96,128]{3,2,1,0:T(8,128)(2,1)S(1)}, u32[]{:S(2)}, u32[]{:S(2)}) collective-permute-start(bf16[2,8,96,128]{3,2,1,0:T(8,128)(2,1)S(1)} %pad_maximum_fusion.5), channel_id=1, source_target_pairs={{0,4},{1,5},{2,6},{3,7},{4,0},{5,1},{6,2},{7,3},{8,12},{9,13},{10,... | collective-permute-start | bytes 1179656 | tf_op jit(solution)/shard_map/ppermute | solution.py:382
  333.2 48.5 %collective-permute-start.20 = (bf16[2,8,96,128]{3,2,1,0:T(8,128)(2,1)S(1)}, bf16[2,8,96,128]{3,2,1,0:T(8,128)(2,1)S(1)}, u32[]{:S(2)}, u32[]{:S(2)}) collective-permute-start(bf16[2,8,96,128]{3,2,1,0:T(8,128)(2,1)S(1)} %pad_maximum_fusion.6), channel_id=1, source_target_pairs={{0,6},{1,7},{2,4},{3,5},{4,2},{5,3},{6,0},{7,1},{8,14},{9,15},{10,... | collective-permute-start | bytes 1179656 | tf_op jit(solution)/shard_map/ppermute | solution.py:382
  335.8 48.4 %copy-start.8 = (bf16[8,192,128]{2,1,0:T(8,128)(2,1)S(1)}, bf16[8,192,128]{2,1,0:T(8,128)(2,1)}, u32[]{:S(2)}) copy-start(bf16[8,192,128]{2,1,0:T(8,128)(2,1)} %get-tuple-element.39) | copy-start | bytes 1179652
  335.9 73.3 %copy-start.11 = (bf16[8,192,128]{2,1,0:T(8,128)(2,1)S(1)}, bf16[8,192,128]{2,1,0:T(8,128)(2,1)}, u32[]{:S(2)}) copy-start(bf16[8,192,128]{2,1,0:T(8,128)(2,1)} %get-tuple-element.29) | copy-start | bytes 1179652
  335.9 79.5 %copy-start.10 = (bf16[8,192,128]{2,1,0:T(8,128)(2,1)S(1)}, bf16[8,192,128]{2,1,0:T(8,128)(2,1)}, u32[]{:S(2)}) copy-start(bf16[8,192,128]{2,1,0:T(8,128)(2,1)} %get-tuple-element.30) | copy-start | bytes 1179652
  335.9 79.5 %copy-start.9 = (bf16[8,192,128]{2,1,0:T(8,128)(2,1)S(1)}, bf16[8,192,128]{2,1,0:T(8,128)(2,1)}, u32[]{:S(2)}) copy-start(bf16[8,192,128]{2,1,0:T(8,128)(2,1)} %get-tuple-element.31) | copy-start | bytes 1179652
  348.8 35.4 %collective-permute-start.21 = (bf16[2,8,96,128]{3,2,1,0:T(8,128)(2,1)S(1)}, bf16[2,8,96,128]{3,2,1,0:T(8,128)(2,1)S(1)}, u32[]{:S(2)}, u32[]{:S(2)}) collective-permute-start(bf16[2,8,96,128]{3,2,1,0:T(8,128)(2,1)S(1)} %pad_maximum_fusion.7), channel_id=1, source_target_pairs={{0,2},{1,3},{2,0},{3,1},{4,6},{5,7},{6,4},{7,5},{8,10},{9,11},{10,... | collective-permute-start | bytes 1179656 | tf_op jit(solution)/shard_map/ppermute | solution.py:382
  381.6 33.7 %collective-permute-start.22 = (bf16[2,8,96,128]{3,2,1,0:T(8,128)(2,1)S(1)}, bf16[2,8,96,128]{3,2,1,0:T(8,128)(2,1)S(1)}, u32[]{:S(2)}, u32[]{:S(2)}) collective-permute-start(bf16[2,8,96,128]{3,2,1,0:T(8,128)(2,1)S(1)} %pad_maximum_fusion.8), channel_id=1, source_target_pairs={{0,4},{1,5},{2,6},{3,7},{4,0},{5,1},{6,2},{7,3},{8,12},{9,13},{10,... | collective-permute-start | bytes 1179656 | tf_op jit(solution)/shard_map/ppermute | solution.py:382
  381.7 33.7 %collective-permute-start.23 = (bf16[2,8,96,128]{3,2,1,0:T(8,128)(2,1)S(1)}, bf16[2,8,96,128]{3,2,1,0:T(8,128)(2,1)S(1)}, u32[]{:S(2)}, u32[]{:S(2)}) collective-permute-start(bf16[2,8,96,128]{3,2,1,0:T(8,128)(2,1)S(1)} %pad_maximum_fusion.9), channel_id=1, source_target_pairs={{0,6},{1,7},{2,4},{3,5},{4,2},{5,3},{6,0},{7,1},{8,14},{9,15},{10,... | collective-permute-start | bytes 1179656 | tf_op jit(solution)/shard_map/ppermute | solution.py:382
  384.2 57.0 %collective-permute-start.3 = (bf16[8,192,128]{2,1,0:T(8,128)(2,1)S(1)}, bf16[8,192,128]{2,1,0:T(8,128)(2,1)S(1)}, u32[]{:S(2)}, u32[]{:S(2)}) collective-permute-start(bf16[8,192,128]{2,1,0:T(8,128)(2,1)S(1)} %copy-done.8), channel_id=1, source_target_pairs={{0,2},{1,3},{2,0},{3,1},{4,6},{5,7},{6,4},{7,5},{8,10},{9,11},{10,... | collective-permute-start | bytes 1179656 | tf_op jit(solution)/shard_map/ppermute | solution.py:382
  409.2 32.1 %collective-permute-start.11 = (bf16[8,192,128]{2,1,0:T(8,128)(2,1)S(1)}, bf16[8,192,128]{2,1,0:T(8,128)(2,1)S(1)}, u32[]{:S(2)}, u32[]{:S(2)}) collective-permute-start(bf16[8,192,128]{2,1,0:T(8,128)(2,1)S(1)} %copy-done.11), channel_id=1, source_target_pairs={{0,6},{1,7},{2,4},{3,5},{4,2},{5,3},{6,0},{7,1},{8,14},{9,15},{10,... | collective-permute-start | bytes 1179656 | tf_op jit(solution)/shard_map/ppermute | solution.py:382
  415.4 41.7 %collective-permute-start.10 = (bf16[8,192,128]{2,1,0:T(8,128)(2,1)S(1)}, bf16[8,192,128]{2,1,0:T(8,128)(2,1)S(1)}, u32[]{:S(2)}, u32[]{:S(2)}) collective-permute-start(bf16[8,192,128]{2,1,0:T(8,128)(2,1)S(1)} %copy-done.10), channel_id=1, source_target_pairs={{0,4},{1,5},{2,6},{3,7},{4,0},{5,1},{6,2},{7,3},{8,12},{9,13},{10,... | collective-permute-start | bytes 1179656 | tf_op jit(solution)/shard_map/ppermute | solution.py:382
  415.4 42.5 %collective-permute-start.9 = (bf16[8,192,128]{2,1,0:T(8,128)(2,1)S(1)}, bf16[8,192,128]{2,1,0:T(8,128)(2,1)S(1)}, u32[]{:S(2)}, u32[]{:S(2)}) collective-permute-start(bf16[8,192,128]{2,1,0:T(8,128)(2,1)S(1)} %copy-done.9), channel_id=1, source_target_pairs={{0,2},{1,3},{2,0},{3,1},{4,6},{5,7},{6,4},{7,5},{8,10},{9,11},{10,... | collective-permute-start | bytes 1179656 | tf_op jit(solution)/shard_map/ppermute | solution.py:382
  467.6 9.7 %copy-start.1 = (bf16[16,128,128]{2,1,0:T(8,128)(2,1)S(1)}, bf16[16,128,128]{2,1,0:T(8,128)(2,1)}, u32[]{:S(2)}) copy-start(bf16[16,128,128]{2,1,0:T(8,128)(2,1)} %param.9) | copy-start | bytes 1572868

commit v2 on v1

--- a/solution.py
+++ b/solution.py
@@ -13,6 +13,10 @@
 ROWS = 8
 LANES = 128
 VMEM = 48 * 2**20
+LONG = pl.CostEstimate(flops=10**13, bytes_accessed=10**8, transcendentals=0)
+SHORT = pl.CostEstimate(flops=1, bytes_accessed=1, transcendentals=0)
+SIN = (-1.0 / 39916800, 1.0 / 362880, -1.0 / 5040, 1.0 / 120, -1.0 / 6, 1.0)
+ANYWHERE = pl.BlockSpec(memory_space=pl.ANY)
 
 
 def fourier_basis(wavenumbers, points):
@@ -111,59 +115,70 @@
     return lax.dot_general(a, b, (dims, ((), ())), preferred_element_type=jnp.float32)
 
 
+def cos_turn(steps, points):
+    rest = steps - points * jnp.floor(steps * (1.0 / points) + 0.5)
+    angle = (points // 4 - jnp.abs(rest)) * (2.0 * math.pi / points)
+    square = angle * angle
+    total = jnp.full_like(square, SIN[0])
+    for c in SIN[1:]:
+        total = total * square + c
+    return total * angle
+
+
 def make_table(wave, points, scale):
     rows = wave.shape[0]
-    unit = 2.0 * math.pi / points
     lane = lax.broadcasted_iota(jnp.int32, (rows, LANES), 1).astype(jnp.float32)
+    part = lax.broadcasted_iota(jnp.int32, (rows, LANES), 0) % 2
+    shift = (part * (points // 4)).astype(jnp.float32)
     waves = jnp.broadcast_to(wave, (rows, LANES)).astype(jnp.float32)
-
-    def turn(steps):
-        return (steps - points * jnp.floor(steps * (1.0 / points))) * unit
-
-    fine = turn(waves * lane)
-    coarse = turn(waves * (lane * LANES))
-    cos_fine, sin_fine = jnp.cos(fine), jnp.sin(fine)
-    cos_coarse, sin_coarse = jnp.cos(coarse) * scale, jnp.sin(coarse) * scale
-    part = lax.broadcasted_iota(jnp.int32, (rows, LANES), 0) % 2
-    by_cos = jnp.where(part == 0, cos_coarse, -sin_coarse)
-    by_sin = jnp.where(part == 0, -sin_coarse, -cos_coarse)
-    pieces = [
-        by_cos[:, a : a + 1] * cos_fine + by_sin[:, a : a + 1] * sin_fine
-        for a in range(points // LANES)
-    ]
-    return jnp.concatenate(pieces, axis=1).astype(jnp.bfloat16)
-
-
-def fourier_kernel(parity_ref, wave_ref, grid_ref, out_ref, table_ref):
-    step = pl.program_id(0)
+    twice = 2.0 * cos_turn(waves * LANES, points)
+    tiles = [cos_turn(waves * (lane + i * LANES) + shift, points) * scale for i in range(2)]
+    while len(tiles) < points // LANES:
+        tiles.append(twice * tiles[-1] - tiles[-2])
+    return jnp.concatenate(tiles, axis=1).astype(jnp.bfloat16)
+
+
+def fourier_kernel(parity_ref, wave_ref, grid_ref, *refs):
+    out_refs, table_ref = refs[:-1], refs[-1]
     points = grid_ref.shape[-1]
-
-    @pl.when(step == 0)
+    rows = sum(ref.shape[0] for ref in out_refs) * ROWS
+
+    @pl.when(pl.program_id(0) == 0)
     def _():
-        table_ref[...] = make_table(wave_ref[...], points, 1.0 / math.sqrt(points))
+        block = ROWS * 32
+
+        def fill(i, _):
+            at = pl.ds(pl.multiple_of(i * block, block), block)
+            table_ref[at, :] = make_table(wave_ref[at, :], points, 1.0 / math.sqrt(points))
+            return 0
+
+        lax.fori_loop(0, rows // block, fill, 0)
 
     half = LANES // 2
     whole = pl.ds(pl.multiple_of(half * parity_ref[0], half), LANES)
     rest = pl.ds(pl.multiple_of(LANES * (1 - parity_ref[0]), half), half)
-    rows = []
+    lines = []
     for j in range(2):
-        rows += [grid_ref[t, 0, j, whole, :] for t in range(2)]
-        rows += [grid_ref[t, 0, j, rest, :] for t in range(2)]
-    sums = dot(table_ref[...], jnp.concatenate(rows, axis=0), ((1,), (1,)))
+        lines += [grid_ref[t, 0, j, whole, :] for t in range(2)]
+        lines += [grid_ref[t, 0, j, rest, :] for t in range(2)]
+    lines = jnp.concatenate(lines, axis=0)
+    sums = dot(table_ref[...], lines, ((1,), (1,)))
     sums = sums.reshape(-1, ROWS, sums.shape[1])
-    tiles = [sums[:, :, t * LANES : (t + 1) * LANES] for t in range(6)]
-    at = pl.ds(pl.multiple_of(step * 6 * ROWS, 6 * ROWS), 6 * ROWS)
-    out_ref[:, at, :] = jnp.concatenate(tiles, axis=1).astype(jnp.bfloat16)
-
-
-def fourier_chunk(grid, wave, parity):
+    start = 0
+    for ref in out_refs:
+        part = sums[start : start + ref.shape[0]]
+        tiles = [part[:, :, t * LANES : (t + 1) * LANES] for t in range(6)]
+        ref[...] = jnp.concatenate(tiles, axis=1).astype(jnp.bfloat16)
+        start += ref.shape[0]
+
+
+def fourier_all(grid, wave, parity, slots):
     _, steps, _, lat_rows, points = grid.shape
     columns = wave.shape[0]
-    rows = steps * 6 * ROWS
-    slots = columns // ROWS
+    rows = 6 * ROWS
     return pl.pallas_call(
         fourier_kernel,
-        out_shape=jax.ShapeDtypeStruct((slots, rows, LANES), jnp.bfloat16),
+        out_shape=[jax.ShapeDtypeStruct((n, steps * rows, LANES), jnp.bfloat16) for n in slots],
         grid_spec=pltpu.PrefetchScalarGridSpec(
             num_scalar_prefetch=1,
             grid=(steps,),
@@ -171,56 +186,65 @@
                 pl.BlockSpec((columns, 1), lambda s, _: (0, 0)),
                 pl.BlockSpec((2, 1, 2, lat_rows, points), lambda s, _: (0, s, 0, 0, 0)),
             ],
-            out_specs=pl.BlockSpec((slots, rows, LANES), lambda s, _: (0, 0, 0)),
+            out_specs=[pl.BlockSpec((n, rows, LANES), lambda s, _: (0, s, 0)) for n in slots],
             scratch_shapes=[pltpu.VMEM((columns, points), jnp.bfloat16)],
         ),
         compiler_params=pltpu.CompilerParams(vmem_limit_bytes=VMEM),
-        cost_estimate=pl.CostEstimate(
-            flops=2 * columns * grid.size, bytes_accessed=2 * grid.size, transcendentals=0
-        ),
-        name="fourier_chunk",
+        cost_estimate=SHORT,
+        name="fourier_all",
     )(parity, wave, grid)
 
 
-def table_kernel(wave_ref, out_ref):
+def table_kernel(wave_ref, *refs):
+    out_ref = refs[-1]
     out_ref[...] = make_table(wave_ref[...], out_ref.shape[1], 1.0 / math.sqrt(N))
 
 
-def synthesis_rows(wave, points, block):
+def synthesis_rows(wave, points, block, *ready):
     columns = wave.shape[0]
     return pl.pallas_call(
         table_kernel,
         out_shape=jax.ShapeDtypeStruct((columns, points), jnp.bfloat16),
         grid=(columns // block,),
-        in_specs=[pl.BlockSpec((block, 1), lambda s: (s, 0))],
+        in_specs=[pl.BlockSpec((block, 1), lambda s: (s, 0))] + [ANYWHERE] * len(ready),
         out_specs=pl.BlockSpec((block, points), lambda s: (s, 0)),
         compiler_params=pltpu.CompilerParams(vmem_limit_bytes=VMEM),
+        cost_estimate=LONG,
         name="synthesis_rows",
-    )(wave)
-
-
-def spectral_kernel(
-    lower_ref, field_ref, table_ref, vertical_ref, first_ref, second_ref, out_ref, field_all, out_all
-):
+    )(wave, *ready)
+
+
+def spectral_kernel(pieces, lower_ref, *refs):
+    field_refs = refs[:pieces]
+    table_ref, vertical_ref, first_ref, second_ref = refs[pieces : pieces + 4]
+    out_ref, field_all, out_all = refs[-3:]
     pair = pl.program_id(0)
-    lats, levs, wire_rows, _ = field_ref.shape
+    lats, levs, wire_rows, _ = out_ref.shape
     stride = 3 * ROWS
     count = levs * wire_rows // stride
     block = levs * wire_rows
     half = LANES // 2
     packed = table_ref.shape[1]
-    matrices = vertical_ref.shape[0] // LANES
+    couples = vertical_ref.shape[0] // LANES
+    middle_row = N // 2
 
     @pl.when(pair == 0)
     def _():
-        field_all[...] = field_ref[...].reshape(field_all.shape).astype(jnp.float32)
+        plane, rows, _ = field_refs[0].shape
+        for i in range(plane):
+            for k, ref in enumerate(field_refs):
+                start = (i * pieces + k) * rows
+                field_all[start : start + rows, :] = ref[i].astype(jnp.float32)
 
     left = lax.broadcasted_iota(jnp.int32, (count, LANES), 1) < half
     lower = lower_ref[pair]
     row = lax.broadcasted_iota(jnp.int32, (packed, LANES), 0)
     own = row < N - lower
-    valid = row <= N
     operator = jnp.where(own, first_ref[pl.ds(lower, packed), :], second_ref[...])
+    couple = operator // 2
+    odd = operator % 2 == 1
+    own = own[middle_row:]
+    valid = row[middle_row:] <= N
 
     def at(lat, t, column):
         return pl.ds(lat * block + t * ROWS + column, count, stride=stride)
@@ -252,58 +276,65 @@
             out_all[at(lat + 1, 2, column), :] = jnp.where(left, swap(parts[1][0]), parts[1][1])
 
     for r in range(2):
-        state = []
+        columns = [4 * pair + 2 * e + r for e in range(2)]
+        tables = [table_ref.at[r, :N], table_ref.at[2 + r, middle_row:]]
+        state = [dot(tables[e][...], read_field(columns[e]), ((1,), (1,))) for e in range(2)]
+        upper = jnp.concatenate(
+            [state[0][middle_row:], jnp.zeros((packed - N, LANES), jnp.float32)], axis=0
+        )
+        upper = jnp.where(own, upper, jnp.where(valid, state[1], 0.0))
+        spectral = jnp.concatenate([state[0][:middle_row], upper], axis=0)
+        spectral = spectral.astype(jnp.bfloat16).astype(jnp.float32)
+        spread = [jnp.where(couple == g, spectral, 0.0).astype(jnp.bfloat16) for g in range(couples)]
+        solved = dot(jnp.concatenate(spread, axis=1), vertical_ref[...], ((1,), (0,)))
+        solved = jnp.where(odd, solved[:, LANES:], solved[:, :LANES])
+        upper = solved[middle_row:]
+        mine = [
+            jnp.concatenate(
+                [solved[:middle_row], jnp.where(own, upper, 0.0)[: N - middle_row]], axis=0
+            ),
+            jnp.where(own, 0.0, upper),
+        ]
         for e in range(2):
-            field = read_field(4 * pair + 2 * e + r)
-            state.append(dot(table_ref[2 * e + r], field, ((1,), (1,))))
-        spectral = jnp.where(own, state[0], jnp.where(valid, state[1], 0.0))
-        spectral = spectral.astype(jnp.bfloat16).astype(jnp.float32)
-        spread = [
-            jnp.where(operator == g, spectral, 0.0).astype(jnp.bfloat16) for g in range(matrices)
-        ]
-        solved = dot(jnp.concatenate(spread, axis=1), vertical_ref[...], ((1,), (0,)))
-        for e in range(2):
-            mine = jnp.where(own, solved, 0.0) if e == 0 else jnp.where(own, 0.0, solved)
-            value = dot(mine.astype(jnp.bfloat16), table_ref[2 * e + r], ((0,), (0,)))
-            write_field(4 * pair + 2 * e + r, value)
+            value = dot(mine[e].astype(jnp.bfloat16), tables[e][...], ((0,), (0,)))
+            write_field(columns[e], value)
 
     @pl.when(pair == pl.num_programs(0) - 1)
     def _():
         out_ref[...] = out_all[...].astype(jnp.bfloat16).reshape(out_ref.shape)
 
 
-def spectral_chunk(field, table, vertical, first, second, lower, chunk):
-    lats, levs, wire_rows, _ = field.shape
+def spectral_chunk(pieces, table, vertical, first, second, lower, chunk, shape, *ready):
+    lats, levs, wire_rows, _ = shape
     columns, packed, all_lats = table.shape
     pairs = ROWS // 4
     rows = lats * levs * wire_rows
+    plane = pieces[0].shape[0]
+    block = (plane, rows // plane // len(pieces), LANES)
     return pl.pallas_call(
-        spectral_kernel,
-        out_shape=jax.ShapeDtypeStruct(field.shape, jnp.bfloat16),
+        functools.partial(spectral_kernel, len(pieces)),
+        out_shape=jax.ShapeDtypeStruct(shape, jnp.bfloat16),
         grid_spec=pltpu.PrefetchScalarGridSpec(
             num_scalar_prefetch=1,
             grid=(pairs,),
-            in_specs=[
-                pl.BlockSpec(field.shape, lambda p, _: (0, 0, 0, 0)),
+            in_specs=[pl.BlockSpec(block, lambda p, _: (0, 0, 0))] * len(pieces)
+            + [
                 pl.BlockSpec((4, packed, all_lats), lambda p, _: (chunk * pairs + p, 0, 0)),
                 pl.BlockSpec(vertical.shape, lambda p, _: (0, 0)),
                 pl.BlockSpec(first.shape, lambda p, _: (0, 0)),
                 pl.BlockSpec(second.shape, lambda p, _: (0, 0)),
-            ],
-            out_specs=pl.BlockSpec(field.shape, lambda p, _: (0, 0, 0, 0)),
+            ]
+            + [ANYWHERE] * len(ready),
+            out_specs=pl.BlockSpec(shape, lambda p, _: (0, 0, 0, 0)),
             scratch_shapes=[
                 pltpu.VMEM((rows, LANES), jnp.float32),
                 pltpu.VMEM((rows, LANES), jnp.float32),
             ],
         ),
         compiler_params=pltpu.CompilerParams(vmem_limit_bytes=VMEM),
-        cost_estimate=pl.CostEstimate(
-            flops=4 * ROWS * packed * all_lats * LANES + pairs * 4 * packed * vertical.size,
-            bytes_accessed=2 * ROWS * packed * all_lats,
-            transcendentals=0,
-        ),
+        cost_estimate=LONG,
         name="spectral_chunk",
-    )(lower, field, table, vertical, first, second)
+    )(lower, *pieces, table, vertical, first, second, *ready)
 
 
 def synthesis_kernel(pieces, parity_ref, *refs):
@@ -352,7 +383,7 @@
     operands = [f for f, _ in fields] + [table, wind]
     aliases = {}
     if before is not None:
-        in_specs.append(pl.BlockSpec(memory_space=pl.ANY))
+        in_specs.append(ANYWHERE)
         aliases = {1 + len(operands): 0}
         operands.append(before)
     part = 4 * steps * lat_rows * points
@@ -367,19 +398,81 @@
         ),
         input_output_aliases=aliases,
         compiler_params=pltpu.CompilerParams(vmem_limit_bytes=VMEM),
-        cost_estimate=pl.CostEstimate(
-            flops=2 * columns * part, bytes_accessed=4 * part, transcendentals=0
-        ),
+        cost_estimate=LONG,
         name="synthesis_part",
     )(parity, *operands)
 
 
+def after_kernel(*refs):
+    del refs
+
+
+def after(x, *ready):
+    return pl.pallas_call(
+        after_kernel,
+        out_shape=jax.ShapeDtypeStruct(x.shape, x.dtype),
+        in_specs=[ANYWHERE] * (1 + len(ready)),
+        out_specs=ANYWHERE,
+        input_output_aliases={0: 0},
+        cost_estimate=LONG,
+        name="after",
+    )(x, *ready)
+
+
+def join_kernel(count, *refs):
+    out_ref = refs[-1]
+    rows = refs[0].shape[1]
+    for k in range(count):
+        out_ref[:, k * rows : (k + 1) * rows, :] = refs[k][...]
+
+
+def join_slots(pieces, *ready):
+    plane, rows, _ = pieces[0].shape
+    all_rows = len(pieces) * rows
+    return pl.pallas_call(
+        functools.partial(join_kernel, len(pieces)),
+        out_shape=jax.ShapeDtypeStruct((plane, all_rows, LANES), jnp.bfloat16),
+        grid=(2,),
+        in_specs=[pl.BlockSpec((plane // 2, rows, LANES), lambda s: (s, 0, 0))] * len(pieces)
+        + [ANYWHERE] * len(ready),
+        out_specs=pl.BlockSpec((plane // 2, all_rows, LANES), lambda s: (s, 0, 0)),
+        cost_estimate=LONG,
+        name="join_slots",
+    )(*pieces, *ready)
+
+
+def part_kernel(layers, parts, *refs):
+    in_ref, out_refs = refs[0], refs[len(refs) - parts * (layers - 1) :]
+    size = in_ref.shape[1] // layers // parts
+    for i, out_ref in enumerate(out_refs):
+        p, k = divmod(i, layers - 1)
+        start = ((k + 1) * parts + p) * size
+        out_ref[...] = in_ref[:, start : start + size, :]
+
+
+def part_slots(joined, layers, parts, *ready):
+    plane, rows, _ = joined.shape
+    size = rows // layers // parts
+    count = parts * (layers - 1)
+    slots = pl.pallas_call(
+        functools.partial(part_kernel, layers, parts),
+        out_shape=[jax.ShapeDtypeStruct((plane, size, LANES), jnp.bfloat16)] * count,
+        grid=(2,),
+        in_specs=[pl.BlockSpec((plane // 2, rows, LANES), lambda s: (s, 0, 0))]
+        + [ANYWHERE] * len(ready),
+        out_specs=[pl.BlockSpec((plane // 2, size, LANES), lambda s: (s, 0, 0))] * count,
+        cost_estimate=LONG,
+        name="part_slots",
+    )(joined, *ready)
+    return [slots[p * (layers - 1) : (p + 1) * (layers - 1)] for p in range(parts)]
+
+
 def swap_along_z(slots):
     lev_devices = lax.axis_size("lev")
-    moved = [slots[0]]
-    for kz in range(1, len(slots)):
+    moved = []
+    for kz, slot in enumerate(slots, 1):
         pairs = [(b, b ^ (CORES * kz)) for b in range(lev_devices)]
-        moved.append(lax.ppermute(slots[kz], "lev", pairs))
+        moved.append(lax.ppermute(slot, "lev", pairs))
     return moved
 
 
@@ -424,7 +517,8 @@
     table_pairs = xor_order(pair_table.reshape(lats, layers, CORES, chunks, pairs), 1, layer)
     table_pairs = table_pairs.transpose(3, 1, 0, 2, 4)
     waves = jnp.stack([table_pairs, N - 1 - table_pairs], axis=-1)
-    waves = jnp.broadcast_to(waves[..., None], waves.shape + (2,)).reshape(chunks, -1, 1)
+    waves = jnp.broadcast_to(waves[..., None], waves.shape + (2,))
+    waves = waves.reshape(chunks, layers, plane, ROWS)
 
     grid = adjoint_grid.reshape(2, steps, 2, lat_rows, points)
     wind = wind.reshape(2, steps, 2, lat_rows, points)
@@ -437,7 +531,8 @@
     operators = jnp.einsum(
         "gao,bo->gab", operators.astype(jnp.bfloat16), order, preferred_element_type=jnp.float32
     )
-    operators = operators.astype(jnp.bfloat16).reshape(matrices * levels, levels)
+    operators = operators.astype(jnp.bfloat16).reshape(matrices // 2, 2, levels, levels)
+    operators = operators.transpose(0, 2, 1, 3).reshape(matrices // 2 * levels, 2 * levels)
 
     by_degree = jnp.concatenate([degree_matrix, jnp.broadcast_to(degree_matrix[-1:], (packed,))])
     second = jnp.concatenate([degree_matrix[:1], by_degree[: packed - 1]])
@@ -446,38 +541,68 @@
     first_pair = (lat * levs + lev) * (slots // 4)
     lower = lax.dynamic_slice(pair_table, (first_pair,), (slots // 4,)).reshape(chunks, pairs)
 
-    returned = []
-    for q in range(chunks):
-        sent = fourier_chunk(grid, waves[q], parity)
-        sent = sent.reshape(layers, plane, wire_rows, LANES)
-        moved = swap_along_z([sent[k] for k in range(layers)])
-        moved = jnp.stack(moved, axis=1).reshape(plane, layers * wire_rows, LANES)
-        field = exchange_in_plane(moved, groups).reshape(lats, levs, wire_rows, LANES)
-        field = spectral_chunk(field, table, operators, first, second, lower[q], q)
-        moved = exchange_in_plane(field.reshape(plane, layers * wire_rows, LANES), groups)
-        returned.append(moved.reshape(plane, layers, wire_rows, LANES))
-
-    synthesis = synthesis_rows(waves.reshape(-1, 1), points, ROWS * layers * plane)
-    early = chunks // 2
-    fields = []
-    for q in range(early):
-        fields += swap_along_z([returned[q][:, k] for k in range(layers)])
+    joined_shape = (plane, layers * wire_rows, LANES)
+
+    def across(x):
+        return exchange_in_plane(x, groups)
+
+    def along(first_slot, slots):
+        return [first_slot] + swap_along_z(slots)
+
+    def solve(q, pieces, *ready):
+        shape = (lats, levs, wire_rows, LANES)
+        x = spectral_chunk(pieces, table, operators, first, second, lower[q], q, shape, *ready)
+        return x.reshape(joined_shape)
+
+    rows = [waves[0], waves[1], waves[2].transpose(1, 0, 2), waves[3].transpose(1, 0, 2)]
+    rows = jnp.stack([w.reshape(-1) for w in rows]).reshape(-1, 1)
+    sent = fourier_all(grid, rows, parity, [plane] * (2 * layers) + [plane * layers] * 2)
+    x2, x3 = [x.reshape(joined_shape) for x in sent[2 * layers :]]
+    z0 = along(sent[0], sent[1:layers])
+    z1 = along(sent[layers], sent[layers + 1 : 2 * layers])
+    p2 = across(x2)
+    x3 = after(x3, p2)
+    p3 = across(x3)
+    j0 = join_slots(z0, x3)
+    u2 = part_slots(p2, layers, 1, x3)[0]
+    z2 = along(p2, u2)
+    j1 = join_slots(z1, u2[0])
+    j0 = after(j0, p3, j1)
+    p0 = across(j0)
+    u3 = part_slots(p3, layers, 1, j0)[0]
+    z3 = along(p3, u3)
+    s0 = solve(0, [p0], u3[0])
+    r0 = across(s0)
+    s2 = solve(2, z2, s0)
+    j1 = after(j1, r0, s2)
+    p1 = across(j1)
+    b0 = part_slots(r0, layers, 1, j1)[0]
+    back0 = along(r0, b0)
+    s3 = solve(3, z3, b0[0])
+    s2 = after(s2, p1, s3)
+    r2 = across(s2)
+    s1 = solve(1, [p1], s2)
+    s1 = after(s1, r2)
+    r1 = across(s1)
+    b2 = part_slots(r2, layers, 1, s1)[0]
+    back2 = along(r2, b2)
+    synthesis = synthesis_rows(waves.reshape(-1, 1), points, ROWS * layers * plane, b2[0])
+    s3 = after(s3, r1, synthesis)
+    r3 = across(s3)
+    b1 = part_slots(r1, layers, 1, s3)[0]
+    back1 = along(r1, b1)
+    late = [along(r3, part) for part in part_slots(r3, layers, steps, b1[0])]
+    fields = back0 + back1 + back2
+
     out = None
-    rows = 6 * ROWS
-    parts = steps // 2 if steps % 2 == 0 else 1
-    parts = steps if parts == 0 else steps // parts
-    for first_step in range(0, steps, parts):
-        cut = slice(first_step * rows, (first_step + parts) * rows)
-        sent = [jnp.stack([x[:, k, cut] for x in returned[early:]]) for k in range(layers)]
-        moved = swap_along_z(sent)
-        late = [moved[k][i] for i in range(chunks - early) for k in range(layers)]
+    for step in range(steps):
         out = synthesis_part(
-            [(f, 0) for f in fields] + [(f, first_step) for f in late],
+            [(f, 0) for f in fields] + [(late[step][0], 0)] + [(f, step) for f in late[step][1:]],
             synthesis,
             wind,
             parity,
-            first_step,
-            parts,
+            step,
+            1,
             out,
         )
     return out.reshape(level_rows, lat_rows, points)
@@ -493,10 +618,12 @@
         and lats % 2 == 0
         and lat_rows == LANES + LANES // 2
         and level_rows % 16 == 0
+        and vertical.shape[0] % 2 == 0
         and vertical.shape[1] == LANES
         and points % LANES == 0
         and points // LANES <= LANES
-        and legendre.shape[0] % (2 * ROWS) == 0
+        and legendre.shape[0] % ROWS == 0
+        and legendre.shape[0] // ROWS == 4
         and legendre.shape[2] % 8 == 0
         and legendre.shape[2] > N
         and pair_table.shape[0] * 4 == legendre.shape[0] * lats * levs

time: 486 us -> 365 us (0.75); the launches traced: 478 us -> 364 us
  waiting for transfers between devices: 216 us -> 64.9 us
  starting transfers between devices: 115 us -> 170 us
  Pallas kernels: 118 us -> 105 us
    ppermute x24 -> x33, waiting for transfers between devices: 190 us -> 14 us  [swap_along_z(): moved.append(lax.ppermute(slot, 'lev', pairs))]
    ppermute x24 -> x33, starting transfers between devices: 82.2 us -> 134 us  [swap_along_z(): moved.append(lax.ppermute(slot, 'lev', pairs))]
    all_to_all x8, waiting for transfers between devices: 26.2 us -> 51 us  [exchange_in_plane(): lax.all_to_all(x, ('lat', 'lev'), split_axis=0, concat_axis=0, tiled=True...]
    pallas_call x8 -> x19, Pallas kernels: 90.5 us -> 73 us  [the longest x4 39 us: spectral_chunk(): pl.pallas_call(functools.partial(spectral_kernel, len(pieces)), out_shape...]
    pallas_call x2 -> x4, Pallas kernels: 19.3 us -> 29.5 us  [synthesis_part(): pl.pallas_call(functools.partial(synthesis_kernel, len(fields)), out_shap...]
    unnamed x28 -> x43, local copies, waits for them, and re-layouts: 4.81 us -> 13.4 us
    another operation x10 -> x2, local copies, waits for them, and re-layouts: 8.22 us -> 0.2 us  [pipelined_body(): rows = jnp.stack([w.reshape(-1) for w in rows]).reshape(-1, 1)]
    pallas_call x1, Pallas kernels: 7.69 us -> 2.06 us  [synthesis_rows(): pl.pallas_call(table_kernel, out_shape=jax.ShapeDtypeStruct((columns, poi...]
  transfers between devices with their start and end apart: 32 -> 41, of which waited for: 18 -> 10; matrix products, arithmetic and copies ran while one was open for 4% -> 2% of each run, Pallas kernels for 19% -> 22%
where the time goes in v2:
time: 365 us; the launch traced here: 364 us
  starting transfers between devices  170 us (47%)
  Pallas kernels  105 us (29%)
  waiting for transfers between devices  64.9 us (18%)
  local copies, waits for them, and re-layouts  21.1 us (6%)
    ppermute x33, starting transfers between devices, swap_along_z(): moved.append(lax.ppermute(slot, 'lev', pairs))  134 us
    all_to_all x8, waiting for transfers between devices, exchange_in_plane(): lax.all_to_all(x, ('lat', 'lev'), split_axis=0, concat_axis=0, tiled=True...  51 us
    pallas_call x4, Pallas kernels, spectral_chunk(): pl.pallas_call(functools.partial(spectral_kernel, len(pieces)), out_shape...  39 us
    all_to_all x8, starting transfers between devices, exchange_in_plane(): lax.all_to_all(x, ('lat', 'lev'), split_axis=0, concat_axis=0, tiled=True...  36.1 us
    pallas_call x4, Pallas kernels, synthesis_part(): pl.pallas_call(functools.partial(synthesis_kernel, len(fields)), out_shap...  29.5 us
    pallas_call x1, Pallas kernels, fourier_all(): pl.pallas_call(fourier_kernel, out_shape=[jax.ShapeDtypeStruct((n, steps...  15.6 us
    ppermute x33, waiting for transfers between devices, swap_along_z(): moved.append(lax.ppermute(slot, 'lev', pairs))  14 us
    pallas_call x6, Pallas kernels, part_slots(): pl.pallas_call(functools.partial(part_kernel, layers, parts), out_shape=[...  13.6 us
  transfers between devices with their start and end apart: 41, of which 10 were waited for; matrix products, arithmetic and copies ran while one was open for 2% of the time, Pallas kernels for 22%

profile of v2, /device:TPU:0, one launch (start us, length us, event | category | flops | bytes accessed | tf_op | source)
XLA Modules:
  0.0 363.5 jit_solution(8602977071054498500)
XLA Ops:
  3.3 15.6 %fourier_all.1 = (bf16[8,192,128]{2,1,0:T(8,128)(2,1)S(1)}, bf16[8,192,128]{2,1,0:T(8,128)(2,1)}, bf16[8,192,128]{2,1,0:T(8,128)(2,1)}, bf16[8,192,128]{2,1,0:T(...) custom-call(s32[1]{0:T(128)} %bitcast.parity_ref, ...), custom_call_target="tpu_custom_call" | custom-call | flops 1 | bytes 1 | tf_op jit(solution)/shard_map/fourier_all/pallas_call | solution.py:179
  18.9 1.2 copy-done.4
  21.6 5.3 %all-to-all-start = ((bf16[8,768,128]{2,1,0:T(8,128)(2,1)}), bf16[8,768,128]{2,1,0:T(8,128)(2,1)S(1)}, u32[]{:S(2)}, u32[]{:S(2)}) async-start(bf16[8,768,128]{2,1,0:T(8,128)(2,1)} %bitcast.66), calls=%async_computation | async-start | bytes 3145728 | tf_op jit(solution)/shard_map/all_to_all | solution.py:480
  26.9 1.6 collective-permute-start
  28.4 2.6 collective-permute-start.1
  31.9 3.5 collective-permute-start.4
  36.1 1.2 concatenate.6
  40.5 1.3 pad_add_fusion.1
  41.9 6.0 %all-to-all-done.refs_1_.refs_0_ = bf16[8,768,128]{2,1,0:T(8,128)(2,1)S(1)} async-done(((bf16[8,768,128]{2,1,0:T(8,128)(2,1)}), bf16[8,768,128]{2,1,0:T(8,128)(2,1)S(1)}, u32[]{:S(2)}, u32[]{:S(2)}) %all-to-all-start) | async-done | bytes 1572896 | tf_op jit(solution)/shard_map/all_to_all | solution.py:480
  47.9 1.2 copy-done.2
  49.0 4.3 %all-to-all-start.1 = ((bf16[8,768,128]{2,1,0:T(8,128)(2,1)}), bf16[8,768,128]{2,1,0:T(8,128)(2,1)}, u32[]{:S(2)}, u32[]{:S(2)}) async-start(bf16[8,768,128]{2,1,0:T(8,128)(2,1)} %after.6.refs_4_.refs_1_), calls=%async_computation.1 | async-start | bytes 3145728 | tf_op jit(solution)/shard_map/all_to_all | solution.py:480
  53.4 2.3 part_slots.6
  55.6 3.6 collective-permute-start.5
  59.3 1.9 collective-permute-start.8
  61.2 2.5 join_slots.2.refs_0_
  64.0 41.3 %collective-permute-start.6 = (bf16[8,192,128]{2,1,0:T(8,128)(2,1)}, bf16[8,192,128]{2,1,0:T(8,128)(2,1)}, u32[]{:S(2)}, u32[]{:S(2)}) collective-permute-start(bf16[8,192,128]{2,1,0:T(8,128)(2,1)} %get-tuple-element.52.refs_4_), channel_id=1, source_target_pairs={{0,2},{1,3},{2,0},{3,1},{4,6},{5,7},{6,4},{7,5},{8,10},{9,11},{10,... | collective-permute-start | bytes 1179656 | tf_op jit(solution)/shard_map/ppermute | solution.py:475
  105.3 3.9 %collective-permute-done.4.refs_2_ = bf16[8,192,128]{2,1,0:T(8,128)(2,1)} collective-permute-done((bf16[8,192,128]{2,1,0:T(8,128)(2,1)}, bf16[8,192,128]{2,1,0:T(8,128)(2,1)}, u32[]{:S(2)}, u32[]{:S(2)}) %collective-permute-start.4) | collective-permute-done | bytes 393248 | tf_op jit(solution)/shard_map/ppermute | solution.py:475
  109.1 2.5 join_slots.3.refs_2_.refs_0_
  111.6 4.3 %all-to-all-start.2 = ((bf16[8,768,128]{2,1,0:T(8,128)(2,1)}), bf16[8,768,128]{2,1,0:T(8,128)(2,1)}, u32[]{:S(2)}, u32[]{:S(2)}) async-start(bf16[8,768,128]{2,1,0:T(8,128)(2,1)} %after.7.refs_1_), calls=%async_computation.2 | async-start | bytes 3145728 | tf_op jit(solution)/shard_map/all_to_all | solution.py:480
  115.9 2.3 part_slots.7
  118.2 10.0 %collective-permute-start.13 = (bf16[8,192,128]{2,1,0:T(8,128)(2,1)}, bf16[8,192,128]{2,1,0:T(8,128)(2,1)}, u32[]{:S(2)}, u32[]{:S(2)}) collective-permute-start(bf16[8,192,128]{2,1,0:T(8,128)(2,1)} %get-tuple-element.59), channel_id=1, source_target_pairs={{0,4},{1,5},{2,6},{3,7},{4,0},{5,1},{6,2},{7,3},{8,12},{9,13},{10,... | collective-permute-start | bytes 1179656 | tf_op jit(solution)/shard_map/ppermute | solution.py:475
  128.2 8.7 %all-to-all-done.2.refs_0_ = bf16[8,768,128]{2,1,0:T(8,128)(2,1)} async-done(((bf16[8,768,128]{2,1,0:T(8,128)(2,1)}), bf16[8,768,128]{2,1,0:T(8,128)(2,1)}, u32[]{:S(2)}, u32[]{:S(2)}) %all-to-all-start.2) | async-done | bytes 1572896 | tf_op jit(solution)/shard_map/all_to_all | solution.py:480
  138.3 9.8 %spectral_chunk.4 = bf16[4,8,192,128]{3,2,1,0:T(8,128)(2,1)S(1)} custom-call(s32[2]{0:T(128)S(1)} %get-tuple-element.88.lower_ref, bf16[8,768,128]{2,1,0:T(8,128)(2,1)} %all-to-all-done.2.refs_0_, bf16[32,520,768]{2,1,0:T(8,128)(2,1)} %bitcast.89, bf16[1024,256]{1,0:T(8,128)(2,1)S(1)} %bitcast.74, s32[1032,128]{1,0:T(8,128)S(1)} %broadcast_in_dim.49.refs_3_.refs_6_, ...), custom_call_target="tpu_custom_call" | custom-call | flops 9999999827968 | bytes 100000000 | tf_op jit(solution)/shard_map/spectral_chunk/pallas_call | solution.py:314
  148.1 1.1 copy-done.8
  149.2 4.6 %all-to-all-start.3 = ((bf16[8,768,128]{2,1,0:T(8,128)(2,1)}), bf16[8,768,128]{2,1,0:T(8,128)(2,1)}, u32[]{:S(2)}, u32[]{:S(2)}) async-start(bf16[8,768,128]{2,1,0:T(8,128)(2,1)} %bitcast.71), calls=%async_computation.3 | async-start | bytes 3145728 | tf_op jit(solution)/shard_map/all_to_all | solution.py:480
  153.9 2.5 collective-permute-start.14
  156.4 9.6 %spectral_chunk.5 = bf16[4,8,192,128]{3,2,1,0:T(8,128)(2,1)S(1)} custom-call(s32[2]{0:T(128)S(1)} %get-tuple-element.87.lower_ref, bf16[8,768,128]{2,1,0:T(8,128)(2,1)S(1)} %copy-done.3, bf16[8,192,128]{2,1,0:T(8,128)(2,1)} %collective-permute-done.6.refs_1_, bf16[8,192,128]{2,1,0:T(8,128)(2,1)} %collective-permute-done.7.refs_2_, ...), custom_call_target="tpu_custom_call" | custom-call | flops 9999999827968 | bytes 100000000 | tf_op jit(solution)/shard_map/spectral_chunk/pallas_call | solution.py:314
  166.1 1.2 copy-done.5
  167.2 7.5 %all-to-all-done.3.refs_1_.refs_0_ = bf16[8,768,128]{2,1,0:T(8,128)(2,1)} async-done(((bf16[8,768,128]{2,1,0:T(8,128)(2,1)}), bf16[8,768,128]{2,1,0:T(8,128)(2,1)}, u32[]{:S(2)}, u32[]{:S(2)}) %all-to-all-start.3) | async-done | bytes 1572896 | tf_op jit(solution)/shard_map/all_to_all | solution.py:480
  174.7 4.3 %all-to-all-start.4 = ((bf16[8,768,128]{2,1,0:T(8,128)(2,1)}), bf16[8,768,128]{2,1,0:T(8,128)(2,1)}, u32[]{:S(2)}, u32[]{:S(2)}) async-start(bf16[8,768,128]{2,1,0:T(8,128)(2,1)} %after.8.refs_1_), calls=%async_computation.4 | async-start | bytes 3145728 | tf_op jit(solution)/shard_map/all_to_all | solution.py:480
  179.0 2.3 part_slots.8
  181.3 10.0 %collective-permute-start.10 = (bf16[8,192,128]{2,1,0:T(8,128)(2,1)}, bf16[8,192,128]{2,1,0:T(8,128)(2,1)}, u32[]{:S(2)}, u32[]{:S(2)}) collective-permute-start(bf16[8,192,128]{2,1,0:T(8,128)(2,1)} %get-tuple-element.57), channel_id=1, source_target_pairs={{0,4},{1,5},{2,6},{3,7},{4,0},{5,1},{6,2},{7,3},{8,12},{9,13},{10,... | collective-permute-start | bytes 1179656 | tf_op jit(solution)/shard_map/ppermute | solution.py:475
  191.3 1.3 collective-permute-start.11
  193.7 9.8 %spectral_chunk.6 = bf16[4,8,192,128]{3,2,1,0:T(8,128)(2,1)S(1)} custom-call(s32[2]{0:T(128)S(1)} %get-tuple-element.85.lower_ref, bf16[8,768,128]{2,1,0:T(8,128)(2,1)} %all-to-all-done.1.refs_1_.refs_0_, bf16[8,192,128]{2,1,0:T(8,128)(2,1)} %collective-permute-done.12.refs_1_, bf16[8,192,128]{2,1,0:T(8,128)(2,1)} %collective-permute-done.13.refs_2_, ...), custom_call_target="tpu_custom_call" | custom-call | flops 9999999827968 | bytes 100000000 | tf_op jit(solution)/shard_map/spectral_chunk/pallas_call | solution.py:314
  203.5 1.1 copy-done.7
  204.6 4.4 %all-to-all-start.5 = ((bf16[8,768,128]{2,1,0:T(8,128)(2,1)}), bf16[8,768,128]{2,1,0:T(8,128)(2,1)}, u32[]{:S(2)}, u32[]{:S(2)}) async-start(bf16[8,768,128]{2,1,0:T(8,128)(2,1)} %after.9.refs_5_), calls=%async_computation.5 | async-start | bytes 3145728 | tf_op jit(solution)/shard_map/all_to_all | solution.py:480
  209.1 9.8 %spectral_chunk.7 = bf16[4,8,192,128]{3,2,1,0:T(8,128)(2,1)S(1)} custom-call(s32[2]{0:T(128)S(1)} %get-tuple-element.86.lower_ref, bf16[8,768,128]{2,1,0:T(8,128)(2,1)} %all-to-all-done.4.refs_1_.refs_0_, bf16[32,520,768]{2,1,0:T(8,128)(2,1)} %bitcast.92, bf16[1024,256]{1,0:T(8,128)(2,1)S(1)} %bitcast.77, s32[1032,128]{1,0:T(8,128)S(1)} %broadcast_in_dim.49.refs_3_.refs_6_, ...), custom_call_target="tpu_custom_call" | custom-call | flops 9999999827968 | bytes 100000000 | tf_op jit(solution)/shard_map/spectral_chunk/pallas_call | solution.py:314
  218.9 1.2 copy-done.9
  220.0 10.1 %all-to-all-done.5.refs_1_.refs_0_.refs_8_ = bf16[8,768,128]{2,1,0:T(8,128)(2,1)} async-done(((bf16[8,768,128]{2,1,0:T(8,128)(2,1)}), bf16[8,768,128]{2,1,0:T(8,128)(2,1)}, u32[]{:S(2)}, u32[]{:S(2)}) %all-to-all-start.5) | async-done | bytes 1572896 | tf_op jit(solution)/shard_map/all_to_all | solution.py:480
  230.1 4.3 %all-to-all-start.6 = ((bf16[8,768,128]{2,1,0:T(8,128)(2,1)}), bf16[8,768,128]{2,1,0:T(8,128)(2,1)}, u32[]{:S(2)}, u32[]{:S(2)}) async-start(bf16[8,768,128]{2,1,0:T(8,128)(2,1)} %after.10.refs_1_), calls=%async_computation.6 | async-start | bytes 3145728 | tf_op jit(solution)/shard_map/all_to_all | solution.py:480
  234.4 2.3 part_slots.9
  236.7 5.5 %collective-permute-start.19 = (bf16[8,192,128]{2,1,0:T(8,128)(2,1)}, bf16[8,192,128]{2,1,0:T(8,128)(2,1)}, u32[]{:S(2)}, u32[]{:S(2)}) collective-permute-start(bf16[8,192,128]{2,1,0:T(8,128)(2,1)} %get-tuple-element.65), channel_id=1, source_target_pairs={{0,4},{1,5},{2,6},{3,7},{4,0},{5,1},{6,2},{7,3},{8,12},{9,13},{10,... | collective-permute-start | bytes 1179656 | tf_op jit(solution)/shard_map/ppermute | solution.py:475
  243.2 2.1 synthesis_rows.1.refs_2_.refs_16_
  245.2 1.6 copy-done.15
  246.9 8.6 %all-to-all-done.6.refs_1_.refs_0_.refs_4_ = bf16[8,768,128]{2,1,0:T(8,128)(2,1)} async-done(((bf16[8,768,128]{2,1,0:T(8,128)(2,1)}), bf16[8,768,128]{2,1,0:T(8,128)(2,1)}, u32[]{:S(2)}, u32[]{:S(2)}) %all-to-all-start.6) | async-done | bytes 1572896 | tf_op jit(solution)/shard_map/all_to_all | solution.py:480
  255.4 4.5 %all-to-all-start.7 = ((bf16[8,768,128]{2,1,0:T(8,128)(2,1)}), bf16[8,768,128]{2,1,0:T(8,128)(2,1)}, u32[]{:S(2)}, u32[]{:S(2)}) async-start(bf16[8,768,128]{2,1,0:T(8,128)(2,1)} %after.11.refs_1_), calls=%async_computation.7 | async-start | bytes 3145728 | tf_op jit(solution)/shard_map/all_to_all | solution.py:480
  260.0 2.3 part_slots.10
  262.3 2.5 collective-permute-start.20
  264.7 3.4 collective-permute-start.16
  268.1 2.5 collective-permute-start.17
  270.6 10.1 %all-to-all-done.7.refs_0_.refs_12_ = bf16[8,768,128]{2,1,0:T(8,128)(2,1)} async-done(((bf16[8,768,128]{2,1,0:T(8,128)(2,1)}), bf16[8,768,128]{2,1,0:T(8,128)(2,1)}, u32[]{:S(2)}, u32[]{:S(2)}) %all-to-all-start.7) | async-done | bytes 1572896 | tf_op jit(solution)/shard_map/all_to_all | solution.py:480
  280.8 2.2 part_slots.11
  283.0 18.4 %collective-permute-start.30 = (bf16[8,48,128]{2,1,0:T(8,128)(2,1)}, bf16[8,48,128]{2,1,0:T(8,128)(2,1)S(1)}, u32[]{:S(2)}, u32[]{:S(2)}) collective-permute-start(bf16[8,48,128]{2,1,0:T(8,128)(2,1)} %get-tuple-element.76), channel_id=1, source_target_pairs={{0,2},{1,3},{2,0},{3,1},{4,6},{5,7},{6,4},{7,5},{8,10},{9,11},{10,... | collective-permute-start | bytes 294920 | tf_op jit(solution)/shard_map/ppermute | solution.py:475
  302.5 9.0 %collective-permute-done.16.refs_6_ = bf16[8,192,128]{2,1,0:T(8,128)(2,1)} collective-permute-done((bf16[8,192,128]{2,1,0:T(8,128)(2,1)}, bf16[8,192,128]{2,1,0:T(8,128)(2,1)}, u32[]{:S(2)}, u32[]{:S(2)}) %collective-permute-start.16) | collective-permute-done | bytes 393248 | tf_op jit(solution)/shard_map/ppermute | solution.py:475
  311.5 2.5 collective-permute-start.32
  314.0 8.6 %collective-permute-start.21 = (bf16[8,48,128]{2,1,0:T(8,128)(2,1)}, bf16[8,48,128]{2,1,0:T(8,128)(2,1)}, u32[]{:S(2)}, u32[]{:S(2)}) collective-permute-start(bf16[8,48,128]{2,1,0:T(8,128)(2,1)} %get-tuple-element.67), channel_id=1, source_target_pairs={{0,2},{1,3},{2,0},{3,1},{4,6},{5,7},{6,4},{7,5},{8,10},{9,11},{10,... | collective-permute-start | bytes 294920 | tf_op jit(solution)/shard_map/ppermute | solution.py:475
  323.6 2.0 collective-permute-start.27
  325.7 2.4 collective-permute-start.29
  328.1 7.3 %synthesis_part.4.refs_18_ = bf16[2,4,2,192,1536]{4,3,2,1,0:T(8,128)(2,1)} custom-call(s32[1]{0:T(128)} %bitcast.parity_ref, bf16[8,768,128]{2,1,0:T(8,128)(2,1)} %all-to-all-done.3.refs_1_.refs_0_, bf16[8,192,128]{2,1,0:T(8,128)(2,1)} %collective-permute-done.9.refs_1_, bf16[8,192,128]{2,1,0:T(8,128)(2,1)} %collective-permute-done.10.refs_2_, ...), custom_call_target="tpu_custom_call" | custom-call | flops 9999999827968 | bytes 100000000 | tf_op jit(solution)/shard_map/synthesis_part/pallas_call | solution.py:390
  337.4 2.4 collective-permute-start.26
  339.7 7.4 %synthesis_part.5.refs_18_ = bf16[2,4,2,192,1536]{4,3,2,1,0:T(8,128)(2,1)} custom-call(s32[1]{0:T(128)} %bitcast.parity_ref, bf16[8,768,128]{2,1,0:T(8,128)(2,1)} %all-to-all-done.3.refs_1_.refs_0_, bf16[8,192,128]{2,1,0:T(8,128)(2,1)} %collective-permute-done.9.refs_1_, ...), custom_call_target="tpu_custom_call", output_to_operand_aliasing={{}: (19, {})} | custom-call | flops 9999999827968 | bytes 100000000 | tf_op jit(solution)/shard_map/synthesis_part/pallas_call | solution.py:390
  347.1 1.5 collective-permute-start.23
  348.7 7.4 %synthesis_part.6.refs_18_ = bf16[2,4,2,192,1536]{4,3,2,1,0:T(8,128)(2,1)} custom-call(s32[1]{0:T(128)} %bitcast.parity_ref, bf16[8,768,128]{2,1,0:T(8,128)(2,1)} %all-to-all-done.3.refs_1_.refs_0_, bf16[8,192,128]{2,1,0:T(8,128)(2,1)} %collective-permute-done.9.refs_1_, ...), custom_call_target="tpu_custom_call", output_to_operand_aliasing={{}: (19, {})} | custom-call | flops 9999999827968 | bytes 100000000 | tf_op jit(solution)/shard_map/synthesis_part/pallas_call | solution.py:390
  356.1 7.4 %synthesis_part.7 = bf16[2,4,2,192,1536]{4,3,2,1,0:T(8,128)(2,1)} custom-call(s32[1]{0:T(128)} %bitcast.parity_ref, bf16[8,768,128]{2,1,0:T(8,128)(2,1)} %all-to-all-done.3.refs_1_.refs_0_, bf16[8,192,128]{2,1,0:T(8,128)(2,1)} %collective-permute-done.9.refs_1_, ...), custom_call_target="tpu_custom_call", output_to_operand_aliasing={{}: (19, {})} | custom-call | flops 9999999827968 | bytes 100000000 | tf_op jit(solution)/shard_map/synthesis_part/pallas_call | solution.py:390
  (125 shorter events, 17.5 us)
Async XLA Ops:
  0.0 38.7 %copy-start = (bf16[16,128,128]{2,1,0:T(8,128)(2,1)S(1)}, bf16[16,128,128]{2,1,0:T(8,128)(2,1)}, u32[]{:S(2)}) copy-start(bf16[16,128,128]{2,1,0:T(8,128)(2,1)} %param.9) | copy-start | bytes 1572868
  18.9 1.2 copy-start.4
  20.0 0.7 copy-start.10
  20.8 0.8 copy-start.11
  21.6 13.9 %copy-start.18 = (s32[512]{0:T(512)S(1)}, s32[512]{0:T(512)}, u32[]{:S(2)}) copy-start(s32[512]{0:T(512)} %param.11) | copy-start | bytes 6148
  21.6 14.5 %copy-start.19 = (s32[256]{0:T(256)S(1)}, s32[256]{0:T(256)}, u32[]{:S(2)}) copy-start(s32[256]{0:T(256)} %param.10) | copy-start | bytes 3076
  21.6 26.3 %all-to-all-start = ((bf16[8,768,128]{2,1,0:T(8,128)(2,1)}), bf16[8,768,128]{2,1,0:T(8,128)(2,1)S(1)}, u32[]{:S(2)}, u32[]{:S(2)}) async-start(bf16[8,768,128]{2,1,0:T(8,128)(2,1)} %bitcast.66), calls=%async_computation | async-start | bytes 3145728 | tf_op jit(solution)/shard_map/all_to_all | solution.py:480
  26.9 28.8 %collective-permute-start = (bf16[8,192,128]{2,1,0:T(8,128)(2,1)}, bf16[8,192,128]{2,1,0:T(8,128)(2,1)}, u32[]{:S(2)}, u32[]{:S(2)}) collective-permute-start(bf16[8,192,128]{2,1,0:T(8,128)(2,1)} %get-tuple-element.43), channel_id=1, source_target_pairs={{0,2},{1,3},{2,0},{3,1},{4,6},{5,7},{6,4},{7,5},{8,10},{9,11},{10,... | collective-permute-start | bytes 1179656 | tf_op jit(solution)/shard_map/ppermute | solution.py:475
  28.4 30.8 %collective-permute-start.1 = (bf16[8,192,128]{2,1,0:T(8,128)(2,1)}, bf16[8,192,128]{2,1,0:T(8,128)(2,1)}, u32[]{:S(2)}, u32[]{:S(2)}) collective-permute-start(bf16[8,192,128]{2,1,0:T(8,128)(2,1)} %get-tuple-element.44), channel_id=1, source_target_pairs={{0,4},{1,5},{2,6},{3,7},{4,0},{5,1},{6,2},{7,3},{8,12},{9,13},{10,... | collective-permute-start | bytes 1179656 | tf_op jit(solution)/shard_map/ppermute | solution.py:475
  31.0 28.2 %collective-permute-start.2 = (bf16[8,192,128]{2,1,0:T(8,128)(2,1)}, bf16[8,192,128]{2,1,0:T(8,128)(2,1)}, u32[]{:S(2)}, u32[]{:S(2)}) collective-permute-start(bf16[8,192,128]{2,1,0:T(8,128)(2,1)} %get-tuple-element.45), channel_id=1, source_target_pairs={{0,6},{1,7},{2,4},{3,5},{4,2},{5,3},{6,0},{7,1},{8,14},{9,15},{10,... | collective-permute-start | bytes 1179656 | tf_op jit(solution)/shard_map/ppermute | solution.py:475
  31.2 32.7 %collective-permute-start.3 = (bf16[8,192,128]{2,1,0:T(8,128)(2,1)}, bf16[8,192,128]{2,1,0:T(8,128)(2,1)}, u32[]{:S(2)}, u32[]{:S(2)}) collective-permute-start(bf16[8,192,128]{2,1,0:T(8,128)(2,1)} %get-tuple-element.49), channel_id=1, source_target_pairs={{0,2},{1,3},{2,0},{3,1},{4,6},{5,7},{6,4},{7,5},{8,10},{9,11},{10,... | collective-permute-start | bytes 1179656 | tf_op jit(solution)/shard_map/ppermute | solution.py:475
  31.9 77.2 %collective-permute-start.4 = (bf16[8,192,128]{2,1,0:T(8,128)(2,1)}, bf16[8,192,128]{2,1,0:T(8,128)(2,1)}, u32[]{:S(2)}, u32[]{:S(2)}) collective-permute-start(bf16[8,192,128]{2,1,0:T(8,128)(2,1)} %get-tuple-element.50), channel_id=1, source_target_pairs={{0,4},{1,5},{2,6},{3,7},{4,0},{5,1},{6,2},{7,3},{8,12},{9,13},{10,... | collective-permute-start | bytes 1179656 | tf_op jit(solution)/shard_map/ppermute | solution.py:475
  47.9 1.2 copy-start.2
  49.0 62.6 %all-to-all-start.1 = ((bf16[8,768,128]{2,1,0:T(8,128)(2,1)}), bf16[8,768,128]{2,1,0:T(8,128)(2,1)}, u32[]{:S(2)}, u32[]{:S(2)}) async-start(bf16[8,768,128]{2,1,0:T(8,128)(2,1)} %after.6.refs_4_.refs_1_), calls=%async_computation.1 | async-start | bytes 3145728 | tf_op jit(solution)/shard_map/all_to_all | solution.py:480
  55.6 53.5 %collective-permute-start.5 = (bf16[8,192,128]{2,1,0:T(8,128)(2,1)}, bf16[8,192,128]{2,1,0:T(8,128)(2,1)}, u32[]{:S(2)}, u32[]{:S(2)}) collective-permute-start(bf16[8,192,128]{2,1,0:T(8,128)(2,1)} %get-tuple-element.51), channel_id=1, source_target_pairs={{0,6},{1,7},{2,4},{3,5},{4,2},{5,3},{6,0},{7,1},{8,14},{9,15},{10,... | collective-permute-start | bytes 1179656 | tf_op jit(solution)/shard_map/ppermute | solution.py:475
  59.2 94.6 %collective-permute-start.7 = (bf16[8,192,128]{2,1,0:T(8,128)(2,1)}, bf16[8,192,128]{2,1,0:T(8,128)(2,1)}, u32[]{:S(2)}, u32[]{:S(2)}) collective-permute-start(bf16[8,192,128]{2,1,0:T(8,128)(2,1)} %get-tuple-element.54), channel_id=1, source_target_pairs={{0,4},{1,5},{2,6},{3,7},{4,0},{5,1},{6,2},{7,3},{8,12},{9,13},{10,... | collective-permute-start | bytes 1179656 | tf_op jit(solution)/shard_map/ppermute | solution.py:475
  59.3 97.2 %collective-permute-start.8 = (bf16[8,192,128]{2,1,0:T(8,128)(2,1)}, bf16[8,192,128]{2,1,0:T(8,128)(2,1)}, u32[]{:S(2)}, u32[]{:S(2)}) collective-permute-start(bf16[8,192,128]{2,1,0:T(8,128)(2,1)} %get-tuple-element.55), channel_id=1, source_target_pairs={{0,6},{1,7},{2,4},{3,5},{4,2},{5,3},{6,0},{7,1},{8,14},{9,15},{10,... | collective-permute-start | bytes 1179656 | tf_op jit(solution)/shard_map/ppermute | solution.py:475
  64.0 92.4 %collective-permute-start.6 = (bf16[8,192,128]{2,1,0:T(8,128)(2,1)}, bf16[8,192,128]{2,1,0:T(8,128)(2,1)}, u32[]{:S(2)}, u32[]{:S(2)}) collective-permute-start(bf16[8,192,128]{2,1,0:T(8,128)(2,1)} %get-tuple-element.52.refs_4_), channel_id=1, source_target_pairs={{0,2},{1,3},{2,0},{3,1},{4,6},{5,7},{6,4},{7,5},{8,10},{9,11},{10,... | collective-permute-start | bytes 1179656 | tf_op jit(solution)/shard_map/ppermute | solution.py:475
  111.6 25.3 %all-to-all-start.2 = ((bf16[8,768,128]{2,1,0:T(8,128)(2,1)}), bf16[8,768,128]{2,1,0:T(8,128)(2,1)}, u32[]{:S(2)}, u32[]{:S(2)}) async-start(bf16[8,768,128]{2,1,0:T(8,128)(2,1)} %after.7.refs_1_), calls=%async_computation.2 | async-start | bytes 3145728 | tf_op jit(solution)/shard_map/all_to_all | solution.py:480
  115.9 21.0 %copy-start.17 = (s32[520]{0:T(1024)S(1)}, s32[520]{0:T(1024)}, u32[]{:S(2)}) copy-start(s32[520]{0:T(1024)} %pad_add_fusion.1) | copy-start | bytes 6244
  115.9 21.2 %copy-start.16 = (s32[1032]{0:T(1024)S(1)}, s32[1032]{0:T(1024)}, u32[]{:S(2)}) copy-start(s32[1032]{0:T(1024)} %concatenate.6) | copy-start | bytes 12388
  118.2 74.5 %collective-permute-start.13 = (bf16[8,192,128]{2,1,0:T(8,128)(2,1)}, bf16[8,192,128]{2,1,0:T(8,128)(2,1)}, u32[]{:S(2)}, u32[]{:S(2)}) collective-permute-start(bf16[8,192,128]{2,1,0:T(8,128)(2,1)} %get-tuple-element.59), channel_id=1, source_target_pairs={{0,4},{1,5},{2,6},{3,7},{4,0},{5,1},{6,2},{7,3},{8,12},{9,13},{10,... | collective-permute-start | bytes 1179656 | tf_op jit(solution)/shard_map/ppermute | solution.py:475
  128.2 64.4 %collective-permute-start.12 = (bf16[8,192,128]{2,1,0:T(8,128)(2,1)}, bf16[8,192,128]{2,1,0:T(8,128)(2,1)}, u32[]{:S(2)}, u32[]{:S(2)}) collective-permute-start(bf16[8,192,128]{2,1,0:T(8,128)(2,1)} %get-tuple-element.53.refs_5_), channel_id=1, source_target_pairs={{0,2},{1,3},{2,0},{3,1},{4,6},{5,7},{6,4},{7,5},{8,10},{9,11},{10,... | collective-permute-start | bytes 1179656 | tf_op jit(solution)/shard_map/ppermute | solution.py:475
  137.3 1.0 copy-start.14
  148.1 1.1 copy-start.8
  149.2 7.2 %copy-start.3 = (bf16[8,768,128]{2,1,0:T(8,128)(2,1)S(1)}, bf16[8,768,128]{2,1,0:T(8,128)(2,1)}, u32[]{:S(2)}) copy-start(bf16[8,768,128]{2,1,0:T(8,128)(2,1)} %copy-done.2) | copy-start | bytes 4718596
  149.2 25.5 %all-to-all-start.3 = ((bf16[8,768,128]{2,1,0:T(8,128)(2,1)}), bf16[8,768,128]{2,1,0:T(8,128)(2,1)}, u32[]{:S(2)}, u32[]{:S(2)}) async-start(bf16[8,768,128]{2,1,0:T(8,128)(2,1)} %bitcast.71), calls=%async_computation.3 | async-start | bytes 3145728 | tf_op jit(solution)/shard_map/all_to_all | solution.py:480
  153.9 38.8 %collective-permute-start.14 = (bf16[8,192,128]{2,1,0:T(8,128)(2,1)}, bf16[8,192,128]{2,1,0:T(8,128)(2,1)}, u32[]{:S(2)}, u32[]{:S(2)}) collective-permute-start(bf16[8,192,128]{2,1,0:T(8,128)(2,1)} %get-tuple-element.60), channel_id=1, source_target_pairs={{0,6},{1,7},{2,4},{3,5},{4,2},{5,3},{6,0},{7,1},{8,14},{9,15},{10,... | collective-permute-start | bytes 1179656 | tf_op jit(solution)/shard_map/ppermute | solution.py:475
  166.0 1.2 copy-start.5
  174.7 29.9 %all-to-all-start.4 = ((bf16[8,768,128]{2,1,0:T(8,128)(2,1)}), bf16[8,768,128]{2,1,0:T(8,128)(2,1)}, u32[]{:S(2)}, u32[]{:S(2)}) async-start(bf16[8,768,128]{2,1,0:T(8,128)(2,1)} %after.8.refs_1_), calls=%async_computation.4 | async-start | bytes 3145728 | tf_op jit(solution)/shard_map/all_to_all | solution.py:480
  181.3 80.9 %collective-permute-start.10 = (bf16[8,192,128]{2,1,0:T(8,128)(2,1)}, bf16[8,192,128]{2,1,0:T(8,128)(2,1)}, u32[]{:S(2)}, u32[]{:S(2)}) collective-permute-start(bf16[8,192,128]{2,1,0:T(8,128)(2,1)} %get-tuple-element.57), channel_id=1, source_target_pairs={{0,4},{1,5},{2,6},{3,7},{4,0},{5,1},{6,2},{7,3},{8,12},{9,13},{10,... | collective-permute-start | bytes 1179656 | tf_op jit(solution)/shard_map/ppermute | solution.py:475
  191.3 73.4 %collective-permute-start.11 = (bf16[8,192,128]{2,1,0:T(8,128)(2,1)}, bf16[8,192,128]{2,1,0:T(8,128)(2,1)}, u32[]{:S(2)}, u32[]{:S(2)}) collective-permute-start(bf16[8,192,128]{2,1,0:T(8,128)(2,1)} %get-tuple-element.58), channel_id=1, source_target_pairs={{0,6},{1,7},{2,4},{3,5},{4,2},{5,3},{6,0},{7,1},{8,14},{9,15},{10,... | collective-permute-start | bytes 1179656 | tf_op jit(solution)/shard_map/ppermute | solution.py:475
  192.7 75.5 %collective-permute-start.9 = (bf16[8,192,128]{2,1,0:T(8,128)(2,1)}, bf16[8,192,128]{2,1,0:T(8,128)(2,1)}, u32[]{:S(2)}, u32[]{:S(2)}) collective-permute-start(bf16[8,192,128]{2,1,0:T(8,128)(2,1)} %get-tuple-element.56.refs_8_), channel_id=1, source_target_pairs={{0,2},{1,3},{2,0},{3,1},{4,6},{5,7},{6,4},{7,5},{8,10},{9,11},{10,... | collective-permute-start | bytes 1179656 | tf_op jit(solution)/shard_map/ppermute | solution.py:475
  192.7 1.0 copy-start.12
  203.5 1.1 copy-start.7
  204.6 4.5 %copy-start.6 = (bf16[8,768,128]{2,1,0:T(8,128)(2,1)S(1)}, bf16[8,768,128]{2,1,0:T(8,128)(2,1)}, u32[]{:S(2)}) copy-start(bf16[8,768,128]{2,1,0:T(8,128)(2,1)} %after.9.refs_5_) | copy-start | bytes 4718596
  204.6 25.5 %all-to-all-start.5 = ((bf16[8,768,128]{2,1,0:T(8,128)(2,1)}), bf16[8,768,128]{2,1,0:T(8,128)(2,1)}, u32[]{:S(2)}, u32[]{:S(2)}) async-start(bf16[8,768,128]{2,1,0:T(8,128)(2,1)} %after.9.refs_5_), calls=%async_computation.5 | async-start | bytes 3145728 | tf_op jit(solution)/shard_map/all_to_all | solution.py:480
  218.9 1.2 copy-start.9
  230.1 25.3 %all-to-all-start.6 = ((bf16[8,768,128]{2,1,0:T(8,128)(2,1)}), bf16[8,768,128]{2,1,0:T(8,128)(2,1)}, u32[]{:S(2)}, u32[]{:S(2)}) async-start(bf16[8,768,128]{2,1,0:T(8,128)(2,1)} %after.10.refs_1_), calls=%async_computation.6 | async-start | bytes 3145728 | tf_op jit(solution)/shard_map/all_to_all | solution.py:480
  236.7 34.0 %collective-permute-start.19 = (bf16[8,192,128]{2,1,0:T(8,128)(2,1)}, bf16[8,192,128]{2,1,0:T(8,128)(2,1)}, u32[]{:S(2)}, u32[]{:S(2)}) collective-permute-start(bf16[8,192,128]{2,1,0:T(8,128)(2,1)} %get-tuple-element.65), channel_id=1, source_target_pairs={{0,4},{1,5},{2,6},{3,7},{4,0},{5,1},{6,2},{7,3},{8,12},{9,13},{10,... | collective-permute-start | bytes 1179656 | tf_op jit(solution)/shard_map/ppermute | solution.py:475
  242.1 59.3 %collective-permute-start.18 = (bf16[8,192,128]{2,1,0:T(8,128)(2,1)}, bf16[8,192,128]{2,1,0:T(8,128)(2,1)}, u32[]{:S(2)}, u32[]{:S(2)}) collective-permute-start(bf16[8,192,128]{2,1,0:T(8,128)(2,1)} %get-tuple-element.61.refs_0_), channel_id=1, source_target_pairs={{0,2},{1,3},{2,0},{3,1},{4,6},{5,7},{6,4},{7,5},{8,10},{9,11},{10,... | collective-permute-start | bytes 1179656 | tf_op jit(solution)/shard_map/ppermute | solution.py:475
  242.1 1.0 copy-start.13
  245.2 1.6 copy-start.15
  255.4 25.3 %all-to-all-start.7 = ((bf16[8,768,128]{2,1,0:T(8,128)(2,1)}), bf16[8,768,128]{2,1,0:T(8,128)(2,1)}, u32[]{:S(2)}, u32[]{:S(2)}) async-start(bf16[8,768,128]{2,1,0:T(8,128)(2,1)} %after.11.refs_1_), calls=%async_computation.7 | async-start | bytes 3145728 | tf_op jit(solution)/shard_map/all_to_all | solution.py:480
  262.3 20.8 %collective-permute-start.20 = (bf16[8,192,128]{2,1,0:T(8,128)(2,1)}, bf16[8,192,128]{2,1,0:T(8,128)(2,1)}, u32[]{:S(2)}, u32[]{:S(2)}) collective-permute-start(bf16[8,192,128]{2,1,0:T(8,128)(2,1)} %get-tuple-element.66), channel_id=1, source_target_pairs={{0,6},{1,7},{2,4},{3,5},{4,2},{5,3},{6,0},{7,1},{8,14},{9,15},{10,... | collective-permute-start | bytes 1179656 | tf_op jit(solution)/shard_map/ppermute | solution.py:475
  264.7 46.7 %collective-permute-start.16 = (bf16[8,192,128]{2,1,0:T(8,128)(2,1)}, bf16[8,192,128]{2,1,0:T(8,128)(2,1)}, u32[]{:S(2)}, u32[]{:S(2)}) collective-permute-start(bf16[8,192,128]{2,1,0:T(8,128)(2,1)} %get-tuple-element.63), channel_id=1, source_target_pairs={{0,4},{1,5},{2,6},{3,7},{4,0},{5,1},{6,2},{7,3},{8,12},{9,13},{10,... | collective-permute-start | bytes 1179656 | tf_op jit(solution)/shard_map/ppermute | solution.py:475
  268.1 45.8 %collective-permute-start.17 = (bf16[8,192,128]{2,1,0:T(8,128)(2,1)}, bf16[8,192,128]{2,1,0:T(8,128)(2,1)}, u32[]{:S(2)}, u32[]{:S(2)}) collective-permute-start(bf16[8,192,128]{2,1,0:T(8,128)(2,1)} %get-tuple-element.64), channel_id=1, source_target_pairs={{0,6},{1,7},{2,4},{3,5},{4,2},{5,3},{6,0},{7,1},{8,14},{9,15},{10,... | collective-permute-start | bytes 1179656 | tf_op jit(solution)/shard_map/ppermute | solution.py:475
  270.6 51.9 %collective-permute-start.15 = (bf16[8,192,128]{2,1,0:T(8,128)(2,1)}, bf16[8,192,128]{2,1,0:T(8,128)(2,1)}, u32[]{:S(2)}, u32[]{:S(2)}) collective-permute-start(bf16[8,192,128]{2,1,0:T(8,128)(2,1)} %get-tuple-element.62.refs_1_), channel_id=1, source_target_pairs={{0,2},{1,3},{2,0},{3,1},{4,6},{5,7},{6,4},{7,5},{8,10},{9,11},{10,... | collective-permute-start | bytes 1179656 | tf_op jit(solution)/shard_map/ppermute | solution.py:475
  283.0 40.6 %collective-permute-start.30 = (bf16[8,48,128]{2,1,0:T(8,128)(2,1)}, bf16[8,48,128]{2,1,0:T(8,128)(2,1)S(1)}, u32[]{:S(2)}, u32[]{:S(2)}) collective-permute-start(bf16[8,48,128]{2,1,0:T(8,128)(2,1)} %get-tuple-element.76), channel_id=1, source_target_pairs={{0,2},{1,3},{2,0},{3,1},{4,6},{5,7},{6,4},{7,5},{8,10},{9,11},{10,... | collective-permute-start | bytes 294920 | tf_op jit(solution)/shard_map/ppermute | solution.py:475
  301.5 24.2 %collective-permute-start.31 = (bf16[8,48,128]{2,1,0:T(8,128)(2,1)}, bf16[8,48,128]{2,1,0:T(8,128)(2,1)S(1)}, u32[]{:S(2)}, u32[]{:S(2)}) collective-permute-start(bf16[8,48,128]{2,1,0:T(8,128)(2,1)} %get-tuple-element.77), channel_id=1, source_target_pairs={{0,4},{1,5},{2,6},{3,7},{4,0},{5,1},{6,2},{7,3},{8,12},{9,13},{10,... | collective-permute-start | bytes 294920 | tf_op jit(solution)/shard_map/ppermute | solution.py:475
  311.5 14.2 %collective-permute-start.32 = (bf16[8,48,128]{2,1,0:T(8,128)(2,1)}, bf16[8,48,128]{2,1,0:T(8,128)(2,1)S(1)}, u32[]{:S(2)}, u32[]{:S(2)}) collective-permute-start(bf16[8,48,128]{2,1,0:T(8,128)(2,1)} %get-tuple-element.78), channel_id=1, source_target_pairs={{0,6},{1,7},{2,4},{3,5},{4,2},{5,3},{6,0},{7,1},{8,14},{9,15},{10,... | collective-permute-start | bytes 294920 | tf_op jit(solution)/shard_map/ppermute | solution.py:475
  314.0 42.1 %collective-permute-start.21 = (bf16[8,48,128]{2,1,0:T(8,128)(2,1)}, bf16[8,48,128]{2,1,0:T(8,128)(2,1)}, u32[]{:S(2)}, u32[]{:S(2)}) collective-permute-start(bf16[8,48,128]{2,1,0:T(8,128)(2,1)} %get-tuple-element.67), channel_id=1, source_target_pairs={{0,2},{1,3},{2,0},{3,1},{4,6},{5,7},{6,4},{7,5},{8,10},{9,11},{10,... | collective-permute-start | bytes 294920 | tf_op jit(solution)/shard_map/ppermute | solution.py:475
  322.6 33.5 %collective-permute-start.22 = (bf16[8,48,128]{2,1,0:T(8,128)(2,1)}, bf16[8,48,128]{2,1,0:T(8,128)(2,1)}, u32[]{:S(2)}, u32[]{:S(2)}) collective-permute-start(bf16[8,48,128]{2,1,0:T(8,128)(2,1)} %get-tuple-element.68), channel_id=1, source_target_pairs={{0,4},{1,5},{2,6},{3,7},{4,0},{5,1},{6,2},{7,3},{8,12},{9,13},{10,... | collective-permute-start | bytes 294920 | tf_op jit(solution)/shard_map/ppermute | solution.py:475
  323.6 11.7 %collective-permute-start.27 = (bf16[8,48,128]{2,1,0:T(8,128)(2,1)}, bf16[8,48,128]{2,1,0:T(8,128)(2,1)}, u32[]{:S(2)}, u32[]{:S(2)}) collective-permute-start(bf16[8,48,128]{2,1,0:T(8,128)(2,1)} %get-tuple-element.73), channel_id=1, source_target_pairs={{0,2},{1,3},{2,0},{3,1},{4,6},{5,7},{6,4},{7,5},{8,10},{9,11},{10,... | collective-permute-start | bytes 294920 | tf_op jit(solution)/shard_map/ppermute | solution.py:475
  325.6 11.5 %collective-permute-start.28 = (bf16[8,48,128]{2,1,0:T(8,128)(2,1)}, bf16[8,48,128]{2,1,0:T(8,128)(2,1)}, u32[]{:S(2)}, u32[]{:S(2)}) collective-permute-start(bf16[8,48,128]{2,1,0:T(8,128)(2,1)} %get-tuple-element.74), channel_id=1, source_target_pairs={{0,4},{1,5},{2,6},{3,7},{4,0},{5,1},{6,2},{7,3},{8,12},{9,13},{10,... | collective-permute-start | bytes 294920 | tf_op jit(solution)/shard_map/ppermute | solution.py:475
  325.7 11.7 %collective-permute-start.29 = (bf16[8,48,128]{2,1,0:T(8,128)(2,1)}, bf16[8,48,128]{2,1,0:T(8,128)(2,1)}, u32[]{:S(2)}, u32[]{:S(2)}) collective-permute-start(bf16[8,48,128]{2,1,0:T(8,128)(2,1)} %get-tuple-element.75), channel_id=1, source_target_pairs={{0,6},{1,7},{2,4},{3,5},{4,2},{5,3},{6,0},{7,1},{8,14},{9,15},{10,... | collective-permute-start | bytes 294920 | tf_op jit(solution)/shard_map/ppermute | solution.py:475
  335.3 11.8 %collective-permute-start.24 = (bf16[8,48,128]{2,1,0:T(8,128)(2,1)}, bf16[8,48,128]{2,1,0:T(8,128)(2,1)}, u32[]{:S(2)}, u32[]{:S(2)}) collective-permute-start(bf16[8,48,128]{2,1,0:T(8,128)(2,1)} %get-tuple-element.70), channel_id=1, source_target_pairs={{0,2},{1,3},{2,0},{3,1},{4,6},{5,7},{6,4},{7,5},{8,10},{9,11},{10,... | collective-permute-start | bytes 294920 | tf_op jit(solution)/shard_map/ppermute | solution.py:475
  337.1 11.5 %collective-permute-start.25 = (bf16[8,48,128]{2,1,0:T(8,128)(2,1)}, bf16[8,48,128]{2,1,0:T(8,128)(2,1)}, u32[]{:S(2)}, u32[]{:S(2)}) collective-permute-start(bf16[8,48,128]{2,1,0:T(8,128)(2,1)} %get-tuple-element.71), channel_id=1, source_target_pairs={{0,4},{1,5},{2,6},{3,7},{4,0},{5,1},{6,2},{7,3},{8,12},{9,13},{10,... | collective-permute-start | bytes 294920 | tf_op jit(solution)/shard_map/ppermute | solution.py:475
  337.4 11.3 %collective-permute-start.26 = (bf16[8,48,128]{2,1,0:T(8,128)(2,1)}, bf16[8,48,128]{2,1,0:T(8,128)(2,1)}, u32[]{:S(2)}, u32[]{:S(2)}) collective-permute-start(bf16[8,48,128]{2,1,0:T(8,128)(2,1)} %get-tuple-element.72), channel_id=1, source_target_pairs={{0,6},{1,7},{2,4},{3,5},{4,2},{5,3},{6,0},{7,1},{8,14},{9,15},{10,... | collective-permute-start | bytes 294920 | tf_op jit(solution)/shard_map/ppermute | solution.py:475
  347.1 8.9 %collective-permute-start.23 = (bf16[8,48,128]{2,1,0:T(8,128)(2,1)}, bf16[8,48,128]{2,1,0:T(8,128)(2,1)}, u32[]{:S(2)}, u32[]{:S(2)}) collective-permute-start(bf16[8,48,128]{2,1,0:T(8,128)(2,1)} %get-tuple-element.69), channel_id=1, source_target_pairs={{0,6},{1,7},{2,4},{3,5},{4,2},{5,3},{6,0},{7,1},{8,14},{9,15},{10,... | collective-permute-start | bytes 294920 | tf_op jit(solution)/shard_map/ppermute | solution.py:475
  356.1 7.5 %copy-start.1 = (bf16[16,128,128]{2,1,0:T(8,128)(2,1)S(1)}, bf16[16,128,128]{2,1,0:T(8,128)(2,1)}, u32[]{:S(2)}) copy-start(bf16[16,128,128]{2,1,0:T(8,128)(2,1)} %param.9) | copy-start | bytes 1572868

commit v3 on v2

--- a/solution.py
+++ b/solution.py
@@ -339,17 +339,18 @@
 
 def synthesis_kernel(pieces, parity_ref, *refs):
     field_refs, (table_ref, wind_ref) = refs[:pieces], refs[pieces : pieces + 2]
-    out_ref = refs[-1]
+    out_ref, lines_ref = refs[-2:]
     half = LANES // 2
     whole = pl.ds(pl.multiple_of(half * parity_ref[0], half), LANES)
     rest = pl.ds(pl.multiple_of(LANES * (1 - parity_ref[0]), half), half)
+
     fields = [ref[...].astype(jnp.float32) for ref in field_refs]
-    fields = jnp.concatenate([f.reshape(-1, f.shape[-2], LANES) for f in fields], axis=0)
-    tiles = [
-        fields[:, t * ROWS : (t + 1) * ROWS, :].reshape(-1, LANES).astype(jnp.bfloat16)
-        for t in range(6)
-    ]
-    sums = dot(jnp.concatenate(tiles, axis=1), table_ref[...], ((0,), (0,)))
+    fields = jnp.concatenate(fields, axis=0)
+    for t in range(6):
+        tile = fields[:, t * ROWS : (t + 1) * ROWS, :].reshape(-1, LANES)
+        lines_ref[t * LANES : (t + 1) * LANES, :] = tile.astype(jnp.bfloat16).T
+
+    sums = dot(lines_ref[...], table_ref[...], ((1,), (0,)))
 
     def put(t, j, rows, value):
         gain = wind_ref[t, 0, j, rows, :].astype(jnp.float32)
@@ -363,38 +364,34 @@
             put(t, j, rest, sums[start : start + half])
 
 
-def synthesis_part(fields, table, wind, parity, first_step, steps, before):
+def synthesis_part(fields, table, wind, parity, start, count, before):
     _, _, _, lat_rows, points = wind.shape
     columns = table.shape[0]
     rows = 6 * ROWS
 
-    def field_spec(array, offset):
-        lead = array.ndim - 2
-        return pl.BlockSpec(
-            array.shape[:-2] + (rows, LANES),
-            lambda s, _: (0,) * lead + (s + first_step - offset, 0),
-        )
+    def field_spec(array, first):
+        return pl.BlockSpec((array.shape[0], rows, LANES), lambda s, _: (0, first + s, 0))
 
     grid_spec = pl.BlockSpec(
-        (2, 1, 2, lat_rows, points), lambda s, _: (0, s + first_step, 0, 0, 0)
+        (2, 1, 2, lat_rows, points), lambda s, _: (0, start + s, 0, 0, 0)
     )
     in_specs = [field_spec(*f) for f in fields]
-    in_specs += [pl.BlockSpec(table.shape, lambda s, _: (0, 0)), grid_spec]
+    in_specs += [pl.BlockSpec((columns, points), lambda s, _: (0, 0)), grid_spec]
     operands = [f for f, _ in fields] + [table, wind]
     aliases = {}
     if before is not None:
         in_specs.append(ANYWHERE)
         aliases = {1 + len(operands): 0}
         operands.append(before)
-    part = 4 * steps * lat_rows * points
     return pl.pallas_call(
         functools.partial(synthesis_kernel, len(fields)),
         out_shape=jax.ShapeDtypeStruct(wind.shape, jnp.bfloat16),
         grid_spec=pltpu.PrefetchScalarGridSpec(
             num_scalar_prefetch=1,
-            grid=(steps,),
+            grid=(count,),
             in_specs=in_specs,
             out_specs=grid_spec,
+            scratch_shapes=[pltpu.VMEM((6 * LANES, columns), jnp.bfloat16)],
         ),
         input_output_aliases=aliases,
         compiler_params=pltpu.CompilerParams(vmem_limit_bytes=VMEM),
@@ -467,11 +464,11 @@
     return [slots[p * (layers - 1) : (p + 1) * (layers - 1)] for p in range(parts)]
 
 
-def swap_along_z(slots):
+def turn_along_z(slots, sign):
     lev_devices = lax.axis_size("lev")
     moved = []
-    for kz, slot in enumerate(slots, 1):
-        pairs = [(b, b ^ (CORES * kz)) for b in range(lev_devices)]
+    for k, slot in enumerate(slots, 1):
+        pairs = [(b, (b + sign * CORES * k) % lev_devices) for b in range(lev_devices)]
         moved.append(lax.ppermute(slot, "lev", pairs))
     return moved
 
@@ -482,16 +479,9 @@
     )
 
 
-def xor_order(x, axis, index):
+def turned(x, axis, start):
     size = x.shape[axis]
-    bit = 1
-    while bit < size:
-        split = x.shape[:axis] + (size // (2 * bit), 2, bit) + x.shape[axis + 1 :]
-        halves = x.reshape(split)
-        halves = jnp.where(index & bit != 0, jnp.flip(halves, axis + 1), halves)
-        x = halves.reshape(x.shape)
-        bit *= 2
-    return x
+    return lax.dynamic_slice_in_dim(jnp.concatenate([x, x], axis=axis), start, size, axis)
 
 
 def pipelined_body(adjoint_grid, wind, legendre, vertical, pair_table, degree_matrix):
@@ -514,7 +504,7 @@
         [a * levs + z * CORES + c for a in range(lats) for c in range(CORES)] for z in range(layers)
     ]
 
-    table_pairs = xor_order(pair_table.reshape(lats, layers, CORES, chunks, pairs), 1, layer)
+    table_pairs = turned(pair_table.reshape(lats, layers, CORES, chunks, pairs), 1, layer)
     table_pairs = table_pairs.transpose(3, 1, 0, 2, 4)
     waves = jnp.stack([table_pairs, N - 1 - table_pairs], axis=-1)
     waves = jnp.broadcast_to(waves[..., None], waves.shape + (2,))
@@ -525,7 +515,8 @@
     table = legendre.transpose(0, 2, 1)
 
     slot_level = jnp.arange(levels, dtype=jnp.int32).reshape(layers, CORES, 2, level_rows // 2)
-    slot_level = xor_order(slot_level, 0, layer).transpose(2, 1, 0, 3).reshape(levels)
+    slot_level = turned(jnp.flip(slot_level, 0), 0, layers - 1 - layer)
+    slot_level = slot_level.transpose(2, 1, 0, 3).reshape(levels)
     order = (slot_level[:, None] == jnp.arange(levels)[None, :]).astype(jnp.bfloat16)
     operators = jnp.einsum("av,gvo->gao", order, vertical, preferred_element_type=jnp.float32)
     operators = jnp.einsum(
@@ -541,13 +532,17 @@
     first_pair = (lat * levs + lev) * (slots // 4)
     lower = lax.dynamic_slice(pair_table, (first_pair,), (slots // 4,)).reshape(chunks, pairs)
 
+    parts = 2 if steps % 2 == 0 else 1
     joined_shape = (plane, layers * wire_rows, LANES)
 
     def across(x):
         return exchange_in_plane(x, groups)
 
     def along(first_slot, slots):
-        return [first_slot] + swap_along_z(slots)
+        return [first_slot] + turn_along_z(slots, 1)
+
+    def home(first_slot, slots):
+        return [first_slot] + turn_along_z(slots, -1)
 
     def solve(q, pieces, *ready):
         shape = (lats, levs, wire_rows, LANES)
@@ -559,52 +554,44 @@
     sent = fourier_all(grid, rows, parity, [plane] * (2 * layers) + [plane * layers] * 2)
     x2, x3 = [x.reshape(joined_shape) for x in sent[2 * layers :]]
     z0 = along(sent[0], sent[1:layers])
-    z1 = along(sent[layers], sent[layers + 1 : 2 * layers])
     p2 = across(x2)
-    x3 = after(x3, p2)
+    rows = jnp.stack([waves[0], waves[2], waves[3], waves[1]]).reshape(-1, 1)
+    synthesis = synthesis_rows(rows, points, ROWS * layers * plane, x2)
+    x3 = after(x3, p2, synthesis)
     p3 = across(x3)
-    j0 = join_slots(z0, x3)
-    u2 = part_slots(p2, layers, 1, x3)[0]
+    z1 = along(sent[layers], [after(x, x3) for x in sent[layers + 1 : 2 * layers]])
+    j0 = after(join_slots(z0, x3), p3)
+    p0 = across(j0)
+    u2 = part_slots(p2, layers, 1, j0)[0]
     z2 = along(p2, u2)
-    j1 = join_slots(z1, u2[0])
-    j0 = after(j0, p3, j1)
-    p0 = across(j0)
-    u3 = part_slots(p3, layers, 1, j0)[0]
+    s0 = solve(0, [p0], u2[0])
+    r0 = across(s0)
+    j1 = join_slots(z1, s0)
+    u3 = part_slots(p3, layers, 1, j1)[0]
     z3 = along(p3, u3)
-    s0 = solve(0, [p0], u3[0])
-    r0 = across(s0)
-    s2 = solve(2, z2, s0)
-    j1 = after(j1, r0, s2)
+    j1 = after(j1, r0, u3[0])
     p1 = across(j1)
     b0 = part_slots(r0, layers, 1, j1)[0]
-    back0 = along(r0, b0)
-    s3 = solve(3, z3, b0[0])
-    s2 = after(s2, p1, s3)
+    back0 = home(r0, b0)
+    s2 = after(solve(2, z2, b0[0]), p1)
     r2 = across(s2)
-    s1 = solve(1, [p1], s2)
-    s1 = after(s1, r2)
+    s3 = after(solve(3, z3, s2), r2)
+    r3 = across(s3)
+    b2 = part_slots(r2, layers, 1, s3)[0]
+    back2 = home(r2, b2)
+    s1 = after(solve(1, [p1], b2[0]), r3)
     r1 = across(s1)
-    b2 = part_slots(r2, layers, 1, s1)[0]
-    back2 = along(r2, b2)
-    synthesis = synthesis_rows(waves.reshape(-1, 1), points, ROWS * layers * plane, b2[0])
-    s3 = after(s3, r1, synthesis)
-    r3 = across(s3)
-    b1 = part_slots(r1, layers, 1, s3)[0]
-    back1 = along(r1, b1)
-    late = [along(r3, part) for part in part_slots(r3, layers, steps, b1[0])]
-    fields = back0 + back1 + back2
+    b3 = part_slots(r3, layers, 1, s1)[0]
+    back3 = home(r3, b3)
+    late = [home(r1, part) for part in part_slots(r1, layers, parts, b3[0])]
+    fields = back0 + back2 + back3
 
     out = None
-    for step in range(steps):
-        out = synthesis_part(
-            [(f, 0) for f in fields] + [(late[step][0], 0)] + [(f, step) for f in late[step][1:]],
-            synthesis,
-            wind,
-            parity,
-            step,
-            1,
-            out,
-        )
+    for i in range(parts):
+        first = i * (steps // parts)
+        here = [(f, first) for f in fields] + [(late[i][0], first)]
+        here += [(f, 0) for f in late[i][1:]]
+        out = synthesis_part(here, synthesis, wind, parity, first, steps // parts, out)
     return out.reshape(level_rows, lat_rows, points)
 
 
@@ -614,7 +601,6 @@
     layers = levs // CORES
     fits = (
         levs % CORES == 0
-        and layers & (layers - 1) == 0
         and lats % 2 == 0
         and lat_rows == LANES + LANES // 2
         and level_rows % 16 == 0

time: 365 us -> 325 us (0.89)
  starting transfers between devices: 170 us -> 152 us
  waiting for transfers between devices: 64.9 us -> 54.1 us
  Pallas kernels: 105 us -> 96.6 us
    ppermute x33 -> x27, starting transfers between devices: 134 us -> 117 us  [turn_along_z(): moved.append(lax.ppermute(slot, 'lev', pairs))]
    all_to_all x8, waiting for transfers between devices: 51 us -> 38.5 us  [exchange_in_plane(): lax.all_to_all(x, ('lat', 'lev'), split_axis=0, concat_axis=0, tiled=True...]
    pallas_call x4 -> x2, Pallas kernels: 29.5 us -> 20.3 us  [synthesis_part(): pl.pallas_call(functools.partial(synthesis_kernel, len(fields)), out_shap...]
    unnamed x43 -> x45, local copies, waits for them, and re-layouts: 13.4 us -> 11.4 us
    ppermute x33 -> x27, waiting for transfers between devices: 14 us -> 15.6 us  [turn_along_z(): moved.append(lax.ppermute(slot, 'lev', pairs))]
  transfers between devices with their start and end apart: 41 -> 35, of which waited for: 10 -> 9; matrix products, arithmetic and copies ran while one was open for 2% -> 2% of each run, Pallas kernels for 22% -> 22%
where the time goes in v3:
time: 325 us; the launch traced here: 323 us
  starting transfers between devices  152 us (47%)
  Pallas kernels  96.6 us (30%)
  waiting for transfers between devices  54.1 us (17%)
  local copies, waits for them, and re-layouts  17.7 us (5%)
    ppermute x27, starting transfers between devices, turn_along_z(): moved.append(lax.ppermute(slot, 'lev', pairs))  117 us
    pallas_call x4, Pallas kernels, spectral_chunk(): pl.pallas_call(functools.partial(spectral_kernel, len(pieces)), out_shape...  40.2 us
    all_to_all x8, waiting for transfers between devices, exchange_in_plane(): lax.all_to_all(x, ('lat', 'lev'), split_axis=0, concat_axis=0, tiled=True...  38.5 us
    all_to_all x8, starting transfers between devices, exchange_in_plane(): lax.all_to_all(x, ('lat', 'lev'), split_axis=0, concat_axis=0, tiled=True...  35.3 us
    pallas_call x2, Pallas kernels, synthesis_part(): pl.pallas_call(functools.partial(synthesis_kernel, len(fields)), out_shap...  20.3 us
    ppermute x27, waiting for transfers between devices, turn_along_z(): moved.append(lax.ppermute(slot, 'lev', pairs))  15.6 us
    pallas_call x1, Pallas kernels, fourier_all(): pl.pallas_call(fourier_kernel, out_shape=[jax.ShapeDtypeStruct((n, steps...  15.6 us
    pallas_call x6, Pallas kernels, part_slots(): pl.pallas_call(functools.partial(part_kernel, layers, parts), out_shape=[...  13.6 us
  transfers between devices with their start and end apart: 35, of which 9 were waited for; matrix products, arithmetic and copies ran while one was open for 2% of the time, Pallas kernels for 22%

profile of v3, /device:TPU:0, one launch (start us, length us, event | category | flops | bytes accessed | tf_op | source)
XLA Modules:
  0.0 323.5 jit_solution(12715671061667191186)
XLA Ops:
  0.0 0.9 reshape.112
  3.3 15.6 %fourier_all.1 = (bf16[8,192,128]{2,1,0:T(8,128)(2,1)S(1)}, bf16[8,192,128]{2,1,0:T(8,128)(2,1)}, bf16[8,192,128]{2,1,0:T(8,128)(2,1)}, bf16[8,192,128]{2,1,0:T(...) custom-call(s32[1]{0:T(128)} %bitcast.parity_ref, ...), custom_call_target="tpu_custom_call" | custom-call | flops 1 | bytes 1 | tf_op jit(solution)/shard_map/fourier_all/pallas_call | solution.py:179
  21.2 5.2 %all-to-all-start = ((bf16[8,768,128]{2,1,0:T(8,128)(2,1)}), bf16[8,768,128]{2,1,0:T(8,128)(2,1)}, u32[]{:S(2)}, u32[]{:S(2)}) async-start(bf16[8,768,128]{2,1,0:T(8,128)(2,1)} %bitcast.14.refs_0_), calls=%async_computation | async-start | bytes 3145728 | tf_op jit(solution)/shard_map/all_to_all | solution.py:477
  26.4 2.2 collective-permute-start
  28.6 2.6 collective-permute-start.1
  31.2 1.3 collective-permute-start.2
  33.1 2.1 synthesis_rows.1.refs_2_.refs_16_
  35.2 1.6 copy-done.15
  37.5 1.2 concatenate.14
  40.7 1.3 pad_add_fusion.2
  42.1 5.5 %all-to-all-done.refs_1_.refs_0_ = bf16[8,768,128]{2,1,0:T(8,128)(2,1)} async-done(((bf16[8,768,128]{2,1,0:T(8,128)(2,1)}), bf16[8,768,128]{2,1,0:T(8,128)(2,1)}, u32[]{:S(2)}, u32[]{:S(2)}) %all-to-all-start) | async-done | bytes 1572896 | tf_op jit(solution)/shard_map/all_to_all | solution.py:477
  47.5 4.3 %all-to-all-start.1 = ((bf16[8,768,128]{2,1,0:T(8,128)(2,1)}), bf16[8,768,128]{2,1,0:T(8,128)(2,1)}, u32[]{:S(2)}, u32[]{:S(2)}) async-start(bf16[8,768,128]{2,1,0:T(8,128)(2,1)} %after.9.refs_4_.refs_1_), calls=%async_computation.1 | async-start | bytes 3145728 | tf_op jit(solution)/shard_map/all_to_all | solution.py:477
  51.9 2.1 collective-permute-start.3
  54.0 2.6 collective-permute-start.4
  56.6 1.3 collective-permute-start.5
  57.9 2.4 join_slots.2.refs_0_
  60.3 12.5 %all-to-all-done.1.refs_1_.refs_0_ = bf16[8,768,128]{2,1,0:T(8,128)(2,1)} async-done(((bf16[8,768,128]{2,1,0:T(8,128)(2,1)}), bf16[8,768,128]{2,1,0:T(8,128)(2,1)}, u32[]{:S(2)}, u32[]{:S(2)}) %all-to-all-start.1) | async-done | bytes 1572896 | tf_op jit(solution)/shard_map/all_to_all | solution.py:477
  72.9 4.3 %all-to-all-start.2 = ((bf16[8,768,128]{2,1,0:T(8,128)(2,1)}), bf16[8,768,128]{2,1,0:T(8,128)(2,1)}, u32[]{:S(2)}, u32[]{:S(2)}) async-start(bf16[8,768,128]{2,1,0:T(8,128)(2,1)} %after.10.refs_1_), calls=%async_computation.2 | async-start | bytes 3145728 | tf_op jit(solution)/shard_map/all_to_all | solution.py:477
  77.2 2.3 part_slots.6
  79.5 11.9 %collective-permute-start.10 = (bf16[8,192,128]{2,1,0:T(8,128)(2,1)}, bf16[8,192,128]{2,1,0:T(8,128)(2,1)}, u32[]{:S(2)}, u32[]{:S(2)}) collective-permute-start(bf16[8,192,128]{2,1,0:T(8,128)(2,1)} %get-tuple-element.51), channel_id=1, source_target_pairs={{0,4},{1,5},{2,6},{3,7},{4,0},{5,1},{6,2},{7,3},{8,12},{9,13},{10,... | collective-permute-start | bytes 1179656 | tf_op jit(solution)/shard_map/ppermute | solution.py:472
  91.4 3.2 collective-permute-start.9
  94.5 3.7 %all-to-all-done.2.refs_0_ = bf16[8,768,128]{2,1,0:T(8,128)(2,1)} async-done(((bf16[8,768,128]{2,1,0:T(8,128)(2,1)}), bf16[8,768,128]{2,1,0:T(8,128)(2,1)}, u32[]{:S(2)}, u32[]{:S(2)}) %all-to-all-start.2) | async-done | bytes 1572896 | tf_op jit(solution)/shard_map/all_to_all | solution.py:477
  98.6 1.2 copy-done.13
  99.8 10.9 %spectral_chunk.4 = bf16[4,8,192,128]{3,2,1,0:T(8,128)(2,1)} custom-call(s32[2]{0:T(128)S(1)} %get-tuple-element.76.lower_ref, bf16[8,768,128]{2,1,0:T(8,128)(2,1)} %all-to-all-done.2.refs_0_, bf16[32,520,768]{2,1,0:T(8,128)(2,1)} %bitcast.85, bf16[1024,256]{1,0:T(8,128)(2,1)S(1)} %bitcast.64, s32[1032,128]{1,0:T(8,128)S(1)} %broadcast_in_dim.59.refs_3_.refs_6_, ...), custom_call_target="tpu_custom_call" | custom-call | flops 9999999827968 | bytes 100000000 | tf_op jit(solution)/shard_map/spectral_chunk/pallas_call | solution.py:314
  110.7 4.3 %all-to-all-start.3 = ((bf16[8,768,128]{2,1,0:T(8,128)(2,1)}), bf16[8,768,128]{2,1,0:T(8,128)(2,1)}, u32[]{:S(2)}, u32[]{:S(2)}) async-start(bf16[8,768,128]{2,1,0:T(8,128)(2,1)} %bitcast.26.refs_4_), calls=%async_computation.3 | async-start | bytes 3145728 | tf_op jit(solution)/shard_map/all_to_all | solution.py:477
  115.0 14.5 %collective-permute-start.11 = (bf16[8,192,128]{2,1,0:T(8,128)(2,1)}, bf16[8,192,128]{2,1,0:T(8,128)(2,1)}, u32[]{:S(2)}, u32[]{:S(2)}) collective-permute-start(bf16[8,192,128]{2,1,0:T(8,128)(2,1)} %get-tuple-element.52), channel_id=1, source_target_pairs={{0,6},{1,7},{2,0},{3,1},{4,2},{5,3},{6,4},{7,5},{8,14},{9,15},{10,... | collective-permute-start | bytes 1179656 | tf_op jit(solution)/shard_map/ppermute | solution.py:472
  129.6 2.4 join_slots.3.refs_1_.refs_0_
  132.0 2.3 part_slots.7
  134.9 1.2 all-to-all-done.3.refs_1_.refs_0_
  136.0 4.3 %all-to-all-start.4 = ((bf16[8,768,128]{2,1,0:T(8,128)(2,1)}), bf16[8,768,128]{2,1,0:T(8,128)(2,1)}, u32[]{:S(2)}, u32[]{:S(2)}) async-start(bf16[8,768,128]{2,1,0:T(8,128)(2,1)} %after.14.refs_1_), calls=%async_computation.4 | async-start | bytes 3145728 | tf_op jit(solution)/shard_map/all_to_all | solution.py:477
  140.4 2.3 part_slots.8
  142.7 14.5 %collective-permute-start.14 = (bf16[8,192,128]{2,1,0:T(8,128)(2,1)}, bf16[8,192,128]{2,1,0:T(8,128)(2,1)}, u32[]{:S(2)}, u32[]{:S(2)}) collective-permute-start(bf16[8,192,128]{2,1,0:T(8,128)(2,1)} %get-tuple-element.54), channel_id=1, source_target_pairs={{0,6},{1,7},{2,0},{3,1},{4,2},{5,3},{6,4},{7,5},{8,14},{9,15},{10,... | collective-permute-start | bytes 1179656 | tf_op jit(solution)/shard_map/ppermute | solution.py:472
  157.2 2.2 collective-permute-start.6
  159.5 1.0 copy-done.11
  160.5 9.7 %spectral_chunk.5 = bf16[4,8,192,128]{3,2,1,0:T(8,128)(2,1)S(1)} custom-call(s32[2]{0:T(128)S(1)} %get-tuple-element.75.lower_ref, bf16[8,768,128]{2,1,0:T(8,128)(2,1)} %all-to-all-done.refs_1_.refs_0_, bf16[8,192,128]{2,1,0:T(8,128)(2,1)} %collective-permute-done.9.refs_1_, bf16[8,192,128]{2,1,0:T(8,128)(2,1)} %collective-permute-done.10.refs_2_, ...), custom_call_target="tpu_custom_call" | custom-call | flops 9999999827968 | bytes 100000000 | tf_op jit(solution)/shard_map/spectral_chunk/pallas_call | solution.py:314
  170.2 1.1 copy-done.2
  171.4 4.3 %all-to-all-start.5 = ((bf16[8,768,128]{2,1,0:T(8,128)(2,1)}), bf16[8,768,128]{2,1,0:T(8,128)(2,1)}, u32[]{:S(2)}, u32[]{:S(2)}) async-start(bf16[8,768,128]{2,1,0:T(8,128)(2,1)} %after.15.refs_8_), calls=%async_computation.5 | async-start | bytes 3145728 | tf_op jit(solution)/shard_map/all_to_all | solution.py:477
  175.7 3.0 collective-permute-start.8
  178.7 9.7 %spectral_chunk.6 = bf16[4,8,192,128]{3,2,1,0:T(8,128)(2,1)S(1)} custom-call(s32[2]{0:T(128)S(1)} %get-tuple-element.74.lower_ref, bf16[8,768,128]{2,1,0:T(8,128)(2,1)} %all-to-all-done.1.refs_1_.refs_0_, bf16[8,192,128]{2,1,0:T(8,128)(2,1)} %collective-permute-done.12.refs_1_, bf16[8,192,128]{2,1,0:T(8,128)(2,1)} %collective-permute-done.13.refs_2_, ...), custom_call_target="tpu_custom_call" | custom-call | flops 9999999827968 | bytes 100000000 | tf_op jit(solution)/shard_map/spectral_chunk/pallas_call | solution.py:314
  188.5 1.2 copy-done.3
  189.6 7.1 %all-to-all-done.5.refs_1_.refs_0_.refs_4_ = bf16[8,768,128]{2,1,0:T(8,128)(2,1)} async-done(((bf16[8,768,128]{2,1,0:T(8,128)(2,1)}), bf16[8,768,128]{2,1,0:T(8,128)(2,1)}, u32[]{:S(2)}, u32[]{:S(2)}) %all-to-all-start.5) | async-done | bytes 1572896 | tf_op jit(solution)/shard_map/all_to_all | solution.py:477
  196.7 4.3 %all-to-all-start.6 = ((bf16[8,768,128]{2,1,0:T(8,128)(2,1)}), bf16[8,768,128]{2,1,0:T(8,128)(2,1)}, u32[]{:S(2)}, u32[]{:S(2)}) async-start(bf16[8,768,128]{2,1,0:T(8,128)(2,1)} %after.16.refs_1_), calls=%async_computation.6 | async-start | bytes 3145728 | tf_op jit(solution)/shard_map/all_to_all | solution.py:477
  201.0 2.2 part_slots.9
  203.3 7.0 %collective-permute-start.16 = (bf16[8,192,128]{2,1,0:T(8,128)(2,1)}, bf16[8,192,128]{2,1,0:T(8,128)(2,1)}, u32[]{:S(2)}, u32[]{:S(2)}) collective-permute-start(bf16[8,192,128]{2,1,0:T(8,128)(2,1)} %get-tuple-element.56), channel_id=1, source_target_pairs={{0,4},{1,5},{2,6},{3,7},{4,0},{5,1},{6,2},{7,3},{8,12},{9,13},{10,... | collective-permute-start | bytes 1179656 | tf_op jit(solution)/shard_map/ppermute | solution.py:472
  210.7 1.0 copy-done.14
  211.7 9.8 %spectral_chunk.7 = bf16[4,8,192,128]{3,2,1,0:T(8,128)(2,1)S(1)} custom-call(s32[2]{0:T(128)S(1)} %get-tuple-element.73.lower_ref, bf16[8,768,128]{2,1,0:T(8,128)(2,1)} %all-to-all-done.4.refs_1_.refs_0_, bf16[32,520,768]{2,1,0:T(8,128)(2,1)} %bitcast.88, bf16[1024,256]{1,0:T(8,128)(2,1)S(1)} %bitcast.67, s32[1032,128]{1,0:T(8,128)S(1)} %copy-done.6, ...), custom_call_target="tpu_custom_call" | custom-call | flops 9999999827968 | bytes 100000000 | tf_op jit(solution)/shard_map/spectral_chunk/pallas_call | solution.py:314
  221.5 1.1 copy-done.4
  222.7 4.3 %all-to-all-start.7 = ((bf16[8,768,128]{2,1,0:T(8,128)(2,1)}), bf16[8,768,128]{2,1,0:T(8,128)(2,1)}, u32[]{:S(2)}, u32[]{:S(2)}) async-start(bf16[8,768,128]{2,1,0:T(8,128)(2,1)} %after.17.refs_1_), calls=%async_computation.7 | async-start | bytes 3145728 | tf_op jit(solution)/shard_map/all_to_all | solution.py:477
  227.0 2.3 part_slots.10
  229.3 4.5 %collective-permute-start.17 = (bf16[8,192,128]{2,1,0:T(8,128)(2,1)}, bf16[8,192,128]{2,1,0:T(8,128)(2,1)}, u32[]{:S(2)}, u32[]{:S(2)}) collective-permute-start(bf16[8,192,128]{2,1,0:T(8,128)(2,1)} %get-tuple-element.57), channel_id=1, source_target_pairs={{0,2},{1,3},{2,4},{3,5},{4,6},{5,7},{6,0},{7,1},{8,10},{9,11},{10,... | collective-permute-start | bytes 1179656 | tf_op jit(solution)/shard_map/ppermute | solution.py:472
  233.7 2.0 collective-permute-start.19
  236.3 3.3 %collective-permute-start.18 = (bf16[8,192,128]{2,1,0:T(8,128)(2,1)}, bf16[8,192,128]{2,1,0:T(8,128)(2,1)}, u32[]{:S(2)}, u32[]{:S(2)}) collective-permute-start(bf16[8,192,128]{2,1,0:T(8,128)(2,1)} %get-tuple-element.58.refs_1_), channel_id=1, source_target_pairs={{0,6},{1,7},{2,0},{3,1},{4,2},{5,3},{6,4},{7,5},{8,14},{9,15},{10,... | collective-permute-start | bytes 1179656 | tf_op jit(solution)/shard_map/ppermute | solution.py:472
  239.6 8.5 %all-to-all-done.7.refs_0_.refs_12_ = bf16[8,768,128]{2,1,0:T(8,128)(2,1)} async-done(((bf16[8,768,128]{2,1,0:T(8,128)(2,1)}), bf16[8,768,128]{2,1,0:T(8,128)(2,1)}, u32[]{:S(2)}, u32[]{:S(2)}) %all-to-all-start.7) | async-done | bytes 1572896 | tf_op jit(solution)/shard_map/all_to_all | solution.py:477
  248.0 2.2 part_slots.11
  250.2 4.0 %collective-permute-start.24 = (bf16[8,96,128]{2,1,0:T(8,128)(2,1)}, bf16[8,96,128]{2,1,0:T(8,128)(2,1)S(1)}, u32[]{:S(2)}, u32[]{:S(2)}) collective-permute-start(bf16[8,96,128]{2,1,0:T(8,128)(2,1)} %get-tuple-element.64), channel_id=1, source_target_pairs={{0,6},{1,7},{2,0},{3,1},{4,2},{5,3},{6,4},{7,5},{8,14},{9,15},{10,... | collective-permute-start | bytes 589832 | tf_op jit(solution)/shard_map/ppermute | solution.py:472
  254.2 8.0 %collective-permute-start.25 = (bf16[8,96,128]{2,1,0:T(8,128)(2,1)}, bf16[8,96,128]{2,1,0:T(8,128)(2,1)S(1)}, u32[]{:S(2)}, u32[]{:S(2)}) collective-permute-start(bf16[8,96,128]{2,1,0:T(8,128)(2,1)} %get-tuple-element.65), channel_id=1, source_target_pairs={{0,4},{1,5},{2,6},{3,7},{4,0},{5,1},{6,2},{7,3},{8,12},{9,13},{10,... | collective-permute-start | bytes 589832 | tf_op jit(solution)/shard_map/ppermute | solution.py:472
  262.2 8.9 %collective-permute-done.19.refs_10_ = bf16[8,192,128]{2,1,0:T(8,128)(2,1)} collective-permute-done((bf16[8,192,128]{2,1,0:T(8,128)(2,1)}, bf16[8,192,128]{2,1,0:T(8,128)(2,1)}, u32[]{:S(2)}, u32[]{:S(2)}) %collective-permute-start.19) | collective-permute-done | bytes 393248 | tf_op jit(solution)/shard_map/ppermute | solution.py:472
  271.1 8.6 %collective-permute-start.26 = (bf16[8,96,128]{2,1,0:T(8,128)(2,1)}, bf16[8,96,128]{2,1,0:T(8,128)(2,1)S(1)}, u32[]{:S(2)}, u32[]{:S(2)}) collective-permute-start(bf16[8,96,128]{2,1,0:T(8,128)(2,1)} %get-tuple-element.66), channel_id=1, source_target_pairs={{0,2},{1,3},{2,4},{3,5},{4,6},{5,7},{6,0},{7,1},{8,10},{9,11},{10,... | collective-permute-start | bytes 589832 | tf_op jit(solution)/shard_map/ppermute | solution.py:472
  279.7 2.8 collective-permute-start.21
  282.5 11.7 %collective-permute-start.22 = (bf16[8,96,128]{2,1,0:T(8,128)(2,1)}, bf16[8,96,128]{2,1,0:T(8,128)(2,1)}, u32[]{:S(2)}, u32[]{:S(2)}) collective-permute-start(bf16[8,96,128]{2,1,0:T(8,128)(2,1)} %get-tuple-element.62), channel_id=1, source_target_pairs={{0,4},{1,5},{2,6},{3,7},{4,0},{5,1},{6,2},{7,3},{8,12},{9,13},{10,... | collective-permute-start | bytes 589832 | tf_op jit(solution)/shard_map/ppermute | solution.py:472
  294.3 2.0 collective-permute-start.23
  296.3 10.1 %synthesis_part.2.refs_18_ = bf16[2,4,2,192,1536]{4,3,2,1,0:T(8,128)(2,1)} custom-call(s32[1]{0:T(128)} %bitcast.parity_ref, bf16[8,768,128]{2,1,0:T(8,128)(2,1)} %all-to-all-done.3.refs_1_.refs_0_, bf16[8,192,128]{2,1,0:T(8,128)(2,1)} %collective-permute-done.6.refs_1_, bf16[8,192,128]{2,1,0:T(8,128)(2,1)} %collective-permute-done.7.refs_2_, ...), custom_call_target="tpu_custom_call" | custom-call | flops 9999999827968 | bytes 100000000 | tf_op jit(solution)/shard_map/synthesis_part/pallas_call | solution.py:386
  306.4 6.6 %collective-permute-done.22.refs_14_ = bf16[8,96,128]{2,1,0:T(8,128)(2,1)} collective-permute-done((bf16[8,96,128]{2,1,0:T(8,128)(2,1)}, bf16[8,96,128]{2,1,0:T(8,128)(2,1)}, u32[]{:S(2)}, u32[]{:S(2)}) %collective-permute-start.22) | collective-permute-done | bytes 196640 | tf_op jit(solution)/shard_map/ppermute | solution.py:472
  313.0 10.2 %synthesis_part.3 = bf16[2,4,2,192,1536]{4,3,2,1,0:T(8,128)(2,1)} custom-call(s32[1]{0:T(128)} %bitcast.parity_ref, bf16[8,768,128]{2,1,0:T(8,128)(2,1)} %all-to-all-done.3.refs_1_.refs_0_, bf16[8,192,128]{2,1,0:T(8,128)(2,1)} %collective-permute-done.6.refs_1_, ...), custom_call_target="tpu_custom_call", output_to_operand_aliasing={{}: (19, {})} | custom-call | flops 9999999827968 | bytes 100000000 | tf_op jit(solution)/shard_map/synthesis_part/pallas_call | solution.py:386
  (115 shorter events, 9.9 us)
Async XLA Ops:
  0.0 38.9 %copy-start = (bf16[16,128,128]{2,1,0:T(8,128)(2,1)S(1)}, bf16[16,128,128]{2,1,0:T(8,128)(2,1)}, u32[]{:S(2)}) copy-start(bf16[16,128,128]{2,1,0:T(8,128)(2,1)} %param.9) | copy-start | bytes 1572868
  18.9 0.8 copy-start.9
  19.7 0.8 copy-start.10
  20.5 0.7 copy-start.12
  21.2 26.3 %all-to-all-start = ((bf16[8,768,128]{2,1,0:T(8,128)(2,1)}), bf16[8,768,128]{2,1,0:T(8,128)(2,1)}, u32[]{:S(2)}, u32[]{:S(2)}) async-start(bf16[8,768,128]{2,1,0:T(8,128)(2,1)} %bitcast.14.refs_0_), calls=%async_computation | async-start | bytes 3145728 | tf_op jit(solution)/shard_map/all_to_all | solution.py:477
  26.4 30.2 %collective-permute-start = (bf16[8,192,128]{2,1,0:T(8,128)(2,1)}, bf16[8,192,128]{2,1,0:T(8,128)(2,1)}, u32[]{:S(2)}, u32[]{:S(2)}) collective-permute-start(bf16[8,192,128]{2,1,0:T(8,128)(2,1)} %get-tuple-element.37), channel_id=1, source_target_pairs={{0,2},{1,3},{2,4},{3,5},{4,6},{5,7},{6,0},{7,1},{8,10},{9,11},{10,... | collective-permute-start | bytes 1179656 | tf_op jit(solution)/shard_map/ppermute | solution.py:472
  28.6 29.3 %collective-permute-start.1 = (bf16[8,192,128]{2,1,0:T(8,128)(2,1)}, bf16[8,192,128]{2,1,0:T(8,128)(2,1)}, u32[]{:S(2)}, u32[]{:S(2)}) collective-permute-start(bf16[8,192,128]{2,1,0:T(8,128)(2,1)} %get-tuple-element.38), channel_id=1, source_target_pairs={{0,4},{1,5},{2,6},{3,7},{4,0},{5,1},{6,2},{7,3},{8,12},{9,13},{10,... | collective-permute-start | bytes 1179656 | tf_op jit(solution)/shard_map/ppermute | solution.py:472
  31.2 26.7 %collective-permute-start.2 = (bf16[8,192,128]{2,1,0:T(8,128)(2,1)}, bf16[8,192,128]{2,1,0:T(8,128)(2,1)}, u32[]{:S(2)}, u32[]{:S(2)}) collective-permute-start(bf16[8,192,128]{2,1,0:T(8,128)(2,1)} %get-tuple-element.39), channel_id=1, source_target_pairs={{0,6},{1,7},{2,0},{3,1},{4,2},{5,3},{6,4},{7,5},{8,14},{9,15},{10,... | collective-permute-start | bytes 1179656 | tf_op jit(solution)/shard_map/ppermute | solution.py:472
  33.1 3.7 %copy-start.19 = (s32[256]{0:T(256)S(1)}, s32[256]{0:T(256)}, u32[]{:S(2)}) copy-start(s32[256]{0:T(256)} %param.10) | copy-start | bytes 3076
  33.1 3.8 %copy-start.18 = (s32[512]{0:T(512)S(1)}, s32[512]{0:T(512)}, u32[]{:S(2)}) copy-start(s32[512]{0:T(512)} %param.11) | copy-start | bytes 6148
  35.2 1.6 copy-start.15
  47.5 25.4 %all-to-all-start.1 = ((bf16[8,768,128]{2,1,0:T(8,128)(2,1)}), bf16[8,768,128]{2,1,0:T(8,128)(2,1)}, u32[]{:S(2)}, u32[]{:S(2)}) async-start(bf16[8,768,128]{2,1,0:T(8,128)(2,1)} %after.9.refs_4_.refs_1_), calls=%async_computation.1 | async-start | bytes 3145728 | tf_op jit(solution)/shard_map/all_to_all | solution.py:477
  51.9 63.1 %collective-permute-start.3 = (bf16[8,192,128]{2,1,0:T(8,128)(2,1)}, bf16[8,192,128]{2,1,0:T(8,128)(2,1)}, u32[]{:S(2)}, u32[]{:S(2)}) collective-permute-start(bf16[8,192,128]{2,1,0:T(8,128)(2,1)} %after.11), channel_id=1, source_target_pairs={{0,2},{1,3},{2,4},{3,5},{4,6},{5,7},{6,0},{7,1},{8,10},{9,11},{10,... | collective-permute-start | bytes 1179656 | tf_op jit(solution)/shard_map/ppermute | solution.py:472
  54.0 75.6 %collective-permute-start.4 = (bf16[8,192,128]{2,1,0:T(8,128)(2,1)}, bf16[8,192,128]{2,1,0:T(8,128)(2,1)}, u32[]{:S(2)}, u32[]{:S(2)}) collective-permute-start(bf16[8,192,128]{2,1,0:T(8,128)(2,1)} %after.12), channel_id=1, source_target_pairs={{0,4},{1,5},{2,6},{3,7},{4,0},{5,1},{6,2},{7,3},{8,12},{9,13},{10,... | collective-permute-start | bytes 1179656 | tf_op jit(solution)/shard_map/ppermute | solution.py:472
  56.6 73.0 %collective-permute-start.5 = (bf16[8,192,128]{2,1,0:T(8,128)(2,1)}, bf16[8,192,128]{2,1,0:T(8,128)(2,1)}, u32[]{:S(2)}, u32[]{:S(2)}) collective-permute-start(bf16[8,192,128]{2,1,0:T(8,128)(2,1)} %after.13), channel_id=1, source_target_pairs={{0,6},{1,7},{2,0},{3,1},{4,2},{5,3},{6,4},{7,5},{8,14},{9,15},{10,... | collective-permute-start | bytes 1179656 | tf_op jit(solution)/shard_map/ppermute | solution.py:472
  72.9 25.3 %all-to-all-start.2 = ((bf16[8,768,128]{2,1,0:T(8,128)(2,1)}), bf16[8,768,128]{2,1,0:T(8,128)(2,1)}, u32[]{:S(2)}, u32[]{:S(2)}) async-start(bf16[8,768,128]{2,1,0:T(8,128)(2,1)} %after.10.refs_1_), calls=%async_computation.2 | async-start | bytes 3145728 | tf_op jit(solution)/shard_map/all_to_all | solution.py:477
  77.2 21.0 %copy-start.17 = (s32[520]{0:T(1024)S(1)}, s32[520]{0:T(1024)}, u32[]{:S(2)}) copy-start(s32[520]{0:T(1024)} %pad_add_fusion.2) | copy-start | bytes 6244
  77.2 21.2 %copy-start.16 = (s32[1032]{0:T(1024)S(1)}, s32[1032]{0:T(1024)}, u32[]{:S(2)}) copy-start(s32[1032]{0:T(1024)} %concatenate.14) | copy-start | bytes 12388
  79.5 63.2 %collective-permute-start.10 = (bf16[8,192,128]{2,1,0:T(8,128)(2,1)}, bf16[8,192,128]{2,1,0:T(8,128)(2,1)}, u32[]{:S(2)}, u32[]{:S(2)}) collective-permute-start(bf16[8,192,128]{2,1,0:T(8,128)(2,1)} %get-tuple-element.51), channel_id=1, source_target_pairs={{0,4},{1,5},{2,6},{3,7},{4,0},{5,1},{6,2},{7,3},{8,12},{9,13},{10,... | collective-permute-start | bytes 1179656 | tf_op jit(solution)/shard_map/ppermute | solution.py:472
  91.4 65.8 %collective-permute-start.9 = (bf16[8,192,128]{2,1,0:T(8,128)(2,1)}, bf16[8,192,128]{2,1,0:T(8,128)(2,1)}, u32[]{:S(2)}, u32[]{:S(2)}) collective-permute-start(bf16[8,192,128]{2,1,0:T(8,128)(2,1)} %get-tuple-element.42.refs_5_), channel_id=1, source_target_pairs={{0,2},{1,3},{2,4},{3,5},{4,6},{5,7},{6,0},{7,1},{8,10},{9,11},{10,... | collective-permute-start | bytes 1179656 | tf_op jit(solution)/shard_map/ppermute | solution.py:472
  98.4 12.3 %copy-start.7 = (s32[520,128]{1,0:T(8,128)}, s32[520,128]{1,0:T(8,128)S(1)}, u32[]{:S(2)}) copy-start(s32[520,128]{1,0:T(8,128)S(1)} %broadcast_in_dim.60.refs_4_.refs_7_) | copy-start | bytes 798724
  98.6 12.1 %copy-start.5 = (s32[1032,128]{1,0:T(8,128)}, s32[1032,128]{1,0:T(8,128)S(1)}, u32[]{:S(2)}) copy-start(s32[1032,128]{1,0:T(8,128)S(1)} %broadcast_in_dim.59.refs_3_.refs_6_) | copy-start | bytes 1585156
  98.6 1.2 copy-start.13
  110.7 25.3 %all-to-all-start.3 = ((bf16[8,768,128]{2,1,0:T(8,128)(2,1)}), bf16[8,768,128]{2,1,0:T(8,128)(2,1)}, u32[]{:S(2)}, u32[]{:S(2)}) async-start(bf16[8,768,128]{2,1,0:T(8,128)(2,1)} %bitcast.26.refs_4_), calls=%async_computation.3 | async-start | bytes 3145728 | tf_op jit(solution)/shard_map/all_to_all | solution.py:477
  115.0 42.2 %collective-permute-start.11 = (bf16[8,192,128]{2,1,0:T(8,128)(2,1)}, bf16[8,192,128]{2,1,0:T(8,128)(2,1)}, u32[]{:S(2)}, u32[]{:S(2)}) collective-permute-start(bf16[8,192,128]{2,1,0:T(8,128)(2,1)} %get-tuple-element.52), channel_id=1, source_target_pairs={{0,6},{1,7},{2,0},{3,1},{4,2},{5,3},{6,4},{7,5},{8,14},{9,15},{10,... | collective-permute-start | bytes 1179656 | tf_op jit(solution)/shard_map/ppermute | solution.py:472
  134.3 41.4 %collective-permute-start.13 = (bf16[8,192,128]{2,1,0:T(8,128)(2,1)}, bf16[8,192,128]{2,1,0:T(8,128)(2,1)}, u32[]{:S(2)}, u32[]{:S(2)}) collective-permute-start(bf16[8,192,128]{2,1,0:T(8,128)(2,1)} %get-tuple-element.53), channel_id=1, source_target_pairs={{0,4},{1,5},{2,6},{3,7},{4,0},{5,1},{6,2},{7,3},{8,12},{9,13},{10,... | collective-permute-start | bytes 1179656 | tf_op jit(solution)/shard_map/ppermute | solution.py:472
  134.3 44.4 %collective-permute-start.12 = (bf16[8,192,128]{2,1,0:T(8,128)(2,1)}, bf16[8,192,128]{2,1,0:T(8,128)(2,1)}, u32[]{:S(2)}, u32[]{:S(2)}) collective-permute-start(bf16[8,192,128]{2,1,0:T(8,128)(2,1)} %get-tuple-element.47.refs_2_), channel_id=1, source_target_pairs={{0,2},{1,3},{2,4},{3,5},{4,6},{5,7},{6,0},{7,1},{8,10},{9,11},{10,... | collective-permute-start | bytes 1179656 | tf_op jit(solution)/shard_map/ppermute | solution.py:472
  136.0 35.3 %all-to-all-start.4 = ((bf16[8,768,128]{2,1,0:T(8,128)(2,1)}), bf16[8,768,128]{2,1,0:T(8,128)(2,1)}, u32[]{:S(2)}, u32[]{:S(2)}) async-start(bf16[8,768,128]{2,1,0:T(8,128)(2,1)} %after.14.refs_1_), calls=%async_computation.4 | async-start | bytes 3145728 | tf_op jit(solution)/shard_map/all_to_all | solution.py:477
  140.4 19.1 %copy-start.6 = (s32[1032,128]{1,0:T(8,128)S(1)}, s32[1032,128]{1,0:T(8,128)}, u32[]{:S(2)}) copy-start(s32[1032,128]{1,0:T(8,128)} %copy-done.5) | copy-start | bytes 1585156
  140.4 19.1 %copy-start.8 = (s32[520,128]{1,0:T(8,128)S(1)}, s32[520,128]{1,0:T(8,128)}, u32[]{:S(2)}) copy-start(s32[520,128]{1,0:T(8,128)} %copy-done.7) | copy-start | bytes 798724
  142.7 36.0 %collective-permute-start.14 = (bf16[8,192,128]{2,1,0:T(8,128)(2,1)}, bf16[8,192,128]{2,1,0:T(8,128)(2,1)}, u32[]{:S(2)}, u32[]{:S(2)}) collective-permute-start(bf16[8,192,128]{2,1,0:T(8,128)(2,1)} %get-tuple-element.54), channel_id=1, source_target_pairs={{0,6},{1,7},{2,0},{3,1},{4,2},{5,3},{6,4},{7,5},{8,14},{9,15},{10,... | collective-permute-start | bytes 1179656 | tf_op jit(solution)/shard_map/ppermute | solution.py:472
  157.2 72.0 %collective-permute-start.7 = (bf16[8,192,128]{2,1,0:T(8,128)(2,1)}, bf16[8,192,128]{2,1,0:T(8,128)(2,1)}, u32[]{:S(2)}, u32[]{:S(2)}) collective-permute-start(bf16[8,192,128]{2,1,0:T(8,128)(2,1)} %get-tuple-element.49), channel_id=1, source_target_pairs={{0,4},{1,5},{2,6},{3,7},{4,0},{5,1},{6,2},{7,3},{8,12},{9,13},{10,... | collective-permute-start | bytes 1179656 | tf_op jit(solution)/shard_map/ppermute | solution.py:472
  157.2 78.5 %collective-permute-start.6 = (bf16[8,192,128]{2,1,0:T(8,128)(2,1)}, bf16[8,192,128]{2,1,0:T(8,128)(2,1)}, u32[]{:S(2)}, u32[]{:S(2)}) collective-permute-start(bf16[8,192,128]{2,1,0:T(8,128)(2,1)} %get-tuple-element.48.refs_8_), channel_id=1, source_target_pairs={{0,6},{1,7},{2,0},{3,1},{4,2},{5,3},{6,4},{7,5},{8,14},{9,15},{10,... | collective-permute-start | bytes 1179656 | tf_op jit(solution)/shard_map/ppermute | solution.py:472
  159.5 1.0 copy-start.11
  170.2 1.1 copy-start.2
  171.4 25.4 %all-to-all-start.5 = ((bf16[8,768,128]{2,1,0:T(8,128)(2,1)}), bf16[8,768,128]{2,1,0:T(8,128)(2,1)}, u32[]{:S(2)}, u32[]{:S(2)}) async-start(bf16[8,768,128]{2,1,0:T(8,128)(2,1)} %after.15.refs_8_), calls=%async_computation.5 | async-start | bytes 3145728 | tf_op jit(solution)/shard_map/all_to_all | solution.py:477
  175.7 58.0 %collective-permute-start.8 = (bf16[8,192,128]{2,1,0:T(8,128)(2,1)}, bf16[8,192,128]{2,1,0:T(8,128)(2,1)}, u32[]{:S(2)}, u32[]{:S(2)}) collective-permute-start(bf16[8,192,128]{2,1,0:T(8,128)(2,1)} %get-tuple-element.50), channel_id=1, source_target_pairs={{0,2},{1,3},{2,4},{3,5},{4,6},{5,7},{6,0},{7,1},{8,10},{9,11},{10,... | collective-permute-start | bytes 1179656 | tf_op jit(solution)/shard_map/ppermute | solution.py:472
  188.5 1.2 copy-start.3
  196.7 25.9 %all-to-all-start.6 = ((bf16[8,768,128]{2,1,0:T(8,128)(2,1)}), bf16[8,768,128]{2,1,0:T(8,128)(2,1)}, u32[]{:S(2)}, u32[]{:S(2)}) async-start(bf16[8,768,128]{2,1,0:T(8,128)(2,1)} %after.16.refs_1_), calls=%async_computation.6 | async-start | bytes 3145728 | tf_op jit(solution)/shard_map/all_to_all | solution.py:477
  203.3 33.0 %collective-permute-start.16 = (bf16[8,192,128]{2,1,0:T(8,128)(2,1)}, bf16[8,192,128]{2,1,0:T(8,128)(2,1)}, u32[]{:S(2)}, u32[]{:S(2)}) collective-permute-start(bf16[8,192,128]{2,1,0:T(8,128)(2,1)} %get-tuple-element.56), channel_id=1, source_target_pairs={{0,4},{1,5},{2,6},{3,7},{4,0},{5,1},{6,2},{7,3},{8,12},{9,13},{10,... | collective-permute-start | bytes 1179656 | tf_op jit(solution)/shard_map/ppermute | solution.py:472
  210.3 44.0 %collective-permute-start.15 = (bf16[8,192,128]{2,1,0:T(8,128)(2,1)}, bf16[8,192,128]{2,1,0:T(8,128)(2,1)}, u32[]{:S(2)}, u32[]{:S(2)}) collective-permute-start(bf16[8,192,128]{2,1,0:T(8,128)(2,1)} %get-tuple-element.55.refs_5_), channel_id=1, source_target_pairs={{0,6},{1,7},{2,0},{3,1},{4,2},{5,3},{6,4},{7,5},{8,14},{9,15},{10,... | collective-permute-start | bytes 1179656 | tf_op jit(solution)/shard_map/ppermute | solution.py:472
  210.7 1.0 copy-start.14
  221.5 1.1 copy-start.4
  222.7 25.4 %all-to-all-start.7 = ((bf16[8,768,128]{2,1,0:T(8,128)(2,1)}), bf16[8,768,128]{2,1,0:T(8,128)(2,1)}, u32[]{:S(2)}, u32[]{:S(2)}) async-start(bf16[8,768,128]{2,1,0:T(8,128)(2,1)} %after.17.refs_1_), calls=%async_computation.7 | async-start | bytes 3145728 | tf_op jit(solution)/shard_map/all_to_all | solution.py:477
  229.3 21.0 %collective-permute-start.17 = (bf16[8,192,128]{2,1,0:T(8,128)(2,1)}, bf16[8,192,128]{2,1,0:T(8,128)(2,1)}, u32[]{:S(2)}, u32[]{:S(2)}) collective-permute-start(bf16[8,192,128]{2,1,0:T(8,128)(2,1)} %get-tuple-element.57), channel_id=1, source_target_pairs={{0,2},{1,3},{2,4},{3,5},{4,6},{5,7},{6,0},{7,1},{8,10},{9,11},{10,... | collective-permute-start | bytes 1179656 | tf_op jit(solution)/shard_map/ppermute | solution.py:472
  233.7 37.4 %collective-permute-start.19 = (bf16[8,192,128]{2,1,0:T(8,128)(2,1)}, bf16[8,192,128]{2,1,0:T(8,128)(2,1)}, u32[]{:S(2)}, u32[]{:S(2)}) collective-permute-start(bf16[8,192,128]{2,1,0:T(8,128)(2,1)} %get-tuple-element.59), channel_id=1, source_target_pairs={{0,4},{1,5},{2,6},{3,7},{4,0},{5,1},{6,2},{7,3},{8,12},{9,13},{10,... | collective-permute-start | bytes 1179656 | tf_op jit(solution)/shard_map/ppermute | solution.py:472
  235.7 44.0 %collective-permute-start.20 = (bf16[8,192,128]{2,1,0:T(8,128)(2,1)}, bf16[8,192,128]{2,1,0:T(8,128)(2,1)}, u32[]{:S(2)}, u32[]{:S(2)}) collective-permute-start(bf16[8,192,128]{2,1,0:T(8,128)(2,1)} %get-tuple-element.60), channel_id=1, source_target_pairs={{0,2},{1,3},{2,4},{3,5},{4,6},{5,7},{6,0},{7,1},{8,10},{9,11},{10,... | collective-permute-start | bytes 1179656 | tf_op jit(solution)/shard_map/ppermute | solution.py:472
  236.3 46.2 %collective-permute-start.18 = (bf16[8,192,128]{2,1,0:T(8,128)(2,1)}, bf16[8,192,128]{2,1,0:T(8,128)(2,1)}, u32[]{:S(2)}, u32[]{:S(2)}) collective-permute-start(bf16[8,192,128]{2,1,0:T(8,128)(2,1)} %get-tuple-element.58.refs_1_), channel_id=1, source_target_pairs={{0,6},{1,7},{2,0},{3,1},{4,2},{5,3},{6,4},{7,5},{8,14},{9,15},{10,... | collective-permute-start | bytes 1179656 | tf_op jit(solution)/shard_map/ppermute | solution.py:472
  250.2 44.0 %collective-permute-start.24 = (bf16[8,96,128]{2,1,0:T(8,128)(2,1)}, bf16[8,96,128]{2,1,0:T(8,128)(2,1)S(1)}, u32[]{:S(2)}, u32[]{:S(2)}) collective-permute-start(bf16[8,96,128]{2,1,0:T(8,128)(2,1)} %get-tuple-element.64), channel_id=1, source_target_pairs={{0,6},{1,7},{2,0},{3,1},{4,2},{5,3},{6,4},{7,5},{8,14},{9,15},{10,... | collective-permute-start | bytes 589832 | tf_op jit(solution)/shard_map/ppermute | solution.py:472
  254.2 42.1 %collective-permute-start.25 = (bf16[8,96,128]{2,1,0:T(8,128)(2,1)}, bf16[8,96,128]{2,1,0:T(8,128)(2,1)S(1)}, u32[]{:S(2)}, u32[]{:S(2)}) collective-permute-start(bf16[8,96,128]{2,1,0:T(8,128)(2,1)} %get-tuple-element.65), channel_id=1, source_target_pairs={{0,4},{1,5},{2,6},{3,7},{4,0},{5,1},{6,2},{7,3},{8,12},{9,13},{10,... | collective-permute-start | bytes 589832 | tf_op jit(solution)/shard_map/ppermute | solution.py:472
  271.1 25.2 %collective-permute-start.26 = (bf16[8,96,128]{2,1,0:T(8,128)(2,1)}, bf16[8,96,128]{2,1,0:T(8,128)(2,1)S(1)}, u32[]{:S(2)}, u32[]{:S(2)}) collective-permute-start(bf16[8,96,128]{2,1,0:T(8,128)(2,1)} %get-tuple-element.66), channel_id=1, source_target_pairs={{0,2},{1,3},{2,4},{3,5},{4,6},{5,7},{6,0},{7,1},{8,10},{9,11},{10,... | collective-permute-start | bytes 589832 | tf_op jit(solution)/shard_map/ppermute | solution.py:472
  279.7 26.7 %collective-permute-start.21 = (bf16[8,96,128]{2,1,0:T(8,128)(2,1)}, bf16[8,96,128]{2,1,0:T(8,128)(2,1)}, u32[]{:S(2)}, u32[]{:S(2)}) collective-permute-start(bf16[8,96,128]{2,1,0:T(8,128)(2,1)} %get-tuple-element.61), channel_id=1, source_target_pairs={{0,6},{1,7},{2,0},{3,1},{4,2},{5,3},{6,4},{7,5},{8,14},{9,15},{10,... | collective-permute-start | bytes 589832 | tf_op jit(solution)/shard_map/ppermute | solution.py:472
  282.5 30.5 %collective-permute-start.22 = (bf16[8,96,128]{2,1,0:T(8,128)(2,1)}, bf16[8,96,128]{2,1,0:T(8,128)(2,1)}, u32[]{:S(2)}, u32[]{:S(2)}) collective-permute-start(bf16[8,96,128]{2,1,0:T(8,128)(2,1)} %get-tuple-element.62), channel_id=1, source_target_pairs={{0,4},{1,5},{2,6},{3,7},{4,0},{5,1},{6,2},{7,3},{8,12},{9,13},{10,... | collective-permute-start | bytes 589832 | tf_op jit(solution)/shard_map/ppermute | solution.py:472
  294.3 18.8 %collective-permute-start.23 = (bf16[8,96,128]{2,1,0:T(8,128)(2,1)}, bf16[8,96,128]{2,1,0:T(8,128)(2,1)}, u32[]{:S(2)}, u32[]{:S(2)}) collective-permute-start(bf16[8,96,128]{2,1,0:T(8,128)(2,1)} %get-tuple-element.63), channel_id=1, source_target_pairs={{0,2},{1,3},{2,4},{3,5},{4,6},{5,7},{6,0},{7,1},{8,10},{9,11},{10,... | collective-permute-start | bytes 589832 | tf_op jit(solution)/shard_map/ppermute | solution.py:472
  313.0 10.2 %copy-start.1 = (bf16[16,128,128]{2,1,0:T(8,128)(2,1)S(1)}, bf16[16,128,128]{2,1,0:T(8,128)(2,1)}, u32[]{:S(2)}) copy-start(bf16[16,128,128]{2,1,0:T(8,128)(2,1)} %param.9) | copy-start | bytes 1572868

commit v4 on v3

--- a/solution.py
+++ b/solution.py
@@ -14,7 +14,6 @@
 LANES = 128
 VMEM = 48 * 2**20
 LONG = pl.CostEstimate(flops=10**13, bytes_accessed=10**8, transcendentals=0)
-SHORT = pl.CostEstimate(flops=1, bytes_accessed=1, transcendentals=0)
 SIN = (-1.0 / 39916800, 1.0 / 362880, -1.0 / 5040, 1.0 / 120, -1.0 / 6, 1.0)
 ANYWHERE = pl.BlockSpec(memory_space=pl.ANY)
 
@@ -138,8 +137,8 @@
     return jnp.concatenate(tiles, axis=1).astype(jnp.bfloat16)
 
 
-def fourier_kernel(parity_ref, wave_ref, grid_ref, *refs):
-    out_refs, table_ref = refs[:-1], refs[-1]
+def fourier_kernel(waits, parity_ref, wave_ref, grid_ref, *refs):
+    out_refs, table_ref = refs[waits:-1], refs[-1]
     points = grid_ref.shape[-1]
     rows = sum(ref.shape[0] for ref in out_refs) * ROWS
 
@@ -172,12 +171,12 @@
         start += ref.shape[0]
 
 
-def fourier_all(grid, wave, parity, slots):
+def fourier_some(grid, wave, parity, slots, *ready):
     _, steps, _, lat_rows, points = grid.shape
     columns = wave.shape[0]
     rows = 6 * ROWS
     return pl.pallas_call(
-        fourier_kernel,
+        functools.partial(fourier_kernel, len(ready)),
         out_shape=[jax.ShapeDtypeStruct((n, steps * rows, LANES), jnp.bfloat16) for n in slots],
         grid_spec=pltpu.PrefetchScalarGridSpec(
             num_scalar_prefetch=1,
@@ -185,14 +184,15 @@
             in_specs=[
                 pl.BlockSpec((columns, 1), lambda s, _: (0, 0)),
                 pl.BlockSpec((2, 1, 2, lat_rows, points), lambda s, _: (0, s, 0, 0, 0)),
-            ],
+            ]
+            + [ANYWHERE] * len(ready),
             out_specs=[pl.BlockSpec((n, rows, LANES), lambda s, _: (0, s, 0)) for n in slots],
             scratch_shapes=[pltpu.VMEM((columns, points), jnp.bfloat16)],
         ),
         compiler_params=pltpu.CompilerParams(vmem_limit_bytes=VMEM),
-        cost_estimate=SHORT,
-        name="fourier_all",
-    )(parity, wave, grid)
+        cost_estimate=LONG,
+        name="fourier_some",
+    )(parity, wave, grid, *ready)
 
 
 def table_kernel(wave_ref, *refs):
@@ -301,7 +301,7 @@
 
     @pl.when(pair == pl.num_programs(0) - 1)
     def _():
-        out_ref[...] = out_all[...].astype(jnp.bfloat16).reshape(out_ref.shape)
+        out_ref[...] = out_all[: lats * block, :].astype(jnp.bfloat16).reshape(out_ref.shape)
 
 
 def spectral_chunk(pieces, table, vertical, first, second, lower, chunk, shape, *ready):
@@ -327,8 +327,8 @@
             + [ANYWHERE] * len(ready),
             out_specs=pl.BlockSpec(shape, lambda p, _: (0, 0, 0, 0)),
             scratch_shapes=[
-                pltpu.VMEM((rows, LANES), jnp.float32),
-                pltpu.VMEM((rows, LANES), jnp.float32),
+                pltpu.VMEM((rows + 4 * ROWS, LANES), jnp.float32),
+                pltpu.VMEM((rows + 4 * ROWS, LANES), jnp.float32),
             ],
         ),
         compiler_params=pltpu.CompilerParams(vmem_limit_bytes=VMEM),
@@ -343,9 +343,7 @@
     half = LANES // 2
     whole = pl.ds(pl.multiple_of(half * parity_ref[0], half), LANES)
     rest = pl.ds(pl.multiple_of(LANES * (1 - parity_ref[0]), half), half)
-
-    fields = [ref[...].astype(jnp.float32) for ref in field_refs]
-    fields = jnp.concatenate(fields, axis=0)
+    fields = jnp.concatenate([ref[...].astype(jnp.float32) for ref in field_refs], axis=0)
     for t in range(6):
         tile = fields[:, t * ROWS : (t + 1) * ROWS, :].reshape(-1, LANES)
         lines_ref[t * LANES : (t + 1) * LANES, :] = tile.astype(jnp.bfloat16).T
@@ -376,7 +374,10 @@
         (2, 1, 2, lat_rows, points), lambda s, _: (0, start + s, 0, 0, 0)
     )
     in_specs = [field_spec(*f) for f in fields]
-    in_specs += [pl.BlockSpec((columns, points), lambda s, _: (0, 0)), grid_spec]
+    in_specs += [
+        pl.BlockSpec((columns, points), lambda s, _: (0, 0)),
+        grid_spec,
+    ]
     operands = [f for f, _ in fields] + [table, wind]
     aliases = {}
     if before is not None:
@@ -424,7 +425,7 @@
 
 
 def join_slots(pieces, *ready):
-    plane, rows, _ = pieces[0].shape
+    plane, rows, _ = pieces[-1].shape
     all_rows = len(pieces) * rows
     return pl.pallas_call(
         functools.partial(join_kernel, len(pieces)),
@@ -438,30 +439,30 @@
     )(*pieces, *ready)
 
 
-def part_kernel(layers, parts, *refs):
-    in_ref, out_refs = refs[0], refs[len(refs) - parts * (layers - 1) :]
-    size = in_ref.shape[1] // layers // parts
+def part_kernel(layers, cuts, *refs):
+    in_ref, out_refs = refs[0], refs[len(refs) - len(cuts) * (layers - 1) :]
+    rows = in_ref.shape[1] // layers
     for i, out_ref in enumerate(out_refs):
         p, k = divmod(i, layers - 1)
-        start = ((k + 1) * parts + p) * size
-        out_ref[...] = in_ref[:, start : start + size, :]
-
-
-def part_slots(joined, layers, parts, *ready):
+        start = (k + 1) * rows + cuts[p][0]
+        out_ref[...] = in_ref[:, start : start + cuts[p][1], :]
+
+
+def part_slots(joined, layers, cuts, *ready):
     plane, rows, _ = joined.shape
-    size = rows // layers // parts
-    count = parts * (layers - 1)
+    cuts = cuts or [(0, rows // layers)]
+    sizes = [size for _, size in cuts for _ in range(layers - 1)]
     slots = pl.pallas_call(
-        functools.partial(part_kernel, layers, parts),
-        out_shape=[jax.ShapeDtypeStruct((plane, size, LANES), jnp.bfloat16)] * count,
+        functools.partial(part_kernel, layers, cuts),
+        out_shape=[jax.ShapeDtypeStruct((plane, n, LANES), jnp.bfloat16) for n in sizes],
         grid=(2,),
         in_specs=[pl.BlockSpec((plane // 2, rows, LANES), lambda s: (s, 0, 0))]
         + [ANYWHERE] * len(ready),
-        out_specs=[pl.BlockSpec((plane // 2, size, LANES), lambda s: (s, 0, 0))] * count,
+        out_specs=[pl.BlockSpec((plane // 2, n, LANES), lambda s: (s, 0, 0)) for n in sizes],
         cost_estimate=LONG,
         name="part_slots",
     )(joined, *ready)
-    return [slots[p * (layers - 1) : (p + 1) * (layers - 1)] for p in range(parts)]
+    return [slots[p * (layers - 1) : (p + 1) * (layers - 1)] for p in range(len(cuts))]
 
 
 def turn_along_z(slots, sign):
@@ -532,7 +533,6 @@
     first_pair = (lat * levs + lev) * (slots // 4)
     lower = lax.dynamic_slice(pair_table, (first_pair,), (slots // 4,)).reshape(chunks, pairs)
 
-    parts = 2 if steps % 2 == 0 else 1
     joined_shape = (plane, layers * wire_rows, LANES)
 
     def across(x):
@@ -549,49 +549,52 @@
         x = spectral_chunk(pieces, table, operators, first, second, lower[q], q, shape, *ready)
         return x.reshape(joined_shape)
 
-    rows = [waves[0], waves[1], waves[2].transpose(1, 0, 2), waves[3].transpose(1, 0, 2)]
-    rows = jnp.stack([w.reshape(-1) for w in rows]).reshape(-1, 1)
-    sent = fourier_all(grid, rows, parity, [plane] * (2 * layers) + [plane * layers] * 2)
-    x2, x3 = [x.reshape(joined_shape) for x in sent[2 * layers :]]
+    turned_waves = waves.transpose(0, 2, 1, 3)
+    rows = jnp.stack([waves[0].reshape(-1), turned_waves[2].reshape(-1)]).reshape(-1, 1)
+    sent = fourier_some(grid, rows, parity, [plane] * layers + [plane * layers])
     z0 = along(sent[0], sent[1:layers])
+    x2 = sent[layers].reshape(joined_shape)
+    rows = jnp.stack([turned_waves[1], turned_waves[3]]).reshape(-1, 1)
+    sent = fourier_some(grid, rows, parity, [plane * layers] * 2, x2)
+    x1, x3 = [x.reshape(joined_shape) for x in sent]
     p2 = across(x2)
     rows = jnp.stack([waves[0], waves[2], waves[3], waves[1]]).reshape(-1, 1)
     synthesis = synthesis_rows(rows, points, ROWS * layers * plane, x2)
     x3 = after(x3, p2, synthesis)
     p3 = across(x3)
-    z1 = along(sent[layers], [after(x, x3) for x in sent[layers + 1 : 2 * layers]])
+    z1 = along(x1, part_slots(x1, layers, None, x3)[0])
     j0 = after(join_slots(z0, x3), p3)
     p0 = across(j0)
-    u2 = part_slots(p2, layers, 1, j0)[0]
+    u2 = part_slots(p2, layers, None, j0)[0]
     z2 = along(p2, u2)
     s0 = solve(0, [p0], u2[0])
     r0 = across(s0)
     j1 = join_slots(z1, s0)
-    u3 = part_slots(p3, layers, 1, j1)[0]
+    u3 = part_slots(p3, layers, None, j1)[0]
     z3 = along(p3, u3)
     j1 = after(j1, r0, u3[0])
     p1 = across(j1)
-    b0 = part_slots(r0, layers, 1, j1)[0]
+    b0 = part_slots(r0, layers, None, j1)[0]
     back0 = home(r0, b0)
     s2 = after(solve(2, z2, b0[0]), p1)
     r2 = across(s2)
     s3 = after(solve(3, z3, s2), r2)
     r3 = across(s3)
-    b2 = part_slots(r2, layers, 1, s3)[0]
+    b2 = part_slots(r2, layers, None, s3)[0]
     back2 = home(r2, b2)
     s1 = after(solve(1, [p1], b2[0]), r3)
     r1 = across(s1)
-    b3 = part_slots(r3, layers, 1, s1)[0]
+    b3 = part_slots(r3, layers, None, s1)[0]
     back3 = home(r3, b3)
-    late = [home(r1, part) for part in part_slots(r1, layers, parts, b3[0])]
-    fields = back0 + back2 + back3
+    parts = [(0, steps // 2), (steps // 2, steps // 2)] if steps % 2 == 0 else [(0, steps)]
+    cuts = [(6 * ROWS * first, 6 * ROWS * count) for first, count in parts]
+    late = [home(r1, part) for part in part_slots(r1, layers, cuts, b3[0])]
 
     out = None
-    for i in range(parts):
-        first = i * (steps // parts)
-        here = [(f, first) for f in fields] + [(late[i][0], first)]
-        here += [(f, 0) for f in late[i][1:]]
-        out = synthesis_part(here, synthesis, wind, parity, first, steps // parts, out)
+    for (first, count), part in zip(parts, late):
+        here = [(f, first) for f in [*back0, *back2, *back3, part[0]]]
+        here += [(f, 0) for f in part[1:]]
+        out = synthesis_part(here, synthesis, wind, parity, first, count, out)
     return out.reshape(level_rows, lat_rows, points)
 
 

time: 325 us -> 315 us (0.969)
  starting transfers between devices: 152 us -> 115 us
  waiting for transfers between devices: 54.1 us -> 74.4 us
  Pallas kernels: 96.6 us -> 102 us
    ppermute x27, starting transfers between devices: 117 us -> 79.6 us  [turn_along_z(): moved.append(lax.ppermute(slot, 'lev', pairs))]
    all_to_all x8, waiting for transfers between devices: 38.5 us -> 52.9 us  [exchange_in_plane(): lax.all_to_all(x, ('lat', 'lev'), split_axis=0, concat_axis=0, tiled=True...]
    ppermute x27, waiting for transfers between devices: 15.6 us -> 21.5 us  [turn_along_z(): moved.append(lax.ppermute(slot, 'lev', pairs))]
    pallas_call x7 -> x9, Pallas kernels: 29.2 us -> 34.5 us  [the longest x2 18.7 us: fourier_some(): pl.pallas_call(functools.partial(fourier_kernel, len(ready)), out_shape=[...]
    unnamed x45 -> x58, local copies, waits for them, and re-layouts: 11.4 us -> 11.9 us
  transfers between devices with their start and end apart: 35 -> 35, of which waited for: 9 -> 9; matrix products, arithmetic and copies ran while one was open for 2% -> 2% of each run, Pallas kernels for 22% -> 26%
where the time goes in v4:
time: 315 us; the launch traced here: 314 us
  starting transfers between devices  115 us (37%)
  Pallas kernels  102 us (32%)
  waiting for transfers between devices  74.4 us (24%)
  local copies, waits for them, and re-layouts  18.6 us (6%)
    ppermute x27, starting transfers between devices, turn_along_z(): moved.append(lax.ppermute(slot, 'lev', pairs))  79.6 us
    all_to_all x8, waiting for transfers between devices, exchange_in_plane(): lax.all_to_all(x, ('lat', 'lev'), split_axis=0, concat_axis=0, tiled=True...  52.9 us
    pallas_call x4, Pallas kernels, spectral_chunk(): pl.pallas_call(functools.partial(spectral_kernel, len(pieces)), out_shape...  40.2 us
    all_to_all x8, starting transfers between devices, exchange_in_plane(): lax.all_to_all(x, ('lat', 'lev'), split_axis=0, concat_axis=0, tiled=True...  35.5 us
    ppermute x27, waiting for transfers between devices, turn_along_z(): moved.append(lax.ppermute(slot, 'lev', pairs))  21.5 us
    pallas_call x2, Pallas kernels, synthesis_part(): pl.pallas_call(functools.partial(synthesis_kernel, len(fields)), out_shap...  20.3 us
    pallas_call x2, Pallas kernels, fourier_some(): pl.pallas_call(functools.partial(fourier_kernel, len(ready)), out_shape=[...  18.7 us
    pallas_call x7, Pallas kernels, part_slots(): pl.pallas_call(functools.partial(part_kernel, layers, cuts), out_shape=[j...  15.8 us
  transfers between devices with their start and end apart: 35, of which 9 were waited for; matrix products, arithmetic and copies ran while one was open for 2% of the time, Pallas kernels for 26%

profile of v4, /device:TPU:0, one launch (start us, length us, event | category | flops | bytes accessed | tf_op | source)
XLA Modules:
  0.0 313.6 jit_solution(12543435694102255427)
XLA Ops:
  3.8 9.9 %fourier_some.2 = (bf16[8,192,128]{2,1,0:T(8,128)(2,1)S(1)}, bf16[8,192,128]{2,1,0:T(8,128)(2,1)}, bf16[8,192,128]{2,1,0:T(8,128)(2,1)}, bf16[8,192,128]{2,1,0:T(8,128)(2,1)}, bf16[32,192,128]{2,1,0:T(8,128)(2,1)}) custom-call(s32[1]{0:T(128)} %bitcast.parity_ref, s32[512,1]{1,0:T(8,128)S(1)} %bitcast.66, bf16[2,4,2,192,1536]{4,3,2,1,0:T(8,128)(2,1)} %bitcast.86), custom_call_target="tpu_custom_call" | custom-call | flops 9999999827968 | bytes 100000000 | tf_op jit(solution)/shard_map/fourier_some/pallas_call | solution.py:178
  14.5 5.3 %all-to-all-start = ((bf16[8,768,128]{2,1,0:T(8,128)(2,1)}), bf16[8,768,128]{2,1,0:T(8,128)(2,1)}, u32[]{:S(2)}, u32[]{:S(2)}) async-start(bf16[8,768,128]{2,1,0:T(8,128)(2,1)} %bitcast.9.refs_0_), calls=%async_computation | async-start | bytes 3145728 | tf_op jit(solution)/shard_map/all_to_all | solution.py:478
  19.8 2.2 collective-permute-start
  22.0 2.6 collective-permute-start.1
  24.6 1.3 collective-permute-start.2
  27.0 2.1 synthesis_rows.1.refs_2_.refs_16_
  29.1 1.6 copy-done.14
  30.7 8.8 %fourier_some.3 = (bf16[32,192,128]{2,1,0:T(8,128)(2,1)S(1)}, bf16[32,192,128]{2,1,0:T(8,128)(2,1)S(1)}) custom-call(s32[1]{0:T(128)} %bitcast.parity_ref, s32[512,1]{1,0:T(8,128)S(1)} %reshape.140.wave_ref, bf16[2,4,2,192,1536]{4,3,2,1,0:T(8,128)(2,1)} %bitcast.87, bf16[8,768,128]{2,1,0:T(8,128)(2,1)} %bitcast.9.refs_0_), custom_call_target="tpu_custom_call" | custom-call | flops 9999999827968 | bytes 100000000 | tf_op jit(solution)/shard_map/fourier_some/pallas_call | solution.py:178
  39.5 1.2 copy-done.2
  40.7 1.1 copy-done.13
  42.5 1.2 concatenate.14
  45.7 1.3 pad_add_fusion.3
  47.0 4.3 %all-to-all-start.1 = ((bf16[8,768,128]{2,1,0:T(8,128)(2,1)}), bf16[8,768,128]{2,1,0:T(8,128)(2,1)}, u32[]{:S(2)}, u32[]{:S(2)}) async-start(bf16[8,768,128]{2,1,0:T(8,128)(2,1)} %after.6.refs_4_.refs_1_), calls=%async_computation.1 | async-start | bytes 3145728 | tf_op jit(solution)/shard_map/all_to_all | solution.py:478
  51.3 2.3 part_slots.8
  54.6 2.8 collective-permute-start.5
  57.4 2.4 join_slots.2.refs_0_
  59.8 12.5 %all-to-all-done.1.refs_1_.refs_0_ = bf16[8,768,128]{2,1,0:T(8,128)(2,1)} async-done(((bf16[8,768,128]{2,1,0:T(8,128)(2,1)}), bf16[8,768,128]{2,1,0:T(8,128)(2,1)}, u32[]{:S(2)}, u32[]{:S(2)}) %all-to-all-start.1) | async-done | bytes 1572896 | tf_op jit(solution)/shard_map/all_to_all | solution.py:478
  72.3 4.3 %all-to-all-start.2 = ((bf16[8,768,128]{2,1,0:T(8,128)(2,1)}), bf16[8,768,128]{2,1,0:T(8,128)(2,1)}, u32[]{:S(2)}, u32[]{:S(2)}) async-start(bf16[8,768,128]{2,1,0:T(8,128)(2,1)} %after.7.refs_1_), calls=%async_computation.2 | async-start | bytes 3145728 | tf_op jit(solution)/shard_map/all_to_all | solution.py:478
  76.7 2.3 part_slots.7
  78.9 5.7 %collective-permute-start.10 = (bf16[8,192,128]{2,1,0:T(8,128)(2,1)}, bf16[8,192,128]{2,1,0:T(8,128)(2,1)}, u32[]{:S(2)}, u32[]{:S(2)}) collective-permute-start(bf16[8,192,128]{2,1,0:T(8,128)(2,1)} %get-tuple-element.51), channel_id=1, source_target_pairs={{0,4},{1,5},{2,6},{3,7},{4,0},{5,1},{6,2},{7,3},{8,12},{9,13},{10,... | collective-permute-start | bytes 1179656 | tf_op jit(solution)/shard_map/ppermute | solution.py:473
  84.6 1.2 collective-permute-start.9
  85.8 11.8 %all-to-all-done.2.refs_0_ = bf16[8,768,128]{2,1,0:T(8,128)(2,1)} async-done(((bf16[8,768,128]{2,1,0:T(8,128)(2,1)}), bf16[8,768,128]{2,1,0:T(8,128)(2,1)}, u32[]{:S(2)}, u32[]{:S(2)}) %all-to-all-start.2) | async-done | bytes 1572896 | tf_op jit(solution)/shard_map/all_to_all | solution.py:478
  98.1 1.2 copy-done.11
  99.2 10.9 %spectral_chunk.4 = bf16[4,8,192,128]{3,2,1,0:T(8,128)(2,1)} custom-call(s32[2]{0:T(128)S(1)} %get-tuple-element.79.lower_ref, bf16[8,768,128]{2,1,0:T(8,128)(2,1)} %all-to-all-done.2.refs_0_, bf16[32,520,768]{2,1,0:T(8,128)(2,1)} %bitcast.82, bf16[1024,256]{1,0:T(8,128)(2,1)S(1)} %bitcast.62, s32[1032,128]{1,0:T(8,128)S(1)} %broadcast_in_dim.53.refs_3_.refs_6_, ...), custom_call_target="tpu_custom_call" | custom-call | flops 9999999827968 | bytes 100000000 | tf_op jit(solution)/shard_map/spectral_chunk/pallas_call | solution.py:314
  110.2 4.3 %all-to-all-start.3 = ((bf16[8,768,128]{2,1,0:T(8,128)(2,1)}), bf16[8,768,128]{2,1,0:T(8,128)(2,1)}, u32[]{:S(2)}, u32[]{:S(2)}) async-start(bf16[8,768,128]{2,1,0:T(8,128)(2,1)} %bitcast.25.refs_4_), calls=%async_computation.3 | async-start | bytes 3145728 | tf_op jit(solution)/shard_map/all_to_all | solution.py:478
  115.0 2.4 join_slots.3.refs_1_.refs_0_
  117.4 2.2 part_slots.9
  119.7 7.9 %collective-permute-start.13 = (bf16[8,192,128]{2,1,0:T(8,128)(2,1)}, bf16[8,192,128]{2,1,0:T(8,128)(2,1)}, u32[]{:S(2)}, u32[]{:S(2)}) collective-permute-start(bf16[8,192,128]{2,1,0:T(8,128)(2,1)} %get-tuple-element.53), channel_id=1, source_target_pairs={{0,4},{1,5},{2,6},{3,7},{4,0},{5,1},{6,2},{7,3},{8,12},{9,13},{10,... | collective-permute-start | bytes 1179656 | tf_op jit(solution)/shard_map/ppermute | solution.py:473
  127.5 8.0 %all-to-all-done.3.refs_1_.refs_0_ = bf16[8,768,128]{2,1,0:T(8,128)(2,1)} async-done(((bf16[8,768,128]{2,1,0:T(8,128)(2,1)}), bf16[8,768,128]{2,1,0:T(8,128)(2,1)}, u32[]{:S(2)}, u32[]{:S(2)}) %all-to-all-start.3) | async-done | bytes 1572896 | tf_op jit(solution)/shard_map/all_to_all | solution.py:478
  135.5 4.3 %all-to-all-start.4 = ((bf16[8,768,128]{2,1,0:T(8,128)(2,1)}), bf16[8,768,128]{2,1,0:T(8,128)(2,1)}, u32[]{:S(2)}, u32[]{:S(2)}) async-start(bf16[8,768,128]{2,1,0:T(8,128)(2,1)} %after.8.refs_1_), calls=%async_computation.4 | async-start | bytes 3145728 | tf_op jit(solution)/shard_map/all_to_all | solution.py:478
  139.9 2.3 part_slots.10
  142.6 7.9 %collective-permute-start.7 = (bf16[8,192,128]{2,1,0:T(8,128)(2,1)}, bf16[8,192,128]{2,1,0:T(8,128)(2,1)}, u32[]{:S(2)}, u32[]{:S(2)}) collective-permute-start(bf16[8,192,128]{2,1,0:T(8,128)(2,1)} %get-tuple-element.49), channel_id=1, source_target_pairs={{0,4},{1,5},{2,6},{3,7},{4,0},{5,1},{6,2},{7,3},{8,12},{9,13},{10,... | collective-permute-start | bytes 1179656 | tf_op jit(solution)/shard_map/ppermute | solution.py:473
  150.5 2.4 collective-permute-start.6
  153.9 9.8 %spectral_chunk.5 = bf16[4,8,192,128]{3,2,1,0:T(8,128)(2,1)S(1)} custom-call(s32[2]{0:T(128)S(1)} %get-tuple-element.78.lower_ref, bf16[8,768,128]{2,1,0:T(8,128)(2,1)} %all-to-all-done.refs_1_.refs_0_, bf16[8,192,128]{2,1,0:T(8,128)(2,1)} %collective-permute-done.9.refs_1_, bf16[8,192,128]{2,1,0:T(8,128)(2,1)} %collective-permute-done.10.refs_2_, ...), custom_call_target="tpu_custom_call" | custom-call | flops 9999999827968 | bytes 100000000 | tf_op jit(solution)/shard_map/spectral_chunk/pallas_call | solution.py:314
  163.7 1.1 copy-done.3
  164.8 4.3 %all-to-all-start.5 = ((bf16[8,768,128]{2,1,0:T(8,128)(2,1)}), bf16[8,768,128]{2,1,0:T(8,128)(2,1)}, u32[]{:S(2)}, u32[]{:S(2)}) async-start(bf16[8,768,128]{2,1,0:T(8,128)(2,1)} %after.9.refs_8_), calls=%async_computation.5 | async-start | bytes 3145728 | tf_op jit(solution)/shard_map/all_to_all | solution.py:478
  169.2 3.0 collective-permute-start.8
  172.1 9.8 %spectral_chunk.6 = bf16[4,8,192,128]{3,2,1,0:T(8,128)(2,1)S(1)} custom-call(s32[2]{0:T(128)S(1)} %get-tuple-element.77.lower_ref, bf16[8,768,128]{2,1,0:T(8,128)(2,1)} %all-to-all-done.1.refs_1_.refs_0_, bf16[8,192,128]{2,1,0:T(8,128)(2,1)} %collective-permute-done.12.refs_1_, bf16[8,192,128]{2,1,0:T(8,128)(2,1)} %collective-permute-done.13.refs_2_, ...), custom_call_target="tpu_custom_call" | custom-call | flops 9999999827968 | bytes 100000000 | tf_op jit(solution)/shard_map/spectral_chunk/pallas_call | solution.py:314
  181.9 1.1 copy-done.4
  183.1 7.1 %all-to-all-done.5.refs_1_.refs_0_.refs_4_ = bf16[8,768,128]{2,1,0:T(8,128)(2,1)} async-done(((bf16[8,768,128]{2,1,0:T(8,128)(2,1)}), bf16[8,768,128]{2,1,0:T(8,128)(2,1)}, u32[]{:S(2)}, u32[]{:S(2)}) %all-to-all-start.5) | async-done | bytes 1572896 | tf_op jit(solution)/shard_map/all_to_all | solution.py:478
  190.2 4.3 %all-to-all-start.6 = ((bf16[8,768,128]{2,1,0:T(8,128)(2,1)}), bf16[8,768,128]{2,1,0:T(8,128)(2,1)}, u32[]{:S(2)}, u32[]{:S(2)}) async-start(bf16[8,768,128]{2,1,0:T(8,128)(2,1)} %after.10.refs_1_), calls=%async_computation.6 | async-start | bytes 3145728 | tf_op jit(solution)/shard_map/all_to_all | solution.py:478
  194.5 2.2 part_slots.11
  196.7 1.7 collective-permute-start.16
  198.4 3.6 %collective-permute-start.15 = (bf16[8,192,128]{2,1,0:T(8,128)(2,1)}, bf16[8,192,128]{2,1,0:T(8,128)(2,1)}, u32[]{:S(2)}, u32[]{:S(2)}) collective-permute-start(bf16[8,192,128]{2,1,0:T(8,128)(2,1)} %get-tuple-element.55.refs_5_), channel_id=1, source_target_pairs={{0,6},{1,7},{2,0},{3,1},{4,2},{5,3},{6,4},{7,5},{8,14},{9,15},{10,... | collective-permute-start | bytes 1179656 | tf_op jit(solution)/shard_map/ppermute | solution.py:473
  202.0 1.0 copy-done.12
  203.1 9.8 %spectral_chunk.7 = bf16[4,8,192,128]{3,2,1,0:T(8,128)(2,1)S(1)} custom-call(s32[2]{0:T(128)S(1)} %get-tuple-element.76.lower_ref, bf16[8,768,128]{2,1,0:T(8,128)(2,1)} %all-to-all-done.4.refs_1_.refs_0_, bf16[32,520,768]{2,1,0:T(8,128)(2,1)} %bitcast.85, bf16[1024,256]{1,0:T(8,128)(2,1)S(1)} %bitcast.65, s32[1032,128]{1,0:T(8,128)S(1)} %copy-done.7, ...), custom_call_target="tpu_custom_call" | custom-call | flops 9999999827968 | bytes 100000000 | tf_op jit(solution)/shard_map/spectral_chunk/pallas_call | solution.py:314
  212.9 1.1 copy-done.5
  214.0 1.5 all-to-all-done.6.refs_1_.refs_0_.refs_8_
  215.5 4.3 %all-to-all-start.7 = ((bf16[8,768,128]{2,1,0:T(8,128)(2,1)}), bf16[8,768,128]{2,1,0:T(8,128)(2,1)}, u32[]{:S(2)}, u32[]{:S(2)}) async-start(bf16[8,768,128]{2,1,0:T(8,128)(2,1)} %after.11.refs_1_), calls=%async_computation.7 | async-start | bytes 3145728 | tf_op jit(solution)/shard_map/all_to_all | solution.py:478
  219.9 2.2 part_slots.12
  222.1 2.9 collective-permute-start.17
  225.1 1.5 collective-permute-start.20
  226.5 2.4 collective-permute-start.18
  229.0 11.9 %all-to-all-done.7.refs_0_.refs_12_ = bf16[8,768,128]{2,1,0:T(8,128)(2,1)} async-done(((bf16[8,768,128]{2,1,0:T(8,128)(2,1)}), bf16[8,768,128]{2,1,0:T(8,128)(2,1)}, u32[]{:S(2)}, u32[]{:S(2)}) %all-to-all-start.7) | async-done | bytes 1572896 | tf_op jit(solution)/shard_map/all_to_all | solution.py:478
  240.9 2.2 part_slots.13
  243.2 4.4 %collective-permute-start.25 = (bf16[8,96,128]{2,1,0:T(8,128)(2,1)}, bf16[8,96,128]{2,1,0:T(8,128)(2,1)S(1)}, u32[]{:S(2)}, u32[]{:S(2)}) collective-permute-start(bf16[8,96,128]{2,1,0:T(8,128)(2,1)} %get-tuple-element.65), channel_id=1, source_target_pairs={{0,4},{1,5},{2,6},{3,7},{4,0},{5,1},{6,2},{7,3},{8,12},{9,13},{10,... | collective-permute-start | bytes 589832 | tf_op jit(solution)/shard_map/ppermute | solution.py:473
  247.5 13.5 %collective-permute-done.19.refs_10_ = bf16[8,192,128]{2,1,0:T(8,128)(2,1)} collective-permute-done((bf16[8,192,128]{2,1,0:T(8,128)(2,1)}, bf16[8,192,128]{2,1,0:T(8,128)(2,1)}, u32[]{:S(2)}, u32[]{:S(2)}) %collective-permute-start.19) | collective-permute-done | bytes 393248 | tf_op jit(solution)/shard_map/ppermute | solution.py:473
  261.1 3.8 %collective-permute-start.21 = (bf16[8,96,128]{2,1,0:T(8,128)(2,1)}, bf16[8,96,128]{2,1,0:T(8,128)(2,1)}, u32[]{:S(2)}, u32[]{:S(2)}) collective-permute-start(bf16[8,96,128]{2,1,0:T(8,128)(2,1)} %get-tuple-element.61), channel_id=1, source_target_pairs={{0,6},{1,7},{2,0},{3,1},{4,2},{5,3},{6,4},{7,5},{8,14},{9,15},{10,... | collective-permute-start | bytes 589832 | tf_op jit(solution)/shard_map/ppermute | solution.py:473
  264.9 18.2 %collective-permute-start.22 = (bf16[8,96,128]{2,1,0:T(8,128)(2,1)}, bf16[8,96,128]{2,1,0:T(8,128)(2,1)}, u32[]{:S(2)}, u32[]{:S(2)}) collective-permute-start(bf16[8,96,128]{2,1,0:T(8,128)(2,1)} %get-tuple-element.62), channel_id=1, source_target_pairs={{0,4},{1,5},{2,6},{3,7},{4,0},{5,1},{6,2},{7,3},{8,12},{9,13},{10,... | collective-permute-start | bytes 589832 | tf_op jit(solution)/shard_map/ppermute | solution.py:473
  283.2 2.0 collective-permute-start.23
  285.2 1.1 collective-permute-done.25.refs_14_
  286.3 10.1 %synthesis_part.2.refs_18_ = bf16[2,4,2,192,1536]{4,3,2,1,0:T(8,128)(2,1)} custom-call(s32[1]{0:T(128)} %bitcast.parity_ref, bf16[8,768,128]{2,1,0:T(8,128)(2,1)} %all-to-all-done.3.refs_1_.refs_0_, bf16[8,192,128]{2,1,0:T(8,128)(2,1)} %collective-permute-done.6.refs_1_, bf16[8,192,128]{2,1,0:T(8,128)(2,1)} %collective-permute-done.7.refs_2_, ...), custom_call_target="tpu_custom_call" | custom-call | flops 9999999827968 | bytes 100000000 | tf_op jit(solution)/shard_map/synthesis_part/pallas_call | solution.py:387
  296.4 6.8 %collective-permute-done.22.refs_14_ = bf16[8,96,128]{2,1,0:T(8,128)(2,1)} collective-permute-done((bf16[8,96,128]{2,1,0:T(8,128)(2,1)}, bf16[8,96,128]{2,1,0:T(8,128)(2,1)}, u32[]{:S(2)}, u32[]{:S(2)}) %collective-permute-start.22) | collective-permute-done | bytes 196640 | tf_op jit(solution)/shard_map/ppermute | solution.py:473
  303.2 10.2 %synthesis_part.3 = bf16[2,4,2,192,1536]{4,3,2,1,0:T(8,128)(2,1)} custom-call(s32[1]{0:T(128)} %bitcast.parity_ref, bf16[8,768,128]{2,1,0:T(8,128)(2,1)} %all-to-all-done.3.refs_1_.refs_0_, bf16[8,192,128]{2,1,0:T(8,128)(2,1)} %collective-permute-done.6.refs_1_, ...), custom_call_target="tpu_custom_call", output_to_operand_aliasing={{}: (19, {})} | custom-call | flops 9999999827968 | bytes 100000000 | tf_op jit(solution)/shard_map/synthesis_part/pallas_call | solution.py:387
  (130 shorter events, 11.6 us)
Async XLA Ops:
  0.0 43.9 %copy-start = (bf16[16,128,128]{2,1,0:T(8,128)(2,1)S(1)}, bf16[16,128,128]{2,1,0:T(8,128)(2,1)}, u32[]{:S(2)}) copy-start(bf16[16,128,128]{2,1,0:T(8,128)(2,1)} %param.9) | copy-start | bytes 1572868
  2.1 1.5 copy-start.16
  13.7 0.8 copy-start.15
  14.5 11.5 %copy-start.17 = (s32[1,4,4,2,2,2]{1,0,4,3,2,5:T(1,128)S(1)}, s32[1,4,4,2,2,2]{1,0,4,3,2,5:T(1,128)}, u32[]{:S(2)}) copy-start(s32[1,4,4,2,2,2]{1,0,4,3,2,5:T(1,128)} %copy-done.16) | copy-start | bytes 1540
  14.5 11.5 %copy-start.22 = (s32[1,4,4,2,2,2]{1,0,4,3,2,5:T(1,128)S(1)}, s32[1,4,4,2,2,2]{1,0,4,3,2,5:T(1,128)}, u32[]{:S(2)}) copy-start(s32[1,4,4,2,2,2]{1,0,4,3,2,5:T(1,128)} %get-tuple-element.70) | copy-start | bytes 1540
  14.5 11.5 %copy-start.21 = (s32[1,4,4,2,2,2]{1,0,4,3,2,5:T(1,128)S(1)}, s32[1,4,4,2,2,2]{1,0,4,3,2,5:T(1,128)}, u32[]{:S(2)}) copy-start(s32[1,4,4,2,2,2]{1,0,4,3,2,5:T(1,128)} %get-tuple-element.72) | copy-start | bytes 1540
  14.5 11.6 %copy-start.20 = (s32[1,4,4,2,2,2]{1,0,4,3,2,5:T(1,128)S(1)}, s32[1,4,4,2,2,2]{1,0,4,3,2,5:T(1,128)}, u32[]{:S(2)}) copy-start(s32[1,4,4,2,2,2]{1,0,4,3,2,5:T(1,128)} %get-tuple-element.73) | copy-start | bytes 1540
  14.5 11.9 %copy-start.18 = (s32[1,8,4,8]{2,3,1,0:T(8,128)S(1)}, s32[1,8,4,8]{2,3,1,0:T(8,128)}, u32[]{:S(2)}) copy-start(s32[1,8,4,8]{2,3,1,0:T(8,128)} %get-tuple-element.67) | copy-start | bytes 3076
  14.5 11.9 %copy-start.19 = (s32[1,8,4,8]{2,3,1,0:T(8,128)S(1)}, s32[1,8,4,8]{2,3,1,0:T(8,128)}, u32[]{:S(2)}) copy-start(s32[1,8,4,8]{2,3,1,0:T(8,128)} %get-tuple-element.68) | copy-start | bytes 3076
  14.5 32.5 %all-to-all-start = ((bf16[8,768,128]{2,1,0:T(8,128)(2,1)}), bf16[8,768,128]{2,1,0:T(8,128)(2,1)}, u32[]{:S(2)}, u32[]{:S(2)}) async-start(bf16[8,768,128]{2,1,0:T(8,128)(2,1)} %bitcast.9.refs_0_), calls=%async_computation | async-start | bytes 3145728 | tf_op jit(solution)/shard_map/all_to_all | solution.py:478
  19.8 34.8 %collective-permute-start = (bf16[8,192,128]{2,1,0:T(8,128)(2,1)}, bf16[8,192,128]{2,1,0:T(8,128)(2,1)}, u32[]{:S(2)}, u32[]{:S(2)}) collective-permute-start(bf16[8,192,128]{2,1,0:T(8,128)(2,1)} %get-tuple-element.37), channel_id=1, source_target_pairs={{0,2},{1,3},{2,4},{3,5},{4,6},{5,7},{6,0},{7,1},{8,10},{9,11},{10,... | collective-permute-start | bytes 1179656 | tf_op jit(solution)/shard_map/ppermute | solution.py:473
  22.0 35.4 %collective-permute-start.1 = (bf16[8,192,128]{2,1,0:T(8,128)(2,1)}, bf16[8,192,128]{2,1,0:T(8,128)(2,1)}, u32[]{:S(2)}, u32[]{:S(2)}) collective-permute-start(bf16[8,192,128]{2,1,0:T(8,128)(2,1)} %get-tuple-element.38), channel_id=1, source_target_pairs={{0,4},{1,5},{2,6},{3,7},{4,0},{5,1},{6,2},{7,3},{8,12},{9,13},{10,... | collective-permute-start | bytes 1179656 | tf_op jit(solution)/shard_map/ppermute | solution.py:473
  24.6 32.8 %collective-permute-start.2 = (bf16[8,192,128]{2,1,0:T(8,128)(2,1)}, bf16[8,192,128]{2,1,0:T(8,128)(2,1)}, u32[]{:S(2)}, u32[]{:S(2)}) collective-permute-start(bf16[8,192,128]{2,1,0:T(8,128)(2,1)} %get-tuple-element.39), channel_id=1, source_target_pairs={{0,6},{1,7},{2,0},{3,1},{4,2},{5,3},{6,4},{7,5},{8,14},{9,15},{10,... | collective-permute-start | bytes 1179656 | tf_op jit(solution)/shard_map/ppermute | solution.py:473
  29.0 1.6 copy-start.14
  30.7 11.2 %copy-start.26 = (s32[256]{0:T(256)S(1)}, s32[256]{0:T(256)}, u32[]{:S(2)}) copy-start(s32[256]{0:T(256)} %param.10) | copy-start | bytes 3076
  30.7 11.3 %copy-start.25 = (s32[512]{0:T(512)S(1)}, s32[512]{0:T(512)}, u32[]{:S(2)}) copy-start(s32[512]{0:T(512)} %param.11) | copy-start | bytes 6148
  39.5 1.2 copy-start.2
  40.7 1.1 copy-start.13
  47.0 25.3 %all-to-all-start.1 = ((bf16[8,768,128]{2,1,0:T(8,128)(2,1)}), bf16[8,768,128]{2,1,0:T(8,128)(2,1)}, u32[]{:S(2)}, u32[]{:S(2)}) async-start(bf16[8,768,128]{2,1,0:T(8,128)(2,1)} %after.6.refs_4_.refs_1_), calls=%async_computation.1 | async-start | bytes 3145728 | tf_op jit(solution)/shard_map/all_to_all | solution.py:478
  53.6 60.9 %collective-permute-start.3 = (bf16[8,192,128]{2,1,0:T(8,128)(2,1)}, bf16[8,192,128]{2,1,0:T(8,128)(2,1)}, u32[]{:S(2)}, u32[]{:S(2)}) collective-permute-start(bf16[8,192,128]{2,1,0:T(8,128)(2,1)} %get-tuple-element.44), channel_id=1, source_target_pairs={{0,2},{1,3},{2,4},{3,5},{4,6},{5,7},{6,0},{7,1},{8,10},{9,11},{10,... | collective-permute-start | bytes 1179656 | tf_op jit(solution)/shard_map/ppermute | solution.py:473
  54.3 60.7 %collective-permute-start.4 = (bf16[8,192,128]{2,1,0:T(8,128)(2,1)}, bf16[8,192,128]{2,1,0:T(8,128)(2,1)}, u32[]{:S(2)}, u32[]{:S(2)}) collective-permute-start(bf16[8,192,128]{2,1,0:T(8,128)(2,1)} %get-tuple-element.45), channel_id=1, source_target_pairs={{0,4},{1,5},{2,6},{3,7},{4,0},{5,1},{6,2},{7,3},{8,12},{9,13},{10,... | collective-permute-start | bytes 1179656 | tf_op jit(solution)/shard_map/ppermute | solution.py:473
  54.6 60.4 %collective-permute-start.5 = (bf16[8,192,128]{2,1,0:T(8,128)(2,1)}, bf16[8,192,128]{2,1,0:T(8,128)(2,1)}, u32[]{:S(2)}, u32[]{:S(2)}) collective-permute-start(bf16[8,192,128]{2,1,0:T(8,128)(2,1)} %get-tuple-element.46), channel_id=1, source_target_pairs={{0,6},{1,7},{2,0},{3,1},{4,2},{5,3},{6,4},{7,5},{8,14},{9,15},{10,... | collective-permute-start | bytes 1179656 | tf_op jit(solution)/shard_map/ppermute | solution.py:473
  72.3 25.3 %all-to-all-start.2 = ((bf16[8,768,128]{2,1,0:T(8,128)(2,1)}), bf16[8,768,128]{2,1,0:T(8,128)(2,1)}, u32[]{:S(2)}, u32[]{:S(2)}) async-start(bf16[8,768,128]{2,1,0:T(8,128)(2,1)} %after.7.refs_1_), calls=%async_computation.2 | async-start | bytes 3145728 | tf_op jit(solution)/shard_map/all_to_all | solution.py:478
  76.6 21.0 %copy-start.24 = (s32[520]{0:T(1024)S(1)}, s32[520]{0:T(1024)}, u32[]{:S(2)}) copy-start(s32[520]{0:T(1024)} %pad_add_fusion.3) | copy-start | bytes 6244
  76.7 21.2 %copy-start.23 = (s32[1032]{0:T(1024)S(1)}, s32[1032]{0:T(1024)}, u32[]{:S(2)}) copy-start(s32[1032]{0:T(1024)} %concatenate.14) | copy-start | bytes 12388
  78.9 63.2 %collective-permute-start.10 = (bf16[8,192,128]{2,1,0:T(8,128)(2,1)}, bf16[8,192,128]{2,1,0:T(8,128)(2,1)}, u32[]{:S(2)}, u32[]{:S(2)}) collective-permute-start(bf16[8,192,128]{2,1,0:T(8,128)(2,1)} %get-tuple-element.51), channel_id=1, source_target_pairs={{0,4},{1,5},{2,6},{3,7},{4,0},{5,1},{6,2},{7,3},{8,12},{9,13},{10,... | collective-permute-start | bytes 1179656 | tf_op jit(solution)/shard_map/ppermute | solution.py:473
  84.6 65.9 %collective-permute-start.9 = (bf16[8,192,128]{2,1,0:T(8,128)(2,1)}, bf16[8,192,128]{2,1,0:T(8,128)(2,1)}, u32[]{:S(2)}, u32[]{:S(2)}) collective-permute-start(bf16[8,192,128]{2,1,0:T(8,128)(2,1)} %get-tuple-element.42.refs_5_), channel_id=1, source_target_pairs={{0,2},{1,3},{2,4},{3,5},{4,6},{5,7},{6,0},{7,1},{8,10},{9,11},{10,... | collective-permute-start | bytes 1179656 | tf_op jit(solution)/shard_map/ppermute | solution.py:473
  97.8 12.3 %copy-start.8 = (s32[520,128]{1,0:T(8,128)}, s32[520,128]{1,0:T(8,128)S(1)}, u32[]{:S(2)}) copy-start(s32[520,128]{1,0:T(8,128)S(1)} %broadcast_in_dim.54.refs_4_.refs_7_) | copy-start | bytes 798724
  98.0 12.1 %copy-start.6 = (s32[1032,128]{1,0:T(8,128)}, s32[1032,128]{1,0:T(8,128)S(1)}, u32[]{:S(2)}) copy-start(s32[1032,128]{1,0:T(8,128)S(1)} %broadcast_in_dim.53.refs_3_.refs_6_) | copy-start | bytes 1585156
  98.0 1.2 copy-start.11
  110.2 25.3 %all-to-all-start.3 = ((bf16[8,768,128]{2,1,0:T(8,128)(2,1)}), bf16[8,768,128]{2,1,0:T(8,128)(2,1)}, u32[]{:S(2)}, u32[]{:S(2)}) async-start(bf16[8,768,128]{2,1,0:T(8,128)(2,1)} %bitcast.25.refs_4_), calls=%async_computation.3 | async-start | bytes 3145728 | tf_op jit(solution)/shard_map/all_to_all | solution.py:478
  114.5 28.2 %collective-permute-start.11 = (bf16[8,192,128]{2,1,0:T(8,128)(2,1)}, bf16[8,192,128]{2,1,0:T(8,128)(2,1)}, u32[]{:S(2)}, u32[]{:S(2)}) collective-permute-start(bf16[8,192,128]{2,1,0:T(8,128)(2,1)} %get-tuple-element.52), channel_id=1, source_target_pairs={{0,6},{1,7},{2,0},{3,1},{4,2},{5,3},{6,4},{7,5},{8,14},{9,15},{10,... | collective-permute-start | bytes 1179656 | tf_op jit(solution)/shard_map/ppermute | solution.py:473
  119.7 49.5 %collective-permute-start.13 = (bf16[8,192,128]{2,1,0:T(8,128)(2,1)}, bf16[8,192,128]{2,1,0:T(8,128)(2,1)}, u32[]{:S(2)}, u32[]{:S(2)}) collective-permute-start(bf16[8,192,128]{2,1,0:T(8,128)(2,1)} %get-tuple-element.53), channel_id=1, source_target_pairs={{0,4},{1,5},{2,6},{3,7},{4,0},{5,1},{6,2},{7,3},{8,12},{9,13},{10,... | collective-permute-start | bytes 1179656 | tf_op jit(solution)/shard_map/ppermute | solution.py:473
  127.5 44.6 %collective-permute-start.12 = (bf16[8,192,128]{2,1,0:T(8,128)(2,1)}, bf16[8,192,128]{2,1,0:T(8,128)(2,1)}, u32[]{:S(2)}, u32[]{:S(2)}) collective-permute-start(bf16[8,192,128]{2,1,0:T(8,128)(2,1)} %get-tuple-element.47.refs_2_), channel_id=1, source_target_pairs={{0,2},{1,3},{2,4},{3,5},{4,6},{5,7},{6,0},{7,1},{8,10},{9,11},{10,... | collective-permute-start | bytes 1179656 | tf_op jit(solution)/shard_map/ppermute | solution.py:473
  135.5 29.3 %all-to-all-start.4 = ((bf16[8,768,128]{2,1,0:T(8,128)(2,1)}), bf16[8,768,128]{2,1,0:T(8,128)(2,1)}, u32[]{:S(2)}, u32[]{:S(2)}) async-start(bf16[8,768,128]{2,1,0:T(8,128)(2,1)} %after.8.refs_1_), calls=%async_computation.4 | async-start | bytes 3145728 | tf_op jit(solution)/shard_map/all_to_all | solution.py:478
  139.8 13.1 %copy-start.7 = (s32[1032,128]{1,0:T(8,128)S(1)}, s32[1032,128]{1,0:T(8,128)}, u32[]{:S(2)}) copy-start(s32[1032,128]{1,0:T(8,128)} %copy-done.6) | copy-start | bytes 1585156
  139.8 13.0 %copy-start.9 = (s32[520,128]{1,0:T(8,128)S(1)}, s32[520,128]{1,0:T(8,128)}, u32[]{:S(2)}) copy-start(s32[520,128]{1,0:T(8,128)} %copy-done.8) | copy-start | bytes 798724
  142.2 30.0 %collective-permute-start.14 = (bf16[8,192,128]{2,1,0:T(8,128)(2,1)}, bf16[8,192,128]{2,1,0:T(8,128)(2,1)}, u32[]{:S(2)}, u32[]{:S(2)}) collective-permute-start(bf16[8,192,128]{2,1,0:T(8,128)(2,1)} %get-tuple-element.54), channel_id=1, source_target_pairs={{0,6},{1,7},{2,0},{3,1},{4,2},{5,3},{6,4},{7,5},{8,14},{9,15},{10,... | collective-permute-start | bytes 1179656 | tf_op jit(solution)/shard_map/ppermute | solution.py:473
  142.6 79.5 %collective-permute-start.7 = (bf16[8,192,128]{2,1,0:T(8,128)(2,1)}, bf16[8,192,128]{2,1,0:T(8,128)(2,1)}, u32[]{:S(2)}, u32[]{:S(2)}) collective-permute-start(bf16[8,192,128]{2,1,0:T(8,128)(2,1)} %get-tuple-element.49), channel_id=1, source_target_pairs={{0,4},{1,5},{2,6},{3,7},{4,0},{5,1},{6,2},{7,3},{8,12},{9,13},{10,... | collective-permute-start | bytes 1179656 | tf_op jit(solution)/shard_map/ppermute | solution.py:473
  150.5 74.5 %collective-permute-start.6 = (bf16[8,192,128]{2,1,0:T(8,128)(2,1)}, bf16[8,192,128]{2,1,0:T(8,128)(2,1)}, u32[]{:S(2)}, u32[]{:S(2)}) collective-permute-start(bf16[8,192,128]{2,1,0:T(8,128)(2,1)} %get-tuple-element.48.refs_8_), channel_id=1, source_target_pairs={{0,6},{1,7},{2,0},{3,1},{4,2},{5,3},{6,4},{7,5},{8,14},{9,15},{10,... | collective-permute-start | bytes 1179656 | tf_op jit(solution)/shard_map/ppermute | solution.py:473
  152.9 1.0 copy-start.10
  163.7 1.1 copy-start.3
  164.8 25.4 %all-to-all-start.5 = ((bf16[8,768,128]{2,1,0:T(8,128)(2,1)}), bf16[8,768,128]{2,1,0:T(8,128)(2,1)}, u32[]{:S(2)}, u32[]{:S(2)}) async-start(bf16[8,768,128]{2,1,0:T(8,128)(2,1)} %after.9.refs_8_), calls=%async_computation.5 | async-start | bytes 3145728 | tf_op jit(solution)/shard_map/all_to_all | solution.py:478
  169.2 55.9 %collective-permute-start.8 = (bf16[8,192,128]{2,1,0:T(8,128)(2,1)}, bf16[8,192,128]{2,1,0:T(8,128)(2,1)}, u32[]{:S(2)}, u32[]{:S(2)}) collective-permute-start(bf16[8,192,128]{2,1,0:T(8,128)(2,1)} %get-tuple-element.50), channel_id=1, source_target_pairs={{0,2},{1,3},{2,4},{3,5},{4,6},{5,7},{6,0},{7,1},{8,10},{9,11},{10,... | collective-permute-start | bytes 1179656 | tf_op jit(solution)/shard_map/ppermute | solution.py:473
  181.9 1.1 copy-start.4
  190.2 25.3 %all-to-all-start.6 = ((bf16[8,768,128]{2,1,0:T(8,128)(2,1)}), bf16[8,768,128]{2,1,0:T(8,128)(2,1)}, u32[]{:S(2)}, u32[]{:S(2)}) async-start(bf16[8,768,128]{2,1,0:T(8,128)(2,1)} %after.10.refs_1_), calls=%async_computation.6 | async-start | bytes 3145728 | tf_op jit(solution)/shard_map/all_to_all | solution.py:478
  196.7 29.8 %collective-permute-start.16 = (bf16[8,192,128]{2,1,0:T(8,128)(2,1)}, bf16[8,192,128]{2,1,0:T(8,128)(2,1)}, u32[]{:S(2)}, u32[]{:S(2)}) collective-permute-start(bf16[8,192,128]{2,1,0:T(8,128)(2,1)} %get-tuple-element.56), channel_id=1, source_target_pairs={{0,4},{1,5},{2,6},{3,7},{4,0},{5,1},{6,2},{7,3},{8,12},{9,13},{10,... | collective-permute-start | bytes 1179656 | tf_op jit(solution)/shard_map/ppermute | solution.py:473
  198.4 44.7 %collective-permute-start.15 = (bf16[8,192,128]{2,1,0:T(8,128)(2,1)}, bf16[8,192,128]{2,1,0:T(8,128)(2,1)}, u32[]{:S(2)}, u32[]{:S(2)}) collective-permute-start(bf16[8,192,128]{2,1,0:T(8,128)(2,1)} %get-tuple-element.55.refs_5_), channel_id=1, source_target_pairs={{0,6},{1,7},{2,0},{3,1},{4,2},{5,3},{6,4},{7,5},{8,14},{9,15},{10,... | collective-permute-start | bytes 1179656 | tf_op jit(solution)/shard_map/ppermute | solution.py:473
  202.0 1.0 copy-start.12
  212.9 1.1 copy-start.5
  215.5 25.4 %all-to-all-start.7 = ((bf16[8,768,128]{2,1,0:T(8,128)(2,1)}), bf16[8,768,128]{2,1,0:T(8,128)(2,1)}, u32[]{:S(2)}, u32[]{:S(2)}) async-start(bf16[8,768,128]{2,1,0:T(8,128)(2,1)} %after.11.refs_1_), calls=%async_computation.7 | async-start | bytes 3145728 | tf_op jit(solution)/shard_map/all_to_all | solution.py:478
  222.1 21.0 %collective-permute-start.17 = (bf16[8,192,128]{2,1,0:T(8,128)(2,1)}, bf16[8,192,128]{2,1,0:T(8,128)(2,1)}, u32[]{:S(2)}, u32[]{:S(2)}) collective-permute-start(bf16[8,192,128]{2,1,0:T(8,128)(2,1)} %get-tuple-element.57), channel_id=1, source_target_pairs={{0,2},{1,3},{2,4},{3,5},{4,6},{5,7},{6,0},{7,1},{8,10},{9,11},{10,... | collective-permute-start | bytes 1179656 | tf_op jit(solution)/shard_map/ppermute | solution.py:473
  225.1 36.0 %collective-permute-start.19 = (bf16[8,192,128]{2,1,0:T(8,128)(2,1)}, bf16[8,192,128]{2,1,0:T(8,128)(2,1)}, u32[]{:S(2)}, u32[]{:S(2)}) collective-permute-start(bf16[8,192,128]{2,1,0:T(8,128)(2,1)} %get-tuple-element.59), channel_id=1, source_target_pairs={{0,4},{1,5},{2,6},{3,7},{4,0},{5,1},{6,2},{7,3},{8,12},{9,13},{10,... | collective-permute-start | bytes 1179656 | tf_op jit(solution)/shard_map/ppermute | solution.py:473
  225.1 36.0 %collective-permute-start.20 = (bf16[8,192,128]{2,1,0:T(8,128)(2,1)}, bf16[8,192,128]{2,1,0:T(8,128)(2,1)}, u32[]{:S(2)}, u32[]{:S(2)}) collective-permute-start(bf16[8,192,128]{2,1,0:T(8,128)(2,1)} %get-tuple-element.60), channel_id=1, source_target_pairs={{0,2},{1,3},{2,4},{3,5},{4,6},{5,7},{6,0},{7,1},{8,10},{9,11},{10,... | collective-permute-start | bytes 1179656 | tf_op jit(solution)/shard_map/ppermute | solution.py:473
  226.5 38.4 %collective-permute-start.18 = (bf16[8,192,128]{2,1,0:T(8,128)(2,1)}, bf16[8,192,128]{2,1,0:T(8,128)(2,1)}, u32[]{:S(2)}, u32[]{:S(2)}) collective-permute-start(bf16[8,192,128]{2,1,0:T(8,128)(2,1)} %get-tuple-element.58.refs_1_), channel_id=1, source_target_pairs={{0,6},{1,7},{2,0},{3,1},{4,2},{5,3},{6,4},{7,5},{8,14},{9,15},{10,... | collective-permute-start | bytes 1179656 | tf_op jit(solution)/shard_map/ppermute | solution.py:473
  243.1 40.0 %collective-permute-start.24 = (bf16[8,96,128]{2,1,0:T(8,128)(2,1)}, bf16[8,96,128]{2,1,0:T(8,128)(2,1)S(1)}, u32[]{:S(2)}, u32[]{:S(2)}) collective-permute-start(bf16[8,96,128]{2,1,0:T(8,128)(2,1)} %get-tuple-element.64), channel_id=1, source_target_pairs={{0,6},{1,7},{2,0},{3,1},{4,2},{5,3},{6,4},{7,5},{8,14},{9,15},{10,... | collective-permute-start | bytes 589832 | tf_op jit(solution)/shard_map/ppermute | solution.py:473
  243.2 43.1 %collective-permute-start.25 = (bf16[8,96,128]{2,1,0:T(8,128)(2,1)}, bf16[8,96,128]{2,1,0:T(8,128)(2,1)S(1)}, u32[]{:S(2)}, u32[]{:S(2)}) collective-permute-start(bf16[8,96,128]{2,1,0:T(8,128)(2,1)} %get-tuple-element.65), channel_id=1, source_target_pairs={{0,4},{1,5},{2,6},{3,7},{4,0},{5,1},{6,2},{7,3},{8,12},{9,13},{10,... | collective-permute-start | bytes 589832 | tf_op jit(solution)/shard_map/ppermute | solution.py:473
  261.1 25.2 %collective-permute-start.26 = (bf16[8,96,128]{2,1,0:T(8,128)(2,1)}, bf16[8,96,128]{2,1,0:T(8,128)(2,1)S(1)}, u32[]{:S(2)}, u32[]{:S(2)}) collective-permute-start(bf16[8,96,128]{2,1,0:T(8,128)(2,1)} %get-tuple-element.66), channel_id=1, source_target_pairs={{0,2},{1,3},{2,4},{3,5},{4,6},{5,7},{6,0},{7,1},{8,10},{9,11},{10,... | collective-permute-start | bytes 589832 | tf_op jit(solution)/shard_map/ppermute | solution.py:473
  261.1 35.3 %collective-permute-start.21 = (bf16[8,96,128]{2,1,0:T(8,128)(2,1)}, bf16[8,96,128]{2,1,0:T(8,128)(2,1)}, u32[]{:S(2)}, u32[]{:S(2)}) collective-permute-start(bf16[8,96,128]{2,1,0:T(8,128)(2,1)} %get-tuple-element.61), channel_id=1, source_target_pairs={{0,6},{1,7},{2,0},{3,1},{4,2},{5,3},{6,4},{7,5},{8,14},{9,15},{10,... | collective-permute-start | bytes 589832 | tf_op jit(solution)/shard_map/ppermute | solution.py:473
  264.9 38.3 %collective-permute-start.22 = (bf16[8,96,128]{2,1,0:T(8,128)(2,1)}, bf16[8,96,128]{2,1,0:T(8,128)(2,1)}, u32[]{:S(2)}, u32[]{:S(2)}) collective-permute-start(bf16[8,96,128]{2,1,0:T(8,128)(2,1)} %get-tuple-element.62), channel_id=1, source_target_pairs={{0,4},{1,5},{2,6},{3,7},{4,0},{5,1},{6,2},{7,3},{8,12},{9,13},{10,... | collective-permute-start | bytes 589832 | tf_op jit(solution)/shard_map/ppermute | solution.py:473
  283.2 20.0 %collective-permute-start.23 = (bf16[8,96,128]{2,1,0:T(8,128)(2,1)}, bf16[8,96,128]{2,1,0:T(8,128)(2,1)}, u32[]{:S(2)}, u32[]{:S(2)}) collective-permute-start(bf16[8,96,128]{2,1,0:T(8,128)(2,1)} %get-tuple-element.63), channel_id=1, source_target_pairs={{0,2},{1,3},{2,4},{3,5},{4,6},{5,7},{6,0},{7,1},{8,10},{9,11},{10,... | collective-permute-start | bytes 589832 | tf_op jit(solution)/shard_map/ppermute | solution.py:473
  303.2 10.2 %copy-start.1 = (bf16[16,128,128]{2,1,0:T(8,128)(2,1)S(1)}, bf16[16,128,128]{2,1,0:T(8,128)(2,1)}, u32[]{:S(2)}) copy-start(bf16[16,128,128]{2,1,0:T(8,128)(2,1)} %param.9) | copy-start | bytes 1572868

commit v5 on v4

--- a/solution.py
+++ b/solution.py
@@ -550,27 +550,27 @@
         return x.reshape(joined_shape)
 
     turned_waves = waves.transpose(0, 2, 1, 3)
-    rows = jnp.stack([waves[0].reshape(-1), turned_waves[2].reshape(-1)]).reshape(-1, 1)
-    sent = fourier_some(grid, rows, parity, [plane] * layers + [plane * layers])
+    sent = fourier_some(grid, waves[0].reshape(-1, 1), parity, [plane] * layers)
     z0 = along(sent[0], sent[1:layers])
-    x2 = sent[layers].reshape(joined_shape)
-    rows = jnp.stack([turned_waves[1], turned_waves[3]]).reshape(-1, 1)
-    sent = fourier_some(grid, rows, parity, [plane * layers] * 2, x2)
-    x1, x3 = [x.reshape(joined_shape) for x in sent]
+    rows = turned_waves[1:].reshape(-1, 1)
+    sent = fourier_some(grid, rows, parity, [plane * layers] * 3, sent[0])
+    x1, x2, x3 = [x.reshape(joined_shape) for x in sent]
     p2 = across(x2)
     rows = jnp.stack([waves[0], waves[2], waves[3], waves[1]]).reshape(-1, 1)
     synthesis = synthesis_rows(rows, points, ROWS * layers * plane, x2)
-    x3 = after(x3, p2, synthesis)
-    p3 = across(x3)
-    z1 = along(x1, part_slots(x1, layers, None, x3)[0])
-    j0 = after(join_slots(z0, x3), p3)
+    u1 = part_slots(x1, layers, None, synthesis, *z0[1:])[0]
+    z1 = along(x1, u1)
+    j0 = after(join_slots(z0, u1[0]), p2)
     p0 = across(j0)
     u2 = part_slots(p2, layers, None, j0)[0]
     z2 = along(p2, u2)
-    s0 = solve(0, [p0], u2[0])
+    x3 = after(x3, p0, u2[0])
+    p3 = across(x3)
+    s0 = solve(0, [p0], x3)
+    j1 = join_slots(z1, s0)
+    s0 = after(s0, p3, j1)
     r0 = across(s0)
-    j1 = join_slots(z1, s0)
-    u3 = part_slots(p3, layers, None, j1)[0]
+    u3 = part_slots(p3, layers, None, s0)[0]
     z3 = along(p3, u3)
     j1 = after(j1, r0, u3[0])
     p1 = across(j1)

time: 315 us -> 310 us (0.984)
  starting transfers between devices: 115 us -> 103 us
  waiting for transfers between devices: 74.4 us -> 82 us
    ppermute x27, starting transfers between devices: 79.6 us -> 68.4 us  [turn_along_z(): moved.append(lax.ppermute(slot, 'lev', pairs))]
    all_to_all x8, waiting for transfers between devices: 52.9 us -> 58 us  [exchange_in_plane(): lax.all_to_all(x, ('lat', 'lev'), split_axis=0, concat_axis=0, tiled=True...]
    unnamed x58 -> x66, local copies, waits for them, and re-layouts: 11.9 us -> 11.3 us
  transfers between devices with their start and end apart: 35 -> 35, of which waited for: 9 -> 11; matrix products, arithmetic and copies ran while one was open for 2% -> 2% of each run, Pallas kernels for 26% -> 27%
where the time goes in v5:
time: 310 us; the launch traced here: 308 us
  starting transfers between devices  103 us (33%)
  Pallas kernels  102 us (33%)
  waiting for transfers between devices  82 us (26%)
  local copies, waits for them, and re-layouts  17.9 us (6%)
    ppermute x27, starting transfers between devices, turn_along_z(): moved.append(lax.ppermute(slot, 'lev', pairs))  68.4 us
    all_to_all x8, waiting for transfers between devices, exchange_in_plane(): lax.all_to_all(x, ('lat', 'lev'), split_axis=0, concat_axis=0, tiled=True...  58 us
    pallas_call x4, Pallas kernels, spectral_chunk(): pl.pallas_call(functools.partial(spectral_kernel, len(pieces)), out_shape...  39.1 us
    all_to_all x8, starting transfers between devices, exchange_in_plane(): lax.all_to_all(x, ('lat', 'lev'), split_axis=0, concat_axis=0, tiled=True...  34.7 us
    ppermute x27, waiting for transfers between devices, turn_along_z(): moved.append(lax.ppermute(slot, 'lev', pairs))  23.9 us
    pallas_call x2, Pallas kernels, synthesis_part(): pl.pallas_call(functools.partial(synthesis_kernel, len(fields)), out_shap...  20.3 us
    pallas_call x2, Pallas kernels, fourier_some(): pl.pallas_call(functools.partial(fourier_kernel, len(ready)), out_shape=[...  19.7 us
    pallas_call x7, Pallas kernels, part_slots(): pl.pallas_call(functools.partial(part_kernel, layers, cuts), out_shape=[j...  15.8 us
  transfers between devices with their start and end apart: 35, of which 11 were waited for; matrix products, arithmetic and copies ran while one was open for 2% of the time, Pallas kernels for 27%

profile of v5, /device:TPU:0, one launch (start us, length us, event | category | flops | bytes accessed | tf_op | source)
XLA Modules:
  0.0 308.5 jit_solution(3330701646278673070)
XLA Ops:
  3.0 7.4 %fourier_some.2 = (bf16[8,192,128]{2,1,0:T(8,128)(2,1)S(1)}, bf16[8,192,128]{2,1,0:T(8,128)(2,1)}, bf16[8,192,128]{2,1,0:T(8,128)(2,1)}, bf16[8,192,128]{2,1,0:T(8,128)(2,1)}) custom-call(s32[1]{0:T(128)} %bitcast.parity_ref, s32[256,1]{1,0:T(8,128)S(1)} %broadcast_in_dim.55.wave_ref, bf16[2,4,2,192,1536]{4,3,2,1,0:T(8,128)(2,1)} %bitcast.81), custom_call_target="tpu_custom_call" | custom-call | flops 9999999827968 | bytes 100000000 | tf_op jit(solution)/shard_map/fourier_some/pallas_call | solution.py:178
  10.4 3.0 collective-permute-start
  13.5 2.6 collective-permute-start.1
  16.1 1.3 collective-permute-start.2
  18.0 12.3 %fourier_some.3 = (bf16[32,192,128]{2,1,0:T(8,128)(2,1)S(1)}, bf16[32,192,128]{2,1,0:T(8,128)(2,1)}, bf16[32,192,128]{2,1,0:T(8,128)(2,1)S(1)}) custom-call(s32[1]{0:T(128)} %bitcast.parity_ref, s32[768,1]{1,0:T(8,128)S(1)} %reshape.135.wave_ref, bf16[2,4,2,192,1536]{4,3,2,1,0:T(8,128)(2,1)} %bitcast.82, bf16[8,192,128]{2,1,0:T(8,128)(2,1)S(1)} %get-tuple-element.36.refs_0_), custom_call_target="tpu_custom_call" | custom-call | flops 9999999827968 | bytes 100000000 | tf_op jit(solution)/shard_map/fourier_some/pallas_call | solution.py:178
  30.2 1.1 copy-done.2
  31.4 1.2 copy-done.14
  32.6 4.4 %all-to-all-start = ((bf16[8,768,128]{2,1,0:T(8,128)(2,1)}), bf16[8,768,128]{2,1,0:T(8,128)(2,1)}, u32[]{:S(2)}, u32[]{:S(2)}) async-start(bf16[8,768,128]{2,1,0:T(8,128)(2,1)} %bitcast.16.refs_0_), calls=%async_computation | async-start | bytes 3145728 | tf_op jit(solution)/shard_map/all_to_all | solution.py:478
  38.3 1.2 concatenate.14
  41.5 2.1 synthesis_rows.1.refs_1_.refs_16_
  43.6 1.6 copy-done.15
  45.9 1.3 pad_add_fusion.2
  47.3 2.3 part_slots.7
  49.5 2.5 collective-permute-start.4
  52.0 3.4 %collective-permute-start.5 = (bf16[8,192,128]{2,1,0:T(8,128)(2,1)}, bf16[8,192,128]{2,1,0:T(8,128)(2,1)}, u32[]{:S(2)}, u32[]{:S(2)}) collective-permute-start(bf16[8,192,128]{2,1,0:T(8,128)(2,1)} %get-tuple-element.46), channel_id=1, source_target_pairs={{0,6},{1,7},{2,0},{3,1},{4,2},{5,3},{6,4},{7,5},{8,14},{9,15},{10,... | collective-permute-start | bytes 1179656 | tf_op jit(solution)/shard_map/ppermute | solution.py:473
  55.4 2.5 join_slots.2.refs_0_
  58.1 4.3 %all-to-all-start.1 = ((bf16[8,768,128]{2,1,0:T(8,128)(2,1)}), bf16[8,768,128]{2,1,0:T(8,128)(2,1)}, u32[]{:S(2)}, u32[]{:S(2)}) async-start(bf16[8,768,128]{2,1,0:T(8,128)(2,1)} %after.7.refs_1_), calls=%async_computation.1 | async-start | bytes 3145728 | tf_op jit(solution)/shard_map/all_to_all | solution.py:478
  62.4 2.3 part_slots.8
  65.2 3.7 %collective-permute-start.9 = (bf16[8,192,128]{2,1,0:T(8,128)(2,1)}, bf16[8,192,128]{2,1,0:T(8,128)(2,1)}, u32[]{:S(2)}, u32[]{:S(2)}) collective-permute-start(bf16[8,192,128]{2,1,0:T(8,128)(2,1)} %get-tuple-element.44.refs_2_), channel_id=1, source_target_pairs={{0,2},{1,3},{2,4},{3,5},{4,6},{5,7},{6,0},{7,1},{8,10},{9,11},{10,... | collective-permute-start | bytes 1179656 | tf_op jit(solution)/shard_map/ppermute | solution.py:473
  68.9 14.5 %all-to-all-done.1.refs_1_.refs_0_ = bf16[8,768,128]{2,1,0:T(8,128)(2,1)} async-done(((bf16[8,768,128]{2,1,0:T(8,128)(2,1)}), bf16[8,768,128]{2,1,0:T(8,128)(2,1)}, u32[]{:S(2)}, u32[]{:S(2)}) %all-to-all-start.1) | async-done | bytes 1572896 | tf_op jit(solution)/shard_map/all_to_all | solution.py:478
  83.4 4.4 %all-to-all-start.2 = ((bf16[8,768,128]{2,1,0:T(8,128)(2,1)}), bf16[8,768,128]{2,1,0:T(8,128)(2,1)}, u32[]{:S(2)}, u32[]{:S(2)}) async-start(bf16[8,768,128]{2,1,0:T(8,128)(2,1)} %after.8.refs_5_), calls=%async_computation.2 | async-start | bytes 3145728 | tf_op jit(solution)/shard_map/all_to_all | solution.py:478
  88.3 9.8 %spectral_chunk.4 = bf16[4,8,192,128]{3,2,1,0:T(8,128)(2,1)S(1)} custom-call(s32[2]{0:T(128)S(1)} %get-tuple-element.76.lower_ref, bf16[8,768,128]{2,1,0:T(8,128)(2,1)} %all-to-all-done.1.refs_1_.refs_0_, bf16[32,520,768]{2,1,0:T(8,128)(2,1)} %bitcast.77, bf16[1024,256]{1,0:T(8,128)(2,1)S(1)} %bitcast.59, s32[1032,128]{1,0:T(8,128)S(1)} %broadcast_in_dim.53.refs_3_.refs_6_, ...), custom_call_target="tpu_custom_call" | custom-call | flops 9999999827968 | bytes 100000000 | tf_op jit(solution)/shard_map/spectral_chunk/pallas_call | solution.py:314
  98.1 1.1 copy-done.4
  99.2 3.7 %collective-permute-start.11 = (bf16[8,192,128]{2,1,0:T(8,128)(2,1)}, bf16[8,192,128]{2,1,0:T(8,128)(2,1)}, u32[]{:S(2)}, u32[]{:S(2)}) collective-permute-start(bf16[8,192,128]{2,1,0:T(8,128)(2,1)} %get-tuple-element.52), channel_id=1, source_target_pairs={{0,6},{1,7},{2,0},{3,1},{4,2},{5,3},{6,4},{7,5},{8,14},{9,15},{10,... | collective-permute-start | bytes 1179656 | tf_op jit(solution)/shard_map/ppermute | solution.py:473
  102.9 2.4 join_slots.3.refs_2_.refs_0_
  105.3 3.6 %all-to-all-done.2.refs_1_.refs_0_ = bf16[8,768,128]{2,1,0:T(8,128)(2,1)} async-done(((bf16[8,768,128]{2,1,0:T(8,128)(2,1)}), bf16[8,768,128]{2,1,0:T(8,128)(2,1)}, u32[]{:S(2)}, u32[]{:S(2)}) %all-to-all-start.2) | async-done | bytes 1572896 | tf_op jit(solution)/shard_map/all_to_all | solution.py:478
  108.9 4.3 %all-to-all-start.3 = ((bf16[8,768,128]{2,1,0:T(8,128)(2,1)}), bf16[8,768,128]{2,1,0:T(8,128)(2,1)}, u32[]{:S(2)}, u32[]{:S(2)}) async-start(bf16[8,768,128]{2,1,0:T(8,128)(2,1)} %after.9.refs_1_), calls=%async_computation.3 | async-start | bytes 3145728 | tf_op jit(solution)/shard_map/all_to_all | solution.py:478
  113.2 2.3 part_slots.9
  116.0 3.7 %collective-permute-start.12 = (bf16[8,192,128]{2,1,0:T(8,128)(2,1)}, bf16[8,192,128]{2,1,0:T(8,128)(2,1)}, u32[]{:S(2)}, u32[]{:S(2)}) collective-permute-start(bf16[8,192,128]{2,1,0:T(8,128)(2,1)} %get-tuple-element.47.refs_2_), channel_id=1, source_target_pairs={{0,2},{1,3},{2,4},{3,5},{4,6},{5,7},{6,0},{7,1},{8,10},{9,11},{10,... | collective-permute-start | bytes 1179656 | tf_op jit(solution)/shard_map/ppermute | solution.py:473
  119.7 14.5 %all-to-all-done.3.refs_1_.refs_0_ = bf16[8,768,128]{2,1,0:T(8,128)(2,1)} async-done(((bf16[8,768,128]{2,1,0:T(8,128)(2,1)}), bf16[8,768,128]{2,1,0:T(8,128)(2,1)}, u32[]{:S(2)}, u32[]{:S(2)}) %all-to-all-start.3) | async-done | bytes 1572896 | tf_op jit(solution)/shard_map/all_to_all | solution.py:478
  134.3 4.3 %all-to-all-start.4 = ((bf16[8,768,128]{2,1,0:T(8,128)(2,1)}), bf16[8,768,128]{2,1,0:T(8,128)(2,1)}, u32[]{:S(2)}, u32[]{:S(2)}) async-start(bf16[8,768,128]{2,1,0:T(8,128)(2,1)} %after.10.refs_1_), calls=%async_computation.4 | async-start | bytes 3145728 | tf_op jit(solution)/shard_map/all_to_all | solution.py:478
  138.6 2.3 part_slots.10
  140.9 3.7 %collective-permute-start.14 = (bf16[8,192,128]{2,1,0:T(8,128)(2,1)}, bf16[8,192,128]{2,1,0:T(8,128)(2,1)}, u32[]{:S(2)}, u32[]{:S(2)}) collective-permute-start(bf16[8,192,128]{2,1,0:T(8,128)(2,1)} %get-tuple-element.54), channel_id=1, source_target_pairs={{0,6},{1,7},{2,0},{3,1},{4,2},{5,3},{6,4},{7,5},{8,14},{9,15},{10,... | collective-permute-start | bytes 1179656 | tf_op jit(solution)/shard_map/ppermute | solution.py:473
  146.3 9.7 %spectral_chunk.5 = bf16[4,8,192,128]{3,2,1,0:T(8,128)(2,1)S(1)} custom-call(s32[2]{0:T(128)S(1)} %get-tuple-element.75.lower_ref, bf16[8,768,128]{2,1,0:T(8,128)(2,1)} %all-to-all-done.refs_1_.refs_0_, bf16[8,192,128]{2,1,0:T(8,128)(2,1)} %collective-permute-done.9.refs_1_, bf16[8,192,128]{2,1,0:T(8,128)(2,1)} %collective-permute-done.10.refs_2_, ...), custom_call_target="tpu_custom_call" | custom-call | flops 9999999827968 | bytes 100000000 | tf_op jit(solution)/shard_map/spectral_chunk/pallas_call | solution.py:314
  156.1 1.1 copy-done.5
  157.2 2.4 all-to-all-done.4.refs_1_.refs_0_
  159.6 4.3 %all-to-all-start.5 = ((bf16[8,768,128]{2,1,0:T(8,128)(2,1)}), bf16[8,768,128]{2,1,0:T(8,128)(2,1)}, u32[]{:S(2)}, u32[]{:S(2)}) async-start(bf16[8,768,128]{2,1,0:T(8,128)(2,1)} %after.11.refs_8_), calls=%async_computation.5 | async-start | bytes 3145728 | tf_op jit(solution)/shard_map/all_to_all | solution.py:478
  163.9 1.2 collective-permute-start.8
  165.1 9.7 %spectral_chunk.6 = bf16[4,8,192,128]{3,2,1,0:T(8,128)(2,1)S(1)} custom-call(s32[2]{0:T(128)S(1)} %get-tuple-element.74.lower_ref, bf16[8,768,128]{2,1,0:T(8,128)(2,1)} %all-to-all-done.2.refs_1_.refs_0_, bf16[8,192,128]{2,1,0:T(8,128)(2,1)} %collective-permute-done.12.refs_1_, bf16[8,192,128]{2,1,0:T(8,128)(2,1)} %collective-permute-done.13.refs_2_, ...), custom_call_target="tpu_custom_call" | custom-call | flops 9999999827968 | bytes 100000000 | tf_op jit(solution)/shard_map/spectral_chunk/pallas_call | solution.py:314
  174.9 1.1 copy-done.6
  176.0 9.0 %all-to-all-done.5.refs_1_.refs_0_.refs_4_ = bf16[8,768,128]{2,1,0:T(8,128)(2,1)} async-done(((bf16[8,768,128]{2,1,0:T(8,128)(2,1)}), bf16[8,768,128]{2,1,0:T(8,128)(2,1)}, u32[]{:S(2)}, u32[]{:S(2)}) %all-to-all-start.5) | async-done | bytes 1572896 | tf_op jit(solution)/shard_map/all_to_all | solution.py:478
  185.0 4.3 %all-to-all-start.6 = ((bf16[8,768,128]{2,1,0:T(8,128)(2,1)}), bf16[8,768,128]{2,1,0:T(8,128)(2,1)}, u32[]{:S(2)}, u32[]{:S(2)}) async-start(bf16[8,768,128]{2,1,0:T(8,128)(2,1)} %after.12.refs_1_), calls=%async_computation.6 | async-start | bytes 3145728 | tf_op jit(solution)/shard_map/all_to_all | solution.py:478
  189.3 2.3 part_slots.11
  192.1 3.1 %collective-permute-start.15 = (bf16[8,192,128]{2,1,0:T(8,128)(2,1)}, bf16[8,192,128]{2,1,0:T(8,128)(2,1)}, u32[]{:S(2)}, u32[]{:S(2)}) collective-permute-start(bf16[8,192,128]{2,1,0:T(8,128)(2,1)} %get-tuple-element.55.refs_5_), channel_id=1, source_target_pairs={{0,6},{1,7},{2,0},{3,1},{4,2},{5,3},{6,4},{7,5},{8,14},{9,15},{10,... | collective-permute-start | bytes 1179656 | tf_op jit(solution)/shard_map/ppermute | solution.py:473
  195.2 1.0 copy-done.13
  196.2 9.8 %spectral_chunk.7 = bf16[4,8,192,128]{3,2,1,0:T(8,128)(2,1)S(1)} custom-call(s32[2]{0:T(128)S(1)} %get-tuple-element.73.lower_ref, bf16[8,768,128]{2,1,0:T(8,128)(2,1)} %all-to-all-done.4.refs_1_.refs_0_, bf16[32,520,768]{2,1,0:T(8,128)(2,1)} %bitcast.80, bf16[1024,256]{1,0:T(8,128)(2,1)S(1)} %bitcast.62, s32[1032,128]{1,0:T(8,128)S(1)} %copy-done.9, ...), custom_call_target="tpu_custom_call" | custom-call | flops 9999999827968 | bytes 100000000 | tf_op jit(solution)/shard_map/spectral_chunk/pallas_call | solution.py:314
  206.0 1.1 copy-done.7
  207.2 3.1 %all-to-all-done.6.refs_1_.refs_0_.refs_8_ = bf16[8,768,128]{2,1,0:T(8,128)(2,1)} async-done(((bf16[8,768,128]{2,1,0:T(8,128)(2,1)}), bf16[8,768,128]{2,1,0:T(8,128)(2,1)}, u32[]{:S(2)}, u32[]{:S(2)}) %all-to-all-start.6) | async-done | bytes 1572896 | tf_op jit(solution)/shard_map/all_to_all | solution.py:478
  210.3 4.3 %all-to-all-start.7 = ((bf16[8,768,128]{2,1,0:T(8,128)(2,1)}), bf16[8,768,128]{2,1,0:T(8,128)(2,1)}, u32[]{:S(2)}, u32[]{:S(2)}) async-start(bf16[8,768,128]{2,1,0:T(8,128)(2,1)} %after.13.refs_1_), calls=%async_computation.7 | async-start | bytes 3145728 | tf_op jit(solution)/shard_map/all_to_all | solution.py:478
  214.6 2.3 part_slots.12
  216.9 1.1 collective-permute-start.17
  218.0 3.1 %collective-permute-start.19 = (bf16[8,192,128]{2,1,0:T(8,128)(2,1)}, bf16[8,192,128]{2,1,0:T(8,128)(2,1)}, u32[]{:S(2)}, u32[]{:S(2)}) collective-permute-start(bf16[8,192,128]{2,1,0:T(8,128)(2,1)} %get-tuple-element.59), channel_id=1, source_target_pairs={{0,4},{1,5},{2,6},{3,7},{4,0},{5,1},{6,2},{7,3},{8,12},{9,13},{10,... | collective-permute-start | bytes 1179656 | tf_op jit(solution)/shard_map/ppermute | solution.py:473
  221.3 3.7 %collective-permute-start.18 = (bf16[8,192,128]{2,1,0:T(8,128)(2,1)}, bf16[8,192,128]{2,1,0:T(8,128)(2,1)}, u32[]{:S(2)}, u32[]{:S(2)}) collective-permute-start(bf16[8,192,128]{2,1,0:T(8,128)(2,1)} %get-tuple-element.58.refs_1_), channel_id=1, source_target_pairs={{0,6},{1,7},{2,0},{3,1},{4,2},{5,3},{6,4},{7,5},{8,14},{9,15},{10,... | collective-permute-start | bytes 1179656 | tf_op jit(solution)/shard_map/ppermute | solution.py:473
  224.9 10.7 %all-to-all-done.7.refs_0_.refs_12_ = bf16[8,768,128]{2,1,0:T(8,128)(2,1)} async-done(((bf16[8,768,128]{2,1,0:T(8,128)(2,1)}), bf16[8,768,128]{2,1,0:T(8,128)(2,1)}, u32[]{:S(2)}, u32[]{:S(2)}) %all-to-all-start.7) | async-done | bytes 1572896 | tf_op jit(solution)/shard_map/all_to_all | solution.py:478
  235.6 2.2 part_slots.13
  237.9 3.7 %collective-permute-start.24 = (bf16[8,96,128]{2,1,0:T(8,128)(2,1)}, bf16[8,96,128]{2,1,0:T(8,128)(2,1)S(1)}, u32[]{:S(2)}, u32[]{:S(2)}) collective-permute-start(bf16[8,96,128]{2,1,0:T(8,128)(2,1)} %get-tuple-element.64), channel_id=1, source_target_pairs={{0,6},{1,7},{2,0},{3,1},{4,2},{5,3},{6,4},{7,5},{8,14},{9,15},{10,... | collective-permute-start | bytes 589832 | tf_op jit(solution)/shard_map/ppermute | solution.py:473
  241.6 14.3 %collective-permute-done.19.refs_10_ = bf16[8,192,128]{2,1,0:T(8,128)(2,1)} collective-permute-done((bf16[8,192,128]{2,1,0:T(8,128)(2,1)}, bf16[8,192,128]{2,1,0:T(8,128)(2,1)}, u32[]{:S(2)}, u32[]{:S(2)}) %collective-permute-start.19) | collective-permute-done | bytes 393248 | tf_op jit(solution)/shard_map/ppermute | solution.py:473
  255.9 6.3 %collective-permute-start.21 = (bf16[8,96,128]{2,1,0:T(8,128)(2,1)}, bf16[8,96,128]{2,1,0:T(8,128)(2,1)}, u32[]{:S(2)}, u32[]{:S(2)}) collective-permute-start(bf16[8,96,128]{2,1,0:T(8,128)(2,1)} %get-tuple-element.61), channel_id=1, source_target_pairs={{0,6},{1,7},{2,0},{3,1},{4,2},{5,3},{6,4},{7,5},{8,14},{9,15},{10,... | collective-permute-start | bytes 589832 | tf_op jit(solution)/shard_map/ppermute | solution.py:473
  262.2 14.2 %collective-permute-start.22 = (bf16[8,96,128]{2,1,0:T(8,128)(2,1)}, bf16[8,96,128]{2,1,0:T(8,128)(2,1)}, u32[]{:S(2)}, u32[]{:S(2)}) collective-permute-start(bf16[8,96,128]{2,1,0:T(8,128)(2,1)} %get-tuple-element.62), channel_id=1, source_target_pairs={{0,4},{1,5},{2,6},{3,7},{4,0},{5,1},{6,2},{7,3},{8,12},{9,13},{10,... | collective-permute-start | bytes 589832 | tf_op jit(solution)/shard_map/ppermute | solution.py:473
  276.4 2.0 collective-permute-start.23
  278.4 2.7 collective-permute-done.25.refs_14_
  281.1 10.1 %synthesis_part.2.refs_18_ = bf16[2,4,2,192,1536]{4,3,2,1,0:T(8,128)(2,1)} custom-call(s32[1]{0:T(128)} %bitcast.parity_ref, bf16[8,768,128]{2,1,0:T(8,128)(2,1)} %all-to-all-done.3.refs_1_.refs_0_, bf16[8,192,128]{2,1,0:T(8,128)(2,1)} %collective-permute-done.6.refs_1_, bf16[8,192,128]{2,1,0:T(8,128)(2,1)} %collective-permute-done.7.refs_2_, ...), custom_call_target="tpu_custom_call" | custom-call | flops 9999999827968 | bytes 100000000 | tf_op jit(solution)/shard_map/synthesis_part/pallas_call | solution.py:387
  291.2 6.8 %collective-permute-done.22.refs_14_ = bf16[8,96,128]{2,1,0:T(8,128)(2,1)} collective-permute-done((bf16[8,96,128]{2,1,0:T(8,128)(2,1)}, bf16[8,96,128]{2,1,0:T(8,128)(2,1)}, u32[]{:S(2)}, u32[]{:S(2)}) %collective-permute-start.22) | collective-permute-done | bytes 196640 | tf_op jit(solution)/shard_map/ppermute | solution.py:473
  298.0 10.2 %synthesis_part.3 = bf16[2,4,2,192,1536]{4,3,2,1,0:T(8,128)(2,1)} custom-call(s32[1]{0:T(128)} %bitcast.parity_ref, bf16[8,768,128]{2,1,0:T(8,128)(2,1)} %all-to-all-done.3.refs_1_.refs_0_, bf16[8,192,128]{2,1,0:T(8,128)(2,1)} %collective-permute-done.6.refs_1_, ...), custom_call_target="tpu_custom_call", output_to_operand_aliasing={{}: (19, {})} | custom-call | flops 9999999827968 | bytes 100000000 | tf_op jit(solution)/shard_map/synthesis_part/pallas_call | solution.py:387
  (135 shorter events, 11.5 us)
Async XLA Ops:
  0.0 40.3 %copy-start = (bf16[16,128,128]{2,1,0:T(8,128)(2,1)S(1)}, bf16[16,128,128]{2,1,0:T(8,128)(2,1)}, u32[]{:S(2)}) copy-start(bf16[16,128,128]{2,1,0:T(8,128)(2,1)} %param.9) | copy-start | bytes 1572868
  1.3 1.0 copy-start.17
  3.0 14.4 %copy-start.18 = (s32[4,4,4,2,2,1]{1,0,4,3,2,5:T(4,128)S(1)}, s32[4,4,4,2,2,1]{1,0,4,3,2,5:T(4,128)}, u32[]{:S(2)}) copy-start(s32[4,4,4,2,2,1]{1,0,4,3,2,5:T(4,128)} %copy-done.17) | copy-start | bytes 3076
  3.0 14.4 %copy-start.20 = (s32[4,4,4,2,2,1]{1,0,4,3,2,5:T(4,128)S(1)}, s32[4,4,4,2,2,1]{1,0,4,3,2,5:T(4,128)}, u32[]{:S(2)}) copy-start(s32[4,4,4,2,2,1]{1,0,4,3,2,5:T(4,128)} %copy-done.19) | copy-start | bytes 3076
  10.4 19.8 %copy-start.16 = (bf16[8,192,128]{2,1,0:T(8,128)(2,1)}, bf16[8,192,128]{2,1,0:T(8,128)(2,1)S(1)}, u32[]{:S(2)}) copy-start(bf16[8,192,128]{2,1,0:T(8,128)(2,1)S(1)} %get-tuple-element.36.refs_0_) | copy-start | bytes 1179652
  10.4 36.8 %collective-permute-start = (bf16[8,192,128]{2,1,0:T(8,128)(2,1)}, bf16[8,192,128]{2,1,0:T(8,128)(2,1)}, u32[]{:S(2)}, u32[]{:S(2)}) collective-permute-start(bf16[8,192,128]{2,1,0:T(8,128)(2,1)} %get-tuple-element.37), channel_id=1, source_target_pairs={{0,2},{1,3},{2,4},{3,5},{4,6},{5,7},{6,0},{7,1},{8,10},{9,11},{10,... | collective-permute-start | bytes 1179656 | tf_op jit(solution)/shard_map/ppermute | solution.py:473
  13.5 33.8 %collective-permute-start.1 = (bf16[8,192,128]{2,1,0:T(8,128)(2,1)}, bf16[8,192,128]{2,1,0:T(8,128)(2,1)}, u32[]{:S(2)}, u32[]{:S(2)}) collective-permute-start(bf16[8,192,128]{2,1,0:T(8,128)(2,1)} %get-tuple-element.38), channel_id=1, source_target_pairs={{0,4},{1,5},{2,6},{3,7},{4,0},{5,1},{6,2},{7,3},{8,12},{9,13},{10,... | collective-permute-start | bytes 1179656 | tf_op jit(solution)/shard_map/ppermute | solution.py:473
  16.1 31.2 %collective-permute-start.2 = (bf16[8,192,128]{2,1,0:T(8,128)(2,1)}, bf16[8,192,128]{2,1,0:T(8,128)(2,1)}, u32[]{:S(2)}, u32[]{:S(2)}) collective-permute-start(bf16[8,192,128]{2,1,0:T(8,128)(2,1)} %get-tuple-element.39), channel_id=1, source_target_pairs={{0,6},{1,7},{2,0},{3,1},{4,2},{5,3},{6,4},{7,5},{8,14},{9,15},{10,... | collective-permute-start | bytes 1179656 | tf_op jit(solution)/shard_map/ppermute | solution.py:473
  30.2 1.1 copy-start.2
  31.4 1.2 copy-start.14
  32.6 4.5 %copy-start.22 = (s32[1,4,4,2,2,2]{1,0,4,3,2,5:T(1,128)S(1)}, s32[1,4,4,2,2,2]{1,0,4,3,2,5:T(1,128)}, u32[]{:S(2)}) copy-start(s32[1,4,4,2,2,2]{1,0,4,3,2,5:T(1,128)} %copy-done.21) | copy-start | bytes 1540
  32.6 4.5 %copy-start.31 = (s32[256]{0:T(256)S(1)}, s32[256]{0:T(256)}, u32[]{:S(2)}) copy-start(s32[256]{0:T(256)} %param.10) | copy-start | bytes 3076
  32.6 5.1 %copy-start.28 = (s32[512]{0:T(512)S(1)}, s32[512]{0:T(512)}, u32[]{:S(2)}) copy-start(s32[512]{0:T(512)} %param.11) | copy-start | bytes 6148
  32.6 7.1 %copy-start.25 = (s32[1,4,4,2,2,2]{1,0,4,3,2,5:T(1,128)S(1)}, s32[1,4,4,2,2,2]{1,0,4,3,2,5:T(1,128)}, u32[]{:S(2)}) copy-start(s32[1,4,4,2,2,2]{1,0,4,3,2,5:T(1,128)} %get-tuple-element.67) | copy-start | bytes 1540
  32.6 7.1 %copy-start.24 = (s32[1,4,4,2,2,2]{1,0,4,3,2,5:T(1,128)S(1)}, s32[1,4,4,2,2,2]{1,0,4,3,2,5:T(1,128)}, u32[]{:S(2)}) copy-start(s32[1,4,4,2,2,2]{1,0,4,3,2,5:T(1,128)} %get-tuple-element.69) | copy-start | bytes 1540
  32.6 7.1 %copy-start.23 = (s32[1,4,4,2,2,2]{1,0,4,3,2,5:T(1,128)S(1)}, s32[1,4,4,2,2,2]{1,0,4,3,2,5:T(1,128)}, u32[]{:S(2)}) copy-start(s32[1,4,4,2,2,2]{1,0,4,3,2,5:T(1,128)} %get-tuple-element.70) | copy-start | bytes 1540
  32.6 25.5 %all-to-all-start = ((bf16[8,768,128]{2,1,0:T(8,128)(2,1)}), bf16[8,768,128]{2,1,0:T(8,128)(2,1)}, u32[]{:S(2)}, u32[]{:S(2)}) async-start(bf16[8,768,128]{2,1,0:T(8,128)(2,1)} %bitcast.16.refs_0_), calls=%async_computation | async-start | bytes 3145728 | tf_op jit(solution)/shard_map/all_to_all | solution.py:478
  41.5 3.7 %copy-start.29 = (s32[512]{0:T(512)S(1)}, s32[512]{0:T(512)}, u32[]{:S(2)}) copy-start(s32[512]{0:T(512)} %param.11) | copy-start | bytes 6148
  41.5 5.7 %copy-start.30 = (s32[8]{0:T(128)S(1)}, s32[8]{0:T(128)}, u32[]{:S(2)}) copy-start(s32[8]{0:T(128)} %dynamic_slice.9) | copy-start | bytes 100
  43.6 1.6 copy-start.15
  49.5 49.7 %collective-permute-start.4 = (bf16[8,192,128]{2,1,0:T(8,128)(2,1)}, bf16[8,192,128]{2,1,0:T(8,128)(2,1)}, u32[]{:S(2)}, u32[]{:S(2)}) collective-permute-start(bf16[8,192,128]{2,1,0:T(8,128)(2,1)} %get-tuple-element.45), channel_id=1, source_target_pairs={{0,4},{1,5},{2,6},{3,7},{4,0},{5,1},{6,2},{7,3},{8,12},{9,13},{10,... | collective-permute-start | bytes 1179656 | tf_op jit(solution)/shard_map/ppermute | solution.py:473
  52.0 50.9 %collective-permute-start.5 = (bf16[8,192,128]{2,1,0:T(8,128)(2,1)}, bf16[8,192,128]{2,1,0:T(8,128)(2,1)}, u32[]{:S(2)}, u32[]{:S(2)}) collective-permute-start(bf16[8,192,128]{2,1,0:T(8,128)(2,1)} %get-tuple-element.46), channel_id=1, source_target_pairs={{0,6},{1,7},{2,0},{3,1},{4,2},{5,3},{6,4},{7,5},{8,14},{9,15},{10,... | collective-permute-start | bytes 1179656 | tf_op jit(solution)/shard_map/ppermute | solution.py:473
  55.4 47.5 %collective-permute-start.3 = (bf16[8,192,128]{2,1,0:T(8,128)(2,1)}, bf16[8,192,128]{2,1,0:T(8,128)(2,1)}, u32[]{:S(2)}, u32[]{:S(2)}) collective-permute-start(bf16[8,192,128]{2,1,0:T(8,128)(2,1)} %get-tuple-element.42.refs_4_), channel_id=1, source_target_pairs={{0,2},{1,3},{2,4},{3,5},{4,6},{5,7},{6,0},{7,1},{8,10},{9,11},{10,... | collective-permute-start | bytes 1179656 | tf_op jit(solution)/shard_map/ppermute | solution.py:473
  58.1 25.3 %all-to-all-start.1 = ((bf16[8,768,128]{2,1,0:T(8,128)(2,1)}), bf16[8,768,128]{2,1,0:T(8,128)(2,1)}, u32[]{:S(2)}, u32[]{:S(2)}) async-start(bf16[8,768,128]{2,1,0:T(8,128)(2,1)} %after.7.refs_1_), calls=%async_computation.1 | async-start | bytes 3145728 | tf_op jit(solution)/shard_map/all_to_all | solution.py:478
  64.7 76.2 %collective-permute-start.10 = (bf16[8,192,128]{2,1,0:T(8,128)(2,1)}, bf16[8,192,128]{2,1,0:T(8,128)(2,1)}, u32[]{:S(2)}, u32[]{:S(2)}) collective-permute-start(bf16[8,192,128]{2,1,0:T(8,128)(2,1)} %get-tuple-element.51), channel_id=1, source_target_pairs={{0,4},{1,5},{2,6},{3,7},{4,0},{5,1},{6,2},{7,3},{8,12},{9,13},{10,... | collective-permute-start | bytes 1179656 | tf_op jit(solution)/shard_map/ppermute | solution.py:473
  65.2 79.4 %collective-permute-start.9 = (bf16[8,192,128]{2,1,0:T(8,128)(2,1)}, bf16[8,192,128]{2,1,0:T(8,128)(2,1)}, u32[]{:S(2)}, u32[]{:S(2)}) collective-permute-start(bf16[8,192,128]{2,1,0:T(8,128)(2,1)} %get-tuple-element.44.refs_2_), channel_id=1, source_target_pairs={{0,2},{1,3},{2,4},{3,5},{4,6},{5,7},{6,0},{7,1},{8,10},{9,11},{10,... | collective-permute-start | bytes 1179656 | tf_op jit(solution)/shard_map/ppermute | solution.py:473
  83.4 4.4 %copy-start.27 = (s32[520]{0:T(1024)S(1)}, s32[520]{0:T(1024)}, u32[]{:S(2)}) copy-start(s32[520]{0:T(1024)} %pad_add_fusion.2) | copy-start | bytes 6244
  83.4 4.6 %copy-start.26 = (s32[1032]{0:T(1024)S(1)}, s32[1032]{0:T(1024)}, u32[]{:S(2)}) copy-start(s32[1032]{0:T(1024)} %concatenate.14) | copy-start | bytes 12388
  83.4 4.8 %copy-start.3 = (bf16[8,768,128]{2,1,0:T(8,128)(2,1)S(1)}, bf16[8,768,128]{2,1,0:T(8,128)(2,1)}, u32[]{:S(2)}) copy-start(bf16[8,768,128]{2,1,0:T(8,128)(2,1)} %after.8.refs_5_) | copy-start | bytes 4718596
  83.4 25.5 %all-to-all-start.2 = ((bf16[8,768,128]{2,1,0:T(8,128)(2,1)}), bf16[8,768,128]{2,1,0:T(8,128)(2,1)}, u32[]{:S(2)}, u32[]{:S(2)}) async-start(bf16[8,768,128]{2,1,0:T(8,128)(2,1)} %after.8.refs_5_), calls=%async_computation.2 | async-start | bytes 3145728 | tf_op jit(solution)/shard_map/all_to_all | solution.py:478
  88.0 10.0 %copy-start.10 = (s32[520,128]{1,0:T(8,128)}, s32[520,128]{1,0:T(8,128)S(1)}, u32[]{:S(2)}) copy-start(s32[520,128]{1,0:T(8,128)S(1)} %broadcast_in_dim.54.refs_4_.refs_7_) | copy-start | bytes 798724
  88.2 9.8 %copy-start.8 = (s32[1032,128]{1,0:T(8,128)}, s32[1032,128]{1,0:T(8,128)S(1)}, u32[]{:S(2)}) copy-start(s32[1032,128]{1,0:T(8,128)S(1)} %broadcast_in_dim.53.refs_3_.refs_6_) | copy-start | bytes 1585156
  98.1 1.1 copy-start.4
  99.2 45.4 %collective-permute-start.11 = (bf16[8,192,128]{2,1,0:T(8,128)(2,1)}, bf16[8,192,128]{2,1,0:T(8,128)(2,1)}, u32[]{:S(2)}, u32[]{:S(2)}) collective-permute-start(bf16[8,192,128]{2,1,0:T(8,128)(2,1)} %get-tuple-element.52), channel_id=1, source_target_pairs={{0,6},{1,7},{2,0},{3,1},{4,2},{5,3},{6,4},{7,5},{8,14},{9,15},{10,... | collective-permute-start | bytes 1179656 | tf_op jit(solution)/shard_map/ppermute | solution.py:473
  108.9 25.3 %all-to-all-start.3 = ((bf16[8,768,128]{2,1,0:T(8,128)(2,1)}), bf16[8,768,128]{2,1,0:T(8,128)(2,1)}, u32[]{:S(2)}, u32[]{:S(2)}) async-start(bf16[8,768,128]{2,1,0:T(8,128)(2,1)} %after.9.refs_1_), calls=%async_computation.3 | async-start | bytes 3145728 | tf_op jit(solution)/shard_map/all_to_all | solution.py:478
  115.5 48.4 %collective-permute-start.13 = (bf16[8,192,128]{2,1,0:T(8,128)(2,1)}, bf16[8,192,128]{2,1,0:T(8,128)(2,1)}, u32[]{:S(2)}, u32[]{:S(2)}) collective-permute-start(bf16[8,192,128]{2,1,0:T(8,128)(2,1)} %get-tuple-element.53), channel_id=1, source_target_pairs={{0,4},{1,5},{2,6},{3,7},{4,0},{5,1},{6,2},{7,3},{8,12},{9,13},{10,... | collective-permute-start | bytes 1179656 | tf_op jit(solution)/shard_map/ppermute | solution.py:473
  116.0 49.0 %collective-permute-start.12 = (bf16[8,192,128]{2,1,0:T(8,128)(2,1)}, bf16[8,192,128]{2,1,0:T(8,128)(2,1)}, u32[]{:S(2)}, u32[]{:S(2)}) collective-permute-start(bf16[8,192,128]{2,1,0:T(8,128)(2,1)} %get-tuple-element.47.refs_2_), channel_id=1, source_target_pairs={{0,2},{1,3},{2,4},{3,5},{4,6},{5,7},{6,0},{7,1},{8,10},{9,11},{10,... | collective-permute-start | bytes 1179656 | tf_op jit(solution)/shard_map/ppermute | solution.py:473
  134.3 25.4 %all-to-all-start.4 = ((bf16[8,768,128]{2,1,0:T(8,128)(2,1)}), bf16[8,768,128]{2,1,0:T(8,128)(2,1)}, u32[]{:S(2)}, u32[]{:S(2)}) async-start(bf16[8,768,128]{2,1,0:T(8,128)(2,1)} %after.10.refs_1_), calls=%async_computation.4 | async-start | bytes 3145728 | tf_op jit(solution)/shard_map/all_to_all | solution.py:478
  138.6 6.7 %copy-start.9 = (s32[1032,128]{1,0:T(8,128)S(1)}, s32[1032,128]{1,0:T(8,128)}, u32[]{:S(2)}) copy-start(s32[1032,128]{1,0:T(8,128)} %copy-done.8) | copy-start | bytes 1585156
  138.6 6.7 %copy-start.11 = (s32[520,128]{1,0:T(8,128)S(1)}, s32[520,128]{1,0:T(8,128)}, u32[]{:S(2)}) copy-start(s32[520,128]{1,0:T(8,128)} %copy-done.10) | copy-start | bytes 798724
  140.9 24.2 %collective-permute-start.14 = (bf16[8,192,128]{2,1,0:T(8,128)(2,1)}, bf16[8,192,128]{2,1,0:T(8,128)(2,1)}, u32[]{:S(2)}, u32[]{:S(2)}) collective-permute-start(bf16[8,192,128]{2,1,0:T(8,128)(2,1)} %get-tuple-element.54), channel_id=1, source_target_pairs={{0,6},{1,7},{2,0},{3,1},{4,2},{5,3},{6,4},{7,5},{8,14},{9,15},{10,... | collective-permute-start | bytes 1179656 | tf_op jit(solution)/shard_map/ppermute | solution.py:473
  144.6 72.3 %collective-permute-start.7 = (bf16[8,192,128]{2,1,0:T(8,128)(2,1)}, bf16[8,192,128]{2,1,0:T(8,128)(2,1)}, u32[]{:S(2)}, u32[]{:S(2)}) collective-permute-start(bf16[8,192,128]{2,1,0:T(8,128)(2,1)} %get-tuple-element.49), channel_id=1, source_target_pairs={{0,4},{1,5},{2,6},{3,7},{4,0},{5,1},{6,2},{7,3},{8,12},{9,13},{10,... | collective-permute-start | bytes 1179656 | tf_op jit(solution)/shard_map/ppermute | solution.py:473
  144.6 76.5 %collective-permute-start.6 = (bf16[8,192,128]{2,1,0:T(8,128)(2,1)}, bf16[8,192,128]{2,1,0:T(8,128)(2,1)}, u32[]{:S(2)}, u32[]{:S(2)}) collective-permute-start(bf16[8,192,128]{2,1,0:T(8,128)(2,1)} %get-tuple-element.48.refs_8_), channel_id=1, source_target_pairs={{0,6},{1,7},{2,0},{3,1},{4,2},{5,3},{6,4},{7,5},{8,14},{9,15},{10,... | collective-permute-start | bytes 1179656 | tf_op jit(solution)/shard_map/ppermute | solution.py:473
  156.1 1.1 copy-start.5
  159.6 25.3 %all-to-all-start.5 = ((bf16[8,768,128]{2,1,0:T(8,128)(2,1)}), bf16[8,768,128]{2,1,0:T(8,128)(2,1)}, u32[]{:S(2)}, u32[]{:S(2)}) async-start(bf16[8,768,128]{2,1,0:T(8,128)(2,1)} %after.11.refs_8_), calls=%async_computation.5 | async-start | bytes 3145728 | tf_op jit(solution)/shard_map/all_to_all | solution.py:478
  163.9 54.1 %collective-permute-start.8 = (bf16[8,192,128]{2,1,0:T(8,128)(2,1)}, bf16[8,192,128]{2,1,0:T(8,128)(2,1)}, u32[]{:S(2)}, u32[]{:S(2)}) collective-permute-start(bf16[8,192,128]{2,1,0:T(8,128)(2,1)} %get-tuple-element.50), channel_id=1, source_target_pairs={{0,2},{1,3},{2,4},{3,5},{4,6},{5,7},{6,0},{7,1},{8,10},{9,11},{10,... | collective-permute-start | bytes 1179656 | tf_op jit(solution)/shard_map/ppermute | solution.py:473
  174.8 1.1 copy-start.6
  185.0 25.3 %all-to-all-start.6 = ((bf16[8,768,128]{2,1,0:T(8,128)(2,1)}), bf16[8,768,128]{2,1,0:T(8,128)(2,1)}, u32[]{:S(2)}, u32[]{:S(2)}) async-start(bf16[8,768,128]{2,1,0:T(8,128)(2,1)} %after.12.refs_1_), calls=%async_computation.6 | async-start | bytes 3145728 | tf_op jit(solution)/shard_map/all_to_all | solution.py:478
  191.5 29.8 %collective-permute-start.16 = (bf16[8,192,128]{2,1,0:T(8,128)(2,1)}, bf16[8,192,128]{2,1,0:T(8,128)(2,1)}, u32[]{:S(2)}, u32[]{:S(2)}) collective-permute-start(bf16[8,192,128]{2,1,0:T(8,128)(2,1)} %get-tuple-element.56), channel_id=1, source_target_pairs={{0,4},{1,5},{2,6},{3,7},{4,0},{5,1},{6,2},{7,3},{8,12},{9,13},{10,... | collective-permute-start | bytes 1179656 | tf_op jit(solution)/shard_map/ppermute | solution.py:473
  192.1 49.5 %collective-permute-start.15 = (bf16[8,192,128]{2,1,0:T(8,128)(2,1)}, bf16[8,192,128]{2,1,0:T(8,128)(2,1)}, u32[]{:S(2)}, u32[]{:S(2)}) collective-permute-start(bf16[8,192,128]{2,1,0:T(8,128)(2,1)} %get-tuple-element.55.refs_5_), channel_id=1, source_target_pairs={{0,6},{1,7},{2,0},{3,1},{4,2},{5,3},{6,4},{7,5},{8,14},{9,15},{10,... | collective-permute-start | bytes 1179656 | tf_op jit(solution)/shard_map/ppermute | solution.py:473
  195.2 1.0 copy-start.13
  206.0 1.1 copy-start.7
  210.3 25.4 %all-to-all-start.7 = ((bf16[8,768,128]{2,1,0:T(8,128)(2,1)}), bf16[8,768,128]{2,1,0:T(8,128)(2,1)}, u32[]{:S(2)}, u32[]{:S(2)}) async-start(bf16[8,768,128]{2,1,0:T(8,128)(2,1)} %after.13.refs_1_), calls=%async_computation.7 | async-start | bytes 3145728 | tf_op jit(solution)/shard_map/all_to_all | solution.py:478
  216.9 21.0 %collective-permute-start.17 = (bf16[8,192,128]{2,1,0:T(8,128)(2,1)}, bf16[8,192,128]{2,1,0:T(8,128)(2,1)}, u32[]{:S(2)}, u32[]{:S(2)}) collective-permute-start(bf16[8,192,128]{2,1,0:T(8,128)(2,1)} %get-tuple-element.57), channel_id=1, source_target_pairs={{0,2},{1,3},{2,4},{3,5},{4,6},{5,7},{6,0},{7,1},{8,10},{9,11},{10,... | collective-permute-start | bytes 1179656 | tf_op jit(solution)/shard_map/ppermute | solution.py:473
  218.0 37.9 %collective-permute-start.19 = (bf16[8,192,128]{2,1,0:T(8,128)(2,1)}, bf16[8,192,128]{2,1,0:T(8,128)(2,1)}, u32[]{:S(2)}, u32[]{:S(2)}) collective-permute-start(bf16[8,192,128]{2,1,0:T(8,128)(2,1)} %get-tuple-element.59), channel_id=1, source_target_pairs={{0,4},{1,5},{2,6},{3,7},{4,0},{5,1},{6,2},{7,3},{8,12},{9,13},{10,... | collective-permute-start | bytes 1179656 | tf_op jit(solution)/shard_map/ppermute | solution.py:473
  221.1 34.8 %collective-permute-start.20 = (bf16[8,192,128]{2,1,0:T(8,128)(2,1)}, bf16[8,192,128]{2,1,0:T(8,128)(2,1)}, u32[]{:S(2)}, u32[]{:S(2)}) collective-permute-start(bf16[8,192,128]{2,1,0:T(8,128)(2,1)} %get-tuple-element.60), channel_id=1, source_target_pairs={{0,2},{1,3},{2,4},{3,5},{4,6},{5,7},{6,0},{7,1},{8,10},{9,11},{10,... | collective-permute-start | bytes 1179656 | tf_op jit(solution)/shard_map/ppermute | solution.py:473
  221.3 40.9 %collective-permute-start.18 = (bf16[8,192,128]{2,1,0:T(8,128)(2,1)}, bf16[8,192,128]{2,1,0:T(8,128)(2,1)}, u32[]{:S(2)}, u32[]{:S(2)}) collective-permute-start(bf16[8,192,128]{2,1,0:T(8,128)(2,1)} %get-tuple-element.58.refs_1_), channel_id=1, source_target_pairs={{0,6},{1,7},{2,0},{3,1},{4,2},{5,3},{6,4},{7,5},{8,14},{9,15},{10,... | collective-permute-start | bytes 1179656 | tf_op jit(solution)/shard_map/ppermute | solution.py:473
  237.9 38.5 %collective-permute-start.24 = (bf16[8,96,128]{2,1,0:T(8,128)(2,1)}, bf16[8,96,128]{2,1,0:T(8,128)(2,1)S(1)}, u32[]{:S(2)}, u32[]{:S(2)}) collective-permute-start(bf16[8,96,128]{2,1,0:T(8,128)(2,1)} %get-tuple-element.64), channel_id=1, source_target_pairs={{0,6},{1,7},{2,0},{3,1},{4,2},{5,3},{6,4},{7,5},{8,14},{9,15},{10,... | collective-permute-start | bytes 589832 | tf_op jit(solution)/shard_map/ppermute | solution.py:473
  241.6 39.6 %collective-permute-start.25 = (bf16[8,96,128]{2,1,0:T(8,128)(2,1)}, bf16[8,96,128]{2,1,0:T(8,128)(2,1)S(1)}, u32[]{:S(2)}, u32[]{:S(2)}) collective-permute-start(bf16[8,96,128]{2,1,0:T(8,128)(2,1)} %get-tuple-element.65), channel_id=1, source_target_pairs={{0,4},{1,5},{2,6},{3,7},{4,0},{5,1},{6,2},{7,3},{8,12},{9,13},{10,... | collective-permute-start | bytes 589832 | tf_op jit(solution)/shard_map/ppermute | solution.py:473
  255.9 25.2 %collective-permute-start.26 = (bf16[8,96,128]{2,1,0:T(8,128)(2,1)}, bf16[8,96,128]{2,1,0:T(8,128)(2,1)S(1)}, u32[]{:S(2)}, u32[]{:S(2)}) collective-permute-start(bf16[8,96,128]{2,1,0:T(8,128)(2,1)} %get-tuple-element.66), channel_id=1, source_target_pairs={{0,2},{1,3},{2,4},{3,5},{4,6},{5,7},{6,0},{7,1},{8,10},{9,11},{10,... | collective-permute-start | bytes 589832 | tf_op jit(solution)/shard_map/ppermute | solution.py:473
  255.9 35.3 %collective-permute-start.21 = (bf16[8,96,128]{2,1,0:T(8,128)(2,1)}, bf16[8,96,128]{2,1,0:T(8,128)(2,1)}, u32[]{:S(2)}, u32[]{:S(2)}) collective-permute-start(bf16[8,96,128]{2,1,0:T(8,128)(2,1)} %get-tuple-element.61), channel_id=1, source_target_pairs={{0,6},{1,7},{2,0},{3,1},{4,2},{5,3},{6,4},{7,5},{8,14},{9,15},{10,... | collective-permute-start | bytes 589832 | tf_op jit(solution)/shard_map/ppermute | solution.py:473
  262.2 35.8 %collective-permute-start.22 = (bf16[8,96,128]{2,1,0:T(8,128)(2,1)}, bf16[8,96,128]{2,1,0:T(8,128)(2,1)}, u32[]{:S(2)}, u32[]{:S(2)}) collective-permute-start(bf16[8,96,128]{2,1,0:T(8,128)(2,1)} %get-tuple-element.62), channel_id=1, source_target_pairs={{0,4},{1,5},{2,6},{3,7},{4,0},{5,1},{6,2},{7,3},{8,12},{9,13},{10,... | collective-permute-start | bytes 589832 | tf_op jit(solution)/shard_map/ppermute | solution.py:473
  276.4 21.6 %collective-permute-start.23 = (bf16[8,96,128]{2,1,0:T(8,128)(2,1)}, bf16[8,96,128]{2,1,0:T(8,128)(2,1)}, u32[]{:S(2)}, u32[]{:S(2)}) collective-permute-start(bf16[8,96,128]{2,1,0:T(8,128)(2,1)} %get-tuple-element.63), channel_id=1, source_target_pairs={{0,2},{1,3},{2,4},{3,5},{4,6},{5,7},{6,0},{7,1},{8,10},{9,11},{10,... | collective-permute-start | bytes 589832 | tf_op jit(solution)/shard_map/ppermute | solution.py:473
  298.0 10.2 %copy-start.1 = (bf16[16,128,128]{2,1,0:T(8,128)(2,1)S(1)}, bf16[16,128,128]{2,1,0:T(8,128)(2,1)}, u32[]{:S(2)}) copy-start(bf16[16,128,128]{2,1,0:T(8,128)(2,1)} %param.9) | copy-start | bytes 1572868
  (3 other events, 2.5 us)

commit v6 on v5

--- a/solution.py
+++ b/solution.py
@@ -552,25 +552,28 @@
     turned_waves = waves.transpose(0, 2, 1, 3)
     sent = fourier_some(grid, waves[0].reshape(-1, 1), parity, [plane] * layers)
     z0 = along(sent[0], sent[1:layers])
-    rows = turned_waves[1:].reshape(-1, 1)
-    sent = fourier_some(grid, rows, parity, [plane * layers] * 3, sent[0])
-    x1, x2, x3 = [x.reshape(joined_shape) for x in sent]
+    rows = turned_waves[2].reshape(-1, 1)
+    x2 = fourier_some(grid, rows, parity, [plane * layers], sent[0])[0].reshape(joined_shape)
+    rows = turned_waves[1].reshape(-1, 1)
+    x1 = fourier_some(grid, rows, parity, [plane * layers], x2)[0].reshape(joined_shape)
     p2 = across(x2)
-    rows = jnp.stack([waves[0], waves[2], waves[3], waves[1]]).reshape(-1, 1)
-    synthesis = synthesis_rows(rows, points, ROWS * layers * plane, x2)
-    u1 = part_slots(x1, layers, None, synthesis, *z0[1:])[0]
+    u1 = [after(x, *z0[1:]) for x in part_slots(x1, layers, None)[0]]
     z1 = along(x1, u1)
-    j0 = after(join_slots(z0, u1[0]), p2)
+    j0 = after(join_slots(z0, *u1), p2)
     p0 = across(j0)
     u2 = part_slots(p2, layers, None, j0)[0]
     z2 = along(p2, u2)
-    x3 = after(x3, p0, u2[0])
+    rows = turned_waves[3].reshape(-1, 1)
+    x3 = fourier_some(grid, rows, parity, [plane * layers], u2[0])[0].reshape(joined_shape)
+    rows = jnp.stack([waves[0], waves[2], waves[3], waves[1]]).reshape(-1, 1)
+    synthesis = synthesis_rows(rows, points, ROWS * layers * plane, x3)
+    x3 = after(x3, p0, synthesis)
     p3 = across(x3)
     s0 = solve(0, [p0], x3)
     j1 = join_slots(z1, s0)
-    s0 = after(s0, p3, j1)
+    s0 = after(s0, p3)
     r0 = across(s0)
-    u3 = part_slots(p3, layers, None, s0)[0]
+    u3 = part_slots(p3, layers, None, s0, j1)[0]
     z3 = along(p3, u3)
     j1 = after(j1, r0, u3[0])
     p1 = across(j1)

time: 310 us -> 308 us (level)
  Pallas kernels: 102 us -> 110 us
  waiting for transfers between devices: 82 us -> 74.6 us
  starting transfers between devices: 103 us -> 99.5 us
    all_to_all x8, waiting for transfers between devices: 58 us -> 45.3 us  [exchange_in_plane(): lax.all_to_all(x, ('lat', 'lev'), split_axis=0, concat_axis=0, tiled=True...]
    pallas_call x2 -> x4, Pallas kernels: 19.7 us -> 27.9 us  [fourier_some(): pl.pallas_call(functools.partial(fourier_kernel, len(ready)), out_shape=[...]
    ppermute x27, waiting for transfers between devices: 23.9 us -> 29.3 us  [turn_along_z(): moved.append(lax.ppermute(slot, 'lev', pairs))]
    ppermute x27, starting transfers between devices: 68.4 us -> 64.8 us  [turn_along_z(): moved.append(lax.ppermute(slot, 'lev', pairs))]
    unnamed x66 -> x72, local copies, waits for them, and re-layouts: 11.3 us -> 11.2 us
  transfers between devices with their start and end apart: 35 -> 35, of which waited for: 11 -> 10; matrix products, arithmetic and copies ran while one was open for 2% -> 3% of each run, Pallas kernels for 27% -> 30%
where the time goes in v6:
time: 308 us; the launch traced here: 307 us
  Pallas kernels  110 us (36%)
  starting transfers between devices  99.5 us (32%)
  waiting for transfers between devices  74.6 us (24%)
  local copies, waits for them, and re-layouts  18.8 us (6%)
    ppermute x27, starting transfers between devices, turn_along_z(): moved.append(lax.ppermute(slot, 'lev', pairs))  64.8 us
    all_to_all x8, waiting for transfers between devices, exchange_in_plane(): lax.all_to_all(x, ('lat', 'lev'), split_axis=0, concat_axis=0, tiled=True...  45.3 us
    pallas_call x4, Pallas kernels, spectral_chunk(): pl.pallas_call(functools.partial(spectral_kernel, len(pieces)), out_shape...  39.1 us
    all_to_all x8, starting transfers between devices, exchange_in_plane(): lax.all_to_all(x, ('lat', 'lev'), split_axis=0, concat_axis=0, tiled=True...  34.7 us
    ppermute x27, waiting for transfers between devices, turn_along_z(): moved.append(lax.ppermute(slot, 'lev', pairs))  29.3 us
    pallas_call x4, Pallas kernels, fourier_some(): pl.pallas_call(functools.partial(fourier_kernel, len(ready)), out_shape=[...  27.9 us
    pallas_call x2, Pallas kernels, synthesis_part(): pl.pallas_call(functools.partial(synthesis_kernel, len(fields)), out_shap...  20.3 us
    pallas_call x7, Pallas kernels, part_slots(): pl.pallas_call(functools.partial(part_kernel, layers, cuts), out_shape=[j...  15.9 us
  transfers between devices with their start and end apart: 35, of which 10 were waited for; matrix products, arithmetic and copies ran while one was open for 3% of the time, Pallas kernels for 30%

profile of v6, /device:TPU:0, one launch (start us, length us, event | category | flops | bytes accessed | tf_op | source)
XLA Modules:
  0.0 306.6 jit_solution(664551570168381214)
XLA Ops:
  3.0 7.4 %fourier_some.4 = (bf16[8,192,128]{2,1,0:T(8,128)(2,1)S(1)}, bf16[8,192,128]{2,1,0:T(8,128)(2,1)}, bf16[8,192,128]{2,1,0:T(8,128)(2,1)}, bf16[8,192,128]{2,1,0:T(8,128)(2,1)}) custom-call(s32[1]{0:T(128)} %bitcast.parity_ref, s32[256,1]{1,0:T(8,128)S(1)} %broadcast_in_dim.55.wave_ref, bf16[2,4,2,192,1536]{4,3,2,1,0:T(8,128)(2,1)} %bitcast.82), custom_call_target="tpu_custom_call" | custom-call | flops 9999999827968 | bytes 100000000 | tf_op jit(solution)/shard_map/fourier_some/pallas_call | solution.py:178
  10.4 3.0 collective-permute-start
  13.4 2.6 collective-permute-start.1
  16.0 1.3 collective-permute-start.2
  18.4 7.4 %fourier_some.5 = bf16[32,192,128]{2,1,0:T(8,128)(2,1)} custom-call(s32[1]{0:T(128)} %bitcast.parity_ref, s32[256,1]{1,0:T(8,128)S(1)} %reshape_squeeze.14.wave_ref, bf16[2,4,2,192,1536]{4,3,2,1,0:T(8,128)(2,1)} %bitcast.83, bf16[8,192,128]{2,1,0:T(8,128)(2,1)S(1)} %get-tuple-element.33.refs_0_), custom_call_target="tpu_custom_call" | custom-call | flops 9999999827968 | bytes 100000000 | tf_op jit(solution)/shard_map/fourier_some/pallas_call | solution.py:178
  25.8 4.5 %all-to-all-start = ((bf16[8,768,128]{2,1,0:T(8,128)(2,1)}), bf16[8,768,128]{2,1,0:T(8,128)(2,1)}, u32[]{:S(2)}, u32[]{:S(2)}) async-start(bf16[8,768,128]{2,1,0:T(8,128)(2,1)} %bitcast.9.refs_0_), calls=%async_computation | async-start | bytes 3145728 | tf_op jit(solution)/shard_map/all_to_all | solution.py:478
  31.6 1.3 concatenate.14
  35.3 6.6 %fourier_some.6 = bf16[32,192,128]{2,1,0:T(8,128)(2,1)S(1)} custom-call(s32[1]{0:T(128)} %bitcast.parity_ref, s32[256,1]{1,0:T(8,128)S(1)} %reshape_squeeze.13.wave_ref, bf16[2,4,2,192,1536]{4,3,2,1,0:T(8,128)(2,1)} %bitcast.84, bf16[8,768,128]{2,1,0:T(8,128)(2,1)} %bitcast.9.refs_0_), custom_call_target="tpu_custom_call" | custom-call | flops 9999999827968 | bytes 100000000 | tf_op jit(solution)/shard_map/fourier_some/pallas_call | solution.py:178
  41.9 1.1 copy-done.15
  43.1 2.3 part_slots.7
  46.0 1.2 pad_add_fusion.2
  47.3 4.4 %collective-permute-start.5 = (bf16[8,192,128]{2,1,0:T(8,128)(2,1)}, bf16[8,192,128]{2,1,0:T(8,128)(2,1)}, u32[]{:S(2)}, u32[]{:S(2)}) collective-permute-start(bf16[8,192,128]{2,1,0:T(8,128)(2,1)} %after.12.refs_6_), channel_id=1, source_target_pairs={{0,6},{1,7},{2,0},{3,1},{4,2},{5,3},{6,4},{7,5},{8,14},{9,15},{10,... | collective-permute-start | bytes 1179656 | tf_op jit(solution)/shard_map/ppermute | solution.py:473
  52.4 2.5 join_slots.2.refs_0_
  54.9 4.3 %all-to-all-start.1 = ((bf16[8,768,128]{2,1,0:T(8,128)(2,1)}), bf16[8,768,128]{2,1,0:T(8,128)(2,1)}, u32[]{:S(2)}, u32[]{:S(2)}) async-start(bf16[8,768,128]{2,1,0:T(8,128)(2,1)} %after.13.refs_1_), calls=%async_computation.1 | async-start | bytes 3145728 | tf_op jit(solution)/shard_map/all_to_all | solution.py:478
  59.2 2.3 part_slots.8
  61.5 2.3 collective-permute-start.10
  63.8 1.9 collective-permute-start.9
  66.8 6.5 %fourier_some.7 = bf16[32,192,128]{2,1,0:T(8,128)(2,1)S(1)} custom-call(s32[1]{0:T(128)} %bitcast.parity_ref, s32[256,1]{1,0:T(8,128)S(1)} %reshape_squeeze.15.wave_ref, bf16[2,4,2,192,1536]{4,3,2,1,0:T(8,128)(2,1)} %bitcast.85, bf16[8,192,128]{2,1,0:T(8,128)(2,1)S(1)} %copy-done.13), custom_call_target="tpu_custom_call" | custom-call | flops 9999999827968 | bytes 100000000 | tf_op jit(solution)/shard_map/fourier_some/pallas_call | solution.py:178
  73.3 2.1 synthesis_rows.1.refs_2_.refs_16_
  75.4 1.6 copy-done.16
  77.0 3.2 %all-to-all-done.1.refs_1_.refs_0_ = bf16[8,768,128]{2,1,0:T(8,128)(2,1)} async-done(((bf16[8,768,128]{2,1,0:T(8,128)(2,1)}), bf16[8,768,128]{2,1,0:T(8,128)(2,1)}, u32[]{:S(2)}, u32[]{:S(2)}) %all-to-all-start.1) | async-done | bytes 1572896 | tf_op jit(solution)/shard_map/all_to_all | solution.py:478
  80.3 4.4 %all-to-all-start.2 = ((bf16[8,768,128]{2,1,0:T(8,128)(2,1)}), bf16[8,768,128]{2,1,0:T(8,128)(2,1)}, u32[]{:S(2)}, u32[]{:S(2)}) async-start(bf16[8,768,128]{2,1,0:T(8,128)(2,1)} %after.14.refs_5_), calls=%async_computation.2 | async-start | bytes 3145728 | tf_op jit(solution)/shard_map/all_to_all | solution.py:478
  85.1 9.8 %spectral_chunk.4 = bf16[4,8,192,128]{3,2,1,0:T(8,128)(2,1)S(1)} custom-call(s32[2]{0:T(128)S(1)} %get-tuple-element.73.lower_ref, bf16[8,768,128]{2,1,0:T(8,128)(2,1)} %all-to-all-done.1.refs_1_.refs_0_, bf16[32,520,768]{2,1,0:T(8,128)(2,1)} %bitcast.78, bf16[1024,256]{1,0:T(8,128)(2,1)S(1)} %bitcast.60, s32[1032,128]{1,0:T(8,128)S(1)} %broadcast_in_dim.46.refs_3_.refs_6_, ...), custom_call_target="tpu_custom_call" | custom-call | flops 9999999827968 | bytes 100000000 | tf_op jit(solution)/shard_map/spectral_chunk/pallas_call | solution.py:314
  94.9 1.1 copy-done.2
  96.1 3.6 %collective-permute-start.11 = (bf16[8,192,128]{2,1,0:T(8,128)(2,1)}, bf16[8,192,128]{2,1,0:T(8,128)(2,1)}, u32[]{:S(2)}, u32[]{:S(2)}) collective-permute-start(bf16[8,192,128]{2,1,0:T(8,128)(2,1)} %get-tuple-element.46), channel_id=1, source_target_pairs={{0,6},{1,7},{2,0},{3,1},{4,2},{5,3},{6,4},{7,5},{8,14},{9,15},{10,... | collective-permute-start | bytes 1179656 | tf_op jit(solution)/shard_map/ppermute | solution.py:473
  99.7 5.0 %collective-permute-done.4.refs_2_ = bf16[8,192,128]{2,1,0:T(8,128)(2,1)} collective-permute-done((bf16[8,192,128]{2,1,0:T(8,128)(2,1)}, bf16[8,192,128]{2,1,0:T(8,128)(2,1)}, u32[]{:S(2)}, u32[]{:S(2)}) %collective-permute-start.4) | collective-permute-done | bytes 393248 | tf_op jit(solution)/shard_map/ppermute | solution.py:473
  104.7 2.4 join_slots.3.refs_2_.refs_0_
  107.1 4.3 %all-to-all-start.3 = ((bf16[8,768,128]{2,1,0:T(8,128)(2,1)}), bf16[8,768,128]{2,1,0:T(8,128)(2,1)}, u32[]{:S(2)}, u32[]{:S(2)}) async-start(bf16[8,768,128]{2,1,0:T(8,128)(2,1)} %after.15.refs_1_), calls=%async_computation.3 | async-start | bytes 3145728 | tf_op jit(solution)/shard_map/all_to_all | solution.py:478
  111.4 2.2 part_slots.9
  114.6 1.9 collective-permute-start.12
  116.5 16.0 %all-to-all-done.3.refs_1_.refs_0_ = bf16[8,768,128]{2,1,0:T(8,128)(2,1)} async-done(((bf16[8,768,128]{2,1,0:T(8,128)(2,1)}), bf16[8,768,128]{2,1,0:T(8,128)(2,1)}, u32[]{:S(2)}, u32[]{:S(2)}) %all-to-all-start.3) | async-done | bytes 1572896 | tf_op jit(solution)/shard_map/all_to_all | solution.py:478
  132.5 4.3 %all-to-all-start.4 = ((bf16[8,768,128]{2,1,0:T(8,128)(2,1)}), bf16[8,768,128]{2,1,0:T(8,128)(2,1)}, u32[]{:S(2)}, u32[]{:S(2)}) async-start(bf16[8,768,128]{2,1,0:T(8,128)(2,1)} %after.16.refs_1_), calls=%async_computation.4 | async-start | bytes 3145728 | tf_op jit(solution)/shard_map/all_to_all | solution.py:478
  136.8 2.4 part_slots.10
  139.2 2.2 collective-permute-start.14
  142.1 1.5 collective-permute-start.6
  144.6 9.7 %spectral_chunk.5 = bf16[4,8,192,128]{3,2,1,0:T(8,128)(2,1)S(1)} custom-call(s32[2]{0:T(128)S(1)} %get-tuple-element.72.lower_ref, bf16[8,768,128]{2,1,0:T(8,128)(2,1)} %all-to-all-done.refs_1_.refs_0_, bf16[8,192,128]{2,1,0:T(8,128)(2,1)} %collective-permute-done.9.refs_1_, bf16[8,192,128]{2,1,0:T(8,128)(2,1)} %collective-permute-done.10.refs_2_, ...), custom_call_target="tpu_custom_call" | custom-call | flops 9999999827968 | bytes 100000000 | tf_op jit(solution)/shard_map/spectral_chunk/pallas_call | solution.py:314
  154.4 1.1 copy-done.3
  155.5 2.3 all-to-all-done.4.refs_1_.refs_0_
  157.8 4.3 %all-to-all-start.5 = ((bf16[8,768,128]{2,1,0:T(8,128)(2,1)}), bf16[8,768,128]{2,1,0:T(8,128)(2,1)}, u32[]{:S(2)}, u32[]{:S(2)}) async-start(bf16[8,768,128]{2,1,0:T(8,128)(2,1)} %after.17.refs_8_), calls=%async_computation.5 | async-start | bytes 3145728 | tf_op jit(solution)/shard_map/all_to_all | solution.py:478
  162.2 1.5 collective-permute-start.8
  163.6 9.8 %spectral_chunk.6 = bf16[4,8,192,128]{3,2,1,0:T(8,128)(2,1)S(1)} custom-call(s32[2]{0:T(128)S(1)} %get-tuple-element.71.lower_ref, bf16[8,768,128]{2,1,0:T(8,128)(2,1)} %all-to-all-done.2.refs_1_.refs_0_, bf16[8,192,128]{2,1,0:T(8,128)(2,1)} %collective-permute-done.12.refs_1_, bf16[8,192,128]{2,1,0:T(8,128)(2,1)} %collective-permute-done.13.refs_2_, ...), custom_call_target="tpu_custom_call" | custom-call | flops 9999999827968 | bytes 100000000 | tf_op jit(solution)/shard_map/spectral_chunk/pallas_call | solution.py:314
  174.5 8.6 %all-to-all-done.5.refs_1_.refs_0_.refs_4_ = bf16[8,768,128]{2,1,0:T(8,128)(2,1)} async-done(((bf16[8,768,128]{2,1,0:T(8,128)(2,1)}), bf16[8,768,128]{2,1,0:T(8,128)(2,1)}, u32[]{:S(2)}, u32[]{:S(2)}) %all-to-all-start.5) | async-done | bytes 1572896 | tf_op jit(solution)/shard_map/all_to_all | solution.py:478
  183.2 4.3 %all-to-all-start.6 = ((bf16[8,768,128]{2,1,0:T(8,128)(2,1)}), bf16[8,768,128]{2,1,0:T(8,128)(2,1)}, u32[]{:S(2)}, u32[]{:S(2)}) async-start(bf16[8,768,128]{2,1,0:T(8,128)(2,1)} %after.18.refs_1_), calls=%async_computation.6 | async-start | bytes 3145728 | tf_op jit(solution)/shard_map/all_to_all | solution.py:478
  187.5 2.3 part_slots.11
  190.6 2.9 collective-permute-start.15
  194.6 9.8 %spectral_chunk.7 = bf16[4,8,192,128]{3,2,1,0:T(8,128)(2,1)S(1)} custom-call(s32[2]{0:T(128)S(1)} %get-tuple-element.70.lower_ref, bf16[8,768,128]{2,1,0:T(8,128)(2,1)} %all-to-all-done.4.refs_1_.refs_0_, bf16[32,520,768]{2,1,0:T(8,128)(2,1)} %bitcast.81, bf16[1024,256]{1,0:T(8,128)(2,1)S(1)} %bitcast.63, s32[1032,128]{1,0:T(8,128)S(1)} %copy-done.9, ...), custom_call_target="tpu_custom_call" | custom-call | flops 9999999827968 | bytes 100000000 | tf_op jit(solution)/shard_map/spectral_chunk/pallas_call | solution.py:314
  205.5 3.0 all-to-all-done.6.refs_1_.refs_0_.refs_8_
  208.5 4.3 %all-to-all-start.7 = ((bf16[8,768,128]{2,1,0:T(8,128)(2,1)}), bf16[8,768,128]{2,1,0:T(8,128)(2,1)}, u32[]{:S(2)}, u32[]{:S(2)}) async-start(bf16[8,768,128]{2,1,0:T(8,128)(2,1)} %after.19.refs_1_), calls=%async_computation.7 | async-start | bytes 3145728 | tf_op jit(solution)/shard_map/all_to_all | solution.py:478
  212.8 2.3 part_slots.12
  215.1 1.4 collective-permute-start.17
  216.6 1.4 collective-permute-start.19
  217.9 1.6 collective-permute-start.20
  219.5 2.2 collective-permute-start.18
  221.7 12.1 %all-to-all-done.7.refs_0_.refs_12_ = bf16[8,768,128]{2,1,0:T(8,128)(2,1)} async-done(((bf16[8,768,128]{2,1,0:T(8,128)(2,1)}), bf16[8,768,128]{2,1,0:T(8,128)(2,1)}, u32[]{:S(2)}, u32[]{:S(2)}) %all-to-all-start.7) | async-done | bytes 1572896 | tf_op jit(solution)/shard_map/all_to_all | solution.py:478
  233.9 2.2 part_slots.13
  236.1 2.3 collective-permute-start.24
  239.0 15.0 %collective-permute-done.19.refs_10_ = bf16[8,192,128]{2,1,0:T(8,128)(2,1)} collective-permute-done((bf16[8,192,128]{2,1,0:T(8,128)(2,1)}, bf16[8,192,128]{2,1,0:T(8,128)(2,1)}, u32[]{:S(2)}, u32[]{:S(2)}) %collective-permute-start.19) | collective-permute-done | bytes 393248 | tf_op jit(solution)/shard_map/ppermute | solution.py:473
  254.1 3.8 %collective-permute-start.21 = (bf16[8,96,128]{2,1,0:T(8,128)(2,1)}, bf16[8,96,128]{2,1,0:T(8,128)(2,1)}, u32[]{:S(2)}, u32[]{:S(2)}) collective-permute-start(bf16[8,96,128]{2,1,0:T(8,128)(2,1)} %get-tuple-element.55), channel_id=1, source_target_pairs={{0,6},{1,7},{2,0},{3,1},{4,2},{5,3},{6,4},{7,5},{8,14},{9,15},{10,... | collective-permute-start | bytes 589832 | tf_op jit(solution)/shard_map/ppermute | solution.py:473
  257.9 17.0 %collective-permute-start.22 = (bf16[8,96,128]{2,1,0:T(8,128)(2,1)}, bf16[8,96,128]{2,1,0:T(8,128)(2,1)}, u32[]{:S(2)}, u32[]{:S(2)}) collective-permute-start(bf16[8,96,128]{2,1,0:T(8,128)(2,1)} %get-tuple-element.56), channel_id=1, source_target_pairs={{0,4},{1,5},{2,6},{3,7},{4,0},{5,1},{6,2},{7,3},{8,12},{9,13},{10,... | collective-permute-start | bytes 589832 | tf_op jit(solution)/shard_map/ppermute | solution.py:473
  274.9 2.0 collective-permute-start.23
  276.9 2.3 collective-permute-done.25.refs_14_
  279.3 10.1 %synthesis_part.2.refs_18_ = bf16[2,4,2,192,1536]{4,3,2,1,0:T(8,128)(2,1)} custom-call(s32[1]{0:T(128)} %bitcast.parity_ref, bf16[8,768,128]{2,1,0:T(8,128)(2,1)} %all-to-all-done.3.refs_1_.refs_0_, bf16[8,192,128]{2,1,0:T(8,128)(2,1)} %collective-permute-done.6.refs_1_, bf16[8,192,128]{2,1,0:T(8,128)(2,1)} %collective-permute-done.7.refs_2_, ...), custom_call_target="tpu_custom_call" | custom-call | flops 9999999827968 | bytes 100000000 | tf_op jit(solution)/shard_map/synthesis_part/pallas_call | solution.py:387
  289.4 6.8 %collective-permute-done.22.refs_14_ = bf16[8,96,128]{2,1,0:T(8,128)(2,1)} collective-permute-done((bf16[8,96,128]{2,1,0:T(8,128)(2,1)}, bf16[8,96,128]{2,1,0:T(8,128)(2,1)}, u32[]{:S(2)}, u32[]{:S(2)}) %collective-permute-start.22) | collective-permute-done | bytes 196640 | tf_op jit(solution)/shard_map/ppermute | solution.py:473
  296.2 10.2 %synthesis_part.3 = bf16[2,4,2,192,1536]{4,3,2,1,0:T(8,128)(2,1)} custom-call(s32[1]{0:T(128)} %bitcast.parity_ref, bf16[8,768,128]{2,1,0:T(8,128)(2,1)} %all-to-all-done.3.refs_1_.refs_0_, bf16[8,192,128]{2,1,0:T(8,128)(2,1)} %collective-permute-done.6.refs_1_, ...), custom_call_target="tpu_custom_call", output_to_operand_aliasing={{}: (19, {})} | custom-call | flops 9999999827968 | bytes 100000000 | tf_op jit(solution)/shard_map/synthesis_part/pallas_call | solution.py:387
  (150 shorter events, 17.8 us)
Async XLA Ops:
  0.0 34.1 %copy-start = (bf16[16,128,128]{2,1,0:T(8,128)(2,1)S(1)}, bf16[16,128,128]{2,1,0:T(8,128)(2,1)}, u32[]{:S(2)}) copy-start(bf16[16,128,128]{2,1,0:T(8,128)(2,1)} %param.9) | copy-start | bytes 1572868
  3.0 14.3 %copy-start.19 = (s32[4,4,4,2,2,1]{1,0,4,3,2,5:T(4,128)S(1)}, s32[4,4,4,2,2,1]{1,0,4,3,2,5:T(4,128)}, u32[]{:S(2)}) copy-start(s32[4,4,4,2,2,1]{1,0,4,3,2,5:T(4,128)} %copy-done.18) | copy-start | bytes 3076
  3.0 14.3 %copy-start.21 = (s32[4,4,4,2,2,1]{1,0,4,3,2,5:T(4,128)S(1)}, s32[4,4,4,2,2,1]{1,0,4,3,2,5:T(4,128)}, u32[]{:S(2)}) copy-start(s32[4,4,4,2,2,1]{1,0,4,3,2,5:T(4,128)} %copy-done.20) | copy-start | bytes 3076
  10.4 15.4 %copy-start.17 = (bf16[8,192,128]{2,1,0:T(8,128)(2,1)}, bf16[8,192,128]{2,1,0:T(8,128)(2,1)S(1)}, u32[]{:S(2)}) copy-start(bf16[8,192,128]{2,1,0:T(8,128)(2,1)S(1)} %get-tuple-element.33.refs_0_) | copy-start | bytes 1179652
  10.4 36.9 %collective-permute-start = (bf16[8,192,128]{2,1,0:T(8,128)(2,1)}, bf16[8,192,128]{2,1,0:T(8,128)(2,1)}, u32[]{:S(2)}, u32[]{:S(2)}) collective-permute-start(bf16[8,192,128]{2,1,0:T(8,128)(2,1)} %get-tuple-element.34), channel_id=1, source_target_pairs={{0,2},{1,3},{2,4},{3,5},{4,6},{5,7},{6,0},{7,1},{8,10},{9,11},{10,... | collective-permute-start | bytes 1179656 | tf_op jit(solution)/shard_map/ppermute | solution.py:473
  13.4 33.9 %collective-permute-start.1 = (bf16[8,192,128]{2,1,0:T(8,128)(2,1)}, bf16[8,192,128]{2,1,0:T(8,128)(2,1)}, u32[]{:S(2)}, u32[]{:S(2)}) collective-permute-start(bf16[8,192,128]{2,1,0:T(8,128)(2,1)} %get-tuple-element.35), channel_id=1, source_target_pairs={{0,4},{1,5},{2,6},{3,7},{4,0},{5,1},{6,2},{7,3},{8,12},{9,13},{10,... | collective-permute-start | bytes 1179656 | tf_op jit(solution)/shard_map/ppermute | solution.py:473
  16.0 31.3 %collective-permute-start.2 = (bf16[8,192,128]{2,1,0:T(8,128)(2,1)}, bf16[8,192,128]{2,1,0:T(8,128)(2,1)}, u32[]{:S(2)}, u32[]{:S(2)}) collective-permute-start(bf16[8,192,128]{2,1,0:T(8,128)(2,1)} %get-tuple-element.36), channel_id=1, source_target_pairs={{0,6},{1,7},{2,0},{3,1},{4,2},{5,3},{6,4},{7,5},{8,14},{9,15},{10,... | collective-permute-start | bytes 1179656 | tf_op jit(solution)/shard_map/ppermute | solution.py:473
  25.8 4.6 %copy-start.23 = (s32[1,4,4,2,2,2]{1,0,4,3,2,5:T(1,128)S(1)}, s32[1,4,4,2,2,2]{1,0,4,3,2,5:T(1,128)}, u32[]{:S(2)}) copy-start(s32[1,4,4,2,2,2]{1,0,4,3,2,5:T(1,128)} %copy-done.22) | copy-start | bytes 1540
  25.8 4.6 %copy-start.34 = (s32[256]{0:T(256)S(1)}, s32[256]{0:T(256)}, u32[]{:S(2)}) copy-start(s32[256]{0:T(256)} %param.10) | copy-start | bytes 3076
  25.8 5.2 %copy-start.31 = (s32[512]{0:T(512)S(1)}, s32[512]{0:T(512)}, u32[]{:S(2)}) copy-start(s32[512]{0:T(512)} %param.11) | copy-start | bytes 6148
  25.8 7.2 %copy-start.28 = (s32[1,4,4,2,2,2]{1,0,4,3,2,5:T(1,128)S(1)}, s32[1,4,4,2,2,2]{1,0,4,3,2,5:T(1,128)}, u32[]{:S(2)}) copy-start(s32[1,4,4,2,2,2]{1,0,4,3,2,5:T(1,128)} %get-tuple-element.64) | copy-start | bytes 1540
  25.8 7.3 %copy-start.27 = (s32[1,4,4,2,2,2]{1,0,4,3,2,5:T(1,128)S(1)}, s32[1,4,4,2,2,2]{1,0,4,3,2,5:T(1,128)}, u32[]{:S(2)}) copy-start(s32[1,4,4,2,2,2]{1,0,4,3,2,5:T(1,128)} %get-tuple-element.66) | copy-start | bytes 1540
  25.8 7.3 %copy-start.26 = (s32[1,4,4,2,2,2]{1,0,4,3,2,5:T(1,128)S(1)}, s32[1,4,4,2,2,2]{1,0,4,3,2,5:T(1,128)}, u32[]{:S(2)}) copy-start(s32[1,4,4,2,2,2]{1,0,4,3,2,5:T(1,128)} %get-tuple-element.67) | copy-start | bytes 1540
  25.8 7.6 %copy-start.25 = (s32[1,8,4,8]{2,3,1,0:T(8,128)S(1)}, s32[1,8,4,8]{2,3,1,0:T(8,128)}, u32[]{:S(2)}) copy-start(s32[1,8,4,8]{2,3,1,0:T(8,128)} %get-tuple-element.61) | copy-start | bytes 3076
  25.8 7.8 %copy-start.24 = (s32[1,8,4,8]{2,3,1,0:T(8,128)S(1)}, s32[1,8,4,8]{2,3,1,0:T(8,128)}, u32[]{:S(2)}) copy-start(s32[1,8,4,8]{2,3,1,0:T(8,128)} %get-tuple-element.63) | copy-start | bytes 3076
  25.8 29.1 %all-to-all-start = ((bf16[8,768,128]{2,1,0:T(8,128)(2,1)}), bf16[8,768,128]{2,1,0:T(8,128)(2,1)}, u32[]{:S(2)}, u32[]{:S(2)}) async-start(bf16[8,768,128]{2,1,0:T(8,128)(2,1)} %bitcast.9.refs_0_), calls=%async_computation | async-start | bytes 3145728 | tf_op jit(solution)/shard_map/all_to_all | solution.py:478
  41.9 1.2 copy-start.15
  43.1 2.3 copy-start.32
  43.1 4.2 %copy-start.33 = (s32[8]{0:T(128)S(1)}, s32[8]{0:T(128)}, u32[]{:S(2)}) copy-start(s32[8]{0:T(128)} %dynamic_slice.9) | copy-start | bytes 100
  47.3 48.7 %collective-permute-start.5 = (bf16[8,192,128]{2,1,0:T(8,128)(2,1)}, bf16[8,192,128]{2,1,0:T(8,128)(2,1)}, u32[]{:S(2)}, u32[]{:S(2)}) collective-permute-start(bf16[8,192,128]{2,1,0:T(8,128)(2,1)} %after.12.refs_6_), channel_id=1, source_target_pairs={{0,6},{1,7},{2,0},{3,1},{4,2},{5,3},{6,4},{7,5},{8,14},{9,15},{10,... | collective-permute-start | bytes 1179656 | tf_op jit(solution)/shard_map/ppermute | solution.py:473
  51.8 52.9 %collective-permute-start.4 = (bf16[8,192,128]{2,1,0:T(8,128)(2,1)}, bf16[8,192,128]{2,1,0:T(8,128)(2,1)}, u32[]{:S(2)}, u32[]{:S(2)}) collective-permute-start(bf16[8,192,128]{2,1,0:T(8,128)(2,1)} %after.11.refs_5_), channel_id=1, source_target_pairs={{0,4},{1,5},{2,6},{3,7},{4,0},{5,1},{6,2},{7,3},{8,12},{9,13},{10,... | collective-permute-start | bytes 1179656 | tf_op jit(solution)/shard_map/ppermute | solution.py:473
  52.2 52.5 %collective-permute-start.3 = (bf16[8,192,128]{2,1,0:T(8,128)(2,1)}, bf16[8,192,128]{2,1,0:T(8,128)(2,1)}, u32[]{:S(2)}, u32[]{:S(2)}) collective-permute-start(bf16[8,192,128]{2,1,0:T(8,128)(2,1)} %after.10.refs_4_), channel_id=1, source_target_pairs={{0,2},{1,3},{2,4},{3,5},{4,6},{5,7},{6,0},{7,1},{8,10},{9,11},{10,... | collective-permute-start | bytes 1179656 | tf_op jit(solution)/shard_map/ppermute | solution.py:473
  54.9 25.3 %all-to-all-start.1 = ((bf16[8,768,128]{2,1,0:T(8,128)(2,1)}), bf16[8,768,128]{2,1,0:T(8,128)(2,1)}, u32[]{:S(2)}, u32[]{:S(2)}) async-start(bf16[8,768,128]{2,1,0:T(8,128)(2,1)} %after.13.refs_1_), calls=%async_computation.1 | async-start | bytes 3145728 | tf_op jit(solution)/shard_map/all_to_all | solution.py:478
  61.5 77.6 %collective-permute-start.10 = (bf16[8,192,128]{2,1,0:T(8,128)(2,1)}, bf16[8,192,128]{2,1,0:T(8,128)(2,1)}, u32[]{:S(2)}, u32[]{:S(2)}) collective-permute-start(bf16[8,192,128]{2,1,0:T(8,128)(2,1)} %get-tuple-element.45), channel_id=1, source_target_pairs={{0,4},{1,5},{2,6},{3,7},{4,0},{5,1},{6,2},{7,3},{8,12},{9,13},{10,... | collective-permute-start | bytes 1179656 | tf_op jit(solution)/shard_map/ppermute | solution.py:473
  63.8 78.3 %collective-permute-start.9 = (bf16[8,192,128]{2,1,0:T(8,128)(2,1)}, bf16[8,192,128]{2,1,0:T(8,128)(2,1)}, u32[]{:S(2)}, u32[]{:S(2)}) collective-permute-start(bf16[8,192,128]{2,1,0:T(8,128)(2,1)} %get-tuple-element.40.refs_0_), channel_id=1, source_target_pairs={{0,2},{1,3},{2,4},{3,5},{4,6},{5,7},{6,0},{7,1},{8,10},{9,11},{10,... | collective-permute-start | bytes 1179656 | tf_op jit(solution)/shard_map/ppermute | solution.py:473
  73.3 2.1 copy-start.6
  75.4 1.6 copy-start.16
  80.3 4.4 %copy-start.30 = (s32[520]{0:T(1024)S(1)}, s32[520]{0:T(1024)}, u32[]{:S(2)}) copy-start(s32[520]{0:T(1024)} %pad_add_fusion.2) | copy-start | bytes 6244
  80.3 4.6 %copy-start.29 = (s32[1032]{0:T(1024)S(1)}, s32[1032]{0:T(1024)}, u32[]{:S(2)}) copy-start(s32[1032]{0:T(1024)} %concatenate.14) | copy-start | bytes 12388
  80.3 4.8 %copy-start.7 = (bf16[8,768,128]{2,1,0:T(8,128)(2,1)S(1)}, bf16[8,768,128]{2,1,0:T(8,128)(2,1)}, u32[]{:S(2)}) copy-start(bf16[8,768,128]{2,1,0:T(8,128)(2,1)} %after.14.refs_5_) | copy-start | bytes 4718596
  80.3 26.9 %all-to-all-start.2 = ((bf16[8,768,128]{2,1,0:T(8,128)(2,1)}), bf16[8,768,128]{2,1,0:T(8,128)(2,1)}, u32[]{:S(2)}, u32[]{:S(2)}) async-start(bf16[8,768,128]{2,1,0:T(8,128)(2,1)} %after.14.refs_5_), calls=%async_computation.2 | async-start | bytes 3145728 | tf_op jit(solution)/shard_map/all_to_all | solution.py:478
  84.8 10.0 %copy-start.10 = (s32[520,128]{1,0:T(8,128)}, s32[520,128]{1,0:T(8,128)S(1)}, u32[]{:S(2)}) copy-start(s32[520,128]{1,0:T(8,128)S(1)} %broadcast_in_dim.47.refs_4_.refs_7_) | copy-start | bytes 798724
  85.1 9.8 %copy-start.8 = (s32[1032,128]{1,0:T(8,128)}, s32[1032,128]{1,0:T(8,128)S(1)}, u32[]{:S(2)}) copy-start(s32[1032,128]{1,0:T(8,128)S(1)} %broadcast_in_dim.46.refs_3_.refs_6_) | copy-start | bytes 1585156
  94.9 1.2 copy-start.2
  96.1 45.3 %collective-permute-start.11 = (bf16[8,192,128]{2,1,0:T(8,128)(2,1)}, bf16[8,192,128]{2,1,0:T(8,128)(2,1)}, u32[]{:S(2)}, u32[]{:S(2)}) collective-permute-start(bf16[8,192,128]{2,1,0:T(8,128)(2,1)} %get-tuple-element.46), channel_id=1, source_target_pairs={{0,6},{1,7},{2,0},{3,1},{4,2},{5,3},{6,4},{7,5},{8,14},{9,15},{10,... | collective-permute-start | bytes 1179656 | tf_op jit(solution)/shard_map/ppermute | solution.py:473
  107.1 25.3 %all-to-all-start.3 = ((bf16[8,768,128]{2,1,0:T(8,128)(2,1)}), bf16[8,768,128]{2,1,0:T(8,128)(2,1)}, u32[]{:S(2)}, u32[]{:S(2)}) async-start(bf16[8,768,128]{2,1,0:T(8,128)(2,1)} %after.15.refs_1_), calls=%async_computation.3 | async-start | bytes 3145728 | tf_op jit(solution)/shard_map/all_to_all | solution.py:478
  113.7 48.5 %collective-permute-start.13 = (bf16[8,192,128]{2,1,0:T(8,128)(2,1)}, bf16[8,192,128]{2,1,0:T(8,128)(2,1)}, u32[]{:S(2)}, u32[]{:S(2)}) collective-permute-start(bf16[8,192,128]{2,1,0:T(8,128)(2,1)} %get-tuple-element.47), channel_id=1, source_target_pairs={{0,4},{1,5},{2,6},{3,7},{4,0},{5,1},{6,2},{7,3},{8,12},{9,13},{10,... | collective-permute-start | bytes 1179656 | tf_op jit(solution)/shard_map/ppermute | solution.py:473
  114.6 49.1 %collective-permute-start.12 = (bf16[8,192,128]{2,1,0:T(8,128)(2,1)}, bf16[8,192,128]{2,1,0:T(8,128)(2,1)}, u32[]{:S(2)}, u32[]{:S(2)}) collective-permute-start(bf16[8,192,128]{2,1,0:T(8,128)(2,1)} %get-tuple-element.41.refs_2_), channel_id=1, source_target_pairs={{0,2},{1,3},{2,4},{3,5},{4,6},{5,7},{6,0},{7,1},{8,10},{9,11},{10,... | collective-permute-start | bytes 1179656 | tf_op jit(solution)/shard_map/ppermute | solution.py:473
  132.5 25.3 %all-to-all-start.4 = ((bf16[8,768,128]{2,1,0:T(8,128)(2,1)}), bf16[8,768,128]{2,1,0:T(8,128)(2,1)}, u32[]{:S(2)}, u32[]{:S(2)}) async-start(bf16[8,768,128]{2,1,0:T(8,128)(2,1)} %after.16.refs_1_), calls=%async_computation.4 | async-start | bytes 3145728 | tf_op jit(solution)/shard_map/all_to_all | solution.py:478
  136.8 6.8 %copy-start.9 = (s32[1032,128]{1,0:T(8,128)S(1)}, s32[1032,128]{1,0:T(8,128)}, u32[]{:S(2)}) copy-start(s32[1032,128]{1,0:T(8,128)} %copy-done.8) | copy-start | bytes 1585156
  136.8 6.8 %copy-start.11 = (s32[520,128]{1,0:T(8,128)S(1)}, s32[520,128]{1,0:T(8,128)}, u32[]{:S(2)}) copy-start(s32[520,128]{1,0:T(8,128)} %copy-done.10) | copy-start | bytes 798724
  139.2 24.5 %collective-permute-start.14 = (bf16[8,192,128]{2,1,0:T(8,128)(2,1)}, bf16[8,192,128]{2,1,0:T(8,128)(2,1)}, u32[]{:S(2)}, u32[]{:S(2)}) collective-permute-start(bf16[8,192,128]{2,1,0:T(8,128)(2,1)} %get-tuple-element.48), channel_id=1, source_target_pairs={{0,6},{1,7},{2,0},{3,1},{4,2},{5,3},{6,4},{7,5},{8,14},{9,15},{10,... | collective-permute-start | bytes 1179656 | tf_op jit(solution)/shard_map/ppermute | solution.py:473
  141.4 73.7 %collective-permute-start.7 = (bf16[8,192,128]{2,1,0:T(8,128)(2,1)}, bf16[8,192,128]{2,1,0:T(8,128)(2,1)}, u32[]{:S(2)}, u32[]{:S(2)}) collective-permute-start(bf16[8,192,128]{2,1,0:T(8,128)(2,1)} %get-tuple-element.43), channel_id=1, source_target_pairs={{0,4},{1,5},{2,6},{3,7},{4,0},{5,1},{6,2},{7,3},{8,12},{9,13},{10,... | collective-permute-start | bytes 1179656 | tf_op jit(solution)/shard_map/ppermute | solution.py:473
  142.1 75.8 %collective-permute-start.6 = (bf16[8,192,128]{2,1,0:T(8,128)(2,1)}, bf16[8,192,128]{2,1,0:T(8,128)(2,1)}, u32[]{:S(2)}, u32[]{:S(2)}) collective-permute-start(bf16[8,192,128]{2,1,0:T(8,128)(2,1)} %get-tuple-element.42.refs_8_), channel_id=1, source_target_pairs={{0,6},{1,7},{2,0},{3,1},{4,2},{5,3},{6,4},{7,5},{8,14},{9,15},{10,... | collective-permute-start | bytes 1179656 | tf_op jit(solution)/shard_map/ppermute | solution.py:473
  154.4 1.1 copy-start.3
  157.8 25.4 %all-to-all-start.5 = ((bf16[8,768,128]{2,1,0:T(8,128)(2,1)}), bf16[8,768,128]{2,1,0:T(8,128)(2,1)}, u32[]{:S(2)}, u32[]{:S(2)}) async-start(bf16[8,768,128]{2,1,0:T(8,128)(2,1)} %after.17.refs_8_), calls=%async_computation.5 | async-start | bytes 3145728 | tf_op jit(solution)/shard_map/all_to_all | solution.py:478
  162.2 54.4 %collective-permute-start.8 = (bf16[8,192,128]{2,1,0:T(8,128)(2,1)}, bf16[8,192,128]{2,1,0:T(8,128)(2,1)}, u32[]{:S(2)}, u32[]{:S(2)}) collective-permute-start(bf16[8,192,128]{2,1,0:T(8,128)(2,1)} %get-tuple-element.44), channel_id=1, source_target_pairs={{0,2},{1,3},{2,4},{3,5},{4,6},{5,7},{6,0},{7,1},{8,10},{9,11},{10,... | collective-permute-start | bytes 1179656 | tf_op jit(solution)/shard_map/ppermute | solution.py:473
  173.4 1.1 copy-start.4
  183.2 25.3 %all-to-all-start.6 = ((bf16[8,768,128]{2,1,0:T(8,128)(2,1)}), bf16[8,768,128]{2,1,0:T(8,128)(2,1)}, u32[]{:S(2)}, u32[]{:S(2)}) async-start(bf16[8,768,128]{2,1,0:T(8,128)(2,1)} %after.18.refs_1_), calls=%async_computation.6 | async-start | bytes 3145728 | tf_op jit(solution)/shard_map/all_to_all | solution.py:478
  189.7 29.8 %collective-permute-start.16 = (bf16[8,192,128]{2,1,0:T(8,128)(2,1)}, bf16[8,192,128]{2,1,0:T(8,128)(2,1)}, u32[]{:S(2)}, u32[]{:S(2)}) collective-permute-start(bf16[8,192,128]{2,1,0:T(8,128)(2,1)} %get-tuple-element.50), channel_id=1, source_target_pairs={{0,4},{1,5},{2,6},{3,7},{4,0},{5,1},{6,2},{7,3},{8,12},{9,13},{10,... | collective-permute-start | bytes 1179656 | tf_op jit(solution)/shard_map/ppermute | solution.py:473
  190.6 47.7 %collective-permute-start.15 = (bf16[8,192,128]{2,1,0:T(8,128)(2,1)}, bf16[8,192,128]{2,1,0:T(8,128)(2,1)}, u32[]{:S(2)}, u32[]{:S(2)}) collective-permute-start(bf16[8,192,128]{2,1,0:T(8,128)(2,1)} %get-tuple-element.49.refs_5_), channel_id=1, source_target_pairs={{0,6},{1,7},{2,0},{3,1},{4,2},{5,3},{6,4},{7,5},{8,14},{9,15},{10,... | collective-permute-start | bytes 1179656 | tf_op jit(solution)/shard_map/ppermute | solution.py:473
  204.4 1.1 copy-start.5
  208.5 25.3 %all-to-all-start.7 = ((bf16[8,768,128]{2,1,0:T(8,128)(2,1)}), bf16[8,768,128]{2,1,0:T(8,128)(2,1)}, u32[]{:S(2)}, u32[]{:S(2)}) async-start(bf16[8,768,128]{2,1,0:T(8,128)(2,1)} %after.19.refs_1_), calls=%async_computation.7 | async-start | bytes 3145728 | tf_op jit(solution)/shard_map/all_to_all | solution.py:478
  215.1 21.0 %collective-permute-start.17 = (bf16[8,192,128]{2,1,0:T(8,128)(2,1)}, bf16[8,192,128]{2,1,0:T(8,128)(2,1)}, u32[]{:S(2)}, u32[]{:S(2)}) collective-permute-start(bf16[8,192,128]{2,1,0:T(8,128)(2,1)} %get-tuple-element.51), channel_id=1, source_target_pairs={{0,2},{1,3},{2,4},{3,5},{4,6},{5,7},{6,0},{7,1},{8,10},{9,11},{10,... | collective-permute-start | bytes 1179656 | tf_op jit(solution)/shard_map/ppermute | solution.py:473
  216.6 37.5 %collective-permute-start.19 = (bf16[8,192,128]{2,1,0:T(8,128)(2,1)}, bf16[8,192,128]{2,1,0:T(8,128)(2,1)}, u32[]{:S(2)}, u32[]{:S(2)}) collective-permute-start(bf16[8,192,128]{2,1,0:T(8,128)(2,1)} %get-tuple-element.53), channel_id=1, source_target_pairs={{0,4},{1,5},{2,6},{3,7},{4,0},{5,1},{6,2},{7,3},{8,12},{9,13},{10,... | collective-permute-start | bytes 1179656 | tf_op jit(solution)/shard_map/ppermute | solution.py:473
  217.9 36.1 %collective-permute-start.20 = (bf16[8,192,128]{2,1,0:T(8,128)(2,1)}, bf16[8,192,128]{2,1,0:T(8,128)(2,1)}, u32[]{:S(2)}, u32[]{:S(2)}) collective-permute-start(bf16[8,192,128]{2,1,0:T(8,128)(2,1)} %get-tuple-element.54), channel_id=1, source_target_pairs={{0,2},{1,3},{2,4},{3,5},{4,6},{5,7},{6,0},{7,1},{8,10},{9,11},{10,... | collective-permute-start | bytes 1179656 | tf_op jit(solution)/shard_map/ppermute | solution.py:473
  219.5 38.4 %collective-permute-start.18 = (bf16[8,192,128]{2,1,0:T(8,128)(2,1)}, bf16[8,192,128]{2,1,0:T(8,128)(2,1)}, u32[]{:S(2)}, u32[]{:S(2)}) collective-permute-start(bf16[8,192,128]{2,1,0:T(8,128)(2,1)} %get-tuple-element.52.refs_1_), channel_id=1, source_target_pairs={{0,6},{1,7},{2,0},{3,1},{4,2},{5,3},{6,4},{7,5},{8,14},{9,15},{10,... | collective-permute-start | bytes 1179656 | tf_op jit(solution)/shard_map/ppermute | solution.py:473
  236.1 38.8 %collective-permute-start.24 = (bf16[8,96,128]{2,1,0:T(8,128)(2,1)}, bf16[8,96,128]{2,1,0:T(8,128)(2,1)S(1)}, u32[]{:S(2)}, u32[]{:S(2)}) collective-permute-start(bf16[8,96,128]{2,1,0:T(8,128)(2,1)} %get-tuple-element.58), channel_id=1, source_target_pairs={{0,6},{1,7},{2,0},{3,1},{4,2},{5,3},{6,4},{7,5},{8,14},{9,15},{10,... | collective-permute-start | bytes 589832 | tf_op jit(solution)/shard_map/ppermute | solution.py:473
  238.3 40.9 %collective-permute-start.25 = (bf16[8,96,128]{2,1,0:T(8,128)(2,1)}, bf16[8,96,128]{2,1,0:T(8,128)(2,1)S(1)}, u32[]{:S(2)}, u32[]{:S(2)}) collective-permute-start(bf16[8,96,128]{2,1,0:T(8,128)(2,1)} %get-tuple-element.59), channel_id=1, source_target_pairs={{0,4},{1,5},{2,6},{3,7},{4,0},{5,1},{6,2},{7,3},{8,12},{9,13},{10,... | collective-permute-start | bytes 589832 | tf_op jit(solution)/shard_map/ppermute | solution.py:473
  254.0 25.2 %collective-permute-start.26 = (bf16[8,96,128]{2,1,0:T(8,128)(2,1)}, bf16[8,96,128]{2,1,0:T(8,128)(2,1)S(1)}, u32[]{:S(2)}, u32[]{:S(2)}) collective-permute-start(bf16[8,96,128]{2,1,0:T(8,128)(2,1)} %get-tuple-element.60), channel_id=1, source_target_pairs={{0,2},{1,3},{2,4},{3,5},{4,6},{5,7},{6,0},{7,1},{8,10},{9,11},{10,... | collective-permute-start | bytes 589832 | tf_op jit(solution)/shard_map/ppermute | solution.py:473
  254.1 35.3 %collective-permute-start.21 = (bf16[8,96,128]{2,1,0:T(8,128)(2,1)}, bf16[8,96,128]{2,1,0:T(8,128)(2,1)}, u32[]{:S(2)}, u32[]{:S(2)}) collective-permute-start(bf16[8,96,128]{2,1,0:T(8,128)(2,1)} %get-tuple-element.55), channel_id=1, source_target_pairs={{0,6},{1,7},{2,0},{3,1},{4,2},{5,3},{6,4},{7,5},{8,14},{9,15},{10,... | collective-permute-start | bytes 589832 | tf_op jit(solution)/shard_map/ppermute | solution.py:473
  257.9 38.3 %collective-permute-start.22 = (bf16[8,96,128]{2,1,0:T(8,128)(2,1)}, bf16[8,96,128]{2,1,0:T(8,128)(2,1)}, u32[]{:S(2)}, u32[]{:S(2)}) collective-permute-start(bf16[8,96,128]{2,1,0:T(8,128)(2,1)} %get-tuple-element.56), channel_id=1, source_target_pairs={{0,4},{1,5},{2,6},{3,7},{4,0},{5,1},{6,2},{7,3},{8,12},{9,13},{10,... | collective-permute-start | bytes 589832 | tf_op jit(solution)/shard_map/ppermute | solution.py:473
  274.9 21.3 %collective-permute-start.23 = (bf16[8,96,128]{2,1,0:T(8,128)(2,1)}, bf16[8,96,128]{2,1,0:T(8,128)(2,1)}, u32[]{:S(2)}, u32[]{:S(2)}) collective-permute-start(bf16[8,96,128]{2,1,0:T(8,128)(2,1)} %get-tuple-element.57), channel_id=1, source_target_pairs={{0,2},{1,3},{2,4},{3,5},{4,6},{5,7},{6,0},{7,1},{8,10},{9,11},{10,... | collective-permute-start | bytes 589832 | tf_op jit(solution)/shard_map/ppermute | solution.py:473
  296.2 10.3 %copy-start.1 = (bf16[16,128,128]{2,1,0:T(8,128)(2,1)S(1)}, bf16[16,128,128]{2,1,0:T(8,128)(2,1)}, u32[]{:S(2)}) copy-start(bf16[16,128,128]{2,1,0:T(8,128)(2,1)} %param.9) | copy-start | bytes 1572868
  (6 other events, 5.6 us)

commit v7 on v6

--- a/solution.py
+++ b/solution.py
@@ -395,7 +395,7 @@
             scratch_shapes=[pltpu.VMEM((6 * LANES, columns), jnp.bfloat16)],
         ),
         input_output_aliases=aliases,
-        compiler_params=pltpu.CompilerParams(vmem_limit_bytes=VMEM),
+        compiler_params=pltpu.CompilerParams(vmem_limit_bytes=VMEM // 3 * 2),
         cost_estimate=LONG,
         name="synthesis_part",
     )(parity, *operands)

time: 308 us -> 307 us (level)
    unnamed x72 -> x74, local copies, waits for them, and re-layouts: 11.2 us -> 13.2 us
where the time goes in v7:
time: 307 us; the launch traced here: 306 us
  Pallas kernels  108 us (35%)
  starting transfers between devices  98.7 us (32%)
  waiting for transfers between devices  74.1 us (24%)
  local copies, waits for them, and re-layouts  20.9 us (7%)
    ppermute x27, starting transfers between devices, turn_along_z(): moved.append(lax.ppermute(slot, 'lev', pairs))  64.1 us
    all_to_all x8, waiting for transfers between devices, exchange_in_plane(): lax.all_to_all(x, ('lat', 'lev'), split_axis=0, concat_axis=0, tiled=True...  45.6 us
    pallas_call x4, Pallas kernels, spectral_chunk(): pl.pallas_call(functools.partial(spectral_kernel, len(pieces)), out_shape...  39.1 us
    all_to_all x8, starting transfers between devices, exchange_in_plane(): lax.all_to_all(x, ('lat', 'lev'), split_axis=0, concat_axis=0, tiled=True...  34.6 us
    ppermute x27, waiting for transfers between devices, turn_along_z(): moved.append(lax.ppermute(slot, 'lev', pairs))  28.6 us
    pallas_call x4, Pallas kernels, fourier_some(): pl.pallas_call(functools.partial(fourier_kernel, len(ready)), out_shape=[...  27.9 us
    pallas_call x2, Pallas kernels, synthesis_part(): pl.pallas_call(functools.partial(synthesis_kernel, len(fields)), out_shap...  18.4 us
    pallas_call x7, Pallas kernels, part_slots(): pl.pallas_call(functools.partial(part_kernel, layers, cuts), out_shape=[j...  15.9 us
  transfers between devices with their start and end apart: 35, of which 10 were waited for; matrix products, arithmetic and copies ran while one was open for 3% of the time, Pallas kernels for 30%

profile of v7, /device:TPU:0, one launch (start us, length us, event | category | flops | bytes accessed | tf_op | source)
XLA Modules:
  0.0 305.7 jit_solution(10859490829726695421)
XLA Ops:
  3.0 7.4 %fourier_some.4 = (bf16[8,192,128]{2,1,0:T(8,128)(2,1)S(1)}, bf16[8,192,128]{2,1,0:T(8,128)(2,1)}, bf16[8,192,128]{2,1,0:T(8,128)(2,1)}, bf16[8,192,128]{2,1,0:T(8,128)(2,1)}) custom-call(s32[1]{0:T(128)} %bitcast.parity_ref, s32[256,1]{1,0:T(8,128)S(1)} %broadcast_in_dim.55.wave_ref, bf16[2,4,2,192,1536]{4,3,2,1,0:T(8,128)(2,1)} %bitcast.82), custom_call_target="tpu_custom_call" | custom-call | flops 9999999827968 | bytes 100000000 | tf_op jit(solution)/shard_map/fourier_some/pallas_call | solution.py:178
  10.4 3.0 collective-permute-start
  13.4 2.6 collective-permute-start.1
  16.0 1.4 collective-permute-start.2
  18.3 7.4 %fourier_some.5 = bf16[32,192,128]{2,1,0:T(8,128)(2,1)} custom-call(s32[1]{0:T(128)} %bitcast.parity_ref, s32[256,1]{1,0:T(8,128)S(1)} %reshape_squeeze.14.wave_ref, bf16[2,4,2,192,1536]{4,3,2,1,0:T(8,128)(2,1)} %bitcast.83, bf16[8,192,128]{2,1,0:T(8,128)(2,1)S(1)} %get-tuple-element.33.refs_0_), custom_call_target="tpu_custom_call" | custom-call | flops 9999999827968 | bytes 100000000 | tf_op jit(solution)/shard_map/fourier_some/pallas_call | solution.py:178
  25.8 4.4 %all-to-all-start = ((bf16[8,768,128]{2,1,0:T(8,128)(2,1)}), bf16[8,768,128]{2,1,0:T(8,128)(2,1)}, u32[]{:S(2)}, u32[]{:S(2)}) async-start(bf16[8,768,128]{2,1,0:T(8,128)(2,1)} %bitcast.9.refs_0_), calls=%async_computation | async-start | bytes 3145728 | tf_op jit(solution)/shard_map/all_to_all | solution.py:478
  31.6 1.3 concatenate.14
  35.3 6.6 %fourier_some.6 = bf16[32,192,128]{2,1,0:T(8,128)(2,1)S(1)} custom-call(s32[1]{0:T(128)} %bitcast.parity_ref, s32[256,1]{1,0:T(8,128)S(1)} %reshape_squeeze.13.wave_ref, bf16[2,4,2,192,1536]{4,3,2,1,0:T(8,128)(2,1)} %bitcast.84, bf16[8,768,128]{2,1,0:T(8,128)(2,1)} %bitcast.9.refs_0_), custom_call_target="tpu_custom_call" | custom-call | flops 9999999827968 | bytes 100000000 | tf_op jit(solution)/shard_map/fourier_some/pallas_call | solution.py:178
  43.0 2.3 part_slots.7
  46.0 1.3 pad_add_fusion.2
  47.4 4.3 %collective-permute-start.5 = (bf16[8,192,128]{2,1,0:T(8,128)(2,1)}, bf16[8,192,128]{2,1,0:T(8,128)(2,1)}, u32[]{:S(2)}, u32[]{:S(2)}) collective-permute-start(bf16[8,192,128]{2,1,0:T(8,128)(2,1)} %after.12.refs_6_), channel_id=1, source_target_pairs={{0,6},{1,7},{2,0},{3,1},{4,2},{5,3},{6,4},{7,5},{8,14},{9,15},{10,... | collective-permute-start | bytes 1179656 | tf_op jit(solution)/shard_map/ppermute | solution.py:473
  52.4 2.5 join_slots.2.refs_0_
  54.9 4.3 %all-to-all-start.1 = ((bf16[8,768,128]{2,1,0:T(8,128)(2,1)}), bf16[8,768,128]{2,1,0:T(8,128)(2,1)}, u32[]{:S(2)}, u32[]{:S(2)}) async-start(bf16[8,768,128]{2,1,0:T(8,128)(2,1)} %after.13.refs_1_), calls=%async_computation.1 | async-start | bytes 3145728 | tf_op jit(solution)/shard_map/all_to_all | solution.py:478
  59.2 2.2 part_slots.8
  61.4 2.3 collective-permute-start.10
  63.7 1.9 collective-permute-start.9
  66.6 6.5 %fourier_some.7 = bf16[32,192,128]{2,1,0:T(8,128)(2,1)S(1)} custom-call(s32[1]{0:T(128)} %bitcast.parity_ref, s32[256,1]{1,0:T(8,128)S(1)} %reshape_squeeze.15.wave_ref, bf16[2,4,2,192,1536]{4,3,2,1,0:T(8,128)(2,1)} %bitcast.85, bf16[8,192,128]{2,1,0:T(8,128)(2,1)S(1)} %copy-done.13), custom_call_target="tpu_custom_call" | custom-call | flops 9999999827968 | bytes 100000000 | tf_op jit(solution)/shard_map/fourier_some/pallas_call | solution.py:178
  73.2 2.1 synthesis_rows.1.refs_2_.refs_16_
  75.3 1.7 copy-done.16
  77.0 3.2 %all-to-all-done.1.refs_1_.refs_0_ = bf16[8,768,128]{2,1,0:T(8,128)(2,1)} async-done(((bf16[8,768,128]{2,1,0:T(8,128)(2,1)}), bf16[8,768,128]{2,1,0:T(8,128)(2,1)}, u32[]{:S(2)}, u32[]{:S(2)}) %all-to-all-start.1) | async-done | bytes 1572896 | tf_op jit(solution)/shard_map/all_to_all | solution.py:478
  80.2 4.4 %all-to-all-start.2 = ((bf16[8,768,128]{2,1,0:T(8,128)(2,1)}), bf16[8,768,128]{2,1,0:T(8,128)(2,1)}, u32[]{:S(2)}, u32[]{:S(2)}) async-start(bf16[8,768,128]{2,1,0:T(8,128)(2,1)} %after.14.refs_5_), calls=%async_computation.2 | async-start | bytes 3145728 | tf_op jit(solution)/shard_map/all_to_all | solution.py:478
  85.0 9.8 %spectral_chunk.4 = bf16[4,8,192,128]{3,2,1,0:T(8,128)(2,1)S(1)} custom-call(s32[2]{0:T(128)S(1)} %get-tuple-element.73.lower_ref, bf16[8,768,128]{2,1,0:T(8,128)(2,1)} %all-to-all-done.1.refs_1_.refs_0_, bf16[32,520,768]{2,1,0:T(8,128)(2,1)} %bitcast.78, bf16[1024,256]{1,0:T(8,128)(2,1)S(1)} %bitcast.60, s32[1032,128]{1,0:T(8,128)S(1)} %broadcast_in_dim.46.refs_3_.refs_6_, ...), custom_call_target="tpu_custom_call" | custom-call | flops 9999999827968 | bytes 100000000 | tf_op jit(solution)/shard_map/spectral_chunk/pallas_call | solution.py:314
  96.0 3.6 %collective-permute-start.11 = (bf16[8,192,128]{2,1,0:T(8,128)(2,1)}, bf16[8,192,128]{2,1,0:T(8,128)(2,1)}, u32[]{:S(2)}, u32[]{:S(2)}) collective-permute-start(bf16[8,192,128]{2,1,0:T(8,128)(2,1)} %get-tuple-element.46), channel_id=1, source_target_pairs={{0,6},{1,7},{2,0},{3,1},{4,2},{5,3},{6,4},{7,5},{8,14},{9,15},{10,... | collective-permute-start | bytes 1179656 | tf_op jit(solution)/shard_map/ppermute | solution.py:473
  99.6 5.1 %collective-permute-done.4.refs_2_ = bf16[8,192,128]{2,1,0:T(8,128)(2,1)} collective-permute-done((bf16[8,192,128]{2,1,0:T(8,128)(2,1)}, bf16[8,192,128]{2,1,0:T(8,128)(2,1)}, u32[]{:S(2)}, u32[]{:S(2)}) %collective-permute-start.4) | collective-permute-done | bytes 393248 | tf_op jit(solution)/shard_map/ppermute | solution.py:473
  104.7 2.5 join_slots.3.refs_2_.refs_0_
  107.2 4.3 %all-to-all-start.3 = ((bf16[8,768,128]{2,1,0:T(8,128)(2,1)}), bf16[8,768,128]{2,1,0:T(8,128)(2,1)}, u32[]{:S(2)}, u32[]{:S(2)}) async-start(bf16[8,768,128]{2,1,0:T(8,128)(2,1)} %after.15.refs_1_), calls=%async_computation.3 | async-start | bytes 3145728 | tf_op jit(solution)/shard_map/all_to_all | solution.py:478
  111.5 2.2 part_slots.9
  114.6 1.9 collective-permute-start.12
  116.5 16.1 %all-to-all-done.3.refs_1_.refs_0_ = bf16[8,768,128]{2,1,0:T(8,128)(2,1)} async-done(((bf16[8,768,128]{2,1,0:T(8,128)(2,1)}), bf16[8,768,128]{2,1,0:T(8,128)(2,1)}, u32[]{:S(2)}, u32[]{:S(2)}) %all-to-all-start.3) | async-done | bytes 1572896 | tf_op jit(solution)/shard_map/all_to_all | solution.py:478
  132.6 4.3 %all-to-all-start.4 = ((bf16[8,768,128]{2,1,0:T(8,128)(2,1)}), bf16[8,768,128]{2,1,0:T(8,128)(2,1)}, u32[]{:S(2)}, u32[]{:S(2)}) async-start(bf16[8,768,128]{2,1,0:T(8,128)(2,1)} %after.16.refs_1_), calls=%async_computation.4 | async-start | bytes 3145728 | tf_op jit(solution)/shard_map/all_to_all | solution.py:478
  136.9 2.3 part_slots.10
  139.2 2.1 collective-permute-start.14
  142.0 1.6 collective-permute-start.6
  144.6 9.7 %spectral_chunk.5 = bf16[4,8,192,128]{3,2,1,0:T(8,128)(2,1)S(1)} custom-call(s32[2]{0:T(128)S(1)} %get-tuple-element.72.lower_ref, bf16[8,768,128]{2,1,0:T(8,128)(2,1)} %all-to-all-done.refs_1_.refs_0_, bf16[8,192,128]{2,1,0:T(8,128)(2,1)} %collective-permute-done.9.refs_1_, bf16[8,192,128]{2,1,0:T(8,128)(2,1)} %collective-permute-done.10.refs_2_, ...), custom_call_target="tpu_custom_call" | custom-call | flops 9999999827968 | bytes 100000000 | tf_op jit(solution)/shard_map/spectral_chunk/pallas_call | solution.py:314
  154.4 1.2 copy-done.3
  155.6 2.3 all-to-all-done.4.refs_1_.refs_0_
  157.9 4.3 %all-to-all-start.5 = ((bf16[8,768,128]{2,1,0:T(8,128)(2,1)}), bf16[8,768,128]{2,1,0:T(8,128)(2,1)}, u32[]{:S(2)}, u32[]{:S(2)}) async-start(bf16[8,768,128]{2,1,0:T(8,128)(2,1)} %after.17.refs_8_), calls=%async_computation.5 | async-start | bytes 3145728 | tf_op jit(solution)/shard_map/all_to_all | solution.py:478
  162.2 1.4 collective-permute-start.8
  163.6 9.8 %spectral_chunk.6 = bf16[4,8,192,128]{3,2,1,0:T(8,128)(2,1)S(1)} custom-call(s32[2]{0:T(128)S(1)} %get-tuple-element.71.lower_ref, bf16[8,768,128]{2,1,0:T(8,128)(2,1)} %all-to-all-done.2.refs_1_.refs_0_, bf16[8,192,128]{2,1,0:T(8,128)(2,1)} %collective-permute-done.12.refs_1_, bf16[8,192,128]{2,1,0:T(8,128)(2,1)} %collective-permute-done.13.refs_2_, ...), custom_call_target="tpu_custom_call" | custom-call | flops 9999999827968 | bytes 100000000 | tf_op jit(solution)/shard_map/spectral_chunk/pallas_call | solution.py:314
  173.4 1.2 copy-done.4
  174.6 8.7 %all-to-all-done.5.refs_1_.refs_0_.refs_4_ = bf16[8,768,128]{2,1,0:T(8,128)(2,1)} async-done(((bf16[8,768,128]{2,1,0:T(8,128)(2,1)}), bf16[8,768,128]{2,1,0:T(8,128)(2,1)}, u32[]{:S(2)}, u32[]{:S(2)}) %all-to-all-start.5) | async-done | bytes 1572896 | tf_op jit(solution)/shard_map/all_to_all | solution.py:478
  183.2 4.3 %all-to-all-start.6 = ((bf16[8,768,128]{2,1,0:T(8,128)(2,1)}), bf16[8,768,128]{2,1,0:T(8,128)(2,1)}, u32[]{:S(2)}, u32[]{:S(2)}) async-start(bf16[8,768,128]{2,1,0:T(8,128)(2,1)} %after.18.refs_1_), calls=%async_computation.6 | async-start | bytes 3145728 | tf_op jit(solution)/shard_map/all_to_all | solution.py:478
  187.5 2.3 part_slots.11
  190.6 2.9 collective-permute-start.15
  194.5 9.8 %spectral_chunk.7 = bf16[4,8,192,128]{3,2,1,0:T(8,128)(2,1)S(1)} custom-call(s32[2]{0:T(128)S(1)} %get-tuple-element.70.lower_ref, bf16[8,768,128]{2,1,0:T(8,128)(2,1)} %all-to-all-done.4.refs_1_.refs_0_, bf16[32,520,768]{2,1,0:T(8,128)(2,1)} %bitcast.81, bf16[1024,256]{1,0:T(8,128)(2,1)S(1)} %bitcast.63, s32[1032,128]{1,0:T(8,128)S(1)} %copy-done.9, ...), custom_call_target="tpu_custom_call" | custom-call | flops 9999999827968 | bytes 100000000 | tf_op jit(solution)/shard_map/spectral_chunk/pallas_call | solution.py:314
  205.5 3.1 %all-to-all-done.6.refs_1_.refs_0_.refs_8_ = bf16[8,768,128]{2,1,0:T(8,128)(2,1)} async-done(((bf16[8,768,128]{2,1,0:T(8,128)(2,1)}), bf16[8,768,128]{2,1,0:T(8,128)(2,1)}, u32[]{:S(2)}, u32[]{:S(2)}) %all-to-all-start.6) | async-done | bytes 1572896 | tf_op jit(solution)/shard_map/all_to_all | solution.py:478
  208.6 4.3 %all-to-all-start.7 = ((bf16[8,768,128]{2,1,0:T(8,128)(2,1)}), bf16[8,768,128]{2,1,0:T(8,128)(2,1)}, u32[]{:S(2)}, u32[]{:S(2)}) async-start(bf16[8,768,128]{2,1,0:T(8,128)(2,1)} %after.19.refs_1_), calls=%async_computation.7 | async-start | bytes 3145728 | tf_op jit(solution)/shard_map/all_to_all | solution.py:478
  212.9 2.3 part_slots.12
  215.2 1.4 collective-permute-start.17
  216.5 1.3 collective-permute-start.19
  217.9 1.7 collective-permute-start.20
  219.6 2.1 collective-permute-start.18
  221.7 12.2 %all-to-all-done.7.refs_0_.refs_12_ = bf16[8,768,128]{2,1,0:T(8,128)(2,1)} async-done(((bf16[8,768,128]{2,1,0:T(8,128)(2,1)}), bf16[8,768,128]{2,1,0:T(8,128)(2,1)}, u32[]{:S(2)}, u32[]{:S(2)}) %all-to-all-start.7) | async-done | bytes 1572896 | tf_op jit(solution)/shard_map/all_to_all | solution.py:478
  233.9 2.2 part_slots.13
  236.1 2.2 collective-permute-start.24
  239.0 15.1 %collective-permute-done.19.refs_10_ = bf16[8,192,128]{2,1,0:T(8,128)(2,1)} collective-permute-done((bf16[8,192,128]{2,1,0:T(8,128)(2,1)}, bf16[8,192,128]{2,1,0:T(8,128)(2,1)}, u32[]{:S(2)}, u32[]{:S(2)}) %collective-permute-start.19) | collective-permute-done | bytes 393248 | tf_op jit(solution)/shard_map/ppermute | solution.py:473
  254.1 3.8 %collective-permute-start.21 = (bf16[8,96,128]{2,1,0:T(8,128)(2,1)}, bf16[8,96,128]{2,1,0:T(8,128)(2,1)}, u32[]{:S(2)}, u32[]{:S(2)}) collective-permute-start(bf16[8,96,128]{2,1,0:T(8,128)(2,1)} %get-tuple-element.55), channel_id=1, source_target_pairs={{0,6},{1,7},{2,0},{3,1},{4,2},{5,3},{6,4},{7,5},{8,14},{9,15},{10,... | collective-permute-start | bytes 589832 | tf_op jit(solution)/shard_map/ppermute | solution.py:473
  258.0 16.9 %collective-permute-start.22 = (bf16[8,96,128]{2,1,0:T(8,128)(2,1)}, bf16[8,96,128]{2,1,0:T(8,128)(2,1)}, u32[]{:S(2)}, u32[]{:S(2)}) collective-permute-start(bf16[8,96,128]{2,1,0:T(8,128)(2,1)} %get-tuple-element.56), channel_id=1, source_target_pairs={{0,4},{1,5},{2,6},{3,7},{4,0},{5,1},{6,2},{7,3},{8,12},{9,13},{10,... | collective-permute-start | bytes 589832 | tf_op jit(solution)/shard_map/ppermute | solution.py:473
  274.9 2.0 collective-permute-start.23
  276.9 2.5 collective-permute-done.25.refs_14_
  279.4 1.9 copy-done.17
  281.2 9.1 %synthesis_part.2.refs_18_ = bf16[2,4,2,192,1536]{4,3,2,1,0:T(8,128)(2,1)} custom-call(s32[1]{0:T(128)} %bitcast.parity_ref, bf16[8,768,128]{2,1,0:T(8,128)(2,1)} %all-to-all-done.3.refs_1_.refs_0_, bf16[8,192,128]{2,1,0:T(8,128)(2,1)} %collective-permute-done.6.refs_1_, bf16[8,192,128]{2,1,0:T(8,128)(2,1)} %collective-permute-done.7.refs_2_, ...), custom_call_target="tpu_custom_call" | custom-call | flops 9999999827968 | bytes 100000000 | tf_op jit(solution)/shard_map/synthesis_part/pallas_call | solution.py:387
  290.4 5.8 %collective-permute-done.22.refs_14_ = bf16[8,96,128]{2,1,0:T(8,128)(2,1)} collective-permute-done((bf16[8,96,128]{2,1,0:T(8,128)(2,1)}, bf16[8,96,128]{2,1,0:T(8,128)(2,1)}, u32[]{:S(2)}, u32[]{:S(2)}) %collective-permute-start.22) | collective-permute-done | bytes 196640 | tf_op jit(solution)/shard_map/ppermute | solution.py:473
  296.2 9.3 %synthesis_part.3 = bf16[2,4,2,192,1536]{4,3,2,1,0:T(8,128)(2,1)} custom-call(s32[1]{0:T(128)} %bitcast.parity_ref, bf16[8,768,128]{2,1,0:T(8,128)(2,1)} %all-to-all-done.3.refs_1_.refs_0_, bf16[8,192,128]{2,1,0:T(8,128)(2,1)} %collective-permute-done.6.refs_1_, ...), custom_call_target="tpu_custom_call", output_to_operand_aliasing={{}: (19, {})} | custom-call | flops 9999999827968 | bytes 100000000 | tf_op jit(solution)/shard_map/synthesis_part/pallas_call | solution.py:387
  (152 shorter events, 18.9 us)
Async XLA Ops:
  0.0 34.1 %copy-start = (bf16[16,128,128]{2,1,0:T(8,128)(2,1)S(1)}, bf16[16,128,128]{2,1,0:T(8,128)(2,1)}, u32[]{:S(2)}) copy-start(bf16[16,128,128]{2,1,0:T(8,128)(2,1)} %param.9) | copy-start | bytes 1572868
  3.0 14.3 %copy-start.20 = (s32[4,4,4,2,2,1]{1,0,4,3,2,5:T(4,128)S(1)}, s32[4,4,4,2,2,1]{1,0,4,3,2,5:T(4,128)}, u32[]{:S(2)}) copy-start(s32[4,4,4,2,2,1]{1,0,4,3,2,5:T(4,128)} %copy-done.19) | copy-start | bytes 3076
  3.0 14.3 %copy-start.22 = (s32[4,4,4,2,2,1]{1,0,4,3,2,5:T(4,128)S(1)}, s32[4,4,4,2,2,1]{1,0,4,3,2,5:T(4,128)}, u32[]{:S(2)}) copy-start(s32[4,4,4,2,2,1]{1,0,4,3,2,5:T(4,128)} %copy-done.21) | copy-start | bytes 3076
  10.4 15.4 %copy-start.18 = (bf16[8,192,128]{2,1,0:T(8,128)(2,1)}, bf16[8,192,128]{2,1,0:T(8,128)(2,1)S(1)}, u32[]{:S(2)}) copy-start(bf16[8,192,128]{2,1,0:T(8,128)(2,1)S(1)} %get-tuple-element.33.refs_0_) | copy-start | bytes 1179652
  10.4 37.0 %collective-permute-start = (bf16[8,192,128]{2,1,0:T(8,128)(2,1)}, bf16[8,192,128]{2,1,0:T(8,128)(2,1)}, u32[]{:S(2)}, u32[]{:S(2)}) collective-permute-start(bf16[8,192,128]{2,1,0:T(8,128)(2,1)} %get-tuple-element.34), channel_id=1, source_target_pairs={{0,2},{1,3},{2,4},{3,5},{4,6},{5,7},{6,0},{7,1},{8,10},{9,11},{10,... | collective-permute-start | bytes 1179656 | tf_op jit(solution)/shard_map/ppermute | solution.py:473
  13.4 34.0 %collective-permute-start.1 = (bf16[8,192,128]{2,1,0:T(8,128)(2,1)}, bf16[8,192,128]{2,1,0:T(8,128)(2,1)}, u32[]{:S(2)}, u32[]{:S(2)}) collective-permute-start(bf16[8,192,128]{2,1,0:T(8,128)(2,1)} %get-tuple-element.35), channel_id=1, source_target_pairs={{0,4},{1,5},{2,6},{3,7},{4,0},{5,1},{6,2},{7,3},{8,12},{9,13},{10,... | collective-permute-start | bytes 1179656 | tf_op jit(solution)/shard_map/ppermute | solution.py:473
  16.0 31.4 %collective-permute-start.2 = (bf16[8,192,128]{2,1,0:T(8,128)(2,1)}, bf16[8,192,128]{2,1,0:T(8,128)(2,1)}, u32[]{:S(2)}, u32[]{:S(2)}) collective-permute-start(bf16[8,192,128]{2,1,0:T(8,128)(2,1)} %get-tuple-element.36), channel_id=1, source_target_pairs={{0,6},{1,7},{2,0},{3,1},{4,2},{5,3},{6,4},{7,5},{8,14},{9,15},{10,... | collective-permute-start | bytes 1179656 | tf_op jit(solution)/shard_map/ppermute | solution.py:473
  25.7 4.5 %copy-start.24 = (s32[1,4,4,2,2,2]{1,0,4,3,2,5:T(1,128)S(1)}, s32[1,4,4,2,2,2]{1,0,4,3,2,5:T(1,128)}, u32[]{:S(2)}) copy-start(s32[1,4,4,2,2,2]{1,0,4,3,2,5:T(1,128)} %copy-done.23) | copy-start | bytes 1540
  25.7 4.6 %copy-start.35 = (s32[256]{0:T(256)S(1)}, s32[256]{0:T(256)}, u32[]{:S(2)}) copy-start(s32[256]{0:T(256)} %param.10) | copy-start | bytes 3076
  25.8 5.2 %copy-start.32 = (s32[512]{0:T(512)S(1)}, s32[512]{0:T(512)}, u32[]{:S(2)}) copy-start(s32[512]{0:T(512)} %param.11) | copy-start | bytes 6148
  25.8 7.3 %copy-start.29 = (s32[1,4,4,2,2,2]{1,0,4,3,2,5:T(1,128)S(1)}, s32[1,4,4,2,2,2]{1,0,4,3,2,5:T(1,128)}, u32[]{:S(2)}) copy-start(s32[1,4,4,2,2,2]{1,0,4,3,2,5:T(1,128)} %get-tuple-element.64) | copy-start | bytes 1540
  25.8 7.3 %copy-start.28 = (s32[1,4,4,2,2,2]{1,0,4,3,2,5:T(1,128)S(1)}, s32[1,4,4,2,2,2]{1,0,4,3,2,5:T(1,128)}, u32[]{:S(2)}) copy-start(s32[1,4,4,2,2,2]{1,0,4,3,2,5:T(1,128)} %get-tuple-element.66) | copy-start | bytes 1540
  25.8 7.3 %copy-start.27 = (s32[1,4,4,2,2,2]{1,0,4,3,2,5:T(1,128)S(1)}, s32[1,4,4,2,2,2]{1,0,4,3,2,5:T(1,128)}, u32[]{:S(2)}) copy-start(s32[1,4,4,2,2,2]{1,0,4,3,2,5:T(1,128)} %get-tuple-element.67) | copy-start | bytes 1540
  25.8 7.7 %copy-start.26 = (s32[1,8,4,8]{2,3,1,0:T(8,128)S(1)}, s32[1,8,4,8]{2,3,1,0:T(8,128)}, u32[]{:S(2)}) copy-start(s32[1,8,4,8]{2,3,1,0:T(8,128)} %get-tuple-element.61) | copy-start | bytes 3076
  25.8 7.8 %copy-start.25 = (s32[1,8,4,8]{2,3,1,0:T(8,128)S(1)}, s32[1,8,4,8]{2,3,1,0:T(8,128)}, u32[]{:S(2)}) copy-start(s32[1,8,4,8]{2,3,1,0:T(8,128)} %get-tuple-element.63) | copy-start | bytes 3076
  25.8 29.0 %all-to-all-start = ((bf16[8,768,128]{2,1,0:T(8,128)(2,1)}), bf16[8,768,128]{2,1,0:T(8,128)(2,1)}, u32[]{:S(2)}, u32[]{:S(2)}) async-start(bf16[8,768,128]{2,1,0:T(8,128)(2,1)} %bitcast.9.refs_0_), calls=%async_computation | async-start | bytes 3145728 | tf_op jit(solution)/shard_map/all_to_all | solution.py:478
  43.0 2.3 copy-start.33
  43.0 4.3 %copy-start.34 = (s32[8]{0:T(128)S(1)}, s32[8]{0:T(128)}, u32[]{:S(2)}) copy-start(s32[8]{0:T(128)} %dynamic_slice.9) | copy-start | bytes 100
  47.4 48.6 %collective-permute-start.5 = (bf16[8,192,128]{2,1,0:T(8,128)(2,1)}, bf16[8,192,128]{2,1,0:T(8,128)(2,1)}, u32[]{:S(2)}, u32[]{:S(2)}) collective-permute-start(bf16[8,192,128]{2,1,0:T(8,128)(2,1)} %after.12.refs_6_), channel_id=1, source_target_pairs={{0,6},{1,7},{2,0},{3,1},{4,2},{5,3},{6,4},{7,5},{8,14},{9,15},{10,... | collective-permute-start | bytes 1179656 | tf_op jit(solution)/shard_map/ppermute | solution.py:473
  51.8 52.9 %collective-permute-start.4 = (bf16[8,192,128]{2,1,0:T(8,128)(2,1)}, bf16[8,192,128]{2,1,0:T(8,128)(2,1)}, u32[]{:S(2)}, u32[]{:S(2)}) collective-permute-start(bf16[8,192,128]{2,1,0:T(8,128)(2,1)} %after.11.refs_5_), channel_id=1, source_target_pairs={{0,4},{1,5},{2,6},{3,7},{4,0},{5,1},{6,2},{7,3},{8,12},{9,13},{10,... | collective-permute-start | bytes 1179656 | tf_op jit(solution)/shard_map/ppermute | solution.py:473
  52.2 52.5 %collective-permute-start.3 = (bf16[8,192,128]{2,1,0:T(8,128)(2,1)}, bf16[8,192,128]{2,1,0:T(8,128)(2,1)}, u32[]{:S(2)}, u32[]{:S(2)}) collective-permute-start(bf16[8,192,128]{2,1,0:T(8,128)(2,1)} %after.10.refs_4_), channel_id=1, source_target_pairs={{0,2},{1,3},{2,4},{3,5},{4,6},{5,7},{6,0},{7,1},{8,10},{9,11},{10,... | collective-permute-start | bytes 1179656 | tf_op jit(solution)/shard_map/ppermute | solution.py:473
  54.9 25.3 %all-to-all-start.1 = ((bf16[8,768,128]{2,1,0:T(8,128)(2,1)}), bf16[8,768,128]{2,1,0:T(8,128)(2,1)}, u32[]{:S(2)}, u32[]{:S(2)}) async-start(bf16[8,768,128]{2,1,0:T(8,128)(2,1)} %after.13.refs_1_), calls=%async_computation.1 | async-start | bytes 3145728 | tf_op jit(solution)/shard_map/all_to_all | solution.py:478
  61.4 77.8 %collective-permute-start.10 = (bf16[8,192,128]{2,1,0:T(8,128)(2,1)}, bf16[8,192,128]{2,1,0:T(8,128)(2,1)}, u32[]{:S(2)}, u32[]{:S(2)}) collective-permute-start(bf16[8,192,128]{2,1,0:T(8,128)(2,1)} %get-tuple-element.45), channel_id=1, source_target_pairs={{0,4},{1,5},{2,6},{3,7},{4,0},{5,1},{6,2},{7,3},{8,12},{9,13},{10,... | collective-permute-start | bytes 1179656 | tf_op jit(solution)/shard_map/ppermute | solution.py:473
  63.7 78.3 %collective-permute-start.9 = (bf16[8,192,128]{2,1,0:T(8,128)(2,1)}, bf16[8,192,128]{2,1,0:T(8,128)(2,1)}, u32[]{:S(2)}, u32[]{:S(2)}) collective-permute-start(bf16[8,192,128]{2,1,0:T(8,128)(2,1)} %get-tuple-element.40.refs_0_), channel_id=1, source_target_pairs={{0,2},{1,3},{2,4},{3,5},{4,6},{5,7},{6,0},{7,1},{8,10},{9,11},{10,... | collective-permute-start | bytes 1179656 | tf_op jit(solution)/shard_map/ppermute | solution.py:473
  73.2 2.1 copy-start.6
  75.3 1.7 copy-start.16
  80.2 4.5 %copy-start.31 = (s32[520]{0:T(1024)S(1)}, s32[520]{0:T(1024)}, u32[]{:S(2)}) copy-start(s32[520]{0:T(1024)} %pad_add_fusion.2) | copy-start | bytes 6244
  80.2 4.6 %copy-start.30 = (s32[1032]{0:T(1024)S(1)}, s32[1032]{0:T(1024)}, u32[]{:S(2)}) copy-start(s32[1032]{0:T(1024)} %concatenate.14) | copy-start | bytes 12388
  80.2 4.8 %copy-start.7 = (bf16[8,768,128]{2,1,0:T(8,128)(2,1)S(1)}, bf16[8,768,128]{2,1,0:T(8,128)(2,1)}, u32[]{:S(2)}) copy-start(bf16[8,768,128]{2,1,0:T(8,128)(2,1)} %after.14.refs_5_) | copy-start | bytes 4718596
  80.2 27.0 %all-to-all-start.2 = ((bf16[8,768,128]{2,1,0:T(8,128)(2,1)}), bf16[8,768,128]{2,1,0:T(8,128)(2,1)}, u32[]{:S(2)}, u32[]{:S(2)}) async-start(bf16[8,768,128]{2,1,0:T(8,128)(2,1)} %after.14.refs_5_), calls=%async_computation.2 | async-start | bytes 3145728 | tf_op jit(solution)/shard_map/all_to_all | solution.py:478
  84.8 10.0 %copy-start.10 = (s32[520,128]{1,0:T(8,128)}, s32[520,128]{1,0:T(8,128)S(1)}, u32[]{:S(2)}) copy-start(s32[520,128]{1,0:T(8,128)S(1)} %broadcast_in_dim.47.refs_4_.refs_7_) | copy-start | bytes 798724
  85.0 9.8 %copy-start.8 = (s32[1032,128]{1,0:T(8,128)}, s32[1032,128]{1,0:T(8,128)S(1)}, u32[]{:S(2)}) copy-start(s32[1032,128]{1,0:T(8,128)S(1)} %broadcast_in_dim.46.refs_3_.refs_6_) | copy-start | bytes 1585156
  94.8 1.1 copy-start.2
  96.0 45.3 %collective-permute-start.11 = (bf16[8,192,128]{2,1,0:T(8,128)(2,1)}, bf16[8,192,128]{2,1,0:T(8,128)(2,1)}, u32[]{:S(2)}, u32[]{:S(2)}) collective-permute-start(bf16[8,192,128]{2,1,0:T(8,128)(2,1)} %get-tuple-element.46), channel_id=1, source_target_pairs={{0,6},{1,7},{2,0},{3,1},{4,2},{5,3},{6,4},{7,5},{8,14},{9,15},{10,... | collective-permute-start | bytes 1179656 | tf_op jit(solution)/shard_map/ppermute | solution.py:473
  107.2 25.4 %all-to-all-start.3 = ((bf16[8,768,128]{2,1,0:T(8,128)(2,1)}), bf16[8,768,128]{2,1,0:T(8,128)(2,1)}, u32[]{:S(2)}, u32[]{:S(2)}) async-start(bf16[8,768,128]{2,1,0:T(8,128)(2,1)} %after.15.refs_1_), calls=%async_computation.3 | async-start | bytes 3145728 | tf_op jit(solution)/shard_map/all_to_all | solution.py:478
  113.8 48.4 %collective-permute-start.13 = (bf16[8,192,128]{2,1,0:T(8,128)(2,1)}, bf16[8,192,128]{2,1,0:T(8,128)(2,1)}, u32[]{:S(2)}, u32[]{:S(2)}) collective-permute-start(bf16[8,192,128]{2,1,0:T(8,128)(2,1)} %get-tuple-element.47), channel_id=1, source_target_pairs={{0,4},{1,5},{2,6},{3,7},{4,0},{5,1},{6,2},{7,3},{8,12},{9,13},{10,... | collective-permute-start | bytes 1179656 | tf_op jit(solution)/shard_map/ppermute | solution.py:473
  114.6 49.0 %collective-permute-start.12 = (bf16[8,192,128]{2,1,0:T(8,128)(2,1)}, bf16[8,192,128]{2,1,0:T(8,128)(2,1)}, u32[]{:S(2)}, u32[]{:S(2)}) collective-permute-start(bf16[8,192,128]{2,1,0:T(8,128)(2,1)} %get-tuple-element.41.refs_2_), channel_id=1, source_target_pairs={{0,2},{1,3},{2,4},{3,5},{4,6},{5,7},{6,0},{7,1},{8,10},{9,11},{10,... | collective-permute-start | bytes 1179656 | tf_op jit(solution)/shard_map/ppermute | solution.py:473
  132.6 25.3 %all-to-all-start.4 = ((bf16[8,768,128]{2,1,0:T(8,128)(2,1)}), bf16[8,768,128]{2,1,0:T(8,128)(2,1)}, u32[]{:S(2)}, u32[]{:S(2)}) async-start(bf16[8,768,128]{2,1,0:T(8,128)(2,1)} %after.16.refs_1_), calls=%async_computation.4 | async-start | bytes 3145728 | tf_op jit(solution)/shard_map/all_to_all | solution.py:478
  136.8 6.8 %copy-start.9 = (s32[1032,128]{1,0:T(8,128)S(1)}, s32[1032,128]{1,0:T(8,128)}, u32[]{:S(2)}) copy-start(s32[1032,128]{1,0:T(8,128)} %copy-done.8) | copy-start | bytes 1585156
  136.9 6.8 %copy-start.11 = (s32[520,128]{1,0:T(8,128)S(1)}, s32[520,128]{1,0:T(8,128)}, u32[]{:S(2)}) copy-start(s32[520,128]{1,0:T(8,128)} %copy-done.10) | copy-start | bytes 798724
  139.2 24.4 %collective-permute-start.14 = (bf16[8,192,128]{2,1,0:T(8,128)(2,1)}, bf16[8,192,128]{2,1,0:T(8,128)(2,1)}, u32[]{:S(2)}, u32[]{:S(2)}) collective-permute-start(bf16[8,192,128]{2,1,0:T(8,128)(2,1)} %get-tuple-element.48), channel_id=1, source_target_pairs={{0,6},{1,7},{2,0},{3,1},{4,2},{5,3},{6,4},{7,5},{8,14},{9,15},{10,... | collective-permute-start | bytes 1179656 | tf_op jit(solution)/shard_map/ppermute | solution.py:473
  141.3 73.8 %collective-permute-start.7 = (bf16[8,192,128]{2,1,0:T(8,128)(2,1)}, bf16[8,192,128]{2,1,0:T(8,128)(2,1)}, u32[]{:S(2)}, u32[]{:S(2)}) collective-permute-start(bf16[8,192,128]{2,1,0:T(8,128)(2,1)} %get-tuple-element.43), channel_id=1, source_target_pairs={{0,4},{1,5},{2,6},{3,7},{4,0},{5,1},{6,2},{7,3},{8,12},{9,13},{10,... | collective-permute-start | bytes 1179656 | tf_op jit(solution)/shard_map/ppermute | solution.py:473
  142.0 75.9 %collective-permute-start.6 = (bf16[8,192,128]{2,1,0:T(8,128)(2,1)}, bf16[8,192,128]{2,1,0:T(8,128)(2,1)}, u32[]{:S(2)}, u32[]{:S(2)}) collective-permute-start(bf16[8,192,128]{2,1,0:T(8,128)(2,1)} %get-tuple-element.42.refs_8_), channel_id=1, source_target_pairs={{0,6},{1,7},{2,0},{3,1},{4,2},{5,3},{6,4},{7,5},{8,14},{9,15},{10,... | collective-permute-start | bytes 1179656 | tf_op jit(solution)/shard_map/ppermute | solution.py:473
  154.4 1.2 copy-start.3
  157.9 25.3 %all-to-all-start.5 = ((bf16[8,768,128]{2,1,0:T(8,128)(2,1)}), bf16[8,768,128]{2,1,0:T(8,128)(2,1)}, u32[]{:S(2)}, u32[]{:S(2)}) async-start(bf16[8,768,128]{2,1,0:T(8,128)(2,1)} %after.17.refs_8_), calls=%async_computation.5 | async-start | bytes 3145728 | tf_op jit(solution)/shard_map/all_to_all | solution.py:478
  162.2 54.4 %collective-permute-start.8 = (bf16[8,192,128]{2,1,0:T(8,128)(2,1)}, bf16[8,192,128]{2,1,0:T(8,128)(2,1)}, u32[]{:S(2)}, u32[]{:S(2)}) collective-permute-start(bf16[8,192,128]{2,1,0:T(8,128)(2,1)} %get-tuple-element.44), channel_id=1, source_target_pairs={{0,2},{1,3},{2,4},{3,5},{4,6},{5,7},{6,0},{7,1},{8,10},{9,11},{10,... | collective-permute-start | bytes 1179656 | tf_op jit(solution)/shard_map/ppermute | solution.py:473
  173.3 1.2 copy-start.4
  183.2 25.4 %all-to-all-start.6 = ((bf16[8,768,128]{2,1,0:T(8,128)(2,1)}), bf16[8,768,128]{2,1,0:T(8,128)(2,1)}, u32[]{:S(2)}, u32[]{:S(2)}) async-start(bf16[8,768,128]{2,1,0:T(8,128)(2,1)} %after.18.refs_1_), calls=%async_computation.6 | async-start | bytes 3145728 | tf_op jit(solution)/shard_map/all_to_all | solution.py:478
  189.8 29.8 %collective-permute-start.16 = (bf16[8,192,128]{2,1,0:T(8,128)(2,1)}, bf16[8,192,128]{2,1,0:T(8,128)(2,1)}, u32[]{:S(2)}, u32[]{:S(2)}) collective-permute-start(bf16[8,192,128]{2,1,0:T(8,128)(2,1)} %get-tuple-element.50), channel_id=1, source_target_pairs={{0,4},{1,5},{2,6},{3,7},{4,0},{5,1},{6,2},{7,3},{8,12},{9,13},{10,... | collective-permute-start | bytes 1179656 | tf_op jit(solution)/shard_map/ppermute | solution.py:473
  190.6 47.7 %collective-permute-start.15 = (bf16[8,192,128]{2,1,0:T(8,128)(2,1)}, bf16[8,192,128]{2,1,0:T(8,128)(2,1)}, u32[]{:S(2)}, u32[]{:S(2)}) collective-permute-start(bf16[8,192,128]{2,1,0:T(8,128)(2,1)} %get-tuple-element.49.refs_5_), channel_id=1, source_target_pairs={{0,6},{1,7},{2,0},{3,1},{4,2},{5,3},{6,4},{7,5},{8,14},{9,15},{10,... | collective-permute-start | bytes 1179656 | tf_op jit(solution)/shard_map/ppermute | solution.py:473
  204.3 1.2 copy-start.5
  208.6 25.3 %all-to-all-start.7 = ((bf16[8,768,128]{2,1,0:T(8,128)(2,1)}), bf16[8,768,128]{2,1,0:T(8,128)(2,1)}, u32[]{:S(2)}, u32[]{:S(2)}) async-start(bf16[8,768,128]{2,1,0:T(8,128)(2,1)} %after.19.refs_1_), calls=%async_computation.7 | async-start | bytes 3145728 | tf_op jit(solution)/shard_map/all_to_all | solution.py:478
  215.2 21.0 %collective-permute-start.17 = (bf16[8,192,128]{2,1,0:T(8,128)(2,1)}, bf16[8,192,128]{2,1,0:T(8,128)(2,1)}, u32[]{:S(2)}, u32[]{:S(2)}) collective-permute-start(bf16[8,192,128]{2,1,0:T(8,128)(2,1)} %get-tuple-element.51), channel_id=1, source_target_pairs={{0,2},{1,3},{2,4},{3,5},{4,6},{5,7},{6,0},{7,1},{8,10},{9,11},{10,... | collective-permute-start | bytes 1179656 | tf_op jit(solution)/shard_map/ppermute | solution.py:473
  216.5 37.6 %collective-permute-start.19 = (bf16[8,192,128]{2,1,0:T(8,128)(2,1)}, bf16[8,192,128]{2,1,0:T(8,128)(2,1)}, u32[]{:S(2)}, u32[]{:S(2)}) collective-permute-start(bf16[8,192,128]{2,1,0:T(8,128)(2,1)} %get-tuple-element.53), channel_id=1, source_target_pairs={{0,4},{1,5},{2,6},{3,7},{4,0},{5,1},{6,2},{7,3},{8,12},{9,13},{10,... | collective-permute-start | bytes 1179656 | tf_op jit(solution)/shard_map/ppermute | solution.py:473
  217.9 36.2 %collective-permute-start.20 = (bf16[8,192,128]{2,1,0:T(8,128)(2,1)}, bf16[8,192,128]{2,1,0:T(8,128)(2,1)}, u32[]{:S(2)}, u32[]{:S(2)}) collective-permute-start(bf16[8,192,128]{2,1,0:T(8,128)(2,1)} %get-tuple-element.54), channel_id=1, source_target_pairs={{0,2},{1,3},{2,4},{3,5},{4,6},{5,7},{6,0},{7,1},{8,10},{9,11},{10,... | collective-permute-start | bytes 1179656 | tf_op jit(solution)/shard_map/ppermute | solution.py:473
  219.6 38.4 %collective-permute-start.18 = (bf16[8,192,128]{2,1,0:T(8,128)(2,1)}, bf16[8,192,128]{2,1,0:T(8,128)(2,1)}, u32[]{:S(2)}, u32[]{:S(2)}) collective-permute-start(bf16[8,192,128]{2,1,0:T(8,128)(2,1)} %get-tuple-element.52.refs_1_), channel_id=1, source_target_pairs={{0,6},{1,7},{2,0},{3,1},{4,2},{5,3},{6,4},{7,5},{8,14},{9,15},{10,... | collective-permute-start | bytes 1179656 | tf_op jit(solution)/shard_map/ppermute | solution.py:473
  236.1 38.7 %collective-permute-start.24 = (bf16[8,96,128]{2,1,0:T(8,128)(2,1)}, bf16[8,96,128]{2,1,0:T(8,128)(2,1)S(1)}, u32[]{:S(2)}, u32[]{:S(2)}) collective-permute-start(bf16[8,96,128]{2,1,0:T(8,128)(2,1)} %get-tuple-element.58), channel_id=1, source_target_pairs={{0,6},{1,7},{2,0},{3,1},{4,2},{5,3},{6,4},{7,5},{8,14},{9,15},{10,... | collective-permute-start | bytes 589832 | tf_op jit(solution)/shard_map/ppermute | solution.py:473
  238.3 41.0 %collective-permute-start.25 = (bf16[8,96,128]{2,1,0:T(8,128)(2,1)}, bf16[8,96,128]{2,1,0:T(8,128)(2,1)S(1)}, u32[]{:S(2)}, u32[]{:S(2)}) collective-permute-start(bf16[8,96,128]{2,1,0:T(8,128)(2,1)} %get-tuple-element.59), channel_id=1, source_target_pairs={{0,4},{1,5},{2,6},{3,7},{4,0},{5,1},{6,2},{7,3},{8,12},{9,13},{10,... | collective-permute-start | bytes 589832 | tf_op jit(solution)/shard_map/ppermute | solution.py:473
  254.1 25.2 %collective-permute-start.26 = (bf16[8,96,128]{2,1,0:T(8,128)(2,1)}, bf16[8,96,128]{2,1,0:T(8,128)(2,1)S(1)}, u32[]{:S(2)}, u32[]{:S(2)}) collective-permute-start(bf16[8,96,128]{2,1,0:T(8,128)(2,1)} %get-tuple-element.60), channel_id=1, source_target_pairs={{0,2},{1,3},{2,4},{3,5},{4,6},{5,7},{6,0},{7,1},{8,10},{9,11},{10,... | collective-permute-start | bytes 589832 | tf_op jit(solution)/shard_map/ppermute | solution.py:473
  254.1 36.2 %collective-permute-start.21 = (bf16[8,96,128]{2,1,0:T(8,128)(2,1)}, bf16[8,96,128]{2,1,0:T(8,128)(2,1)}, u32[]{:S(2)}, u32[]{:S(2)}) collective-permute-start(bf16[8,96,128]{2,1,0:T(8,128)(2,1)} %get-tuple-element.55), channel_id=1, source_target_pairs={{0,6},{1,7},{2,0},{3,1},{4,2},{5,3},{6,4},{7,5},{8,14},{9,15},{10,... | collective-permute-start | bytes 589832 | tf_op jit(solution)/shard_map/ppermute | solution.py:473
  258.0 38.3 %collective-permute-start.22 = (bf16[8,96,128]{2,1,0:T(8,128)(2,1)}, bf16[8,96,128]{2,1,0:T(8,128)(2,1)}, u32[]{:S(2)}, u32[]{:S(2)}) collective-permute-start(bf16[8,96,128]{2,1,0:T(8,128)(2,1)} %get-tuple-element.56), channel_id=1, source_target_pairs={{0,4},{1,5},{2,6},{3,7},{4,0},{5,1},{6,2},{7,3},{8,12},{9,13},{10,... | collective-permute-start | bytes 589832 | tf_op jit(solution)/shard_map/ppermute | solution.py:473
  274.9 21.4 %collective-permute-start.23 = (bf16[8,96,128]{2,1,0:T(8,128)(2,1)}, bf16[8,96,128]{2,1,0:T(8,128)(2,1)}, u32[]{:S(2)}, u32[]{:S(2)}) collective-permute-start(bf16[8,96,128]{2,1,0:T(8,128)(2,1)} %get-tuple-element.57), channel_id=1, source_target_pairs={{0,2},{1,3},{2,4},{3,5},{4,6},{5,7},{6,0},{7,1},{8,10},{9,11},{10,... | collective-permute-start | bytes 589832 | tf_op jit(solution)/shard_map/ppermute | solution.py:473
  279.4 1.9 copy-start.17
  296.2 9.3 %copy-start.1 = (bf16[16,128,128]{2,1,0:T(8,128)(2,1)S(1)}, bf16[16,128,128]{2,1,0:T(8,128)(2,1)}, u32[]{:S(2)}) copy-start(bf16[16,128,128]{2,1,0:T(8,128)(2,1)} %param.9) | copy-start | bytes 1572868
  (7 other events, 6.7 us)
